TPU v7x, 256 devices: a whole 4x4x8 slice. The times are simulated.
256 devices in a mesh: row: 16 (over x_lo, y, core), col: 16 (over z, x_hi).
Axes of the slice: x: 4 (x_hi: 2, x_lo: 2; x = x_hi * 2 + x_lo), y: 4, z: 8, core: 2. Of those that a mesh axis runs over, the one named last changes fastest.
Arguments:
- images: bfloat16 [1152, 16384], P('col', 'row')
- texts: bfloat16 [1152, 16384], P('row', 'col')
- pairs: int32 [16384], P('row'), may hold values from 0 to 16383, as said below
- log_scale: float32 [1], replicated, may hold values from 2 to 2.6
- bias: float32 [1], replicated, may hold values from -8 to -6
Outputs:
- row_loss: float32 [16384], P('row')
- image_grad: float32 [1152, 16384], P('col', 'row')
- text_grad: float32 [1152, 16384], P('row', 'col')
Inputs may be any that keep to these rules, and one draw needn't show every extreme that they name: pairs is a permutation of the 16384 caption indices.
All inputs are finite; a program needn't handle non-finite values.
Results may differ from a plain program's by a relative error of at most 0.0095.
Values may be sent and summed in bfloat16 or wider, within the bound.
No kernel may reach another device: no remote copies, remote signals or barrier semaphores. Data moves between devices by JAX's collectives and lax.ppermute only.
A program may use at most 64 MiB of HBM per device.

v0:
```python
import jax
import jax.numpy as jnp
from jax import lax
from jax.sharding import PartitionSpec as P

EPS = 1e-06


def square_sums(values):
    wide = values.astype(jnp.float32)
    return jnp.sum(wide * wide, axis=0)


def shards(images, texts, pairs, log_scale, bias):
    scale = jnp.exp(log_scale[0])
    shift = bias[0]
    img_full = lax.all_gather(images, "col", axis=0, tiled=True)
    txt_full = lax.all_gather(texts, "row", axis=0, tiled=True)
    img_norm = jnp.sqrt(square_sums(img_full) + EPS)
    txt_norm = jnp.sqrt(square_sums(txt_full) + EPS)
    img_unit = (img_full.astype(jnp.float32) / img_norm[None, :]).astype(jnp.bfloat16)
    txt_unit = (txt_full.astype(jnp.float32) / txt_norm[None, :]).astype(jnp.bfloat16)
    txt_count = txt_unit.shape[1]
    columns = lax.axis_index("col") * txt_count + jnp.arange(txt_count, dtype=jnp.int32)
    logits = (
        lax.dot_general(
            img_unit, txt_unit, (((0,), (0,)), ((), ())), preferred_element_type=jnp.float32
        )
        * scale
        + shift
    )
    sign = jnp.where(pairs[:, None] == columns[None, :], 1.0, -1.0).astype(jnp.float32)
    loss_part = jnp.sum(jax.nn.softplus(-sign * logits), axis=1)
    coeff = (-sign * jax.nn.sigmoid(-sign * logits) * scale).astype(jnp.bfloat16)
    img_pull = lax.dot_general(
        txt_unit, coeff, (((1,), (1,)), ((), ())), preferred_element_type=jnp.float32
    )
    txt_pull = jnp.dot(img_unit, coeff, preferred_element_type=jnp.float32)
    img_wide = img_unit.astype(jnp.float32)
    txt_wide = txt_unit.astype(jnp.float32)
    img_inner = jnp.sum(img_wide * img_pull, axis=0)
    txt_inner = jnp.sum(txt_wide * txt_pull, axis=0)
    img_term = (img_pull - img_wide * img_inner[None, :]) / img_norm[None, :]
    txt_term = (txt_pull - txt_wide * txt_inner[None, :]) / txt_norm[None, :]
    row_loss = lax.psum(loss_part, "col")
    image_grad = lax.psum_scatter(img_term, "col", scatter_dimension=0, tiled=True)
    text_grad = lax.psum_scatter(txt_term, "row", scatter_dimension=0, tiled=True)
    return (row_loss, image_grad, text_grad)


def solution(mesh):
    return jax.shard_map(
        shards,
        mesh=mesh,
        in_specs=(P("col", "row"), P("row", "col"), P("row"), P(), P()),
        out_specs=(P("row"), P("col", "row"), P("row", "col")),
        check_vma=False,
    )
```

profile of v0, /device:TPU:8, one launch (start us, length us, event | category | flops | bytes accessed | tf_op | source)
XLA Modules:
  0.0 448.6 jit_solution(16425954692476607474)
XLA Ops:
  7.2 0.0 copy-start.3
  7.2 0.0 all-gather.5.cloned.1.call-start
  7.2 0.7 all-gather.5.cloned.1.call-update
  7.9 0.0 all-gather.3.cloned.1.call-start
  8.0 0.7 all-gather.3.cloned.1.call-update
  8.7 0.0 reduce-scatter.5.cloned.1.call-start
  10.1 39.3 %all-gather.5.cloned.1.call-done = bf16[1152,1024]{1,0:T(8,128)(2,1)} async-done(((bf16[72,1024]{1,0:T(8,128)(2,1)}), bf16[1152,1024]{1,0:T(8,128)(2,1)}) %all-gather.5.cloned.1.call-update) | async-done | bytes 2359312 | tf_op jit(solution)/shard_map/all_gather | solution.py:18
  49.4 0.0 copy-start
  49.4 2.3 fusion.2
  51.7 88.2 %all-gather.3.cloned.1.call-done = bf16[1152,1024]{1,0:T(8,128)(2,1)} async-done(((bf16[72,1024]{1,0:T(8,128)(2,1)}), bf16[1152,1024]{1,0:T(8,128)(2,1)}) %all-gather.3.cloned.1.call-update) | async-done | bytes 2359312 | tf_op jit(solution)/shard_map/all_gather | solution.py:17
  139.9 2.2 fusion
  142.1 0.0 copy-done.3
  142.1 0.0 copy-done
  142.1 0.0 copy-start.1
  142.1 8.6 %multiply_convert_fusion = (bf16[1024,1024]{0,1:T(8,128)(2,1)S(1)}, f32[1024]{0:T(1024)S(1)}) fusion(f32[]{:T(128)} %bitcast.4, f32[]{:T(128)} %bitcast, s32[1024]{0:T(1024)S(1)} %copy-done.3, s32[1024]{0:T(1024)S(1)} %iota_add_fusion, bf16[1152,1024]{1,0:T(8,128)(2,1)S(1)} %copy-done, f32[1024]{0:T(1024)S(1)} %add_sqrt_fusion, ...), kind=kOutput, calls=%fused_computation.20 | convolution fusion | flops 2442918912 | bytes 6836232 | tf_op jit(solution)/shard_map/dot_general | solution.py:26
  150.8 0.0 copy-start.4
  150.8 0.0 copy-done.1
  150.8 2.8 fusion.7
  153.6 0.0 copy-done.4
  153.6 3.1 fusion.9
  156.7 0.0 reduce-scatter.5.cloned.1.call-update
  156.7 0.2 reduce-scatter.3.cloned.1.call-start
  156.9 0.0 copy-start.2
  156.9 5.2 %fusion.4 = (f32[1024]{0:T(1024)S(1)}, f32[1152,1024]{1,0:T(8,128)S(1)}) fusion(f32[1024]{0:T(1024)S(1)} %add_sqrt_fusion.1, bf16[1152,1024]{1,0:T(8,128)(2,1)} %all-gather.3.cloned.1.call-done, bf16[1024,1024]{0,1:T(8,128)(2,1)} %copy-done.4, bf16[1152,1024]{1,0:T(8,128)(2,1)S(1)} %copy-done, f32[1024]{0:T(1024)S(1)} %add_sqrt_fusion), kind=kOutput, calls=%fused_computation.13 | convolution fusion | flops 2426534912 | bytes 11546624 | tf_op jit(solution)/shard_map/dot_general | solution.py:35
  162.1 0.0 copy-done.2
  162.2 3.1 fusion.6
  165.3 0.0 reduce-scatter.3.cloned.1.call-update
  165.3 38.9 %psum.7 = f32[1024]{0:T(1024)} all-reduce(f32[1024]{0:T(1024)S(1)} %get-tuple-element.4), channel_id=1, replica_groups=mesh['row'=16,'col'=16] {'col'}, use_global_device_ids=true, to_apply=%region_3.4 | all-reduce | flops 1024 | bytes 8192 | tf_op jit(solution)/shard_map/psum | solution.py:45
  204.2 16.3 %reduce-scatter.5.cloned.1.call-done = f32[72,1024]{1,0:T(8,128)} async-done(((f32[1152,1024]{1,0:T(8,128)}), f32[72,1024]{1,0:T(8,128)}) %reduce-scatter.5.cloned.1.call-update) | async-done | bytes 294928 | tf_op jit(solution)/shard_map/reduce_scatter | solution.py:47
  220.5 221.6 %reduce-scatter.3.cloned.1.call-done = f32[72,1024]{1,0:T(8,128)} async-done(((f32[1152,1024]{1,0:T(8,128)}), f32[72,1024]{1,0:T(8,128)}) %reduce-scatter.3.cloned.1.call-update) | async-done | bytes 294928 | tf_op jit(solution)/shard_map/reduce_scatter | solution.py:46
  (3 shorter events, 0.0 us)
Async XLA Ops:
  7.2 134.9 %copy-start.3 = (s32[1024]{0:T(1024)S(1)}, s32[1024]{0:T(1024)}, u32[]{:S(2)}) copy-start(s32[1024]{0:T(1024)} %param.7) | copy-start | bytes 12292
  7.2 42.2 %all-gather.5.cloned.1.call-start = ((), (), s32[]{:S(2)}) async-start(), calls=%async_computation.3 | async-start | bytes 2506752 | tf_op jit(solution)/shard_map/all_gather | solution.py:18
  7.9 132.0 %all-gather.3.cloned.1.call-start = ((), (), s32[]{:S(2)}) async-start(), calls=%async_computation.2 | async-start | bytes 2506752 | tf_op jit(solution)/shard_map/all_gather | solution.py:17
  8.7 211.8 %reduce-scatter.5.cloned.1.call-start = ((), (), s32[]{:S(2)}) async-start(), calls=%async_computation.5 | async-start | bytes 5013504 | tf_op jit(solution)/shard_map/reduce_scatter | solution.py:47
  49.4 92.7 %copy-start = (bf16[1152,1024]{1,0:T(8,128)(2,1)S(1)}, bf16[1152,1024]{1,0:T(8,128)(2,1)}, u32[]{:S(2)}) copy-start(bf16[1152,1024]{1,0:T(8,128)(2,1)} %all-gather.5.cloned.1.call-done) | copy-start | bytes 7077892
  142.1 8.7 %copy-start.1 = (bf16[1152,1024]{1,0:T(8,128)(2,1)S(1)}, bf16[1152,1024]{1,0:T(8,128)(2,1)}, u32[]{:S(2)}) copy-start(bf16[1152,1024]{1,0:T(8,128)(2,1)} %all-gather.3.cloned.1.call-done) | copy-start | bytes 7077892
  150.8 2.8 copy-start.4
  156.7 285.3 %reduce-scatter.3.cloned.1.call-start = ((), (), s32[]{:S(2)}) async-start(), calls=%async_computation.4 | async-start | bytes 5013504 | tf_op jit(solution)/shard_map/reduce_scatter | solution.py:46
  156.9 5.2 %copy-start.2 = (bf16[1152,1024]{1,0:T(8,128)(2,1)S(1)}, bf16[1152,1024]{1,0:T(8,128)(2,1)}, u32[]{:S(2)}) copy-start(bf16[1152,1024]{1,0:T(8,128)(2,1)} %all-gather.3.cloned.1.call-done) | copy-start | bytes 7077892
Sparse Core Ops, SparseCore 0:
  9.9 39.4 all-gather.4
  52.0 87.8 all-gather.2
  156.8 63.5 reduce-scatter.4
  224.9 217.0 reduce-scatter.2
where the time goes:
time: 449 us
  waiting for transfers between devices  367 us (82%)
  blocking collectives  38.9 us (9%)
  matrix products  16.6 us (4%)
  between operations  15.2 us (3%)
  other arithmetic  10.8 us (2%)
    reduce_scatter x1, waiting for transfers between devices, shards(): lax.psum_scatter(img_term, 'col', scatter_dimension=0, tiled=True)  222 us
    all_gather x1, waiting for transfers between devices, shards(): img_full = lax.all_gather(images, 'col', axis=0, tiled=True)  88.2 us
    all_gather x1, waiting for transfers between devices, shards(): txt_full = lax.all_gather(texts, 'row', axis=0, tiled=True)  39.3 us
    psum x1, blocking collectives, shards(): row_loss = lax.psum(loss_part, 'col')  38.9 us
    reduce_scatter x1, waiting for transfers between devices, shards(): lax.psum_scatter(txt_term, 'row', scatter_dimension=0, tiled=True)  16.3 us
  transfers between devices with their start and end apart: 4, of which 4 were waited for; matrix products, arithmetic and copies ran while one was open for 2% of the time, Pallas kernels for 0%

commit v1 on v0

v1 whole, which is shorter than its diff:
```python
import jax
import jax.numpy as jnp
from jax import lax
from jax.experimental import pallas as pl
from jax.experimental.pallas import tpu as pltpu
from jax.sharding import PartitionSpec as P

EPS = 1e-06
F32 = jnp.float32
BF16 = jnp.bfloat16
NZ, NY = 8, 4
SH = 72
BL = 2 * SH
N = 1024
HALF = N // 2
ROWS = 16 * SH
MIB = 1024 * 1024


def row_pairs(f):
    out = []
    for r in range(16):
        a, b, c = f(r // 8, (r // 2) % 4, r % 2)
        out.append((r, (a * 4 + b) * 2 + c))
    return out


def col_pairs(f):
    out = []
    for r in range(16):
        a, b = f(r // 2, r % 2)
        out.append((r, a * 2 + b))
    return out


def shift_z(v, d):
    return lax.ppermute(v, "col", col_pairs(lambda z, h: ((z + d) % NZ, h)))


def shift_y(v, d):
    return lax.ppermute(v, "row", row_pairs(lambda x, y, c: (x, (y + d) % NY, c)))


def swap_xhi(v):
    return lax.ppermute(v, "col", col_pairs(lambda z, h: (z, 1 - h)))


def swap_xlo(v):
    return lax.ppermute(v, "row", row_pairs(lambda x, y, c: (1 - x, y, c)))


def swap_core(v):
    return lax.ppermute(v, "row", row_pairs(lambda x, y, c: (x, y, 1 - c)))


def coords():
    row, col = lax.axis_index("row"), lax.axis_index("col")
    return row // 8, (row // 2) % 4, row % 2, col // 2, col % 2


def halves(v):
    return v[:SH], v[SH:]


def text_kernel(*refs):
    mine, others = refs[:4], refs[4]
    yp, ypt, brow, bcol = refs[5:]
    xlo, y, core, z, xhi = coords()
    same = core == xhi
    total = jnp.zeros((1, N), F32)
    for k in range(NY):
        here = halves(mine[k][...].astype(F32))
        away = halves(others[k].astype(F32))
        for other in range(2):
            a, b = here[other], away[other]
            block = jnp.concatenate([jnp.where(same, a, b), jnp.where(same, b, a)], axis=0)
            g = (xlo + other) % 2 * 4 + (y + k) % 4
            at = (g - z + NZ) % NZ * BL
            yp[pl.ds(pl.multiple_of(at, BL), BL), :] = block.astype(BF16)
            total += jnp.sum(block * block, axis=0, keepdims=True)
    brow[...] = lax.rsqrt(total + EPS)
    for c in range(N // 128):
        v = yp[:, c * 128 : (c + 1) * 128].T
        ypt[c * 128 : (c + 1) * 128, :] = v
        w = v.astype(F32)
        s = jnp.sum(w * w, axis=1, keepdims=True)
        bcol[c * 128 : (c + 1) * 128, :] = jnp.broadcast_to(lax.rsqrt(s + EPS), (128, 128))


LANES = 128
TILE = 64


def image_kernel(*refs):
    pieces = refs[:9]
    pairs, logscale, bias, yp, ypt, bcol = refs[9:15]
    xp, cx, sj, loss = refs[15:19]
    outs = refs[19:28]
    t_ref, cy, acc_sj = refs[28:]
    total = jnp.zeros((1, N), F32)
    at = 0
    for k in range(NZ):
        rows = slice(k * BL, (k + 1) * BL)
        if k == NZ // 2:
            xp[rows, :HALF] = pieces[at][...]
            xp[rows, HALF:] = pieces[at + 1][...]
            at += 2
        else:
            xp[rows, :] = pieces[at][...]
            at += 1
        v = xp[rows, :].astype(F32)
        total += jnp.sum(v * v, axis=0, keepdims=True)
    a = lax.rsqrt(total + EPS)
    scale = jnp.exp(jnp.full((1, N), logscale[0], F32))
    ascale = a * scale
    shift = bias[0]
    acc_sj[...] = jnp.zeros_like(acc_sj)
    first = lax.axis_index("col") * N
    W = 256
    for n in range(N // W):
        t_ref[:, n * W : (n + 1) * W] = jnp.dot(
            ypt[...], xp[:, n * W : (n + 1) * W], preferred_element_type=F32
        )
    sub = TILE // 8
    losses, inners = [], []
    for n in range(N // LANES):
        cols = slice(n * LANES, (n + 1) * LANES)
        ai, asc, sc, pair = a[:, cols], ascale[:, cols], scale[:, cols], pairs[:, cols] - first

        def body(j, carry, cols=cols, ai=ai, asc=asc, sc=sc, pair=pair):
            al, asi = carry
            rows = pl.ds(pl.multiple_of(j * TILE, TILE), TILE)
            b = bcol[rows, :]
            cos = (t_ref[rows, cols] * b) * ai
            logit = cos * sc + shift
            ids = lax.broadcasted_iota(jnp.int32, (TILE, LANES), 0)
            hit = ids == pair - j * TILE
            e = jnp.exp(logit)
            sig = e * pl.reciprocal(1.0 + e)
            d = jnp.where(hit, sig - 1.0, sig)
            dc = d * cos
            cy[rows, cols] = ((d * b) * sc).astype(BF16)
            cx[rows, cols] = (d * asc).astype(BF16)
            acc_sj[rows, :] += dc
            e8 = e.reshape(sub, 8, LANES)
            q = e8[0]
            for m in range(1, sub):
                q = q + (e8[m] + q * e8[m])
            soft = jnp.where(q < 1e-4, (1.0 - 0.5 * q) * q, jnp.log(1.0 + q))
            al = al + soft - jnp.sum(jnp.where(hit, logit, 0.0).reshape(sub, 8, LANES), axis=0)
            asi = asi + jnp.sum(dc.reshape(sub, 8, LANES), axis=0)
            return al, asi

        zero = jnp.zeros((8, LANES), F32)
        al, asi = lax.fori_loop(0, N // TILE, body, (zero, zero))
        losses.append(jnp.sum(al, axis=0, keepdims=True))
        inners.append(jnp.sum(asi, axis=0, keepdims=True) * sc)
    loss[...] = jnp.concatenate(losses, axis=1)
    sj[...] = jnp.sum(acc_sj[...].T, axis=0, keepdims=True) * scale
    si = jnp.concatenate(inners, axis=1)
    for n in range(N // W):
        cols = slice(n * W, (n + 1) * W)
        pull = jnp.dot(yp[...], cy[:, cols], preferred_element_type=F32)
        ai, sn = a[:, cols], si[:, cols]
        at = 0
        for k in range(NZ):
            rows = slice(k * BL, (k + 1) * BL)
            u = xp[rows, cols].astype(F32) * ai
            term = ai * (pull[rows] - u * sn)
            if k == NZ // 2:
                c0 = (n * W) % HALF
                outs[at + (n * W) // HALF][:, c0 : c0 + W] = term.astype(BF16)
                at += 2
            else:
                outs[at][:, cols] = term
                at += 1


def caption_kernel(xp, cx, yp, brow, sj, *refs):
    own, away = refs[:4], refs[4]
    t_ref = refs[5]
    xlo, y, core, z, xhi = coords()
    same = core == xhi
    W = 256
    for n in range(N // W):
        cols = slice(n * W, (n + 1) * W)
        pull = lax.dot_general(
            xp[...], cx[cols, :], (((1,), (1,)), ((), ())), preferred_element_type=F32
        )
        b, s = brow[:, cols], sj[:, cols]
        t_ref[:, cols] = b * (pull - (yp[:, cols].astype(F32) * b) * s)
    for k in range(NY):
        here, there = [], []
        for other in range(2):
            g = (xlo + other) % 2 * 4 + (y + k) % 4
            at = (g - z + NZ) % NZ * BL
            p, q = halves(t_ref[pl.ds(pl.multiple_of(at, BL), BL), :])
            here.append(jnp.where(same, p, q))
            there.append(jnp.where(same, q, p))
        own[k][...] = jnp.concatenate(here, axis=0)
        away[k] = jnp.concatenate(there, axis=0).astype(BF16)


def call(kernel, out_shape, flops, args, scratch=(), smem=(), limit=32 * MIB):
    vm = pl.BlockSpec(memory_space=pltpu.VMEM)
    specs = [pl.BlockSpec(memory_space=pltpu.SMEM) if i in smem else vm for i in range(len(args))]
    moved = sum(x.size * x.dtype.itemsize for x in list(args) + list(out_shape))
    return pl.pallas_call(
        kernel,
        out_shape=out_shape,
        in_specs=specs,
        out_specs=[vm] * len(out_shape),
        scratch_shapes=list(scratch),
        compiler_params=pltpu.CompilerParams(vmem_limit_bytes=limit),
        cost_estimate=pl.CostEstimate(flops=flops, bytes_accessed=moved, transcendentals=0),
    )(*args)


def sds(shape, dtype):
    return jax.ShapeDtypeStruct(shape, dtype)


def wide(v):
    return v.astype(F32)


def run_text(mine, others):
    return call(
        text_kernel,
        [sds((ROWS, N), BF16), sds((N, ROWS), BF16), sds((1, N), F32), sds((N, 128), F32)],
        N * N * 64,
        list(mine) + [others],
    )


def run_image(pieces, pairs, log_scale, bias, yp, ypt, bcol):
    shapes = [sds((ROWS, N), BF16), sds((N, N), BF16), sds((1, N), F32), sds((1, N), F32)]
    for k in range(NZ):
        shapes += [sds((BL, HALF), BF16)] * 2 if k == NZ // 2 else [sds((BL, N), F32)]
    return call(
        image_kernel,
        shapes,
        4 * N * N * ROWS,
        list(pieces) + [pairs.reshape(1, N), log_scale, bias, yp, ypt, bcol],
        [pltpu.VMEM((N, N), F32), pltpu.VMEM((N, N), BF16), pltpu.VMEM((N, 128), F32)],
        smem=(10, 11),
    )


def run_caption(xp, cx, yp, brow, sj):
    return call(
        caption_kernel,
        [sds((BL, N), F32)] * NY + [sds((NY, BL, N), BF16)],
        2 * N * N * ROWS,
        [xp, cx, yp, brow, sj],
        [pltpu.VMEM((ROWS, N), F32)],
    )


def shards(images, texts, pairs, log_scale, bias):
    block = jnp.concatenate([texts, swap_xlo(texts)], axis=0)
    behind = shift_y(block, 1)
    ahead = shift_y(block, -1)
    across = shift_y(behind, 1)
    mine = [block, ahead, across, behind]
    yp, ypt, brow, bcol = run_text(mine, swap_core(jnp.stack(mine)))

    up = down = jnp.concatenate([images, swap_xhi(images)], axis=0)
    ring = [[] for _ in range(NZ)]
    ring[0] = [up]
    for k in range(1, NZ // 2):
        up, down = shift_z(up, 1), shift_z(down, -1)
        ring[NZ - k], ring[k] = [up], [down]
    ring[NZ // 2] = [shift_z(up[:, :HALF], 1), shift_z(down[:, HALF:], -1)]
    res = run_image([p for r in ring for p in r], pairs, log_scale, bias, yp, ypt, bcol)
    xp, cx, sj, loss = res[:4]
    terms = list(res[4:8]) + [None] + list(res[10:13])

    up = jnp.pad(wide(shift_z(res[8], 1)), ((0, 0), (0, HALF)))
    down = jnp.pad(wide(shift_z(res[9], -1)), ((0, 0), (HALF, 0)))
    for k in range(NZ // 2 - 1, 0, -1):
        up = shift_z((terms[k] + wide(up)).astype(BF16), 1)
        down = shift_z((terms[NZ - k] + wide(down)).astype(BF16), -1)
    total = terms[0] + wide(up) + wide(down)
    image_grad = total[:SH] + wide(swap_xhi(total[SH:].astype(BF16)))

    cap = run_caption(xp, cx, yp, brow, sj)
    got = swap_core(cap[NY])
    part = [cap[k] + wide(got[k]) for k in range(NY)]
    up = shift_y(part[2].astype(BF16), 1)
    down = shift_y(part[3].astype(BF16), -1)
    up = shift_y((part[1] + wide(up)).astype(BF16), 1)
    total = part[0] + wide(up) + wide(down)
    text_grad = total[:SH] + wide(swap_xlo(total[SH:].astype(BF16)))

    row_loss = jnp.sum(lax.all_gather(loss, "col", axis=0, tiled=True), axis=0)
    return (row_loss, image_grad, text_grad)


def solution(mesh):
    return jax.shard_map(
        shards,
        mesh=mesh,
        in_specs=(P("col", "row"), P("row", "col"), P("row"), P(), P()),
        out_specs=(P("row"), P("col", "row"), P("row", "col")),
        check_vma=False,
    )
```

time: 449 us -> 167 us (0.37)
  waiting for transfers between devices: 367 us -> 46.7 us
  starting transfers between devices: 0.34 us -> 45.1 us
  Pallas kernels: 0 us -> 18 us
  matrix products: 16.6 us -> 0 us
  between operations: 15.2 us -> 2.21 us
  blocking collectives: 38.9 us -> 44 us
    reduce_scatter x2 -> x0, waiting for transfers between devices: 238 us -> none  [the longest x1 222 us: shards(): lax.psum_scatter(img_term, 'col', scatter_dimension=0, tiled=True)]
    all_gather x2 -> x0, waiting for transfers between devices: 127 us -> none  [the longest x1 88.2 us: shards(): img_full = lax.all_gather(images, 'col', axis=0, tiled=True)]
    ppermute x0 -> x28, waiting for transfers between devices: none -> 46.7 us  [the longest x16 29.2 us: shift_z(): return lax.ppermute(v, 'col', col_pairs(lambda z, h: ((z + d) % NZ, h)))]
    ppermute x0 -> x28, starting transfers between devices: none -> 45.1 us  [the longest x16 30.3 us: shift_z(): return lax.ppermute(v, 'col', col_pairs(lambda z, h: ((z + d) % NZ, h)))]
    all_gather x0 -> x1, blocking collectives: none -> 44 us  [shards(): row_loss = jnp.sum(lax.all_gather(loss, 'col', axis=0, tiled=True), axis=0)]
    psum x1 -> x0, blocking collectives: 38.9 us -> none  [shards(): row_loss = lax.psum(loss_part, 'col')]
    pallas_call x0 -> x3, Pallas kernels: none -> 18 us  [call(): pl.pallas_call(kernel, out_shape=out_shape, in_specs=specs, out_specs=[vm...]
    dot_general x3 -> x0, matrix products: 16.6 us -> none  [the longest x1 8.63 us: shards(): lax.dot_general(img_unit, txt_unit, (((0,), (0,)), ((), ())), preferred_e...]
  transfers between devices with their start and end apart: 4 -> 28, of which waited for: 4 -> 14; matrix products, arithmetic and copies ran while one was open for 2% -> 4% of each run, Pallas kernels for 0% -> 3%
where the time goes in v1:
time: 167 us; the launch traced here: 164 us
  waiting for transfers between devices  46.7 us (28%)
  starting transfers between devices  45.1 us (27%)
  blocking collectives  44 us (26%)
  Pallas kernels  18 us (11%)
  other arithmetic  6.55 us (4%)
  between operations  2.21 us (1%)
  local copies, waits for them, and re-layouts  1.71 us (1%)
    all_gather x1, blocking collectives, shards(): row_loss = jnp.sum(lax.all_gather(loss, 'col', axis=0, tiled=True), axis=0)  44 us
    ppermute x16, starting transfers between devices, shift_z(): return lax.ppermute(v, 'col', col_pairs(lambda z, h: ((z + d) % NZ, h)))  30.3 us
    ppermute x16, waiting for transfers between devices, shift_z(): return lax.ppermute(v, 'col', col_pairs(lambda z, h: ((z + d) % NZ, h)))  29.2 us
    pallas_call x3, Pallas kernels, call(): pl.pallas_call(kernel, out_shape=out_shape, in_specs=specs, out_specs=[vm...  18 us
    ppermute x6, starting transfers between devices, shift_y(): lax.ppermute(v, 'row', row_pairs(lambda x, y, c: (x, (y + d) % NY, c)))  9.4 us
    ppermute x6, waiting for transfers between devices, shift_y(): lax.ppermute(v, 'row', row_pairs(lambda x, y, c: (x, (y + d) % NY, c)))  8.73 us
    ppermute x2, waiting for transfers between devices, swap_xhi(): return lax.ppermute(v, 'col', col_pairs(lambda z, h: (z, 1 - h)))  5.44 us
    ppermute x2, waiting for transfers between devices, swap_xlo(): return lax.ppermute(v, 'row', row_pairs(lambda x, y, c: (1 - x, y, c)))  3.35 us
  transfers between devices with their start and end apart: 28, of which 14 were waited for; matrix products, arithmetic and copies ran while one was open for 4% of the time, Pallas kernels for 3%

profile of v1, /device:TPU:8, one launch (start us, length us, event | category | flops | bytes accessed | tf_op | source)
XLA Modules:
  0.0 164.3 jit_solution(5036117950191160127)
XLA Ops:
  0.6 1.6 collective-permute-start.9
  3.2 3.4 %collective-permute-done.9 = bf16[72,1024]{1,0:T(8,128)(2,1)S(1)} collective-permute-done((bf16[72,1024]{1,0:T(8,128)(2,1)}, bf16[72,1024]{1,0:T(8,128)(2,1)S(1)}, u32[]{:S(2)}, u32[]{:S(2)}) %collective-permute-start.9) | collective-permute-done | bytes 147488 | tf_op jit(solution)/shard_map/ppermute | solution.py:49
  6.5 1.7 %collective-permute-start.11 = (bf16[144,1024]{1,0:T(8,128)(2,1)S(1)}, bf16[144,1024]{1,0:T(8,128)(2,1)S(1)}, u32[]{:S(2)}, u32[]{:S(2)}) collective-permute-start(bf16[144,1024]{1,0:T(8,128)(2,1)S(1)} %constant_dynamic-update-slice_fusion.2.refs_0_), channel_id=1, source_target_pairs={{0,32},{16,48},{32,64},{48,80},{64,96},{80,112},{96,0},{112,16},{1... | collective-permute-start | bytes 884744 | tf_op jit(solution)/shard_map/ppermute | solution.py:41
  8.6 5.8 %collective-permute-done.11.refs_3_ = bf16[144,1024]{1,0:T(8,128)(2,1)S(1)} collective-permute-done((bf16[144,1024]{1,0:T(8,128)(2,1)S(1)}, bf16[144,1024]{1,0:T(8,128)(2,1)S(1)}, u32[]{:S(2)}, u32[]{:S(2)}) %collective-permute-start.11) | collective-permute-done | bytes 294944 | tf_op jit(solution)/shard_map/ppermute | solution.py:41
  14.5 1.6 collective-permute-start.12
  16.1 3.0 %collective-permute-start = (bf16[72,1024]{1,0:T(8,128)(2,1)}, bf16[72,1024]{1,0:T(8,128)(2,1)S(1)}, u32[]{:S(2)}, u32[]{:S(2)}) collective-permute-start(bf16[72,1024]{1,0:T(8,128)(2,1)} %param.5), channel_id=1, source_target_pairs={{0,1},{1,0},{2,3},{3,2},{4,5},{5,4},{6,7},{7,6},{8,9},{9,8},{10,11... | collective-permute-start | bytes 442376 | tf_op jit(solution)/shard_map/ppermute | solution.py:45
  19.1 2.4 %collective-permute-done.12.refs_2_ = bf16[144,1024]{1,0:T(8,128)(2,1)S(1)} collective-permute-done((bf16[144,1024]{1,0:T(8,128)(2,1)S(1)}, bf16[144,1024]{1,0:T(8,128)(2,1)S(1)}, u32[]{:S(2)}, u32[]{:S(2)}) %collective-permute-start.12) | collective-permute-done | bytes 294944 | tf_op jit(solution)/shard_map/ppermute | solution.py:41
  22.9 2.0 %collective-permute-start.4 = (bf16[144,1024]{1,0:T(8,128)(2,1)S(1)}, bf16[144,1024]{1,0:T(8,128)(2,1)S(1)}, u32[]{:S(2)}, u32[]{:S(2)}) collective-permute-start(bf16[144,1024]{1,0:T(8,128)(2,1)S(1)} %constant_dynamic-update-slice_fusion.refs_0_), channel_id=1, source_target_pairs={{0,2},{1,3},{2,4},{3,5},{4,6},{5,7},{6,8},{7,9},{8,10},{9,11},{10,... | collective-permute-start | bytes 884744 | tf_op jit(solution)/shard_map/ppermute | solution.py:37
  24.9 4.0 %collective-permute-start.1 = (bf16[144,1024]{1,0:T(8,128)(2,1)S(1)}, bf16[144,1024]{1,0:T(8,128)(2,1)S(1)}, u32[]{:S(2)}, u32[]{:S(2)}) collective-permute-start(bf16[144,1024]{1,0:T(8,128)(2,1)S(1)} %constant_dynamic-update-slice_fusion.refs_0_), channel_id=1, source_target_pairs={{0,14},{1,15},{2,0},{3,1},{4,2},{5,3},{6,4},{7,5},{8,6},{9,7},{10,... | collective-permute-start | bytes 884744 | tf_op jit(solution)/shard_map/ppermute | solution.py:37
  29.0 6.4 %collective-permute-done.4.refs_8_ = bf16[144,1024]{1,0:T(8,128)(2,1)S(1)} collective-permute-done((bf16[144,1024]{1,0:T(8,128)(2,1)S(1)}, bf16[144,1024]{1,0:T(8,128)(2,1)S(1)}, u32[]{:S(2)}, u32[]{:S(2)}) %collective-permute-start.4) | collective-permute-done | bytes 294944 | tf_op jit(solution)/shard_map/ppermute | solution.py:37
  35.4 3.2 %collective-permute-start.2 = (bf16[144,1024]{1,0:T(8,128)(2,1)S(1)}, bf16[144,1024]{1,0:T(8,128)(2,1)S(1)}, u32[]{:S(2)}, u32[]{:S(2)}) collective-permute-start(bf16[144,1024]{1,0:T(8,128)(2,1)S(1)} %collective-permute-done.1.refs_1_), channel_id=1, source_target_pairs={{0,14},{1,15},{2,0},{3,1},{4,2},{5,3},{6,4},{7,5},{8,6},{9,7},{10,... | collective-permute-start | bytes 884744 | tf_op jit(solution)/shard_map/ppermute | solution.py:37
  38.6 5.6 %collective-permute-done.5.refs_7_ = bf16[144,1024]{1,0:T(8,128)(2,1)S(1)} collective-permute-done((bf16[144,1024]{1,0:T(8,128)(2,1)S(1)}, bf16[144,1024]{1,0:T(8,128)(2,1)S(1)}, u32[]{:S(2)}, u32[]{:S(2)}) %collective-permute-start.5) | collective-permute-done | bytes 294944 | tf_op jit(solution)/shard_map/ppermute | solution.py:37
  44.2 3.2 %collective-permute-start.3 = (bf16[144,1024]{1,0:T(8,128)(2,1)S(1)}, bf16[144,1024]{1,0:T(8,128)(2,1)S(1)}, u32[]{:S(2)}, u32[]{:S(2)}) collective-permute-start(bf16[144,1024]{1,0:T(8,128)(2,1)S(1)} %collective-permute-done.2.refs_2_), channel_id=1, source_target_pairs={{0,14},{1,15},{2,0},{3,1},{4,2},{5,3},{6,4},{7,5},{8,6},{9,7},{10,... | collective-permute-start | bytes 884744 | tf_op jit(solution)/shard_map/ppermute | solution.py:37
  47.5 4.7 %collective-permute-done.6.refs_6_ = bf16[144,1024]{1,0:T(8,128)(2,1)S(1)} collective-permute-done((bf16[144,1024]{1,0:T(8,128)(2,1)S(1)}, bf16[144,1024]{1,0:T(8,128)(2,1)S(1)}, u32[]{:S(2)}, u32[]{:S(2)}) %collective-permute-start.6) | collective-permute-done | bytes 294944 | tf_op jit(solution)/shard_map/ppermute | solution.py:37
  52.3 3.5 %collective-permute-start.8 = (bf16[144,512]{1,0:T(8,128)(2,1)S(1)}, bf16[144,512]{1,0:T(8,128)(2,1)S(1)}, u32[]{:S(2)}, u32[]{:S(2)}) collective-permute-start(bf16[144,512]{1,0:T(8,128)(2,1)S(1)} %slice.43), channel_id=1, source_target_pairs={{0,14},{1,15},{2,0},{3,1},{4,2},{5,3},{6,4},{7,5},{8,6},{9,7},{10,... | collective-permute-start | bytes 442376 | tf_op jit(solution)/shard_map/ppermute | solution.py:37
  57.1 2.1 %shard_map.76 = (bf16[1152,1024]{1,0:T(8,128)(2,1)S(1)}, bf16[1024,1152]{1,0:T(8,128)(2,1)S(1)}, f32[1,1024]{1,0:T(1,128)S(1)}, f32[1024,128]{1,0:T(8,128)S(1)}) custom-call(bf16[144,1024]{1,0:T(8,128)(2,1)S(1)} %constant_dynamic-update-slice_fusion.2.refs_0_, bf16[144,1024]{1,0:T(8,128)(2,1)S(1)} %collective-permute-done.10.refs_1_, ...), custom_call_target="tpu_custom_call" | custom-call | flops 67108864 | bytes 7606272 | tf_op jit(solution)/shard_map/pallas_call | solution.py:208
  59.3 12.3 %shard_map.77 = (bf16[1152,1024]{1,0:T(8,128)(2,1)S(1)}, bf16[1024,1024]{1,0:T(8,128)(2,1)S(1)}, f32[1,1024]{1,0:T(1,128)S(1)}, f32[1,1024]{1,0:T(1,128)S(1)}, f...) custom-call(bf16[144,1024]{1,0:T(8,128)(2,1)S(1)} %constant_dynamic-, ...), custom_call_target="tpu_custom_call" | custom-call | flops 4831838208 | bytes 16494600 | tf_op jit(solution)/shard_map/pallas_call | solution.py:208
  71.6 2.9 %collective-permute-start.18 = (bf16[144,512]{1,0:T(8,128)(2,1)S(1)}, bf16[144,512]{1,0:T(8,128)(2,1)S(1)}, u32[]{:S(2)}, u32[]{:S(2)}) collective-permute-start(bf16[144,512]{1,0:T(8,128)(2,1)S(1)} %get-tuple-element.37), channel_id=1, source_target_pairs={{0,14},{1,15},{2,0},{3,1},{4,2},{5,3},{6,4},{7,5},{8,6},{9,7},{10,... | collective-permute-start | bytes 442376 | tf_op jit(solution)/shard_map/ppermute | solution.py:37
  74.5 3.5 %shard_map.78 = (f32[144,1024]{1,0:T(8,128)S(1)}, f32[144,1024]{1,0:T(8,128)S(1)}, f32[144,1024]{1,0:T(8,128)S(1)}, f32[144,1024]{1,0:T(8,128)S(1)}, bf16[4,144,1024]{2,1,0:T(8,128)(2,1)S(1)}) custom-call(bf16[1152,1024]{1,0:T(8,128)(2,1)S(1)} %get-tuple-element.38.xp, bf16[1024,1024]{1,0:T(8,128)(2,1)S(1)} %get-tuple-element.39.cx, ...), custom_call_target="tpu_custom_call" | custom-call | flops 2415919104 | bytes 10362880 | tf_op jit(solution)/shard_map/pallas_call | solution.py:208
  78.3 3.5 %collective-permute-start.19 = (bf16[144,1024]{1,0:T(8,128)(2,1)S(1)}, bf16[144,1024]{1,0:T(8,128)(2,1)S(1)}, u32[]{:S(2)}, u32[]{:S(2)}) collective-permute-start(bf16[144,1024]{1,0:T(8,128)(2,1)S(1)} %add_convert_fusion.2), channel_id=1, source_target_pairs={{0,14},{1,15},{2,0},{3,1},{4,2},{5,3},{6,4},{7,5},{8,6},{9,7},{10,... | collective-permute-start | bytes 884744 | tf_op jit(solution)/shard_map/ppermute | solution.py:37
  81.8 3.8 %collective-permute-done.14 = bf16[144,512]{1,0:T(8,128)(2,1)S(1)} collective-permute-done((bf16[144,512]{1,0:T(8,128)(2,1)S(1)}, bf16[144,512]{1,0:T(8,128)(2,1)S(1)}, u32[]{:S(2)}, u32[]{:S(2)}) %collective-permute-start.14) | collective-permute-done | bytes 147488 | tf_op jit(solution)/shard_map/ppermute | solution.py:37
  85.8 2.6 %collective-permute-done.19 = bf16[144,1024]{1,0:T(8,128)(2,1)S(1)} collective-permute-done((bf16[144,1024]{1,0:T(8,128)(2,1)S(1)}, bf16[144,1024]{1,0:T(8,128)(2,1)S(1)}, u32[]{:S(2)}, u32[]{:S(2)}) %collective-permute-start.19) | collective-permute-done | bytes 294944 | tf_op jit(solution)/shard_map/ppermute | solution.py:37
  88.5 3.8 %collective-permute-start.20 = (bf16[144,1024]{1,0:T(8,128)(2,1)S(1)}, bf16[144,1024]{1,0:T(8,128)(2,1)S(1)}, u32[]{:S(2)}, u32[]{:S(2)}) collective-permute-start(bf16[144,1024]{1,0:T(8,128)(2,1)S(1)} %add_convert_fusion.1), channel_id=1, source_target_pairs={{0,14},{1,15},{2,0},{3,1},{4,2},{5,3},{6,4},{7,5},{8,6},{9,7},{10,... | collective-permute-start | bytes 884744 | tf_op jit(solution)/shard_map/ppermute | solution.py:37
  92.2 3.3 %collective-permute-done.15 = bf16[144,1024]{1,0:T(8,128)(2,1)S(1)} collective-permute-done((bf16[144,1024]{1,0:T(8,128)(2,1)S(1)}, bf16[144,1024]{1,0:T(8,128)(2,1)S(1)}, u32[]{:S(2)}, u32[]{:S(2)}) %collective-permute-start.15) | collective-permute-done | bytes 294944 | tf_op jit(solution)/shard_map/ppermute | solution.py:37
  95.8 2.2 %collective-permute-start.24 = (bf16[144,1024]{1,0:T(8,128)(2,1)S(1)}, bf16[144,1024]{1,0:T(8,128)(2,1)S(1)}, u32[]{:S(2)}, u32[]{:S(2)}) collective-permute-start(bf16[144,1024]{1,0:T(8,128)(2,1)S(1)} %fusion.1), channel_id=1, source_target_pairs={{0,32},{16,48},{32,64},{48,80},{64,96},{80,112},{96,0},{112,16},{1... | collective-permute-start | bytes 884744 | tf_op jit(solution)/shard_map/ppermute | solution.py:41
  98.1 3.8 %collective-permute-start.21 = (bf16[144,1024]{1,0:T(8,128)(2,1)S(1)}, bf16[144,1024]{1,0:T(8,128)(2,1)S(1)}, u32[]{:S(2)}, u32[]{:S(2)}) collective-permute-start(bf16[144,1024]{1,0:T(8,128)(2,1)S(1)} %add_convert_fusion), channel_id=1, source_target_pairs={{0,14},{1,15},{2,0},{3,1},{4,2},{5,3},{6,4},{7,5},{8,6},{9,7},{10,... | collective-permute-start | bytes 884744 | tf_op jit(solution)/shard_map/ppermute | solution.py:37
  101.8 2.7 %collective-permute-done.16 = bf16[144,1024]{1,0:T(8,128)(2,1)S(1)} collective-permute-done((bf16[144,1024]{1,0:T(8,128)(2,1)S(1)}, bf16[144,1024]{1,0:T(8,128)(2,1)S(1)}, u32[]{:S(2)}, u32[]{:S(2)}) %collective-permute-start.16) | collective-permute-done | bytes 294944 | tf_op jit(solution)/shard_map/ppermute | solution.py:37
  106.9 1.6 collective-permute-start.25
  108.5 2.0 %collective-permute-start.26 = (bf16[144,1024]{1,0:T(8,128)(2,1)}, bf16[144,1024]{1,0:T(8,128)(2,1)}, u32[]{:S(2)}, u32[]{:S(2)}) collective-permute-start(bf16[144,1024]{1,0:T(8,128)(2,1)} %get-tuple-element.48), channel_id=1, source_target_pairs={{0,96},{16,112},{32,0},{48,16},{64,32},{80,48},{96,64},{112,80},{1... | collective-permute-start | bytes 884744 | tf_op jit(solution)/shard_map/ppermute | solution.py:41
  110.5 44.0 %all-gather = f32[16,1,1024]{2,1,0:T(1,128)} all-gather(f32[1,1,1024]{2,1,0:T(1,128)S(1)} %bitcast.30), channel_id=1, replica_groups=mesh['row'=16,'col'=16] {'col'}, dimensions={0}, use_global_device_ids=true | all-gather | bytes 69632 | tf_op jit(solution)/shard_map/all_gather | solution.py:296
  154.4 1.5 reduce_sum.9
  157.9 4.9 %collective-permute-done.22 = bf16[72,1024]{1,0:T(8,128)(2,1)S(1)} collective-permute-done((bf16[72,1024]{1,0:T(8,128)(2,1)S(1)}, bf16[72,1024]{1,0:T(8,128)(2,1)S(1)}, u32[]{:S(2)}, u32[]{:S(2)}) %collective-permute-start.22) | collective-permute-done | bytes 147488 | tf_op jit(solution)/shard_map/ppermute | solution.py:45
  (54 shorter events, 9.6 us)
Async XLA Ops:
  0.6 5.9 %collective-permute-start.9 = (bf16[72,1024]{1,0:T(8,128)(2,1)}, bf16[72,1024]{1,0:T(8,128)(2,1)S(1)}, u32[]{:S(2)}, u32[]{:S(2)}) collective-permute-start(bf16[72,1024]{1,0:T(8,128)(2,1)} %param.6), channel_id=1, source_target_pairs={{0,128},{16,144},{32,160},{48,176},{64,192},{80,208},{96,224},{112... | collective-permute-start | bytes 442376 | tf_op jit(solution)/shard_map/ppermute | solution.py:49
  6.5 8.0 %collective-permute-start.11 = (bf16[144,1024]{1,0:T(8,128)(2,1)S(1)}, bf16[144,1024]{1,0:T(8,128)(2,1)S(1)}, u32[]{:S(2)}, u32[]{:S(2)}) collective-permute-start(bf16[144,1024]{1,0:T(8,128)(2,1)S(1)} %constant_dynamic-update-slice_fusion.2.refs_0_), channel_id=1, source_target_pairs={{0,32},{16,48},{32,64},{48,80},{64,96},{80,112},{96,0},{112,16},{1... | collective-permute-start | bytes 884744 | tf_op jit(solution)/shard_map/ppermute | solution.py:41
  8.2 10.9 %collective-permute-start.10 = (bf16[144,1024]{1,0:T(8,128)(2,1)S(1)}, bf16[144,1024]{1,0:T(8,128)(2,1)S(1)}, u32[]{:S(2)}, u32[]{:S(2)}) collective-permute-start(bf16[144,1024]{1,0:T(8,128)(2,1)S(1)} %constant_dynamic-update-slice_fusion.2.refs_0_), channel_id=1, source_target_pairs={{0,96},{16,112},{32,0},{48,16},{64,32},{80,48},{96,64},{112,80},{1... | collective-permute-start | bytes 884744 | tf_op jit(solution)/shard_map/ppermute | solution.py:41
  14.5 7.0 %collective-permute-start.12 = (bf16[144,1024]{1,0:T(8,128)(2,1)S(1)}, bf16[144,1024]{1,0:T(8,128)(2,1)S(1)}, u32[]{:S(2)}, u32[]{:S(2)}) collective-permute-start(bf16[144,1024]{1,0:T(8,128)(2,1)S(1)} %collective-permute-done.11.refs_3_), channel_id=1, source_target_pairs={{0,32},{16,48},{32,64},{48,80},{64,96},{80,112},{96,0},{112,16},{1... | collective-permute-start | bytes 884744 | tf_op jit(solution)/shard_map/ppermute | solution.py:41
  16.1 6.9 %collective-permute-start = (bf16[72,1024]{1,0:T(8,128)(2,1)}, bf16[72,1024]{1,0:T(8,128)(2,1)S(1)}, u32[]{:S(2)}, u32[]{:S(2)}) collective-permute-start(bf16[72,1024]{1,0:T(8,128)(2,1)} %param.5), channel_id=1, source_target_pairs={{0,1},{1,0},{2,3},{3,2},{4,5},{5,4},{6,7},{7,6},{8,9},{9,8},{10,11... | collective-permute-start | bytes 442376 | tf_op jit(solution)/shard_map/ppermute | solution.py:45
  21.4 0.9 copy-start.1
  21.6 35.5 %collective-permute-start.13 = (bf16[4,144,1024]{2,1,0:T(8,128)(2,1)S(1)}, bf16[4,144,1024]{2,1,0:T(8,128)(2,1)S(1)}, u32[]{:S(2)}, u32[]{:S(2)}) collective-permute-start(bf16[4,144,1024]{2,1,0:T(8,128)(2,1)S(1)} %pad_maximum_fusion), channel_id=1, source_target_pairs={{0,16},{16,0},{32,48},{48,32},{64,80},{80,64},{96,112},{112,96},{1... | collective-permute-start | bytes 3538952 | tf_op jit(solution)/shard_map/ppermute | solution.py:53
  22.9 12.4 %collective-permute-start.4 = (bf16[144,1024]{1,0:T(8,128)(2,1)S(1)}, bf16[144,1024]{1,0:T(8,128)(2,1)S(1)}, u32[]{:S(2)}, u32[]{:S(2)}) collective-permute-start(bf16[144,1024]{1,0:T(8,128)(2,1)S(1)} %constant_dynamic-update-slice_fusion.refs_0_), channel_id=1, source_target_pairs={{0,2},{1,3},{2,4},{3,5},{4,6},{5,7},{6,8},{7,9},{8,10},{9,11},{10,... | collective-permute-start | bytes 884744 | tf_op jit(solution)/shard_map/ppermute | solution.py:37
  24.9 10.5 %collective-permute-start.1 = (bf16[144,1024]{1,0:T(8,128)(2,1)S(1)}, bf16[144,1024]{1,0:T(8,128)(2,1)S(1)}, u32[]{:S(2)}, u32[]{:S(2)}) collective-permute-start(bf16[144,1024]{1,0:T(8,128)(2,1)S(1)} %constant_dynamic-update-slice_fusion.refs_0_), channel_id=1, source_target_pairs={{0,14},{1,15},{2,0},{3,1},{4,2},{5,3},{6,4},{7,5},{8,6},{9,7},{10,... | collective-permute-start | bytes 884744 | tf_op jit(solution)/shard_map/ppermute | solution.py:37
  35.4 8.8 %collective-permute-start.5 = (bf16[144,1024]{1,0:T(8,128)(2,1)S(1)}, bf16[144,1024]{1,0:T(8,128)(2,1)S(1)}, u32[]{:S(2)}, u32[]{:S(2)}) collective-permute-start(bf16[144,1024]{1,0:T(8,128)(2,1)S(1)} %collective-permute-done.4.refs_8_), channel_id=1, source_target_pairs={{0,2},{1,3},{2,4},{3,5},{4,6},{5,7},{6,8},{7,9},{8,10},{9,11},{10,... | collective-permute-start | bytes 884744 | tf_op jit(solution)/shard_map/ppermute | solution.py:37
  35.4 8.8 %collective-permute-start.2 = (bf16[144,1024]{1,0:T(8,128)(2,1)S(1)}, bf16[144,1024]{1,0:T(8,128)(2,1)S(1)}, u32[]{:S(2)}, u32[]{:S(2)}) collective-permute-start(bf16[144,1024]{1,0:T(8,128)(2,1)S(1)} %collective-permute-done.1.refs_1_), channel_id=1, source_target_pairs={{0,14},{1,15},{2,0},{3,1},{4,2},{5,3},{6,4},{7,5},{8,6},{9,7},{10,... | collective-permute-start | bytes 884744 | tf_op jit(solution)/shard_map/ppermute | solution.py:37
  44.2 7.9 %collective-permute-start.6 = (bf16[144,1024]{1,0:T(8,128)(2,1)S(1)}, bf16[144,1024]{1,0:T(8,128)(2,1)S(1)}, u32[]{:S(2)}, u32[]{:S(2)}) collective-permute-start(bf16[144,1024]{1,0:T(8,128)(2,1)S(1)} %collective-permute-done.5.refs_7_), channel_id=1, source_target_pairs={{0,2},{1,3},{2,4},{3,5},{4,6},{5,7},{6,8},{7,9},{8,10},{9,11},{10,... | collective-permute-start | bytes 884744 | tf_op jit(solution)/shard_map/ppermute | solution.py:37
  44.2 8.0 %collective-permute-start.3 = (bf16[144,1024]{1,0:T(8,128)(2,1)S(1)}, bf16[144,1024]{1,0:T(8,128)(2,1)S(1)}, u32[]{:S(2)}, u32[]{:S(2)}) collective-permute-start(bf16[144,1024]{1,0:T(8,128)(2,1)S(1)} %collective-permute-done.2.refs_2_), channel_id=1, source_target_pairs={{0,14},{1,15},{2,0},{3,1},{4,2},{5,3},{6,4},{7,5},{8,6},{9,7},{10,... | collective-permute-start | bytes 884744 | tf_op jit(solution)/shard_map/ppermute | solution.py:37
  52.2 7.1 %collective-permute-start.7 = (bf16[144,512]{1,0:T(8,128)(2,1)S(1)}, bf16[144,512]{1,0:T(8,128)(2,1)S(1)}, u32[]{:S(2)}, u32[]{:S(2)}) collective-permute-start(bf16[144,512]{1,0:T(8,128)(2,1)S(1)} %slice.42), channel_id=1, source_target_pairs={{0,2},{1,3},{2,4},{3,5},{4,6},{5,7},{6,8},{7,9},{8,10},{9,11},{10,... | collective-permute-start | bytes 442376 | tf_op jit(solution)/shard_map/ppermute | solution.py:37
  52.3 7.0 %collective-permute-start.8 = (bf16[144,512]{1,0:T(8,128)(2,1)S(1)}, bf16[144,512]{1,0:T(8,128)(2,1)S(1)}, u32[]{:S(2)}, u32[]{:S(2)}) collective-permute-start(bf16[144,512]{1,0:T(8,128)(2,1)S(1)} %slice.43), channel_id=1, source_target_pairs={{0,14},{1,15},{2,0},{3,1},{4,2},{5,3},{6,4},{7,5},{8,6},{9,7},{10,... | collective-permute-start | bytes 442376 | tf_op jit(solution)/shard_map/ppermute | solution.py:37
  57.1 2.2 %copy-start = (s32[1024]{0:T(1024)S(1)}, s32[1024]{0:T(1024)}, u32[]{:S(2)}) copy-start(s32[1024]{0:T(1024)} %param.7) | copy-start | bytes 12292
  71.6 6.7 %collective-permute-start.18 = (bf16[144,512]{1,0:T(8,128)(2,1)S(1)}, bf16[144,512]{1,0:T(8,128)(2,1)S(1)}, u32[]{:S(2)}, u32[]{:S(2)}) collective-permute-start(bf16[144,512]{1,0:T(8,128)(2,1)S(1)} %get-tuple-element.37), channel_id=1, source_target_pairs={{0,14},{1,15},{2,0},{3,1},{4,2},{5,3},{6,4},{7,5},{8,6},{9,7},{10,... | collective-permute-start | bytes 442376 | tf_op jit(solution)/shard_map/ppermute | solution.py:37
  78.0 17.6 %collective-permute-start.23 = (bf16[4,144,1024]{2,1,0:T(8,128)(2,1)S(1)}, bf16[4,144,1024]{2,1,0:T(8,128)(2,1)S(1)}, u32[]{:S(2)}, u32[]{:S(2)}) collective-permute-start(bf16[4,144,1024]{2,1,0:T(8,128)(2,1)S(1)} %get-tuple-element.43), channel_id=1, source_target_pairs={{0,16},{16,0},{32,48},{48,32},{64,80},{80,64},{96,112},{112,96},{1... | collective-permute-start | bytes 3538952 | tf_op jit(solution)/shard_map/ppermute | solution.py:53
  78.2 7.5 %collective-permute-start.14 = (bf16[144,512]{1,0:T(8,128)(2,1)S(1)}, bf16[144,512]{1,0:T(8,128)(2,1)S(1)}, u32[]{:S(2)}, u32[]{:S(2)}) collective-permute-start(bf16[144,512]{1,0:T(8,128)(2,1)S(1)} %get-tuple-element.33), channel_id=1, source_target_pairs={{0,2},{1,3},{2,4},{3,5},{4,6},{5,7},{6,8},{7,9},{8,10},{9,11},{10,... | collective-permute-start | bytes 442376 | tf_op jit(solution)/shard_map/ppermute | solution.py:37
  78.3 10.1 %collective-permute-start.19 = (bf16[144,1024]{1,0:T(8,128)(2,1)S(1)}, bf16[144,1024]{1,0:T(8,128)(2,1)S(1)}, u32[]{:S(2)}, u32[]{:S(2)}) collective-permute-start(bf16[144,1024]{1,0:T(8,128)(2,1)S(1)} %add_convert_fusion.2), channel_id=1, source_target_pairs={{0,14},{1,15},{2,0},{3,1},{4,2},{5,3},{6,4},{7,5},{8,6},{9,7},{10,... | collective-permute-start | bytes 884744 | tf_op jit(solution)/shard_map/ppermute | solution.py:37
  85.7 9.8 %collective-permute-start.15 = (bf16[144,1024]{1,0:T(8,128)(2,1)S(1)}, bf16[144,1024]{1,0:T(8,128)(2,1)S(1)}, u32[]{:S(2)}, u32[]{:S(2)}) collective-permute-start(bf16[144,1024]{1,0:T(8,128)(2,1)S(1)} %add_convert_fusion.5), channel_id=1, source_target_pairs={{0,2},{1,3},{2,4},{3,5},{4,6},{5,7},{6,8},{7,9},{8,10},{9,11},{10,... | collective-permute-start | bytes 884744 | tf_op jit(solution)/shard_map/ppermute | solution.py:37
  88.5 9.5 %collective-permute-start.20 = (bf16[144,1024]{1,0:T(8,128)(2,1)S(1)}, bf16[144,1024]{1,0:T(8,128)(2,1)S(1)}, u32[]{:S(2)}, u32[]{:S(2)}) collective-permute-start(bf16[144,1024]{1,0:T(8,128)(2,1)S(1)} %add_convert_fusion.1), channel_id=1, source_target_pairs={{0,14},{1,15},{2,0},{3,1},{4,2},{5,3},{6,4},{7,5},{8,6},{9,7},{10,... | collective-permute-start | bytes 884744 | tf_op jit(solution)/shard_map/ppermute | solution.py:37
  95.6 8.9 %collective-permute-start.16 = (bf16[144,1024]{1,0:T(8,128)(2,1)S(1)}, bf16[144,1024]{1,0:T(8,128)(2,1)S(1)}, u32[]{:S(2)}, u32[]{:S(2)}) collective-permute-start(bf16[144,1024]{1,0:T(8,128)(2,1)S(1)} %add_convert_fusion.4), channel_id=1, source_target_pairs={{0,2},{1,3},{2,4},{3,5},{4,6},{5,7},{6,8},{7,9},{8,10},{9,11},{10,... | collective-permute-start | bytes 884744 | tf_op jit(solution)/shard_map/ppermute | solution.py:37
  95.8 10.1 %collective-permute-start.24 = (bf16[144,1024]{1,0:T(8,128)(2,1)S(1)}, bf16[144,1024]{1,0:T(8,128)(2,1)S(1)}, u32[]{:S(2)}, u32[]{:S(2)}) collective-permute-start(bf16[144,1024]{1,0:T(8,128)(2,1)S(1)} %fusion.1), channel_id=1, source_target_pairs={{0,32},{16,48},{32,64},{48,80},{64,96},{80,112},{96,0},{112,16},{1... | collective-permute-start | bytes 884744 | tf_op jit(solution)/shard_map/ppermute | solution.py:41
  98.1 57.8 %collective-permute-start.21 = (bf16[144,1024]{1,0:T(8,128)(2,1)S(1)}, bf16[144,1024]{1,0:T(8,128)(2,1)S(1)}, u32[]{:S(2)}, u32[]{:S(2)}) collective-permute-start(bf16[144,1024]{1,0:T(8,128)(2,1)S(1)} %add_convert_fusion), channel_id=1, source_target_pairs={{0,14},{1,15},{2,0},{3,1},{4,2},{5,3},{6,4},{7,5},{8,6},{9,7},{10,... | collective-permute-start | bytes 884744 | tf_op jit(solution)/shard_map/ppermute | solution.py:37
  105.3 50.6 %collective-permute-start.17 = (bf16[144,1024]{1,0:T(8,128)(2,1)}, bf16[144,1024]{1,0:T(8,128)(2,1)S(1)}, u32[]{:S(2)}, u32[]{:S(2)}) collective-permute-start(bf16[144,1024]{1,0:T(8,128)(2,1)} %add_convert_fusion.3), channel_id=1, source_target_pairs={{0,2},{1,3},{2,4},{3,5},{4,6},{5,7},{6,8},{7,9},{8,10},{9,11},{10,... | collective-permute-start | bytes 884744 | tf_op jit(solution)/shard_map/ppermute | solution.py:37
  106.9 49.2 %collective-permute-start.25 = (bf16[144,1024]{1,0:T(8,128)(2,1)}, bf16[144,1024]{1,0:T(8,128)(2,1)S(1)}, u32[]{:S(2)}, u32[]{:S(2)}) collective-permute-start(bf16[144,1024]{1,0:T(8,128)(2,1)} %get-tuple-element.47), channel_id=1, source_target_pairs={{0,32},{16,48},{32,64},{48,80},{64,96},{80,112},{96,0},{112,16},{1... | collective-permute-start | bytes 884744 | tf_op jit(solution)/shard_map/ppermute | solution.py:41
  108.5 47.7 %collective-permute-start.26 = (bf16[144,1024]{1,0:T(8,128)(2,1)}, bf16[144,1024]{1,0:T(8,128)(2,1)}, u32[]{:S(2)}, u32[]{:S(2)}) collective-permute-start(bf16[144,1024]{1,0:T(8,128)(2,1)} %get-tuple-element.48), channel_id=1, source_target_pairs={{0,96},{16,112},{32,0},{48,16},{64,32},{80,48},{96,64},{112,80},{1... | collective-permute-start | bytes 884744 | tf_op jit(solution)/shard_map/ppermute | solution.py:41
  156.0 6.7 %collective-permute-start.22 = (bf16[72,1024]{1,0:T(8,128)(2,1)S(1)}, bf16[72,1024]{1,0:T(8,128)(2,1)S(1)}, u32[]{:S(2)}, u32[]{:S(2)}) collective-permute-start(bf16[72,1024]{1,0:T(8,128)(2,1)S(1)} %slice.69), channel_id=1, source_target_pairs={{0,1},{1,0},{2,3},{3,2},{4,5},{5,4},{6,7},{7,6},{8,9},{9,8},{10,11... | collective-permute-start | bytes 442376 | tf_op jit(solution)/shard_map/ppermute | solution.py:45
  157.3 6.2 %collective-permute-start.27 = (bf16[72,1024]{1,0:T(8,128)(2,1)S(1)}, bf16[72,1024]{1,0:T(8,128)(2,1)S(1)}, u32[]{:S(2)}, u32[]{:S(2)}) collective-permute-start(bf16[72,1024]{1,0:T(8,128)(2,1)S(1)} %slice.68), channel_id=1, source_target_pairs={{0,128},{16,144},{32,160},{48,176},{64,192},{80,208},{96,224},{112... | collective-permute-start | bytes 442376 | tf_op jit(solution)/shard_map/ppermute | solution.py:49

commit v2 on v1

--- a/solution.py
+++ b/solution.py
@@ -51,6 +51,10 @@
 
 def swap_core(v):
     return lax.ppermute(v, "row", row_pairs(lambda x, y, c: (x, y, 1 - c)))
+
+
+def xor_z(v, b):
+    return lax.ppermute(v, "col", col_pairs(lambda z, h: (z ^ b, h)))
 
 
 def coords():
@@ -257,44 +261,67 @@
     )
 
 
+def together(*values):
+    return lax.optimization_barrier(values)
+
+
 def shards(images, texts, pairs, log_scale, bias):
-    block = jnp.concatenate([texts, swap_xlo(texts)], axis=0)
-    behind = shift_y(block, 1)
-    ahead = shift_y(block, -1)
-    across = shift_y(behind, 1)
-    mine = [block, ahead, across, behind]
-    yp, ypt, brow, bcol = run_text(mine, swap_core(jnp.stack(mine)))
-
-    up = down = jnp.concatenate([images, swap_xhi(images)], axis=0)
+    other_img, other_txt = together(swap_xhi(images), swap_xlo(texts))
+    up = down = jnp.concatenate([images, other_img], axis=0)
+    block = jnp.concatenate([texts, other_txt], axis=0)
     ring = [[] for _ in range(NZ)]
     ring[0] = [up]
-    for k in range(1, NZ // 2):
-        up, down = shift_z(up, 1), shift_z(down, -1)
-        ring[NZ - k], ring[k] = [up], [down]
+    up, down, behind, ahead = together(
+        shift_z(up, 1), shift_z(down, -1), shift_y(block, 1), shift_y(block, -1)
+    )
+    ring[NZ - 1], ring[1] = [up], [down]
+    up, down, across = together(shift_z(up, 1), shift_z(down, -1), shift_y(behind, 1))
+    ring[NZ - 2], ring[2] = [up], [down]
+    mine = [block, ahead, across, behind]
+    up, down, others = together(shift_z(up, 1), shift_z(down, -1), swap_core(jnp.stack(mine)))
+    ring[NZ - 3], ring[3] = [up], [down]
     ring[NZ // 2] = [shift_z(up[:, :HALF], 1), shift_z(down[:, HALF:], -1)]
+    yp, ypt, brow, bcol = run_text(mine, others)
+
     res = run_image([p for r in ring for p in r], pairs, log_scale, bias, yp, ypt, bcol)
     xp, cx, sj, loss = res[:4]
     terms = list(res[4:8]) + [None] + list(res[10:13])
-
-    up = jnp.pad(wide(shift_z(res[8], 1)), ((0, 0), (0, HALF)))
-    down = jnp.pad(wide(shift_z(res[9], -1)), ((0, 0), (HALF, 0)))
-    for k in range(NZ // 2 - 1, 0, -1):
-        up = shift_z((terms[k] + wide(up)).astype(BF16), 1)
-        down = shift_z((terms[NZ - k] + wide(down)).astype(BF16), -1)
+    loss = loss.reshape(8, 128)
+
+    up, down = together(shift_z(res[8], 1), shift_z(res[9], -1))
+    lost, xp, cx = together(swap_xhi(loss), xp, cx)
+    cap = run_caption(xp, cx, yp, brow, sj)
+    loss = loss + lost
+    up = jnp.pad(wide(up), ((0, 0), (0, HALF)))
+    down = jnp.pad(wide(down), ((0, 0), (HALF, 0)))
+    up, down, got, lost = together(
+        shift_z((terms[3] + up).astype(BF16), 1),
+        shift_z((terms[5] + down).astype(BF16), -1),
+        swap_core(cap[NY]),
+        xor_z(loss, 1),
+    )
+    loss = loss + lost
+    part = [cap[k] + wide(got[k]) for k in range(NY)]
+    up, down, tup, tdown, lost = together(
+        shift_z((terms[2] + wide(up)).astype(BF16), 1),
+        shift_z((terms[6] + wide(down)).astype(BF16), -1),
+        shift_y(part[2].astype(BF16), 1),
+        shift_y(part[3].astype(BF16), -1),
+        xor_z(loss, 2),
+    )
+    loss = loss + lost
+    up, down, tup, lost = together(
+        shift_z((terms[1] + wide(up)).astype(BF16), 1),
+        shift_z((terms[7] + wide(down)).astype(BF16), -1),
+        shift_y((part[1] + wide(tup)).astype(BF16), 1),
+        xor_z(loss, 4),
+    )
+    loss = loss + lost
     total = terms[0] + wide(up) + wide(down)
     image_grad = total[:SH] + wide(swap_xhi(total[SH:].astype(BF16)))
-
-    cap = run_caption(xp, cx, yp, brow, sj)
-    got = swap_core(cap[NY])
-    part = [cap[k] + wide(got[k]) for k in range(NY)]
-    up = shift_y(part[2].astype(BF16), 1)
-    down = shift_y(part[3].astype(BF16), -1)
-    up = shift_y((part[1] + wide(up)).astype(BF16), 1)
-    total = part[0] + wide(up) + wide(down)
+    total = part[0] + wide(tup) + wide(tdown)
     text_grad = total[:SH] + wide(swap_xlo(total[SH:].astype(BF16)))
-
-    row_loss = jnp.sum(lax.all_gather(loss, "col", axis=0, tiled=True), axis=0)
-    return (row_loss, image_grad, text_grad)
+    return (loss.reshape(N), image_grad, text_grad)
 
 
 def solution(mesh):

time: 167 us -> 131 us (0.78)
  blocking collectives: 44 us -> 0 us
  waiting for transfers between devices: 46.7 us -> 58.4 us
  other arithmetic: 6.55 us -> 3.19 us
    all_gather x1 -> x0, blocking collectives: 44 us -> none  [shards(): row_loss = jnp.sum(lax.all_gather(loss, 'col', axis=0, tiled=True), axis=0)]
    ppermute x0 -> x3, waiting for transfers between devices: none -> 15 us  [xor_z(): return lax.ppermute(v, 'col', col_pairs(lambda z, h: (z ^ b, h)))]
    ppermute x6, waiting for transfers between devices: 8.73 us -> 4.17 us  [shift_y(): lax.ppermute(v, 'row', row_pairs(lambda x, y, c: (x, (y + d) % NY, c)))]
    ppermute x16, starting transfers between devices: 30.3 us -> 26.8 us  [shift_z(): return lax.ppermute(v, 'col', col_pairs(lambda z, h: ((z + d) % NZ, h)))]
    ppermute x2 -> x3, waiting for transfers between devices: 5.44 us -> 8.27 us  [swap_xhi(): return lax.ppermute(v, 'col', col_pairs(lambda z, h: (z, 1 - h)))]
    ppermute x16, waiting for transfers between devices: 29.2 us -> 26.4 us  [shift_z(): return lax.ppermute(v, 'col', col_pairs(lambda z, h: ((z + d) % NZ, h)))]
    ppermute x2 -> x3, starting transfers between devices: 3.12 us -> 5.89 us  [swap_xhi(): return lax.ppermute(v, 'col', col_pairs(lambda z, h: (z, 1 - h)))]
    ppermute x0 -> x3, starting transfers between devices: none -> 2.47 us  [xor_z(): return lax.ppermute(v, 'col', col_pairs(lambda z, h: (z ^ b, h)))]
  transfers between devices with their start and end apart: 28 -> 32, of which waited for: 14 -> 20; matrix products, arithmetic and copies ran while one was open for 4% -> 3% of each run, Pallas kernels for 3% -> 2%
where the time goes in v2:
time: 131 us; the launch traced here: 128 us
  waiting for transfers between devices  58.4 us (45%)
  starting transfers between devices  44.5 us (34%)
  Pallas kernels  17.9 us (14%)
  other arithmetic  3.19 us (2%)
  between operations  2.19 us (2%)
  local copies, waits for them, and re-layouts  1.93 us (1%)
    ppermute x16, starting transfers between devices, shift_z(): return lax.ppermute(v, 'col', col_pairs(lambda z, h: ((z + d) % NZ, h)))  26.8 us
    ppermute x16, waiting for transfers between devices, shift_z(): return lax.ppermute(v, 'col', col_pairs(lambda z, h: ((z + d) % NZ, h)))  26.4 us
    pallas_call x3, Pallas kernels, call(): pl.pallas_call(kernel, out_shape=out_shape, in_specs=specs, out_specs=[vm...  17.9 us
    ppermute x3, waiting for transfers between devices, xor_z(): return lax.ppermute(v, 'col', col_pairs(lambda z, h: (z ^ b, h)))  15 us
    ppermute x3, waiting for transfers between devices, swap_xhi(): return lax.ppermute(v, 'col', col_pairs(lambda z, h: (z, 1 - h)))  8.27 us
    ppermute x6, starting transfers between devices, shift_y(): lax.ppermute(v, 'row', row_pairs(lambda x, y, c: (x, (y + d) % NY, c)))  7.05 us
    ppermute x3, starting transfers between devices, swap_xhi(): return lax.ppermute(v, 'col', col_pairs(lambda z, h: (z, 1 - h)))  5.89 us
    ppermute x2, waiting for transfers between devices, swap_xlo(): return lax.ppermute(v, 'row', row_pairs(lambda x, y, c: (1 - x, y, c)))  4.54 us
  transfers between devices with their start and end apart: 32, of which 20 were waited for; matrix products, arithmetic and copies ran while one was open for 3% of the time, Pallas kernels for 2%

profile of v2, /device:TPU:8, one launch (start us, length us, event | category | flops | bytes accessed | tf_op | source)
XLA Modules:
  0.0 128.1 jit_solution(11925745608385117259)
XLA Ops:
  0.6 3.1 %collective-permute-start = (bf16[72,1024]{1,0:T(8,128)(2,1)}, bf16[72,1024]{1,0:T(8,128)(2,1)S(1)}, u32[]{:S(2)}, u32[]{:S(2)}) collective-permute-start(bf16[72,1024]{1,0:T(8,128)(2,1)} %param.5), channel_id=1, source_target_pairs={{0,1},{1,0},{2,3},{3,2},{4,5},{5,4},{6,7},{7,6},{8,9},{9,8},{10,11... | collective-permute-start | bytes 442376 | tf_op jit(solution)/shard_map/ppermute | solution.py:45
  6.2 3.0 %collective-permute-done = bf16[72,1024]{1,0:T(8,128)(2,1)S(1)} collective-permute-done((bf16[72,1024]{1,0:T(8,128)(2,1)}, bf16[72,1024]{1,0:T(8,128)(2,1)S(1)}, u32[]{:S(2)}, u32[]{:S(2)}) %collective-permute-start) | collective-permute-done | bytes 147488 | tf_op jit(solution)/shard_map/ppermute | solution.py:45
  9.2 2.1 %collective-permute-done.1 = bf16[72,1024]{1,0:T(8,128)(2,1)S(1)} collective-permute-done((bf16[72,1024]{1,0:T(8,128)(2,1)}, bf16[72,1024]{1,0:T(8,128)(2,1)S(1)}, u32[]{:S(2)}, u32[]{:S(2)}) %collective-permute-start.1) | collective-permute-done | bytes 147488 | tf_op jit(solution)/shard_map/ppermute | solution.py:49
  11.8 1.6 %collective-permute-start.4 = (bf16[144,1024]{1,0:T(8,128)(2,1)S(1)}, bf16[144,1024]{1,0:T(8,128)(2,1)S(1)}, u32[]{:S(2)}, u32[]{:S(2)}) collective-permute-start(bf16[144,1024]{1,0:T(8,128)(2,1)S(1)} %constant_dynamic-update-slice_fusion.2.refs_0_), channel_id=1, source_target_pairs={{0,32},{16,48},{32,64},{48,80},{64,96},{80,112},{96,0},{112,16},{1... | collective-permute-start | bytes 884744 | tf_op jit(solution)/shard_map/ppermute | solution.py:41
  13.4 5.9 %collective-permute-start.3 = (bf16[144,1024]{1,0:T(8,128)(2,1)S(1)}, bf16[144,1024]{1,0:T(8,128)(2,1)S(1)}, u32[]{:S(2)}, u32[]{:S(2)}) collective-permute-start(bf16[144,1024]{1,0:T(8,128)(2,1)S(1)} %constant_dynamic-update-slice_fusion.refs_0_), channel_id=1, source_target_pairs={{0,14},{1,15},{2,0},{3,1},{4,2},{5,3},{6,4},{7,5},{8,6},{9,7},{10,... | collective-permute-start | bytes 884744 | tf_op jit(solution)/shard_map/ppermute | solution.py:37
  20.7 3.5 %collective-permute-done.3.refs_1_ = bf16[144,1024]{1,0:T(8,128)(2,1)S(1)} collective-permute-done((bf16[144,1024]{1,0:T(8,128)(2,1)S(1)}, bf16[144,1024]{1,0:T(8,128)(2,1)S(1)}, u32[]{:S(2)}, u32[]{:S(2)}) %collective-permute-start.3) | collective-permute-done | bytes 294944 | tf_op jit(solution)/shard_map/ppermute | solution.py:37
  24.2 3.4 %collective-permute-done.2.refs_8_ = bf16[144,1024]{1,0:T(8,128)(2,1)S(1)} collective-permute-done((bf16[144,1024]{1,0:T(8,128)(2,1)S(1)}, bf16[144,1024]{1,0:T(8,128)(2,1)S(1)}, u32[]{:S(2)}, u32[]{:S(2)}) %collective-permute-start.2) | collective-permute-done | bytes 294944 | tf_op jit(solution)/shard_map/ppermute | solution.py:37
  27.9 1.7 %collective-permute-start.6 = (bf16[144,1024]{1,0:T(8,128)(2,1)S(1)}, bf16[144,1024]{1,0:T(8,128)(2,1)S(1)}, u32[]{:S(2)}, u32[]{:S(2)}) collective-permute-start(bf16[144,1024]{1,0:T(8,128)(2,1)S(1)} %collective-permute-done.2.refs_8_), channel_id=1, source_target_pairs={{0,2},{1,3},{2,4},{3,5},{4,6},{5,7},{6,8},{7,9},{8,10},{9,11},{10,... | collective-permute-start | bytes 884744 | tf_op jit(solution)/shard_map/ppermute | solution.py:37
  29.6 1.6 %collective-permute-start.8 = (bf16[144,1024]{1,0:T(8,128)(2,1)S(1)}, bf16[144,1024]{1,0:T(8,128)(2,1)S(1)}, u32[]{:S(2)}, u32[]{:S(2)}) collective-permute-start(bf16[144,1024]{1,0:T(8,128)(2,1)S(1)} %collective-permute-done.4.refs_3_), channel_id=1, source_target_pairs={{0,32},{16,48},{32,64},{48,80},{64,96},{80,112},{96,0},{112,16},{1... | collective-permute-start | bytes 884744 | tf_op jit(solution)/shard_map/ppermute | solution.py:41
  31.2 3.1 %collective-permute-done.7.refs_2_ = bf16[144,1024]{1,0:T(8,128)(2,1)S(1)} collective-permute-done((bf16[144,1024]{1,0:T(8,128)(2,1)S(1)}, bf16[144,1024]{1,0:T(8,128)(2,1)S(1)}, u32[]{:S(2)}, u32[]{:S(2)}) %collective-permute-start.7) | collective-permute-done | bytes 294944 | tf_op jit(solution)/shard_map/ppermute | solution.py:37
  36.6 1.6 %collective-permute-start.10 = (bf16[144,1024]{1,0:T(8,128)(2,1)S(1)}, bf16[144,1024]{1,0:T(8,128)(2,1)S(1)}, u32[]{:S(2)}, u32[]{:S(2)}) collective-permute-start(bf16[144,1024]{1,0:T(8,128)(2,1)S(1)} %collective-permute-done.7.refs_2_), channel_id=1, source_target_pairs={{0,14},{1,15},{2,0},{3,1},{4,2},{5,3},{6,4},{7,5},{8,6},{9,7},{10,... | collective-permute-start | bytes 884744 | tf_op jit(solution)/shard_map/ppermute | solution.py:37
  38.7 7.3 %collective-permute-done.10.refs_3_ = bf16[144,1024]{1,0:T(8,128)(2,1)S(1)} collective-permute-done((bf16[144,1024]{1,0:T(8,128)(2,1)S(1)}, bf16[144,1024]{1,0:T(8,128)(2,1)S(1)}, u32[]{:S(2)}, u32[]{:S(2)}) %collective-permute-start.10) | collective-permute-done | bytes 294944 | tf_op jit(solution)/shard_map/ppermute | solution.py:37
  46.0 2.4 %collective-permute-done.9.refs_6_ = bf16[144,1024]{1,0:T(8,128)(2,1)S(1)} collective-permute-done((bf16[144,1024]{1,0:T(8,128)(2,1)S(1)}, bf16[144,1024]{1,0:T(8,128)(2,1)S(1)}, u32[]{:S(2)}, u32[]{:S(2)}) %collective-permute-start.9) | collective-permute-done | bytes 294944 | tf_op jit(solution)/shard_map/ppermute | solution.py:37
  48.6 3.2 %collective-permute-start.13 = (bf16[144,512]{1,0:T(8,128)(2,1)S(1)}, bf16[144,512]{1,0:T(8,128)(2,1)S(1)}, u32[]{:S(2)}, u32[]{:S(2)}) collective-permute-start(bf16[144,512]{1,0:T(8,128)(2,1)S(1)} %slice.33), channel_id=1, source_target_pairs={{0,14},{1,15},{2,0},{3,1},{4,2},{5,3},{6,4},{7,5},{8,6},{9,7},{10,... | collective-permute-start | bytes 442376 | tf_op jit(solution)/shard_map/ppermute | solution.py:37
  53.1 2.1 %shard_map.76 = (bf16[1152,1024]{1,0:T(8,128)(2,1)S(1)}, bf16[1024,1152]{1,0:T(8,128)(2,1)S(1)}, f32[1,1024]{1,0:T(1,128)S(1)}, f32[1024,128]{1,0:T(8,128)S(1)}) custom-call(bf16[144,1024]{1,0:T(8,128)(2,1)S(1)} %constant_dynamic-update-slice_fusion.2.refs_0_, bf16[144,1024]{1,0:T(8,128)(2,1)S(1)} %collective-permute-done.5.refs_1_, ...), custom_call_target="tpu_custom_call" | custom-call | flops 67108864 | bytes 7606272 | tf_op jit(solution)/shard_map/pallas_call | solution.py:212
  55.3 12.2 %shard_map.77 = (bf16[1152,1024]{1,0:T(8,128)(2,1)S(1)}, bf16[1024,1024]{1,0:T(8,128)(2,1)S(1)}, f32[1,1024]{1,0:T(1,128)S(1)}, f32[1,1024]{1,0:T(1,128)S(1)}, f...) custom-call(bf16[144,1024]{1,0:T(8,128)(2,1)S(1)} %constant_dynamic-, ...), custom_call_target="tpu_custom_call" | custom-call | flops 4831838208 | bytes 16494600 | tf_op jit(solution)/shard_map/pallas_call | solution.py:212
  67.5 2.1 %collective-permute-start.14 = (f32[8,128]{1,0:T(8,128)S(1)}, f32[8,128]{1,0:T(8,128)S(1)}, u32[]{:S(2)}, u32[]{:S(2)}) collective-permute-start(f32[8,128]{1,0:T(8,128)S(1)} %bitcast.24), channel_id=1, source_target_pairs={{0,1},{1,0},{2,3},{3,2},{4,5},{5,4},{6,7},{7,6},{8,9},{9,8},{10,11... | collective-permute-start | bytes 12296 | tf_op jit(solution)/shard_map/ppermute | solution.py:45
  69.6 3.1 %collective-permute-done.14 = f32[8,128]{1,0:T(8,128)S(1)} collective-permute-done((f32[8,128]{1,0:T(8,128)S(1)}, f32[8,128]{1,0:T(8,128)S(1)}, u32[]{:S(2)}, u32[]{:S(2)}) %collective-permute-start.14) | collective-permute-done | bytes 4128 | tf_op jit(solution)/shard_map/ppermute | solution.py:45
  72.7 3.5 %shard_map.78 = (f32[144,1024]{1,0:T(8,128)S(1)}, f32[144,1024]{1,0:T(8,128)S(1)}, f32[144,1024]{1,0:T(8,128)S(1)}, f32[144,1024]{1,0:T(8,128)S(1)}, bf16[4,144,1024]{2,1,0:T(8,128)(2,1)S(1)}) custom-call(bf16[1152,1024]{1,0:T(8,128)(2,1)S(1)} %get-tuple-element.80.xp, bf16[1024,1024]{1,0:T(8,128)(2,1)S(1)} %get-tuple-element.81.cx, ...), custom_call_target="tpu_custom_call" | custom-call | flops 2415919104 | bytes 10362880 | tf_op jit(solution)/shard_map/pallas_call | solution.py:212
  76.4 3.2 %collective-permute-start.16 = (bf16[144,512]{1,0:T(8,128)(2,1)S(1)}, bf16[144,512]{1,0:T(8,128)(2,1)S(1)}, u32[]{:S(2)}, u32[]{:S(2)}) collective-permute-start(bf16[144,512]{1,0:T(8,128)(2,1)S(1)} %get-tuple-element.76), channel_id=1, source_target_pairs={{0,14},{1,15},{2,0},{3,1},{4,2},{5,3},{6,4},{7,5},{8,6},{9,7},{10,... | collective-permute-start | bytes 442376 | tf_op jit(solution)/shard_map/ppermute | solution.py:37
  79.7 4.2 %collective-permute-done.15 = bf16[144,512]{1,0:T(8,128)(2,1)S(1)} collective-permute-done((bf16[144,512]{1,0:T(8,128)(2,1)S(1)}, bf16[144,512]{1,0:T(8,128)(2,1)S(1)}, u32[]{:S(2)}, u32[]{:S(2)}) %collective-permute-start.15) | collective-permute-done | bytes 147488 | tf_op jit(solution)/shard_map/ppermute | solution.py:37
  84.0 3.3 %collective-permute-start.18 = (bf16[144,1024]{1,0:T(8,128)(2,1)S(1)}, bf16[144,1024]{1,0:T(8,128)(2,1)S(1)}, u32[]{:S(2)}, u32[]{:S(2)}) collective-permute-start(bf16[144,1024]{1,0:T(8,128)(2,1)S(1)} %add_convert_fusion.4), channel_id=1, source_target_pairs={{0,14},{1,15},{2,0},{3,1},{4,2},{5,3},{6,4},{7,5},{8,6},{9,7},{10,... | collective-permute-start | bytes 884744 | tf_op jit(solution)/shard_map/ppermute | solution.py:37
  87.3 5.4 %collective-permute-done.20 = f32[8,128]{1,0:T(8,128)S(1)} collective-permute-done((f32[8,128]{1,0:T(8,128)S(1)}, f32[8,128]{1,0:T(8,128)S(1)}, u32[]{:S(2)}, u32[]{:S(2)}) %collective-permute-start.20) | collective-permute-done | bytes 4128 | tf_op jit(solution)/shard_map/ppermute | solution.py:57
  94.0 3.3 %collective-permute-start.22 = (bf16[144,1024]{1,0:T(8,128)(2,1)S(1)}, bf16[144,1024]{1,0:T(8,128)(2,1)S(1)}, u32[]{:S(2)}, u32[]{:S(2)}) collective-permute-start(bf16[144,1024]{1,0:T(8,128)(2,1)S(1)} %add_convert_fusion.2), channel_id=1, source_target_pairs={{0,14},{1,15},{2,0},{3,1},{4,2},{5,3},{6,4},{7,5},{8,6},{9,7},{10,... | collective-permute-start | bytes 884744 | tf_op jit(solution)/shard_map/ppermute | solution.py:37
  97.5 3.0 %collective-permute-start.24 = (bf16[144,1024]{1,0:T(8,128)(2,1)S(1)}, bf16[144,1024]{1,0:T(8,128)(2,1)S(1)}, u32[]{:S(2)}, u32[]{:S(2)}) collective-permute-start(bf16[144,1024]{1,0:T(8,128)(2,1)S(1)} %get-tuple-element.107), channel_id=1, source_target_pairs={{0,96},{16,112},{32,0},{48,16},{64,32},{80,48},{96,64},{112,80},{1... | collective-permute-start | bytes 884744 | tf_op jit(solution)/shard_map/ppermute | solution.py:41
  100.5 4.5 %collective-permute-done.25 = f32[8,128]{1,0:T(8,128)S(1)} collective-permute-done((f32[8,128]{1,0:T(8,128)S(1)}, f32[8,128]{1,0:T(8,128)S(1)}, u32[]{:S(2)}, u32[]{:S(2)}) %collective-permute-start.25) | collective-permute-done | bytes 4128 | tf_op jit(solution)/shard_map/ppermute | solution.py:57
  105.1 2.2 %collective-permute-done.23 = bf16[144,1024]{1,0:T(8,128)(2,1)S(1)} collective-permute-done((bf16[144,1024]{1,0:T(8,128)(2,1)S(1)}, bf16[144,1024]{1,0:T(8,128)(2,1)S(1)}, u32[]{:S(2)}, u32[]{:S(2)}) %collective-permute-start.23) | collective-permute-done | bytes 294944 | tf_op jit(solution)/shard_map/ppermute | solution.py:41
  107.5 3.3 %collective-permute-start.27 = (bf16[144,1024]{1,0:T(8,128)(2,1)S(1)}, bf16[144,1024]{1,0:T(8,128)(2,1)S(1)}, u32[]{:S(2)}, u32[]{:S(2)}) collective-permute-start(bf16[144,1024]{1,0:T(8,128)(2,1)S(1)} %add_convert_fusion), channel_id=1, source_target_pairs={{0,14},{1,15},{2,0},{3,1},{4,2},{5,3},{6,4},{7,5},{8,6},{9,7},{10,... | collective-permute-start | bytes 884744 | tf_op jit(solution)/shard_map/ppermute | solution.py:37
  111.3 2.5 %collective-permute-start.29 = (f32[8,128]{1,0:T(8,128)S(1)}, f32[8,128]{1,0:T(8,128)S(1)}, u32[]{:S(2)}, u32[]{:S(2)}) collective-permute-start(f32[8,128]{1,0:T(8,128)S(1)} %add.75), channel_id=1, source_target_pairs={{0,8},{1,9},{2,10},{3,11},{4,12},{5,13},{6,14},{7,15},{8,0},{9,1},... | collective-permute-start | bytes 12296 | tf_op jit(solution)/shard_map/ppermute | solution.py:57
  113.8 5.1 %collective-permute-done.29 = f32[8,128]{1,0:T(8,128)S(1)} collective-permute-done((f32[8,128]{1,0:T(8,128)S(1)}, f32[8,128]{1,0:T(8,128)S(1)}, u32[]{:S(2)}, u32[]{:S(2)}) %collective-permute-start.29) | collective-permute-done | bytes 4128 | tf_op jit(solution)/shard_map/ppermute | solution.py:57
  122.0 2.4 %collective-permute-done.31 = bf16[72,1024]{1,0:T(8,128)(2,1)S(1)} collective-permute-done((bf16[72,1024]{1,0:T(8,128)(2,1)S(1)}, bf16[72,1024]{1,0:T(8,128)(2,1)S(1)}, u32[]{:S(2)}, u32[]{:S(2)}) %collective-permute-start.31) | collective-permute-done | bytes 147488 | tf_op jit(solution)/shard_map/ppermute | solution.py:49
  125.2 2.2 %collective-permute-done.30 = bf16[72,1024]{1,0:T(8,128)(2,1)S(1)} collective-permute-done((bf16[72,1024]{1,0:T(8,128)(2,1)S(1)}, bf16[72,1024]{1,0:T(8,128)(2,1)S(1)}, u32[]{:S(2)}, u32[]{:S(2)}) %collective-permute-start.30) | collective-permute-done | bytes 147488 | tf_op jit(solution)/shard_map/ppermute | solution.py:45
  (62 shorter events, 14.7 us)
Async XLA Ops:
  0.6 8.5 %collective-permute-start = (bf16[72,1024]{1,0:T(8,128)(2,1)}, bf16[72,1024]{1,0:T(8,128)(2,1)S(1)}, u32[]{:S(2)}, u32[]{:S(2)}) collective-permute-start(bf16[72,1024]{1,0:T(8,128)(2,1)} %param.5), channel_id=1, source_target_pairs={{0,1},{1,0},{2,3},{3,2},{4,5},{5,4},{6,7},{7,6},{8,9},{9,8},{10,11... | collective-permute-start | bytes 442376 | tf_op jit(solution)/shard_map/ppermute | solution.py:45
  3.7 7.5 %collective-permute-start.1 = (bf16[72,1024]{1,0:T(8,128)(2,1)}, bf16[72,1024]{1,0:T(8,128)(2,1)S(1)}, u32[]{:S(2)}, u32[]{:S(2)}) collective-permute-start(bf16[72,1024]{1,0:T(8,128)(2,1)} %param.6), channel_id=1, source_target_pairs={{0,128},{16,144},{32,160},{48,176},{64,192},{80,208},{96,224},{112... | collective-permute-start | bytes 442376 | tf_op jit(solution)/shard_map/ppermute | solution.py:49
  11.3 8.1 %collective-permute-start.5 = (bf16[144,1024]{1,0:T(8,128)(2,1)S(1)}, bf16[144,1024]{1,0:T(8,128)(2,1)S(1)}, u32[]{:S(2)}, u32[]{:S(2)}) collective-permute-start(bf16[144,1024]{1,0:T(8,128)(2,1)S(1)} %constant_dynamic-update-slice_fusion.2.refs_0_), channel_id=1, source_target_pairs={{0,96},{16,112},{32,0},{48,16},{64,32},{80,48},{96,64},{112,80},{1... | collective-permute-start | bytes 884744 | tf_op jit(solution)/shard_map/ppermute | solution.py:41
  11.8 8.9 %collective-permute-start.4 = (bf16[144,1024]{1,0:T(8,128)(2,1)S(1)}, bf16[144,1024]{1,0:T(8,128)(2,1)S(1)}, u32[]{:S(2)}, u32[]{:S(2)}) collective-permute-start(bf16[144,1024]{1,0:T(8,128)(2,1)S(1)} %constant_dynamic-update-slice_fusion.2.refs_0_), channel_id=1, source_target_pairs={{0,32},{16,48},{32,64},{48,80},{64,96},{80,112},{96,0},{112,16},{1... | collective-permute-start | bytes 884744 | tf_op jit(solution)/shard_map/ppermute | solution.py:41
  13.4 10.8 %collective-permute-start.3 = (bf16[144,1024]{1,0:T(8,128)(2,1)S(1)}, bf16[144,1024]{1,0:T(8,128)(2,1)S(1)}, u32[]{:S(2)}, u32[]{:S(2)}) collective-permute-start(bf16[144,1024]{1,0:T(8,128)(2,1)S(1)} %constant_dynamic-update-slice_fusion.refs_0_), channel_id=1, source_target_pairs={{0,14},{1,15},{2,0},{3,1},{4,2},{5,3},{6,4},{7,5},{8,6},{9,7},{10,... | collective-permute-start | bytes 884744 | tf_op jit(solution)/shard_map/ppermute | solution.py:37
  19.3 8.2 %collective-permute-start.2 = (bf16[144,1024]{1,0:T(8,128)(2,1)S(1)}, bf16[144,1024]{1,0:T(8,128)(2,1)S(1)}, u32[]{:S(2)}, u32[]{:S(2)}) collective-permute-start(bf16[144,1024]{1,0:T(8,128)(2,1)S(1)} %constant_dynamic-update-slice_fusion.refs_0_), channel_id=1, source_target_pairs={{0,2},{1,3},{2,4},{3,5},{4,6},{5,7},{6,8},{7,9},{8,10},{9,11},{10,... | collective-permute-start | bytes 884744 | tf_op jit(solution)/shard_map/ppermute | solution.py:37
  27.6 6.7 %collective-permute-start.7 = (bf16[144,1024]{1,0:T(8,128)(2,1)S(1)}, bf16[144,1024]{1,0:T(8,128)(2,1)S(1)}, u32[]{:S(2)}, u32[]{:S(2)}) collective-permute-start(bf16[144,1024]{1,0:T(8,128)(2,1)S(1)} %collective-permute-done.3.refs_1_), channel_id=1, source_target_pairs={{0,14},{1,15},{2,0},{3,1},{4,2},{5,3},{6,4},{7,5},{8,6},{9,7},{10,... | collective-permute-start | bytes 884744 | tf_op jit(solution)/shard_map/ppermute | solution.py:37
  27.9 7.9 %collective-permute-start.6 = (bf16[144,1024]{1,0:T(8,128)(2,1)S(1)}, bf16[144,1024]{1,0:T(8,128)(2,1)S(1)}, u32[]{:S(2)}, u32[]{:S(2)}) collective-permute-start(bf16[144,1024]{1,0:T(8,128)(2,1)S(1)} %collective-permute-done.2.refs_8_), channel_id=1, source_target_pairs={{0,2},{1,3},{2,4},{3,5},{4,6},{5,7},{6,8},{7,9},{8,10},{9,11},{10,... | collective-permute-start | bytes 884744 | tf_op jit(solution)/shard_map/ppermute | solution.py:37
  29.6 6.7 %collective-permute-start.8 = (bf16[144,1024]{1,0:T(8,128)(2,1)S(1)}, bf16[144,1024]{1,0:T(8,128)(2,1)S(1)}, u32[]{:S(2)}, u32[]{:S(2)}) collective-permute-start(bf16[144,1024]{1,0:T(8,128)(2,1)S(1)} %collective-permute-done.4.refs_3_), channel_id=1, source_target_pairs={{0,32},{16,48},{32,64},{48,80},{64,96},{80,112},{96,0},{112,16},{1... | collective-permute-start | bytes 884744 | tf_op jit(solution)/shard_map/ppermute | solution.py:41
  36.5 12.0 %collective-permute-start.11 = (bf16[4,144,1024]{2,1,0:T(8,128)(2,1)S(1)}, bf16[4,144,1024]{2,1,0:T(8,128)(2,1)S(1)}, u32[]{:S(2)}, u32[]{:S(2)}) collective-permute-start(bf16[4,144,1024]{2,1,0:T(8,128)(2,1)S(1)} %pad_maximum_fusion), channel_id=1, source_target_pairs={{0,16},{16,0},{32,48},{48,32},{64,80},{80,64},{96,112},{112,96},{1... | collective-permute-start | bytes 3538952 | tf_op jit(solution)/shard_map/ppermute | solution.py:53
  36.6 9.4 %collective-permute-start.10 = (bf16[144,1024]{1,0:T(8,128)(2,1)S(1)}, bf16[144,1024]{1,0:T(8,128)(2,1)S(1)}, u32[]{:S(2)}, u32[]{:S(2)}) collective-permute-start(bf16[144,1024]{1,0:T(8,128)(2,1)S(1)} %collective-permute-done.7.refs_2_), channel_id=1, source_target_pairs={{0,14},{1,15},{2,0},{3,1},{4,2},{5,3},{6,4},{7,5},{8,6},{9,7},{10,... | collective-permute-start | bytes 884744 | tf_op jit(solution)/shard_map/ppermute | solution.py:37
  38.1 10.3 %collective-permute-start.9 = (bf16[144,1024]{1,0:T(8,128)(2,1)S(1)}, bf16[144,1024]{1,0:T(8,128)(2,1)S(1)}, u32[]{:S(2)}, u32[]{:S(2)}) collective-permute-start(bf16[144,1024]{1,0:T(8,128)(2,1)S(1)} %collective-permute-done.6.refs_7_), channel_id=1, source_target_pairs={{0,2},{1,3},{2,4},{3,5},{4,6},{5,7},{6,8},{7,9},{8,10},{9,11},{10,... | collective-permute-start | bytes 884744 | tf_op jit(solution)/shard_map/ppermute | solution.py:37
  48.5 6.8 %collective-permute-start.12 = (bf16[144,512]{1,0:T(8,128)(2,1)S(1)}, bf16[144,512]{1,0:T(8,128)(2,1)S(1)}, u32[]{:S(2)}, u32[]{:S(2)}) collective-permute-start(bf16[144,512]{1,0:T(8,128)(2,1)S(1)} %slice.32), channel_id=1, source_target_pairs={{0,2},{1,3},{2,4},{3,5},{4,6},{5,7},{6,8},{7,9},{8,10},{9,11},{10,... | collective-permute-start | bytes 442376 | tf_op jit(solution)/shard_map/ppermute | solution.py:37
  48.6 6.7 %collective-permute-start.13 = (bf16[144,512]{1,0:T(8,128)(2,1)S(1)}, bf16[144,512]{1,0:T(8,128)(2,1)S(1)}, u32[]{:S(2)}, u32[]{:S(2)}) collective-permute-start(bf16[144,512]{1,0:T(8,128)(2,1)S(1)} %slice.33), channel_id=1, source_target_pairs={{0,14},{1,15},{2,0},{3,1},{4,2},{5,3},{6,4},{7,5},{8,6},{9,7},{10,... | collective-permute-start | bytes 442376 | tf_op jit(solution)/shard_map/ppermute | solution.py:37
  67.5 5.2 %collective-permute-start.14 = (f32[8,128]{1,0:T(8,128)S(1)}, f32[8,128]{1,0:T(8,128)S(1)}, u32[]{:S(2)}, u32[]{:S(2)}) collective-permute-start(f32[8,128]{1,0:T(8,128)S(1)} %bitcast.24), channel_id=1, source_target_pairs={{0,1},{1,0},{2,3},{3,2},{4,5},{5,4},{6,7},{7,6},{8,9},{9,8},{10,11... | collective-permute-start | bytes 12296 | tf_op jit(solution)/shard_map/ppermute | solution.py:45
  76.3 17.5 %collective-permute-start.19 = (bf16[4,144,1024]{2,1,0:T(8,128)(2,1)S(1)}, bf16[4,144,1024]{2,1,0:T(8,128)(2,1)S(1)}, u32[]{:S(2)}, u32[]{:S(2)}) collective-permute-start(bf16[4,144,1024]{2,1,0:T(8,128)(2,1)S(1)} %get-tuple-element.84), channel_id=1, source_target_pairs={{0,16},{16,0},{32,48},{48,32},{64,80},{80,64},{96,112},{112,96},{1... | collective-permute-start | bytes 3538952 | tf_op jit(solution)/shard_map/ppermute | solution.py:53
  76.4 7.5 %collective-permute-start.15 = (bf16[144,512]{1,0:T(8,128)(2,1)S(1)}, bf16[144,512]{1,0:T(8,128)(2,1)S(1)}, u32[]{:S(2)}, u32[]{:S(2)}) collective-permute-start(bf16[144,512]{1,0:T(8,128)(2,1)S(1)} %get-tuple-element.75), channel_id=1, source_target_pairs={{0,2},{1,3},{2,4},{3,5},{4,6},{5,7},{6,8},{7,9},{8,10},{9,11},{10,... | collective-permute-start | bytes 442376 | tf_op jit(solution)/shard_map/ppermute | solution.py:37
  76.4 7.4 %collective-permute-start.16 = (bf16[144,512]{1,0:T(8,128)(2,1)S(1)}, bf16[144,512]{1,0:T(8,128)(2,1)S(1)}, u32[]{:S(2)}, u32[]{:S(2)}) collective-permute-start(bf16[144,512]{1,0:T(8,128)(2,1)S(1)} %get-tuple-element.76), channel_id=1, source_target_pairs={{0,14},{1,15},{2,0},{3,1},{4,2},{5,3},{6,4},{7,5},{8,6},{9,7},{10,... | collective-permute-start | bytes 442376 | tf_op jit(solution)/shard_map/ppermute | solution.py:37
  83.9 9.8 %collective-permute-start.17 = (bf16[144,1024]{1,0:T(8,128)(2,1)S(1)}, bf16[144,1024]{1,0:T(8,128)(2,1)S(1)}, u32[]{:S(2)}, u32[]{:S(2)}) collective-permute-start(bf16[144,1024]{1,0:T(8,128)(2,1)S(1)} %add_convert_fusion.5), channel_id=1, source_target_pairs={{0,2},{1,3},{2,4},{3,5},{4,6},{5,7},{6,8},{7,9},{8,10},{9,11},{10,... | collective-permute-start | bytes 884744 | tf_op jit(solution)/shard_map/ppermute | solution.py:37
  84.0 9.7 %collective-permute-start.18 = (bf16[144,1024]{1,0:T(8,128)(2,1)S(1)}, bf16[144,1024]{1,0:T(8,128)(2,1)S(1)}, u32[]{:S(2)}, u32[]{:S(2)}) collective-permute-start(bf16[144,1024]{1,0:T(8,128)(2,1)S(1)} %add_convert_fusion.4), channel_id=1, source_target_pairs={{0,14},{1,15},{2,0},{3,1},{4,2},{5,3},{6,4},{7,5},{8,6},{9,7},{10,... | collective-permute-start | bytes 884744 | tf_op jit(solution)/shard_map/ppermute | solution.py:37
  87.3 5.4 %collective-permute-start.20 = (f32[8,128]{1,0:T(8,128)S(1)}, f32[8,128]{1,0:T(8,128)S(1)}, u32[]{:S(2)}, u32[]{:S(2)}) collective-permute-start(f32[8,128]{1,0:T(8,128)S(1)} %add.67), channel_id=1, source_target_pairs={{0,2},{1,3},{2,0},{3,1},{4,6},{5,7},{6,4},{7,5},{8,10},{9,11},{10,... | collective-permute-start | bytes 12296 | tf_op jit(solution)/shard_map/ppermute | solution.py:57
  93.8 11.2 %collective-permute-start.21 = (bf16[144,1024]{1,0:T(8,128)(2,1)S(1)}, bf16[144,1024]{1,0:T(8,128)(2,1)S(1)}, u32[]{:S(2)}, u32[]{:S(2)}) collective-permute-start(bf16[144,1024]{1,0:T(8,128)(2,1)S(1)} %add_convert_fusion.3), channel_id=1, source_target_pairs={{0,2},{1,3},{2,4},{3,5},{4,6},{5,7},{6,8},{7,9},{8,10},{9,11},{10,... | collective-permute-start | bytes 884744 | tf_op jit(solution)/shard_map/ppermute | solution.py:37
  94.0 11.0 %collective-permute-start.22 = (bf16[144,1024]{1,0:T(8,128)(2,1)S(1)}, bf16[144,1024]{1,0:T(8,128)(2,1)S(1)}, u32[]{:S(2)}, u32[]{:S(2)}) collective-permute-start(bf16[144,1024]{1,0:T(8,128)(2,1)S(1)} %add_convert_fusion.2), channel_id=1, source_target_pairs={{0,14},{1,15},{2,0},{3,1},{4,2},{5,3},{6,4},{7,5},{8,6},{9,7},{10,... | collective-permute-start | bytes 884744 | tf_op jit(solution)/shard_map/ppermute | solution.py:37
  97.5 7.6 %collective-permute-start.24 = (bf16[144,1024]{1,0:T(8,128)(2,1)S(1)}, bf16[144,1024]{1,0:T(8,128)(2,1)S(1)}, u32[]{:S(2)}, u32[]{:S(2)}) collective-permute-start(bf16[144,1024]{1,0:T(8,128)(2,1)S(1)} %get-tuple-element.107), channel_id=1, source_target_pairs={{0,96},{16,112},{32,0},{48,16},{64,32},{80,48},{96,64},{112,80},{1... | collective-permute-start | bytes 884744 | tf_op jit(solution)/shard_map/ppermute | solution.py:41
  100.5 6.8 %collective-permute-start.23 = (bf16[144,1024]{1,0:T(8,128)(2,1)S(1)}, bf16[144,1024]{1,0:T(8,128)(2,1)S(1)}, u32[]{:S(2)}, u32[]{:S(2)}) collective-permute-start(bf16[144,1024]{1,0:T(8,128)(2,1)S(1)} %get-tuple-element.108), channel_id=1, source_target_pairs={{0,32},{16,48},{32,64},{48,80},{64,96},{80,112},{96,0},{112,16},{1... | collective-permute-start | bytes 884744 | tf_op jit(solution)/shard_map/ppermute | solution.py:41
  100.5 4.5 %collective-permute-start.25 = (f32[8,128]{1,0:T(8,128)S(1)}, f32[8,128]{1,0:T(8,128)S(1)}, u32[]{:S(2)}, u32[]{:S(2)}) collective-permute-start(f32[8,128]{1,0:T(8,128)S(1)} %add.70), channel_id=1, source_target_pairs={{0,4},{1,5},{2,6},{3,7},{4,0},{5,1},{6,2},{7,3},{8,12},{9,13},{10,... | collective-permute-start | bytes 12296 | tf_op jit(solution)/shard_map/ppermute | solution.py:57
  107.4 11.5 %collective-permute-start.26 = (bf16[144,1024]{1,0:T(8,128)(2,1)S(1)}, bf16[144,1024]{1,0:T(8,128)(2,1)S(1)}, u32[]{:S(2)}, u32[]{:S(2)}) collective-permute-start(bf16[144,1024]{1,0:T(8,128)(2,1)S(1)} %add_convert_fusion.1), channel_id=1, source_target_pairs={{0,2},{1,3},{2,4},{3,5},{4,6},{5,7},{6,8},{7,9},{8,10},{9,11},{10,... | collective-permute-start | bytes 884744 | tf_op jit(solution)/shard_map/ppermute | solution.py:37
  107.5 11.3 %collective-permute-start.27 = (bf16[144,1024]{1,0:T(8,128)(2,1)S(1)}, bf16[144,1024]{1,0:T(8,128)(2,1)S(1)}, u32[]{:S(2)}, u32[]{:S(2)}) collective-permute-start(bf16[144,1024]{1,0:T(8,128)(2,1)S(1)} %add_convert_fusion), channel_id=1, source_target_pairs={{0,14},{1,15},{2,0},{3,1},{4,2},{5,3},{6,4},{7,5},{8,6},{9,7},{10,... | collective-permute-start | bytes 884744 | tf_op jit(solution)/shard_map/ppermute | solution.py:37
  111.0 7.9 %collective-permute-start.28 = (bf16[144,1024]{1,0:T(8,128)(2,1)S(1)}, bf16[144,1024]{1,0:T(8,128)(2,1)S(1)}, u32[]{:S(2)}, u32[]{:S(2)}) collective-permute-start(bf16[144,1024]{1,0:T(8,128)(2,1)S(1)} %fusion.3), channel_id=1, source_target_pairs={{0,32},{16,48},{32,64},{48,80},{64,96},{80,112},{96,0},{112,16},{1... | collective-permute-start | bytes 884744 | tf_op jit(solution)/shard_map/ppermute | solution.py:41
  111.3 7.5 %collective-permute-start.29 = (f32[8,128]{1,0:T(8,128)S(1)}, f32[8,128]{1,0:T(8,128)S(1)}, u32[]{:S(2)}, u32[]{:S(2)}) collective-permute-start(f32[8,128]{1,0:T(8,128)S(1)} %add.75), channel_id=1, source_target_pairs={{0,8},{1,9},{2,10},{3,11},{4,12},{5,13},{6,14},{7,15},{8,0},{9,1},... | collective-permute-start | bytes 12296 | tf_op jit(solution)/shard_map/ppermute | solution.py:57
  119.2 5.2 %collective-permute-start.31 = (bf16[72,1024]{1,0:T(8,128)(2,1)S(1)}, bf16[72,1024]{1,0:T(8,128)(2,1)S(1)}, u32[]{:S(2)}, u32[]{:S(2)}) collective-permute-start(bf16[72,1024]{1,0:T(8,128)(2,1)S(1)} %slice.54), channel_id=1, source_target_pairs={{0,128},{16,144},{32,160},{48,176},{64,192},{80,208},{96,224},{112... | collective-permute-start | bytes 442376 | tf_op jit(solution)/shard_map/ppermute | solution.py:49
  120.7 6.6 %collective-permute-start.30 = (bf16[72,1024]{1,0:T(8,128)(2,1)S(1)}, bf16[72,1024]{1,0:T(8,128)(2,1)S(1)}, u32[]{:S(2)}, u32[]{:S(2)}) collective-permute-start(bf16[72,1024]{1,0:T(8,128)(2,1)S(1)} %slice.55), channel_id=1, source_target_pairs={{0,1},{1,0},{2,3},{3,2},{4,5},{5,4},{6,7},{7,6},{8,9},{9,8},{10,11... | collective-permute-start | bytes 442376 | tf_op jit(solution)/shard_map/ppermute | solution.py:45
  (1 other events, 2.2 us)

commit v3 on v2

--- a/solution.py
+++ b/solution.py
@@ -67,14 +67,14 @@
 
 
 def text_kernel(*refs):
-    mine, others = refs[:4], refs[4]
-    yp, ypt, brow, bcol = refs[5:]
+    mine, others = refs[:4], refs[4:8]
+    yp, ypt, brow, bcol = refs[8:]
     xlo, y, core, z, xhi = coords()
     same = core == xhi
     total = jnp.zeros((1, N), F32)
     for k in range(NY):
         here = halves(mine[k][...].astype(F32))
-        away = halves(others[k].astype(F32))
+        away = halves(others[k][...].astype(F32))
         for other in range(2):
             a, b = here[other], away[other]
             block = jnp.concatenate([jnp.where(same, a, b), jnp.where(same, b, a)], axis=0)
@@ -181,8 +181,8 @@
 
 
 def caption_kernel(xp, cx, yp, brow, sj, *refs):
-    own, away = refs[:4], refs[4]
-    t_ref = refs[5]
+    own, away = refs[:4], refs[4:8]
+    t_ref = refs[8]
     xlo, y, core, z, xhi = coords()
     same = core == xhi
     W = 256
@@ -202,7 +202,7 @@
             here.append(jnp.where(same, p, q))
             there.append(jnp.where(same, q, p))
         own[k][...] = jnp.concatenate(here, axis=0)
-        away[k] = jnp.concatenate(there, axis=0).astype(BF16)
+        away[k][...] = jnp.concatenate(there, axis=0).astype(BF16)
 
 
 def call(kernel, out_shape, flops, args, scratch=(), smem=(), limit=32 * MIB):
@@ -233,7 +233,7 @@
         text_kernel,
         [sds((ROWS, N), BF16), sds((N, ROWS), BF16), sds((1, N), F32), sds((N, 128), F32)],
         N * N * 64,
-        list(mine) + [others],
+        list(mine) + list(others),
     )
 
 
@@ -254,32 +254,40 @@
 def run_caption(xp, cx, yp, brow, sj):
     return call(
         caption_kernel,
-        [sds((BL, N), F32)] * NY + [sds((NY, BL, N), BF16)],
+        [sds((BL, N), F32)] * NY + [sds((BL, N), BF16)] * NY,
         2 * N * N * ROWS,
         [xp, cx, yp, brow, sj],
         [pltpu.VMEM((ROWS, N), F32)],
     )
 
 
-def together(*values):
-    return lax.optimization_barrier(values)
+def after(value, *earlier):
+    return lax.optimization_barrier((value, *earlier))[0]
 
 
 def shards(images, texts, pairs, log_scale, bias):
-    other_img, other_txt = together(swap_xhi(images), swap_xlo(texts))
+    other_img, other_txt = swap_xhi(images), swap_xlo(texts)
     up = down = jnp.concatenate([images, other_img], axis=0)
     block = jnp.concatenate([texts, other_txt], axis=0)
     ring = [[] for _ in range(NZ)]
     ring[0] = [up]
-    up, down, behind, ahead = together(
-        shift_z(up, 1), shift_z(down, -1), shift_y(block, 1), shift_y(block, -1)
-    )
+    block = after(block, other_img)
+    behind, ahead = shift_y(block, 1), shift_y(block, -1)
+    others = [swap_core(block)]
+    up, down = shift_z(up, 1), shift_z(down, -1)
     ring[NZ - 1], ring[1] = [up], [down]
-    up, down, across = together(shift_z(up, 1), shift_z(down, -1), shift_y(behind, 1))
+    behind, ahead = after(behind, up, down), after(ahead, up, down)
+    across = shift_y(behind, 1)
+    others += [swap_core(ahead)]
+    last = swap_core(behind)
+    up, down = shift_z(up, 1), shift_z(down, -1)
     ring[NZ - 2], ring[2] = [up], [down]
+    across = after(across, up, down)
+    others += [swap_core(across), last]
     mine = [block, ahead, across, behind]
-    up, down, others = together(shift_z(up, 1), shift_z(down, -1), swap_core(jnp.stack(mine)))
+    up, down = shift_z(up, 1), shift_z(down, -1)
     ring[NZ - 3], ring[3] = [up], [down]
+    mine[0] = after(block, up, down)
     ring[NZ // 2] = [shift_z(up[:, :HALF], 1), shift_z(down[:, HALF:], -1)]
     yp, ypt, brow, bcol = run_text(mine, others)
 
@@ -288,35 +296,25 @@
     terms = list(res[4:8]) + [None] + list(res[10:13])
     loss = loss.reshape(8, 128)
 
-    up, down = together(shift_z(res[8], 1), shift_z(res[9], -1))
-    lost, xp, cx = together(swap_xhi(loss), xp, cx)
+    up, down = shift_z(res[8], 1), shift_z(res[9], -1)
     cap = run_caption(xp, cx, yp, brow, sj)
-    loss = loss + lost
+    loss = loss + swap_xhi(loss)
+    loss = loss + xor_z(after(loss, up, down), 1)
+    got = [swap_core(after(v, up, down)) for v in cap[NY:]]
     up = jnp.pad(wide(up), ((0, 0), (0, HALF)))
     down = jnp.pad(wide(down), ((0, 0), (HALF, 0)))
-    up, down, got, lost = together(
-        shift_z((terms[3] + up).astype(BF16), 1),
-        shift_z((terms[5] + down).astype(BF16), -1),
-        swap_core(cap[NY]),
-        xor_z(loss, 1),
-    )
-    loss = loss + lost
+    up = shift_z((terms[3] + up).astype(BF16), 1)
+    down = shift_z((terms[5] + down).astype(BF16), -1)
+    loss = loss + xor_z(after(loss, up, down), 2)
     part = [cap[k] + wide(got[k]) for k in range(NY)]
-    up, down, tup, tdown, lost = together(
-        shift_z((terms[2] + wide(up)).astype(BF16), 1),
-        shift_z((terms[6] + wide(down)).astype(BF16), -1),
-        shift_y(part[2].astype(BF16), 1),
-        shift_y(part[3].astype(BF16), -1),
-        xor_z(loss, 2),
-    )
-    loss = loss + lost
-    up, down, tup, lost = together(
-        shift_z((terms[1] + wide(up)).astype(BF16), 1),
-        shift_z((terms[7] + wide(down)).astype(BF16), -1),
-        shift_y((part[1] + wide(tup)).astype(BF16), 1),
-        xor_z(loss, 4),
-    )
-    loss = loss + lost
+    far, near = after(part[2].astype(BF16), up, down), after(part[3].astype(BF16), up, down)
+    tup, tdown = shift_y(far, 1), shift_y(near, -1)
+    up = shift_z((terms[2] + wide(up)).astype(BF16), 1)
+    down = shift_z((terms[6] + wide(down)).astype(BF16), -1)
+    loss = loss + xor_z(after(loss, up, down), 4)
+    tup = shift_y(after((part[1] + wide(tup)).astype(BF16), up, down), 1)
+    up = shift_z((terms[1] + wide(up)).astype(BF16), 1)
+    down = shift_z((terms[7] + wide(down)).astype(BF16), -1)
     total = terms[0] + wide(up) + wide(down)
     image_grad = total[:SH] + wide(swap_xhi(total[SH:].astype(BF16)))
     total = part[0] + wide(tup) + wide(tdown)

time: 131 us -> 112 us (0.85); the launches traced: 128 us -> 111 us
  waiting for transfers between devices: 58.4 us -> 30.4 us
  starting transfers between devices: 44.5 us -> 55 us
    ppermute x16, waiting for transfers between devices: 26.4 us -> 13.5 us  [shift_z(): return lax.ppermute(v, 'col', col_pairs(lambda z, h: ((z + d) % NZ, h)))]
    ppermute x3, waiting for transfers between devices: 15 us -> 7.48 us  [xor_z(): return lax.ppermute(v, 'col', col_pairs(lambda z, h: (z ^ b, h)))]
    ppermute x3, starting transfers between devices: 5.89 us -> 10.3 us  [swap_xhi(): return lax.ppermute(v, 'col', col_pairs(lambda z, h: (z, 1 - h)))]
    ppermute x2, waiting for transfers between devices: 4.54 us -> 0.48 us  [swap_xlo(): return lax.ppermute(v, 'row', row_pairs(lambda x, y, c: (1 - x, y, c)))]
    ppermute x6, waiting for transfers between devices: 4.17 us -> 0.27 us  [shift_y(): lax.ppermute(v, 'row', row_pairs(lambda x, y, c: (x, (y + d) % NY, c)))]
    ppermute x16, starting transfers between devices: 26.8 us -> 28.9 us  [shift_z(): return lax.ppermute(v, 'col', col_pairs(lambda z, h: ((z + d) % NZ, h)))]
    ppermute x3, starting transfers between devices: 2.47 us -> 4.4 us  [xor_z(): return lax.ppermute(v, 'col', col_pairs(lambda z, h: (z ^ b, h)))]
    ppermute x2 -> x8, starting transfers between devices: 0.19 us -> 1.6 us  [swap_core(): return lax.ppermute(v, 'row', row_pairs(lambda x, y, c: (x, y, 1 - c)))]
  transfers between devices with their start and end apart: 32 -> 38, of which waited for: 20 -> 17; matrix products, arithmetic and copies ran while one was open for 3% -> 4% of each run, Pallas kernels for 2% -> 5%
where the time goes in v3:
time: 112 us; the launch traced here: 111 us
  starting transfers between devices  55 us (49%)
  waiting for transfers between devices  30.4 us (27%)
  Pallas kernels  18.2 us (16%)
  other arithmetic  3.95 us (4%)
  between operations  2.17 us (2%)
    ppermute x16, starting transfers between devices, shift_z(): return lax.ppermute(v, 'col', col_pairs(lambda z, h: ((z + d) % NZ, h)))  28.9 us
    pallas_call x3, Pallas kernels, call(): pl.pallas_call(kernel, out_shape=out_shape, in_specs=specs, out_specs=[vm...  18.2 us
    ppermute x16, waiting for transfers between devices, shift_z(): return lax.ppermute(v, 'col', col_pairs(lambda z, h: ((z + d) % NZ, h)))  13.5 us
    ppermute x3, starting transfers between devices, swap_xhi(): return lax.ppermute(v, 'col', col_pairs(lambda z, h: (z, 1 - h)))  10.3 us
    ppermute x3, waiting for transfers between devices, swap_xhi(): return lax.ppermute(v, 'col', col_pairs(lambda z, h: (z, 1 - h)))  8.7 us
    ppermute x3, waiting for transfers between devices, xor_z(): return lax.ppermute(v, 'col', col_pairs(lambda z, h: (z ^ b, h)))  7.48 us
    ppermute x6, starting transfers between devices, shift_y(): lax.ppermute(v, 'row', row_pairs(lambda x, y, c: (x, (y + d) % NY, c)))  7.28 us
    ppermute x3, starting transfers between devices, xor_z(): return lax.ppermute(v, 'col', col_pairs(lambda z, h: (z ^ b, h)))  4.4 us
  transfers between devices with their start and end apart: 38, of which 17 were waited for; matrix products, arithmetic and copies ran while one was open for 4% of the time, Pallas kernels for 5%

profile of v3, /device:TPU:8, one launch (start us, length us, event | category | flops | bytes accessed | tf_op | source)
XLA Modules:
  0.0 110.8 jit_solution(9267827929983527938)
XLA Ops:
  0.6 3.1 %collective-permute-start = (bf16[72,1024]{1,0:T(8,128)(2,1)}, bf16[72,1024]{1,0:T(8,128)(2,1)S(1)}, u32[]{:S(2)}, u32[]{:S(2)}) collective-permute-start(bf16[72,1024]{1,0:T(8,128)(2,1)} %param.5), channel_id=1, source_target_pairs={{0,1},{1,0},{2,3},{3,2},{4,5},{5,4},{6,7},{7,6},{8,9},{9,8},{10,11... | collective-permute-start | bytes 442376 | tf_op jit(solution)/shard_map/ppermute | solution.py:45
  4.7 3.3 %collective-permute-done = bf16[72,1024]{1,0:T(8,128)(2,1)S(1)} collective-permute-done((bf16[72,1024]{1,0:T(8,128)(2,1)}, bf16[72,1024]{1,0:T(8,128)(2,1)S(1)}, u32[]{:S(2)}, u32[]{:S(2)}) %collective-permute-start) | collective-permute-done | bytes 147488 | tf_op jit(solution)/shard_map/ppermute | solution.py:45
  8.0 2.0 %collective-permute-start.4 = (bf16[144,1024]{1,0:T(8,128)(2,1)S(1)}, bf16[144,1024]{1,0:T(8,128)(2,1)S(1)}, u32[]{:S(2)}, u32[]{:S(2)}) collective-permute-start(bf16[144,1024]{1,0:T(8,128)(2,1)S(1)} %constant_dynamic-update-slice_fusion.refs_0_), channel_id=1, source_target_pairs={{0,2},{1,3},{2,4},{3,5},{4,6},{5,7},{6,8},{7,9},{8,10},{9,11},{10,... | collective-permute-start | bytes 884744 | tf_op jit(solution)/shard_map/ppermute | solution.py:37
  10.0 1.5 %collective-permute-start.9 = (bf16[72,1024]{1,0:T(8,128)(2,1)}, bf16[72,1024]{1,0:T(8,128)(2,1)S(1)}, u32[]{:S(2)}, u32[]{:S(2)}) collective-permute-start(bf16[72,1024]{1,0:T(8,128)(2,1)} %param.6), channel_id=1, source_target_pairs={{0,128},{16,144},{32,160},{48,176},{64,192},{80,208},{96,224},{112... | collective-permute-start | bytes 442376 | tf_op jit(solution)/shard_map/ppermute | solution.py:49
  11.5 4.0 %collective-permute-start.1 = (bf16[144,1024]{1,0:T(8,128)(2,1)S(1)}, bf16[144,1024]{1,0:T(8,128)(2,1)S(1)}, u32[]{:S(2)}, u32[]{:S(2)}) collective-permute-start(bf16[144,1024]{1,0:T(8,128)(2,1)S(1)} %constant_dynamic-update-slice_fusion.refs_0_), channel_id=1, source_target_pairs={{0,14},{1,15},{2,0},{3,1},{4,2},{5,3},{6,4},{7,5},{8,6},{9,7},{10,... | collective-permute-start | bytes 884744 | tf_op jit(solution)/shard_map/ppermute | solution.py:37
  16.5 1.7 %collective-permute-start.11 = (bf16[144,1024]{1,0:T(8,128)(2,1)S(1)}, bf16[144,1024]{1,0:T(8,128)(2,1)S(1)}, u32[]{:S(2)}, u32[]{:S(2)}) collective-permute-start(bf16[144,1024]{1,0:T(8,128)(2,1)S(1)} %pad_maximum_fusion.refs_0_), channel_id=1, source_target_pairs={{0,32},{16,48},{32,64},{48,80},{64,96},{80,112},{96,0},{112,16},{1... | collective-permute-start | bytes 884744 | tf_op jit(solution)/shard_map/ppermute | solution.py:41
  18.2 2.0 %collective-permute-done.4.refs_8_ = bf16[144,1024]{1,0:T(8,128)(2,1)S(1)} collective-permute-done((bf16[144,1024]{1,0:T(8,128)(2,1)S(1)}, bf16[144,1024]{1,0:T(8,128)(2,1)S(1)}, u32[]{:S(2)}, u32[]{:S(2)}) %collective-permute-start.4) | collective-permute-done | bytes 294944 | tf_op jit(solution)/shard_map/ppermute | solution.py:37
  20.7 3.7 %collective-permute-start.2 = (bf16[144,1024]{1,0:T(8,128)(2,1)S(1)}, bf16[144,1024]{1,0:T(8,128)(2,1)S(1)}, u32[]{:S(2)}, u32[]{:S(2)}) collective-permute-start(bf16[144,1024]{1,0:T(8,128)(2,1)S(1)} %collective-permute-done.1.refs_1_), channel_id=1, source_target_pairs={{0,14},{1,15},{2,0},{3,1},{4,2},{5,3},{6,4},{7,5},{8,6},{9,7},{10,... | collective-permute-start | bytes 884744 | tf_op jit(solution)/shard_map/ppermute | solution.py:37
  24.8 1.6 %collective-permute-start.12 = (bf16[144,1024]{1,0:T(8,128)(2,1)S(1)}, bf16[144,1024]{1,0:T(8,128)(2,1)S(1)}, u32[]{:S(2)}, u32[]{:S(2)}) collective-permute-start(bf16[144,1024]{1,0:T(8,128)(2,1)S(1)} %collective-permute-done.11.refs_3_), channel_id=1, source_target_pairs={{0,32},{16,48},{32,64},{48,80},{64,96},{80,112},{96,0},{112,16},{1... | collective-permute-start | bytes 884744 | tf_op jit(solution)/shard_map/ppermute | solution.py:41
  26.4 2.2 %collective-permute-done.5.refs_7_ = bf16[144,1024]{1,0:T(8,128)(2,1)S(1)} collective-permute-done((bf16[144,1024]{1,0:T(8,128)(2,1)S(1)}, bf16[144,1024]{1,0:T(8,128)(2,1)S(1)}, u32[]{:S(2)}, u32[]{:S(2)}) %collective-permute-start.5) | collective-permute-done | bytes 294944 | tf_op jit(solution)/shard_map/ppermute | solution.py:37
  28.6 3.7 %collective-permute-start.3 = (bf16[144,1024]{1,0:T(8,128)(2,1)S(1)}, bf16[144,1024]{1,0:T(8,128)(2,1)S(1)}, u32[]{:S(2)}, u32[]{:S(2)}) collective-permute-start(bf16[144,1024]{1,0:T(8,128)(2,1)S(1)} %collective-permute-done.2.refs_2_), channel_id=1, source_target_pairs={{0,14},{1,15},{2,0},{3,1},{4,2},{5,3},{6,4},{7,5},{8,6},{9,7},{10,... | collective-permute-start | bytes 884744 | tf_op jit(solution)/shard_map/ppermute | solution.py:37
  32.9 3.6 %collective-permute-done.6.refs_6_ = bf16[144,1024]{1,0:T(8,128)(2,1)S(1)} collective-permute-done((bf16[144,1024]{1,0:T(8,128)(2,1)S(1)}, bf16[144,1024]{1,0:T(8,128)(2,1)S(1)}, u32[]{:S(2)}, u32[]{:S(2)}) %collective-permute-start.6) | collective-permute-done | bytes 294944 | tf_op jit(solution)/shard_map/ppermute | solution.py:37
  37.0 3.5 %collective-permute-start.8 = (bf16[144,512]{1,0:T(8,128)(2,1)S(1)}, bf16[144,512]{1,0:T(8,128)(2,1)S(1)}, u32[]{:S(2)}, u32[]{:S(2)}) collective-permute-start(bf16[144,512]{1,0:T(8,128)(2,1)S(1)} %slice.27), channel_id=1, source_target_pairs={{0,14},{1,15},{2,0},{3,1},{4,2},{5,3},{6,4},{7,5},{8,6},{9,7},{10,... | collective-permute-start | bytes 442376 | tf_op jit(solution)/shard_map/ppermute | solution.py:37
  41.9 2.1 %shard_map.76 = (bf16[1152,1024]{1,0:T(8,128)(2,1)S(1)}, bf16[1024,1152]{1,0:T(8,128)(2,1)S(1)}, f32[1,1024]{1,0:T(1,128)S(1)}, f32[1024,128]{1,0:T(8,128)S(1)}) custom-call(bf16[144,1024]{1,0:T(8,128)(2,1)S(1)} %pad_maximum_fusion.refs_0_, bf16[144,1024]{1,0:T(8,128)(2,1)S(1)} %collective-permute-done.10.refs_1_, ...), custom_call_target="tpu_custom_call" | custom-call | flops 67108864 | bytes 7606272 | tf_op jit(solution)/shard_map/pallas_call | solution.py:212
  44.1 12.5 %shard_map.77 = (bf16[1152,1024]{1,0:T(8,128)(2,1)S(1)}, bf16[1024,1024]{1,0:T(8,128)(2,1)S(1)}, f32[1,1024]{1,0:T(1,128)S(1)}, f32[1,1024]{1,0:T(1,128)S(1)}, f...) custom-call(bf16[144,1024]{1,0:T(8,128)(2,1)S(1)} %constant_dynamic-, ...), custom_call_target="tpu_custom_call" | custom-call | flops 4831838208 | bytes 16494600 | tf_op jit(solution)/shard_map/pallas_call | solution.py:212
  56.6 2.3 %collective-permute-start.18 = (bf16[144,512]{1,0:T(8,128)(2,1)S(1)}, bf16[144,512]{1,0:T(8,128)(2,1)S(1)}, u32[]{:S(2)}, u32[]{:S(2)}) collective-permute-start(bf16[144,512]{1,0:T(8,128)(2,1)S(1)} %get-tuple-element.52), channel_id=1, source_target_pairs={{0,2},{1,3},{2,4},{3,5},{4,6},{5,7},{6,8},{7,9},{8,10},{9,11},{10,... | collective-permute-start | bytes 442376 | tf_op jit(solution)/shard_map/ppermute | solution.py:37
  60.0 3.0 %collective-permute-start.17 = (f32[8,128]{1,0:T(8,128)S(1)}, f32[8,128]{1,0:T(8,128)S(1)}, u32[]{:S(2)}, u32[]{:S(2)}) collective-permute-start(f32[8,128]{1,0:T(8,128)S(1)} %bitcast.4), channel_id=1, source_target_pairs={{0,1},{1,0},{2,3},{3,2},{4,5},{5,4},{6,7},{7,6},{8,9},{9,8},{10,11... | collective-permute-start | bytes 12296 | tf_op jit(solution)/shard_map/ppermute | solution.py:45
  63.0 2.1 %collective-permute-done.17 = f32[8,128]{1,0:T(8,128)S(1)} collective-permute-done((f32[8,128]{1,0:T(8,128)S(1)}, f32[8,128]{1,0:T(8,128)S(1)}, u32[]{:S(2)}, u32[]{:S(2)}) %collective-permute-start.17) | collective-permute-done | bytes 4128 | tf_op jit(solution)/shard_map/ppermute | solution.py:45
  66.2 1.5 %collective-permute-start.22 = (bf16[144,1024]{1,0:T(8,128)(2,1)S(1)}, bf16[144,1024]{1,0:T(8,128)(2,1)S(1)}, u32[]{:S(2)}, u32[]{:S(2)}) collective-permute-start(bf16[144,1024]{1,0:T(8,128)(2,1)S(1)} %add_convert_fusion.7), channel_id=1, source_target_pairs={{0,14},{1,15},{2,0},{3,1},{4,2},{5,3},{6,4},{7,5},{8,6},{9,7},{10,... | collective-permute-start | bytes 884744 | tf_op jit(solution)/shard_map/ppermute | solution.py:37
  68.6 3.5 %shard_map.78 = (f32[144,1024]{1,0:T(8,128)S(1)}, f32[144,1024]{1,0:T(8,128)S(1)}, f32[144,1024]{1,0:T(8,128)S(1)}, f32[144,1024]{1,0:T(8,128)S(1)}, bf16[144,10...) custom-call(bf16[1152,1024]{1,0:T(8,128)(2,1)S(1)} %get-tuple-elemen, ...), custom_call_target="tpu_custom_call" | custom-call | flops 2415919104 | bytes 10362880 | tf_op jit(solution)/shard_map/pallas_call | solution.py:212
  73.4 2.6 %collective-permute-done.21 = bf16[144,1024]{1,0:T(8,128)(2,1)S(1)} collective-permute-done((bf16[144,1024]{1,0:T(8,128)(2,1)S(1)}, bf16[144,1024]{1,0:T(8,128)(2,1)S(1)}, u32[]{:S(2)}, u32[]{:S(2)}) %collective-permute-start.21) | collective-permute-done | bytes 294944 | tf_op jit(solution)/shard_map/ppermute | solution.py:37
  77.0 1.5 %collective-permute-start.24 = (bf16[144,1024]{1,0:T(8,128)(2,1)S(1)}, bf16[144,1024]{1,0:T(8,128)(2,1)S(1)}, u32[]{:S(2)}, u32[]{:S(2)}) collective-permute-start(bf16[144,1024]{1,0:T(8,128)(2,1)S(1)} %add_convert_fusion.6), channel_id=1, source_target_pairs={{0,2},{1,3},{2,4},{3,5},{4,6},{5,7},{6,8},{7,9},{8,10},{9,11},{10,... | collective-permute-start | bytes 884744 | tf_op jit(solution)/shard_map/ppermute | solution.py:37
  78.7 5.1 %collective-permute-done.23 = f32[8,128]{1,0:T(8,128)S(1)} collective-permute-done((f32[8,128]{1,0:T(8,128)S(1)}, f32[8,128]{1,0:T(8,128)S(1)}, u32[]{:S(2)}, u32[]{:S(2)}) %collective-permute-start.23) | collective-permute-done | bytes 4128 | tf_op jit(solution)/shard_map/ppermute | solution.py:57
  83.8 1.6 %collective-permute-start.33 = (bf16[144,1024]{1,0:T(8,128)(2,1)S(1)}, bf16[144,1024]{1,0:T(8,128)(2,1)S(1)}, u32[]{:S(2)}, u32[]{:S(2)}) collective-permute-start(bf16[144,1024]{1,0:T(8,128)(2,1)S(1)} %get-tuple-element.77), channel_id=1, source_target_pairs={{0,32},{16,48},{32,64},{48,80},{64,96},{80,112},{96,0},{112,16},{1... | collective-permute-start | bytes 884744 | tf_op jit(solution)/shard_map/ppermute | solution.py:41
  86.7 1.7 %collective-permute-start.28 = (bf16[144,1024]{1,0:T(8,128)(2,1)S(1)}, bf16[144,1024]{1,0:T(8,128)(2,1)S(1)}, u32[]{:S(2)}, u32[]{:S(2)}) collective-permute-start(bf16[144,1024]{1,0:T(8,128)(2,1)S(1)} %add_convert_fusion.3), channel_id=1, source_target_pairs={{0,14},{1,15},{2,0},{3,1},{4,2},{5,3},{6,4},{7,5},{8,6},{9,7},{10,... | collective-permute-start | bytes 884744 | tf_op jit(solution)/shard_map/ppermute | solution.py:37
  88.5 2.9 %collective-permute-start.26 = (f32[8,128]{1,0:T(8,128)S(1)}, f32[8,128]{1,0:T(8,128)S(1)}, u32[]{:S(2)}, u32[]{:S(2)}) collective-permute-start(f32[8,128]{1,0:T(8,128)S(1)} %add.71), channel_id=1, source_target_pairs={{0,8},{1,9},{2,10},{3,11},{4,12},{5,13},{6,14},{7,15},{8,0},{9,1},... | collective-permute-start | bytes 12296 | tf_op jit(solution)/shard_map/ppermute | solution.py:57
  91.6 2.1 %collective-permute-start.27 = (bf16[144,1024]{1,0:T(8,128)(2,1)S(1)}, bf16[144,1024]{1,0:T(8,128)(2,1)S(1)}, u32[]{:S(2)}, u32[]{:S(2)}) collective-permute-start(bf16[144,1024]{1,0:T(8,128)(2,1)S(1)} %add_convert_fusion.4), channel_id=1, source_target_pairs={{0,2},{1,3},{2,4},{3,5},{4,6},{5,7},{6,8},{7,9},{8,10},{9,11},{10,... | collective-permute-start | bytes 884744 | tf_op jit(solution)/shard_map/ppermute | solution.py:37
  93.8 2.4 %collective-permute-done.26 = f32[8,128]{1,0:T(8,128)S(1)} collective-permute-done((f32[8,128]{1,0:T(8,128)S(1)}, f32[8,128]{1,0:T(8,128)S(1)}, u32[]{:S(2)}, u32[]{:S(2)}) %collective-permute-start.26) | collective-permute-done | bytes 4128 | tf_op jit(solution)/shard_map/ppermute | solution.py:57
  96.2 1.6 %collective-permute-start.34 = (bf16[144,1024]{1,0:T(8,128)(2,1)S(1)}, bf16[144,1024]{1,0:T(8,128)(2,1)S(1)}, u32[]{:S(2)}, u32[]{:S(2)}) collective-permute-start(bf16[144,1024]{1,0:T(8,128)(2,1)S(1)} %add_convert_fusion.1), channel_id=1, source_target_pairs={{0,32},{16,48},{32,64},{48,80},{64,96},{80,112},{96,0},{112,16},{1... | collective-permute-start | bytes 884744 | tf_op jit(solution)/shard_map/ppermute | solution.py:41
  98.4 1.6 %collective-permute-done.27 = bf16[144,1024]{1,0:T(8,128)(2,1)S(1)} collective-permute-done((bf16[144,1024]{1,0:T(8,128)(2,1)S(1)}, bf16[144,1024]{1,0:T(8,128)(2,1)S(1)}, u32[]{:S(2)}, u32[]{:S(2)}) %collective-permute-start.27) | collective-permute-done | bytes 294944 | tf_op jit(solution)/shard_map/ppermute | solution.py:37
  100.1 4.2 %collective-permute-start.29 = (bf16[72,1024]{1,0:T(8,128)(2,1)S(1)}, bf16[72,1024]{1,0:T(8,128)(2,1)S(1)}, u32[]{:S(2)}, u32[]{:S(2)}) collective-permute-start(bf16[72,1024]{1,0:T(8,128)(2,1)S(1)} %slice.37), channel_id=1, source_target_pairs={{0,1},{1,0},{2,3},{3,2},{4,5},{5,4},{6,7},{7,6},{8,9},{9,8},{10,11... | collective-permute-start | bytes 442376 | tf_op jit(solution)/shard_map/ppermute | solution.py:45
  105.6 3.3 %collective-permute-done.29 = bf16[72,1024]{1,0:T(8,128)(2,1)S(1)} collective-permute-done((bf16[72,1024]{1,0:T(8,128)(2,1)S(1)}, bf16[72,1024]{1,0:T(8,128)(2,1)S(1)}, u32[]{:S(2)}, u32[]{:S(2)}) %collective-permute-start.29) | collective-permute-done | bytes 147488 | tf_op jit(solution)/shard_map/ppermute | solution.py:45
  (72 shorter events, 15.4 us)
Async XLA Ops:
  0.6 7.4 %collective-permute-start = (bf16[72,1024]{1,0:T(8,128)(2,1)}, bf16[72,1024]{1,0:T(8,128)(2,1)S(1)}, u32[]{:S(2)}, u32[]{:S(2)}) collective-permute-start(bf16[72,1024]{1,0:T(8,128)(2,1)} %param.5), channel_id=1, source_target_pairs={{0,1},{1,0},{2,3},{3,2},{4,5},{5,4},{6,7},{7,6},{8,9},{9,8},{10,11... | collective-permute-start | bytes 442376 | tf_op jit(solution)/shard_map/ppermute | solution.py:45
  8.0 12.1 %collective-permute-start.4 = (bf16[144,1024]{1,0:T(8,128)(2,1)S(1)}, bf16[144,1024]{1,0:T(8,128)(2,1)S(1)}, u32[]{:S(2)}, u32[]{:S(2)}) collective-permute-start(bf16[144,1024]{1,0:T(8,128)(2,1)S(1)} %constant_dynamic-update-slice_fusion.refs_0_), channel_id=1, source_target_pairs={{0,2},{1,3},{2,4},{3,5},{4,6},{5,7},{6,8},{7,9},{8,10},{9,11},{10,... | collective-permute-start | bytes 884744 | tf_op jit(solution)/shard_map/ppermute | solution.py:37
  11.5 9.2 %collective-permute-start.1 = (bf16[144,1024]{1,0:T(8,128)(2,1)S(1)}, bf16[144,1024]{1,0:T(8,128)(2,1)S(1)}, u32[]{:S(2)}, u32[]{:S(2)}) collective-permute-start(bf16[144,1024]{1,0:T(8,128)(2,1)S(1)} %constant_dynamic-update-slice_fusion.refs_0_), channel_id=1, source_target_pairs={{0,14},{1,15},{2,0},{3,1},{4,2},{5,3},{6,4},{7,5},{8,6},{9,7},{10,... | collective-permute-start | bytes 884744 | tf_op jit(solution)/shard_map/ppermute | solution.py:37
  16.5 8.3 %collective-permute-start.11 = (bf16[144,1024]{1,0:T(8,128)(2,1)S(1)}, bf16[144,1024]{1,0:T(8,128)(2,1)S(1)}, u32[]{:S(2)}, u32[]{:S(2)}) collective-permute-start(bf16[144,1024]{1,0:T(8,128)(2,1)S(1)} %pad_maximum_fusion.refs_0_), channel_id=1, source_target_pairs={{0,32},{16,48},{32,64},{48,80},{64,96},{80,112},{96,0},{112,16},{1... | collective-permute-start | bytes 884744 | tf_op jit(solution)/shard_map/ppermute | solution.py:41
  20.1 8.4 %collective-permute-start.5 = (bf16[144,1024]{1,0:T(8,128)(2,1)S(1)}, bf16[144,1024]{1,0:T(8,128)(2,1)S(1)}, u32[]{:S(2)}, u32[]{:S(2)}) collective-permute-start(bf16[144,1024]{1,0:T(8,128)(2,1)S(1)} %collective-permute-done.4.refs_8_), channel_id=1, source_target_pairs={{0,2},{1,3},{2,4},{3,5},{4,6},{5,7},{6,8},{7,9},{8,10},{9,11},{10,... | collective-permute-start | bytes 884744 | tf_op jit(solution)/shard_map/ppermute | solution.py:37
  20.7 7.9 %collective-permute-start.2 = (bf16[144,1024]{1,0:T(8,128)(2,1)S(1)}, bf16[144,1024]{1,0:T(8,128)(2,1)S(1)}, u32[]{:S(2)}, u32[]{:S(2)}) collective-permute-start(bf16[144,1024]{1,0:T(8,128)(2,1)S(1)} %collective-permute-done.1.refs_1_), channel_id=1, source_target_pairs={{0,14},{1,15},{2,0},{3,1},{4,2},{5,3},{6,4},{7,5},{8,6},{9,7},{10,... | collective-permute-start | bytes 884744 | tf_op jit(solution)/shard_map/ppermute | solution.py:37
  24.4 7.9 %collective-permute-start.10 = (bf16[144,1024]{1,0:T(8,128)(2,1)S(1)}, bf16[144,1024]{1,0:T(8,128)(2,1)S(1)}, u32[]{:S(2)}, u32[]{:S(2)}) collective-permute-start(bf16[144,1024]{1,0:T(8,128)(2,1)S(1)} %pad_maximum_fusion.refs_0_), channel_id=1, source_target_pairs={{0,96},{16,112},{32,0},{48,16},{64,32},{80,48},{96,64},{112,80},{1... | collective-permute-start | bytes 884744 | tf_op jit(solution)/shard_map/ppermute | solution.py:41
  24.8 8.0 %collective-permute-start.12 = (bf16[144,1024]{1,0:T(8,128)(2,1)S(1)}, bf16[144,1024]{1,0:T(8,128)(2,1)S(1)}, u32[]{:S(2)}, u32[]{:S(2)}) collective-permute-start(bf16[144,1024]{1,0:T(8,128)(2,1)S(1)} %collective-permute-done.11.refs_3_), channel_id=1, source_target_pairs={{0,32},{16,48},{32,64},{48,80},{64,96},{80,112},{96,0},{112,16},{1... | collective-permute-start | bytes 884744 | tf_op jit(solution)/shard_map/ppermute | solution.py:41
  28.6 7.9 %collective-permute-start.6 = (bf16[144,1024]{1,0:T(8,128)(2,1)S(1)}, bf16[144,1024]{1,0:T(8,128)(2,1)S(1)}, u32[]{:S(2)}, u32[]{:S(2)}) collective-permute-start(bf16[144,1024]{1,0:T(8,128)(2,1)S(1)} %collective-permute-done.5.refs_7_), channel_id=1, source_target_pairs={{0,2},{1,3},{2,4},{3,5},{4,6},{5,7},{6,8},{7,9},{8,10},{9,11},{10,... | collective-permute-start | bytes 884744 | tf_op jit(solution)/shard_map/ppermute | solution.py:37
  28.6 7.9 %collective-permute-start.3 = (bf16[144,1024]{1,0:T(8,128)(2,1)S(1)}, bf16[144,1024]{1,0:T(8,128)(2,1)S(1)}, u32[]{:S(2)}, u32[]{:S(2)}) collective-permute-start(bf16[144,1024]{1,0:T(8,128)(2,1)S(1)} %collective-permute-done.2.refs_2_), channel_id=1, source_target_pairs={{0,14},{1,15},{2,0},{3,1},{4,2},{5,3},{6,4},{7,5},{8,6},{9,7},{10,... | collective-permute-start | bytes 884744 | tf_op jit(solution)/shard_map/ppermute | solution.py:37
  32.3 9.5 %collective-permute-start.16 = (bf16[144,1024]{1,0:T(8,128)(2,1)S(1)}, bf16[144,1024]{1,0:T(8,128)(2,1)S(1)}, u32[]{:S(2)}, u32[]{:S(2)}) collective-permute-start(bf16[144,1024]{1,0:T(8,128)(2,1)S(1)} %collective-permute-done.11.refs_3_), channel_id=1, source_target_pairs={{0,16},{16,0},{32,48},{48,32},{64,80},{80,64},{96,112},{112,96},{1... | collective-permute-start | bytes 884744 | tf_op jit(solution)/shard_map/ppermute | solution.py:53
  32.8 9.0 %collective-permute-start.14 = (bf16[144,1024]{1,0:T(8,128)(2,1)S(1)}, bf16[144,1024]{1,0:T(8,128)(2,1)S(1)}, u32[]{:S(2)}, u32[]{:S(2)}) collective-permute-start(bf16[144,1024]{1,0:T(8,128)(2,1)S(1)} %collective-permute-done.10.refs_1_), channel_id=1, source_target_pairs={{0,16},{16,0},{32,48},{48,32},{64,80},{80,64},{96,112},{112,96},{1... | collective-permute-start | bytes 884744 | tf_op jit(solution)/shard_map/ppermute | solution.py:53
  36.6 7.5 %collective-permute-start.7 = (bf16[144,512]{1,0:T(8,128)(2,1)S(1)}, bf16[144,512]{1,0:T(8,128)(2,1)S(1)}, u32[]{:S(2)}, u32[]{:S(2)}) collective-permute-start(bf16[144,512]{1,0:T(8,128)(2,1)S(1)} %slice.26), channel_id=1, source_target_pairs={{0,2},{1,3},{2,4},{3,5},{4,6},{5,7},{6,8},{7,9},{8,10},{9,11},{10,... | collective-permute-start | bytes 442376 | tf_op jit(solution)/shard_map/ppermute | solution.py:37
  37.0 7.0 %collective-permute-start.8 = (bf16[144,512]{1,0:T(8,128)(2,1)S(1)}, bf16[144,512]{1,0:T(8,128)(2,1)S(1)}, u32[]{:S(2)}, u32[]{:S(2)}) collective-permute-start(bf16[144,512]{1,0:T(8,128)(2,1)S(1)} %slice.27), channel_id=1, source_target_pairs={{0,14},{1,15},{2,0},{3,1},{4,2},{5,3},{6,4},{7,5},{8,6},{9,7},{10,... | collective-permute-start | bytes 442376 | tf_op jit(solution)/shard_map/ppermute | solution.py:37
  56.6 8.5 %collective-permute-start.18 = (bf16[144,512]{1,0:T(8,128)(2,1)S(1)}, bf16[144,512]{1,0:T(8,128)(2,1)S(1)}, u32[]{:S(2)}, u32[]{:S(2)}) collective-permute-start(bf16[144,512]{1,0:T(8,128)(2,1)S(1)} %get-tuple-element.52), channel_id=1, source_target_pairs={{0,2},{1,3},{2,4},{3,5},{4,6},{5,7},{6,8},{7,9},{8,10},{9,11},{10,... | collective-permute-start | bytes 442376 | tf_op jit(solution)/shard_map/ppermute | solution.py:37
  58.9 6.2 %collective-permute-start.19 = (bf16[144,512]{1,0:T(8,128)(2,1)S(1)}, bf16[144,512]{1,0:T(8,128)(2,1)S(1)}, u32[]{:S(2)}, u32[]{:S(2)}) collective-permute-start(bf16[144,512]{1,0:T(8,128)(2,1)S(1)} %get-tuple-element.53), channel_id=1, source_target_pairs={{0,14},{1,15},{2,0},{3,1},{4,2},{5,3},{6,4},{7,5},{8,6},{9,7},{10,... | collective-permute-start | bytes 442376 | tf_op jit(solution)/shard_map/ppermute | solution.py:37
  65.1 7.6 %collective-permute-start.20 = (f32[8,128]{1,0:T(8,128)S(1)}, f32[8,128]{1,0:T(8,128)S(1)}, u32[]{:S(2)}, u32[]{:S(2)}) collective-permute-start(f32[8,128]{1,0:T(8,128)S(1)} %add.67), channel_id=1, source_target_pairs={{0,2},{1,3},{2,0},{3,1},{4,6},{5,7},{6,4},{7,5},{8,10},{9,11},{10,... | collective-permute-start | bytes 12296 | tf_op jit(solution)/shard_map/ppermute | solution.py:57
  66.2 6.8 %collective-permute-start.22 = (bf16[144,1024]{1,0:T(8,128)(2,1)S(1)}, bf16[144,1024]{1,0:T(8,128)(2,1)S(1)}, u32[]{:S(2)}, u32[]{:S(2)}) collective-permute-start(bf16[144,1024]{1,0:T(8,128)(2,1)S(1)} %add_convert_fusion.7), channel_id=1, source_target_pairs={{0,14},{1,15},{2,0},{3,1},{4,2},{5,3},{6,4},{7,5},{8,6},{9,7},{10,... | collective-permute-start | bytes 884744 | tf_op jit(solution)/shard_map/ppermute | solution.py:37
  67.7 8.2 %collective-permute-start.21 = (bf16[144,1024]{1,0:T(8,128)(2,1)S(1)}, bf16[144,1024]{1,0:T(8,128)(2,1)S(1)}, u32[]{:S(2)}, u32[]{:S(2)}) collective-permute-start(bf16[144,1024]{1,0:T(8,128)(2,1)S(1)} %add_convert_fusion.8), channel_id=1, source_target_pairs={{0,2},{1,3},{2,4},{3,5},{4,6},{5,7},{6,8},{7,9},{8,10},{9,11},{10,... | collective-permute-start | bytes 884744 | tf_op jit(solution)/shard_map/ppermute | solution.py:37
  72.8 15.7 %collective-permute-start.31 = (bf16[144,1024]{1,0:T(8,128)(2,1)S(1)}, bf16[144,1024]{1,0:T(8,128)(2,1)S(1)}, u32[]{:S(2)}, u32[]{:S(2)}) collective-permute-start(bf16[144,1024]{1,0:T(8,128)(2,1)S(1)} %get-tuple-element.73), channel_id=1, source_target_pairs={{0,16},{16,0},{32,48},{48,32},{64,80},{80,64},{96,112},{112,96},{1... | collective-permute-start | bytes 884744 | tf_op jit(solution)/shard_map/ppermute | solution.py:53
  73.0 31.3 %collective-permute-start.30 = (bf16[144,1024]{1,0:T(8,128)(2,1)S(1)}, bf16[144,1024]{1,0:T(8,128)(2,1)S(1)}, u32[]{:S(2)}, u32[]{:S(2)}) collective-permute-start(bf16[144,1024]{1,0:T(8,128)(2,1)S(1)} %get-tuple-element.70), channel_id=1, source_target_pairs={{0,16},{16,0},{32,48},{48,32},{64,80},{80,64},{96,112},{112,96},{1... | collective-permute-start | bytes 884744 | tf_op jit(solution)/shard_map/ppermute | solution.py:53
  76.0 9.5 %collective-permute-start.25 = (bf16[144,1024]{1,0:T(8,128)(2,1)S(1)}, bf16[144,1024]{1,0:T(8,128)(2,1)S(1)}, u32[]{:S(2)}, u32[]{:S(2)}) collective-permute-start(bf16[144,1024]{1,0:T(8,128)(2,1)S(1)} %add_convert_fusion.5), channel_id=1, source_target_pairs={{0,14},{1,15},{2,0},{3,1},{4,2},{5,3},{6,4},{7,5},{8,6},{9,7},{10,... | collective-permute-start | bytes 884744 | tf_op jit(solution)/shard_map/ppermute | solution.py:37
  76.5 7.4 %collective-permute-start.23 = (f32[8,128]{1,0:T(8,128)S(1)}, f32[8,128]{1,0:T(8,128)S(1)}, u32[]{:S(2)}, u32[]{:S(2)}) collective-permute-start(f32[8,128]{1,0:T(8,128)S(1)} %add.68), channel_id=1, source_target_pairs={{0,4},{1,5},{2,6},{3,7},{4,0},{5,1},{6,2},{7,3},{8,12},{9,13},{10,... | collective-permute-start | bytes 12296 | tf_op jit(solution)/shard_map/ppermute | solution.py:57
  77.0 9.7 %collective-permute-start.24 = (bf16[144,1024]{1,0:T(8,128)(2,1)S(1)}, bf16[144,1024]{1,0:T(8,128)(2,1)S(1)}, u32[]{:S(2)}, u32[]{:S(2)}) collective-permute-start(bf16[144,1024]{1,0:T(8,128)(2,1)S(1)} %add_convert_fusion.6), channel_id=1, source_target_pairs={{0,2},{1,3},{2,4},{3,5},{4,6},{5,7},{6,8},{7,9},{8,10},{9,11},{10,... | collective-permute-start | bytes 884744 | tf_op jit(solution)/shard_map/ppermute | solution.py:37
  83.8 7.8 %collective-permute-start.33 = (bf16[144,1024]{1,0:T(8,128)(2,1)S(1)}, bf16[144,1024]{1,0:T(8,128)(2,1)S(1)}, u32[]{:S(2)}, u32[]{:S(2)}) collective-permute-start(bf16[144,1024]{1,0:T(8,128)(2,1)S(1)} %get-tuple-element.77), channel_id=1, source_target_pairs={{0,32},{16,48},{32,64},{48,80},{64,96},{80,112},{96,0},{112,16},{1... | collective-permute-start | bytes 884744 | tf_op jit(solution)/shard_map/ppermute | solution.py:41
  85.4 18.9 %collective-permute-start.36 = (bf16[144,1024]{1,0:T(8,128)(2,1)S(1)}, bf16[144,1024]{1,0:T(8,128)(2,1)S(1)}, u32[]{:S(2)}, u32[]{:S(2)}) collective-permute-start(bf16[144,1024]{1,0:T(8,128)(2,1)S(1)} %get-tuple-element.82), channel_id=1, source_target_pairs={{0,96},{16,112},{32,0},{48,16},{64,32},{80,48},{96,64},{112,80},{1... | collective-permute-start | bytes 884744 | tf_op jit(solution)/shard_map/ppermute | solution.py:41
  86.7 11.7 %collective-permute-start.28 = (bf16[144,1024]{1,0:T(8,128)(2,1)S(1)}, bf16[144,1024]{1,0:T(8,128)(2,1)S(1)}, u32[]{:S(2)}, u32[]{:S(2)}) collective-permute-start(bf16[144,1024]{1,0:T(8,128)(2,1)S(1)} %add_convert_fusion.3), channel_id=1, source_target_pairs={{0,14},{1,15},{2,0},{3,1},{4,2},{5,3},{6,4},{7,5},{8,6},{9,7},{10,... | collective-permute-start | bytes 884744 | tf_op jit(solution)/shard_map/ppermute | solution.py:37
  88.5 7.7 %collective-permute-start.26 = (f32[8,128]{1,0:T(8,128)S(1)}, f32[8,128]{1,0:T(8,128)S(1)}, u32[]{:S(2)}, u32[]{:S(2)}) collective-permute-start(f32[8,128]{1,0:T(8,128)S(1)} %add.71), channel_id=1, source_target_pairs={{0,8},{1,9},{2,10},{3,11},{4,12},{5,13},{6,14},{7,15},{8,0},{9,1},... | collective-permute-start | bytes 12296 | tf_op jit(solution)/shard_map/ppermute | solution.py:57
  91.6 8.4 %collective-permute-start.27 = (bf16[144,1024]{1,0:T(8,128)(2,1)S(1)}, bf16[144,1024]{1,0:T(8,128)(2,1)S(1)}, u32[]{:S(2)}, u32[]{:S(2)}) collective-permute-start(bf16[144,1024]{1,0:T(8,128)(2,1)S(1)} %add_convert_fusion.4), channel_id=1, source_target_pairs={{0,2},{1,3},{2,4},{3,5},{4,6},{5,7},{6,8},{7,9},{8,10},{9,11},{10,... | collective-permute-start | bytes 884744 | tf_op jit(solution)/shard_map/ppermute | solution.py:37
  96.2 8.1 %collective-permute-start.34 = (bf16[144,1024]{1,0:T(8,128)(2,1)S(1)}, bf16[144,1024]{1,0:T(8,128)(2,1)S(1)}, u32[]{:S(2)}, u32[]{:S(2)}) collective-permute-start(bf16[144,1024]{1,0:T(8,128)(2,1)S(1)} %add_convert_fusion.1), channel_id=1, source_target_pairs={{0,32},{16,48},{32,64},{48,80},{64,96},{80,112},{96,0},{112,16},{1... | collective-permute-start | bytes 884744 | tf_op jit(solution)/shard_map/ppermute | solution.py:41
  100.1 8.7 %collective-permute-start.29 = (bf16[72,1024]{1,0:T(8,128)(2,1)S(1)}, bf16[72,1024]{1,0:T(8,128)(2,1)S(1)}, u32[]{:S(2)}, u32[]{:S(2)}) collective-permute-start(bf16[72,1024]{1,0:T(8,128)(2,1)S(1)} %slice.37), channel_id=1, source_target_pairs={{0,1},{1,0},{2,3},{3,2},{4,5},{5,4},{6,7},{7,6},{8,9},{9,8},{10,11... | collective-permute-start | bytes 442376 | tf_op jit(solution)/shard_map/ppermute | solution.py:45
  104.5 5.6 %collective-permute-start.37 = (bf16[72,1024]{1,0:T(8,128)(2,1)S(1)}, bf16[72,1024]{1,0:T(8,128)(2,1)S(1)}, u32[]{:S(2)}, u32[]{:S(2)}) collective-permute-start(bf16[72,1024]{1,0:T(8,128)(2,1)S(1)} %slice.36), channel_id=1, source_target_pairs={{0,128},{16,144},{32,160},{48,176},{64,192},{80,208},{96,224},{112... | collective-permute-start | bytes 442376 | tf_op jit(solution)/shard_map/ppermute | solution.py:49
  (7 other events, 73.2 us)

commit v4 on v3

v4 whole, which is shorter than its diff:
```python
import jax
import jax.numpy as jnp
from jax import lax
from jax.experimental import pallas as pl
from jax.experimental.pallas import tpu as pltpu
from jax.sharding import PartitionSpec as P

EPS = 1e-06
F32 = jnp.float32
BF16 = jnp.bfloat16
NZ, NY = 8, 4
SH = 72
BL = 2 * SH
N = 1024
HALF = N // 2
ROWS = 16 * SH
MIB = 1024 * 1024


def row_pairs(f):
    out = []
    for r in range(16):
        a, b, c = f(r // 8, (r // 2) % 4, r % 2)
        out.append((r, (a * 4 + b) * 2 + c))
    return out


def col_pairs(f):
    out = []
    for r in range(16):
        a, b = f(r // 2, r % 2)
        out.append((r, a * 2 + b))
    return out


def shift_z(v, d):
    return lax.ppermute(v, "col", col_pairs(lambda z, h: ((z + d) % NZ, h)))


def shift_y(v, d):
    return lax.ppermute(v, "row", row_pairs(lambda x, y, c: (x, (y + d) % NY, c)))


def swap_xhi(v):
    return lax.ppermute(v, "col", col_pairs(lambda z, h: (z, 1 - h)))


def swap_xlo(v):
    return lax.ppermute(v, "row", row_pairs(lambda x, y, c: (1 - x, y, c)))


def swap_core(v):
    return lax.ppermute(v, "row", row_pairs(lambda x, y, c: (x, y, 1 - c)))


def xor_z(v, b):
    return lax.ppermute(v, "col", col_pairs(lambda z, h: (z ^ b, h)))


def coords():
    row, col = lax.axis_index("row"), lax.axis_index("col")
    return row // 8, (row // 2) % 4, row % 2, col // 2, col % 2


def halves(v):
    return v[:SH], v[SH:]


def position(k):
    return jnp.where(k < 4, k, jnp.where(k == 4, 7, k - 1))


ORDER = (0, 1, 2, 3, 5, 6, 7, 4)
EARLY = 7 * BL
WIDE = 1024
TAIL = 896


def text_kernel(*refs):
    mine, others = refs[:4], refs[4:8]
    yp, ypt, brow, bcol = refs[8:]
    xlo, y, core, z, xhi = coords()
    same = core == xhi
    total = jnp.zeros((1, N), F32)
    for k in range(NY):
        here = halves(mine[k][...].astype(F32))
        away = halves(others[k][...].astype(F32))
        for other in range(2):
            a, b = here[other], away[other]
            block = jnp.concatenate([jnp.where(same, a, b), jnp.where(same, b, a)], axis=0)
            g = (xlo + other) % 2 * 4 + (y + k) % 4
            at = position((g - z + NZ) % NZ) * BL
            yp[pl.ds(pl.multiple_of(at, BL), BL), :] = block.astype(BF16)
            total += jnp.sum(block * block, axis=0, keepdims=True)
    brow[...] = lax.rsqrt(total + EPS)
    for c in range(N // 128):
        v = yp[:, c * 128 : (c + 1) * 128].T
        ypt[c * 128 : (c + 1) * 128, :] = v
        w = v.astype(F32)
        s = jnp.sum(w * w, axis=1, keepdims=True)
        bcol[c * 128 : (c + 1) * 128, :] = jnp.broadcast_to(lax.rsqrt(s + EPS), (128, 128))


W = 256


def early_kernel(*refs):
    blocks, ypt = refs[:7], refs[7]
    xa, part, square = refs[8:]
    total = jnp.zeros((1, N), F32)
    for i, block in enumerate(blocks):
        v = block[...]
        xa[i * BL : (i + 1) * BL, :] = v
        v = v.astype(F32)
        total += jnp.sum(v * v, axis=0, keepdims=True)
    xa[EARLY:, :] = jnp.zeros((WIDE - EARLY, N), BF16)
    square[...] = total
    for n in range(N // W):
        cols = slice(n * W, (n + 1) * W)
        part[:, cols] = jnp.dot(ypt[:, :WIDE], xa[:, cols], preferred_element_type=F32)


LANES = 512
TILE = 64


def middle_kernel(
    left, right, part, square, pairs, logscale, bias, yp, ypt, bcol,
    x4, cy, cx, sj, si, arow, loss, out_left, out_right, xb, t_ref, acc_sj,
):
    x4[:, :HALF] = left[...]
    x4[:, HALF:] = right[...]
    xb[: EARLY - TAIL, :] = jnp.zeros((EARLY - TAIL, N), BF16)
    xb[EARLY - TAIL :, :] = x4[...]
    v = x4[...].astype(F32)
    a = lax.rsqrt(square[...] + jnp.sum(v * v, axis=0, keepdims=True) + EPS)
    arow[...] = a
    scale = jnp.exp(jnp.full((1, N), logscale[0], F32))
    ascale = a * scale
    shift = bias[0]
    acc_sj[...] = jnp.zeros_like(acc_sj)
    first = lax.axis_index("col") * N
    sub = TILE // 8
    strips = LANES // 128
    for n in range(N // LANES):
        cols = slice(n * LANES, (n + 1) * LANES)
        t_ref[...] = jnp.dot(ypt[:, TAIL:], xb[:, cols], preferred_element_type=F32)
        ai, asc, sc, pair = a[:, cols], ascale[:, cols], scale[:, cols], pairs[:, cols] - first

        def body(j, carry, cols=cols, ai=ai, asc=asc, sc=sc, pair=pair):
            al, asi = carry
            rows = pl.ds(pl.multiple_of(j * TILE, TILE), TILE)
            b = jnp.concatenate([bcol[rows, :]] * strips, axis=1)
            cos = ((t_ref[rows, :] + part[rows, cols]) * b) * ai
            logit = cos * sc + shift
            hit = lax.broadcasted_iota(jnp.int32, (TILE, LANES), 0) == pair - j * TILE
            e = jnp.exp(logit)
            sig = e * pltpu.reciprocal(1.0 + e)
            d = jnp.where(hit, sig - 1.0, sig)
            dc = d * cos
            cy[rows, cols] = ((d * b) * sc).astype(BF16)
            cx[rows, cols] = (d * asc).astype(BF16)
            strip = dc[:, :128]
            for m in range(1, strips):
                strip = strip + dc[:, m * 128 : (m + 1) * 128]
            acc_sj[rows, :] += strip
            e8 = e.reshape(sub, 8, LANES)
            q = e8[0]
            for m in range(1, sub):
                q = q + (e8[m] + q * e8[m])
            soft = jnp.where(q < 1e-4, (1.0 - 0.5 * q) * q, jnp.log(1.0 + q))
            al = al + soft - jnp.sum(jnp.where(hit, logit, 0.0).reshape(sub, 8, LANES), axis=0)
            asi = asi + jnp.sum(dc.reshape(sub, 8, LANES), axis=0)
            return al, asi

        zero = jnp.zeros((8, LANES), F32)
        al, asi = lax.fori_loop(0, N // TILE, body, (zero, zero))
        loss[:, cols] = jnp.sum(al, axis=0, keepdims=True)
        inner = jnp.sum(asi, axis=0, keepdims=True) * sc
        si[:, cols] = inner
        pull = jnp.dot(yp[EARLY:, :], cy[:, cols], preferred_element_type=F32)
        term = ai * (pull - (x4[:, cols].astype(F32) * ai) * inner)
        out = out_left if n * LANES < HALF else out_right
        at = n * LANES % HALF
        out[:, at : at + LANES] = term.astype(BF16)
    sj[...] = jnp.sum(acc_sj[...].T, axis=0, keepdims=True) * scale


def image_kernel(xa, yp, cy, arow, si, *outs):
    for n in range(N // W):
        cols = slice(n * W, (n + 1) * W)
        pull = jnp.dot(yp[:EARLY, :], cy[:, cols], preferred_element_type=F32)
        a, s = arow[:, cols], si[:, cols]
        for i in range(7):
            rows = slice(i * BL, (i + 1) * BL)
            outs[i][:, cols] = a * (pull[rows] - (xa[rows, cols].astype(F32) * a) * s)


def caption_kernel(xa, x4, cx, yp, brow, sj, loss, _up, _down, *refs):
    own, away = refs[:4], refs[4:8]
    t_ref = refs[9]
    refs[8][...] = loss[...]
    xlo, y, core, z, xhi = coords()
    same = core == xhi
    dims = (((1,), (1,)), ((), ()))
    for n in range(N // W):
        cols = slice(n * W, (n + 1) * W)
        b, s = brow[:, cols], sj[:, cols]
        coeff = cx[cols, :]
        for src, at in ((xa, 0), (x4, EARLY)):
            rows = slice(at, at + (EARLY if at == 0 else BL))
            pull = lax.dot_general(src[: rows.stop - at, :], coeff, dims, preferred_element_type=F32)
            t_ref[rows, cols] = b * (pull - (yp[rows, cols].astype(F32) * b) * s)
    for k in range(NY):
        here, there = [], []
        for other in range(2):
            g = (xlo + other) % 2 * 4 + (y + k) % 4
            at = position((g - z + NZ) % NZ) * BL
            p, q = halves(t_ref[pl.ds(pl.multiple_of(at, BL), BL), :])
            here.append(jnp.where(same, p, q))
            there.append(jnp.where(same, q, p))
        own[k][...] = jnp.concatenate(here, axis=0)
        away[k][...] = jnp.concatenate(there, axis=0).astype(BF16)


def call(kernel, out_shape, flops, args, scratch=(), smem=(), unread=(), limit=32 * MIB):
    vm = pl.BlockSpec(memory_space=pltpu.VMEM)
    specs = [vm] * len(args)
    for i in smem:
        specs[i] = pl.BlockSpec(memory_space=pltpu.SMEM)
    for i in unread:
        specs[i] = pl.BlockSpec(memory_space=pl.ANY)
    moved = sum(x.size * x.dtype.itemsize for x in list(args) + list(out_shape))
    return pl.pallas_call(
        kernel,
        out_shape=out_shape,
        in_specs=specs,
        out_specs=[vm] * len(out_shape),
        scratch_shapes=list(scratch),
        compiler_params=pltpu.CompilerParams(vmem_limit_bytes=limit),
        cost_estimate=pl.CostEstimate(flops=flops, bytes_accessed=moved, transcendentals=0),
    )(*args)


def sds(shape, dtype):
    return jax.ShapeDtypeStruct(shape, dtype)


def wide(v):
    return v.astype(F32)


def run_text(mine, others):
    return call(
        text_kernel,
        [sds((ROWS, N), BF16), sds((N, ROWS), BF16), sds((1, N), F32), sds((N, 128), F32)],
        N * N * 64,
        list(mine) + list(others),
    )


def run_early(blocks, ypt):
    return call(
        early_kernel,
        [sds((WIDE, N), BF16), sds((N, N), F32), sds((1, N), F32)],
        2 * N * N * WIDE,
        list(blocks) + [ypt],
    )


def run_middle(left, right, part, square, pairs, log_scale, bias, yp, ypt, bcol):
    row = sds((1, N), F32)
    return call(
        middle_kernel,
        [sds((BL, N), BF16), sds((N, N), BF16), sds((N, N), BF16), row, row, row, row]
        + [sds((BL, HALF), BF16)] * 2,
        2 * N * N * ROWS,
        [left, right, part, square, pairs.reshape(1, N), log_scale, bias, yp, ypt, bcol],
        [
            pltpu.VMEM((ROWS - TAIL, N), BF16),
            pltpu.VMEM((N, LANES), F32),
            pltpu.VMEM((N, 128), F32),
        ],
        smem=(5, 6),
    )


def run_images(xa, yp, cy, arow, si):
    return call(
        image_kernel, [sds((BL, N), F32)] * 7, 2 * N * N * EARLY, [xa, yp, cy, arow, si]
    )


def run_captions(xa, x4, cx, yp, brow, sj, loss, up, down):
    return call(
        caption_kernel,
        [sds((BL, N), F32)] * NY + [sds((BL, N), BF16)] * NY + [sds((1, N), F32)],
        2 * N * N * ROWS,
        [xa, x4, cx, yp, brow, sj, loss, up, down],
        [pltpu.VMEM((ROWS, N), F32)],
        unread=(7, 8),
    )


def split(v):
    high = lax.reduce_precision(v, 8, 7)
    return high, lax.reduce_precision(v - high, 8, 7)


def shards(images, texts, pairs, log_scale, bias):
    other_img, other_txt = swap_xhi(images), swap_xlo(texts)
    up = down = jnp.concatenate([images, other_img], axis=0)
    block = jnp.concatenate([texts, other_txt], axis=0)
    ring = [[] for _ in range(NZ)]
    ring[0] = [up]
    behind, ahead = shift_y(block, 1), shift_y(block, -1)
    others = [swap_core(block)]
    up, down = shift_z(up, 1), shift_z(down, -1)
    ring[NZ - 1], ring[1] = [up], [down]
    across = shift_y(behind, 1)
    others += [swap_core(ahead)]
    last = swap_core(behind)
    up, down = shift_z(up, 1), shift_z(down, -1)
    ring[NZ - 2], ring[2] = [up], [down]
    others += [swap_core(across), last]
    mine = [block, ahead, across, behind]
    up, down = shift_z(up, 1), shift_z(down, -1)
    ring[NZ - 3], ring[3] = [up], [down]
    left, right = shift_z(up[:, :HALF], 1), shift_z(down[:, HALF:], -1)
    yp, ypt, brow, bcol = run_text(mine, others)
    xa, products, square = run_early([ring[k][0] for k in ORDER[:7]], ypt)

    x4, cy, cx, sj, si, arow, loss, up, down = run_middle(
        left, right, products, square, pairs, log_scale, bias, yp, ypt, bcol
    )
    up, down = shift_z(up, 1), shift_z(down, -1)
    found = run_images(xa, yp, cy, arow, si)
    terms = {k: found[i] for i, k in enumerate(ORDER[:7])}
    up = (terms[3] + jnp.pad(wide(up), ((0, 0), (0, HALF)))).astype(BF16)
    down = (terms[5] + jnp.pad(wide(down), ((0, 0), (HALF, 0)))).astype(BF16)
    cap = run_captions(xa, x4, cx, yp, brow, sj, loss, up, down)
    up, down = shift_z(up, 1), shift_z(down, -1)
    part = [cap[k] + wide(swap_core(cap[NY + k])) for k in range(NY)]
    tup = shift_y(part[2].astype(BF16), 1)
    tdown = shift_y(part[3].astype(BF16), -1)
    up = shift_z((terms[2] + wide(up)).astype(BF16), 1)
    down = shift_z((terms[6] + wide(down)).astype(BF16), -1)
    tup = shift_y((part[1] + wide(tup)).astype(BF16), 1)
    up = shift_z((terms[1] + wide(up)).astype(BF16), 1)
    down = shift_z((terms[7] + wide(down)).astype(BF16), -1)
    total = terms[0] + wide(up) + wide(down)

    loss = cap[2 * NY]
    for b in (1, 2, 4):
        loss = loss + xor_z(loss, b)
    high, low = split(loss)
    rows = jnp.concatenate([high, low, jnp.zeros((6, N), F32)], axis=0)
    got = wide(swap_xhi(jnp.concatenate([total[SH:], rows], axis=0).astype(BF16)))
    image_grad = total[:SH] + got[:SH]
    loss = (high + low) + (got[SH : SH + 1] + got[SH + 1 : SH + 2])
    total = part[0] + wide(tup) + wide(tdown)
    text_grad = total[:SH] + wide(swap_xlo(total[SH:].astype(BF16)))
    return (loss.reshape(N), image_grad, text_grad)


def solution(mesh):
    return jax.shard_map(
        shards,
        mesh=mesh,
        in_specs=(P("col", "row"), P("row", "col"), P("row"), P(), P()),
        out_specs=(P("row"), P("col", "row"), P("row", "col")),
        check_vma=False,
    )
```

time: 112 us -> 116 us (1.036)
  waiting for transfers between devices: 30.4 us -> 36.7 us
  Pallas kernels: 18.2 us -> 15.8 us
    ppermute x16, waiting for transfers between devices: 13.5 us -> 23.7 us  [shift_z(): return lax.ppermute(v, 'col', col_pairs(lambda z, h: ((z + d) % NZ, h)))]
    ppermute x3 -> x2, starting transfers between devices: 10.3 us -> 5.92 us  [swap_xhi(): return lax.ppermute(v, 'col', col_pairs(lambda z, h: (z, 1 - h)))]
    ppermute x3, waiting for transfers between devices: 7.48 us -> 3.93 us  [xor_z(): return lax.ppermute(v, 'col', col_pairs(lambda z, h: (z ^ b, h)))]
    ppermute x3, starting transfers between devices: 4.4 us -> 7.81 us  [xor_z(): return lax.ppermute(v, 'col', col_pairs(lambda z, h: (z ^ b, h)))]
    ppermute x3 -> x2, waiting for transfers between devices: 8.7 us -> 6.15 us  [swap_xhi(): return lax.ppermute(v, 'col', col_pairs(lambda z, h: (z, 1 - h)))]
    pallas_call x3 -> x5, Pallas kernels: 18.2 us -> 15.8 us  [call(): pl.pallas_call(kernel, out_shape=out_shape, in_specs=specs, out_specs=[vm...]
    ppermute x6, waiting for transfers between devices: 0.27 us -> 1.74 us  [shift_y(): lax.ppermute(v, 'row', row_pairs(lambda x, y, c: (x, (y + d) % NY, c)))]
  transfers between devices with their start and end apart: 38 -> 37, of which waited for: 17 -> 16; matrix products, arithmetic and copies ran while one was open for 4% -> 3% of each run, Pallas kernels for 5% -> 9%
where the time goes in v4:
time: 116 us; the launch traced here: 115 us
  starting transfers between devices  55.3 us (48%)
  waiting for transfers between devices  36.7 us (32%)
  Pallas kernels  15.8 us (14%)
  other arithmetic  3.16 us (3%)
  between operations  2.29 us (2%)
  local copies, waits for them, and re-layouts  2.07 us (2%)
    ppermute x16, starting transfers between devices, shift_z(): return lax.ppermute(v, 'col', col_pairs(lambda z, h: ((z + d) % NZ, h)))  29.3 us
    ppermute x16, waiting for transfers between devices, shift_z(): return lax.ppermute(v, 'col', col_pairs(lambda z, h: ((z + d) % NZ, h)))  23.7 us
    pallas_call x5, Pallas kernels, call(): pl.pallas_call(kernel, out_shape=out_shape, in_specs=specs, out_specs=[vm...  15.8 us
    ppermute x3, starting transfers between devices, xor_z(): return lax.ppermute(v, 'col', col_pairs(lambda z, h: (z ^ b, h)))  7.81 us
    ppermute x6, starting transfers between devices, shift_y(): lax.ppermute(v, 'row', row_pairs(lambda x, y, c: (x, (y + d) % NY, c)))  7.57 us
    ppermute x2, waiting for transfers between devices, swap_xhi(): return lax.ppermute(v, 'col', col_pairs(lambda z, h: (z, 1 - h)))  6.15 us
    ppermute x2, starting transfers between devices, swap_xhi(): return lax.ppermute(v, 'col', col_pairs(lambda z, h: (z, 1 - h)))  5.92 us
    ppermute x3, waiting for transfers between devices, xor_z(): return lax.ppermute(v, 'col', col_pairs(lambda z, h: (z ^ b, h)))  3.93 us
  transfers between devices with their start and end apart: 37, of which 16 were waited for; matrix products, arithmetic and copies ran while one was open for 3% of the time, Pallas kernels for 9%

profile of v4, /device:TPU:8, one launch (start us, length us, event | category | flops | bytes accessed | tf_op | source)
XLA Modules:
  0.0 115.4 jit_solution(6009580395551411809)
XLA Ops:
  0.6 3.1 %collective-permute-start = (bf16[72,1024]{1,0:T(8,128)(2,1)}, bf16[72,1024]{1,0:T(8,128)(2,1)S(1)}, u32[]{:S(2)}, u32[]{:S(2)}) collective-permute-start(bf16[72,1024]{1,0:T(8,128)(2,1)} %param.5), channel_id=1, source_target_pairs={{0,1},{1,0},{2,3},{3,2},{4,5},{5,4},{6,7},{7,6},{8,9},{9,8},{10,11... | collective-permute-start | bytes 442376 | tf_op jit(solution)/shard_map/ppermute | solution.py:45
  4.7 3.3 %collective-permute-done = bf16[72,1024]{1,0:T(8,128)(2,1)S(1)} collective-permute-done((bf16[72,1024]{1,0:T(8,128)(2,1)}, bf16[72,1024]{1,0:T(8,128)(2,1)S(1)}, u32[]{:S(2)}, u32[]{:S(2)}) %collective-permute-start) | collective-permute-done | bytes 147488 | tf_op jit(solution)/shard_map/ppermute | solution.py:45
  8.0 2.0 %collective-permute-start.4 = (bf16[144,1024]{1,0:T(8,128)(2,1)S(1)}, bf16[144,1024]{1,0:T(8,128)(2,1)S(1)}, u32[]{:S(2)}, u32[]{:S(2)}) collective-permute-start(bf16[144,1024]{1,0:T(8,128)(2,1)S(1)} %constant_dynamic-update-slice_fusion.refs_0_), channel_id=1, source_target_pairs={{0,2},{1,3},{2,4},{3,5},{4,6},{5,7},{6,8},{7,9},{8,10},{9,11},{10,... | collective-permute-start | bytes 884744 | tf_op jit(solution)/shard_map/ppermute | solution.py:37
  12.5 4.1 %collective-permute-start.1 = (bf16[144,1024]{1,0:T(8,128)(2,1)S(1)}, bf16[144,1024]{1,0:T(8,128)(2,1)S(1)}, u32[]{:S(2)}, u32[]{:S(2)}) collective-permute-start(bf16[144,1024]{1,0:T(8,128)(2,1)S(1)} %constant_dynamic-update-slice_fusion.refs_0_), channel_id=1, source_target_pairs={{0,14},{1,15},{2,0},{3,1},{4,2},{5,3},{6,4},{7,5},{8,6},{9,7},{10,... | collective-permute-start | bytes 884744 | tf_op jit(solution)/shard_map/ppermute | solution.py:37
  16.6 1.7 %collective-permute-start.9 = (bf16[144,1024]{1,0:T(8,128)(2,1)S(1)}, bf16[144,1024]{1,0:T(8,128)(2,1)S(1)}, u32[]{:S(2)}, u32[]{:S(2)}) collective-permute-start(bf16[144,1024]{1,0:T(8,128)(2,1)S(1)} %constant_dynamic-update-slice_fusion.2.refs_0_), channel_id=1, source_target_pairs={{0,32},{16,48},{32,64},{48,80},{64,96},{80,112},{96,0},{112,16},{1... | collective-permute-start | bytes 884744 | tf_op jit(solution)/shard_map/ppermute | solution.py:41
  18.3 1.8 %collective-permute-done.4.refs_6_ = bf16[144,1024]{1,0:T(8,128)(2,1)S(1)} collective-permute-done((bf16[144,1024]{1,0:T(8,128)(2,1)S(1)}, bf16[144,1024]{1,0:T(8,128)(2,1)S(1)}, u32[]{:S(2)}, u32[]{:S(2)}) %collective-permute-start.4) | collective-permute-done | bytes 294944 | tf_op jit(solution)/shard_map/ppermute | solution.py:37
  20.1 1.6 %collective-permute-done.1.refs_1_ = bf16[144,1024]{1,0:T(8,128)(2,1)S(1)} collective-permute-done((bf16[144,1024]{1,0:T(8,128)(2,1)S(1)}, bf16[144,1024]{1,0:T(8,128)(2,1)S(1)}, u32[]{:S(2)}, u32[]{:S(2)}) %collective-permute-start.1) | collective-permute-done | bytes 294944 | tf_op jit(solution)/shard_map/ppermute | solution.py:37
  21.7 3.7 %collective-permute-start.2 = (bf16[144,1024]{1,0:T(8,128)(2,1)S(1)}, bf16[144,1024]{1,0:T(8,128)(2,1)S(1)}, u32[]{:S(2)}, u32[]{:S(2)}) collective-permute-start(bf16[144,1024]{1,0:T(8,128)(2,1)S(1)} %collective-permute-done.1.refs_1_), channel_id=1, source_target_pairs={{0,14},{1,15},{2,0},{3,1},{4,2},{5,3},{6,4},{7,5},{8,6},{9,7},{10,... | collective-permute-start | bytes 884744 | tf_op jit(solution)/shard_map/ppermute | solution.py:37
  25.9 1.6 %collective-permute-start.10 = (bf16[144,1024]{1,0:T(8,128)(2,1)S(1)}, bf16[144,1024]{1,0:T(8,128)(2,1)S(1)}, u32[]{:S(2)}, u32[]{:S(2)}) collective-permute-start(bf16[144,1024]{1,0:T(8,128)(2,1)S(1)} %collective-permute-done.9.refs_3_), channel_id=1, source_target_pairs={{0,32},{16,48},{32,64},{48,80},{64,96},{80,112},{96,0},{112,16},{1... | collective-permute-start | bytes 884744 | tf_op jit(solution)/shard_map/ppermute | solution.py:41
  29.6 3.7 %collective-permute-start.3 = (bf16[144,1024]{1,0:T(8,128)(2,1)S(1)}, bf16[144,1024]{1,0:T(8,128)(2,1)S(1)}, u32[]{:S(2)}, u32[]{:S(2)}) collective-permute-start(bf16[144,1024]{1,0:T(8,128)(2,1)S(1)} %collective-permute-done.2.refs_2_), channel_id=1, source_target_pairs={{0,14},{1,15},{2,0},{3,1},{4,2},{5,3},{6,4},{7,5},{8,6},{9,7},{10,... | collective-permute-start | bytes 884744 | tf_op jit(solution)/shard_map/ppermute | solution.py:37
  33.9 2.5 %collective-permute-done.6.refs_4_ = bf16[144,1024]{1,0:T(8,128)(2,1)S(1)} collective-permute-done((bf16[144,1024]{1,0:T(8,128)(2,1)S(1)}, bf16[144,1024]{1,0:T(8,128)(2,1)S(1)}, u32[]{:S(2)}, u32[]{:S(2)}) %collective-permute-start.6) | collective-permute-done | bytes 294944 | tf_op jit(solution)/shard_map/ppermute | solution.py:37
  37.9 3.6 %collective-permute-start.16 = (bf16[144,512]{1,0:T(8,128)(2,1)S(1)}, bf16[144,512]{1,0:T(8,128)(2,1)S(1)}, u32[]{:S(2)}, u32[]{:S(2)}) collective-permute-start(bf16[144,512]{1,0:T(8,128)(2,1)S(1)} %slice.39), channel_id=1, source_target_pairs={{0,14},{1,15},{2,0},{3,1},{4,2},{5,3},{6,4},{7,5},{8,6},{9,7},{10,... | collective-permute-start | bytes 442376 | tf_op jit(solution)/shard_map/ppermute | solution.py:37
  41.6 2.1 %shard_map.76 = (bf16[1152,1024]{1,0:T(8,128)(2,1)S(1)}, bf16[1024,1152]{1,0:T(8,128)(2,1)S(1)}, f32[1,1024]{1,0:T(1,128)S(1)}, f32[1024,128]{1,0:T(8,128)S(1)}) custom-call(bf16[144,1024]{1,0:T(8,128)(2,1)S(1)} %constant_dynamic-update-slice_fusion.2.refs_0_, bf16[144,1024]{1,0:T(8,128)(2,1)S(1)} %collective-permute-done.8.refs_1_, ...), custom_call_target="tpu_custom_call" | custom-call | flops 67108864 | bytes 7606272 | tf_op jit(solution)/shard_map/pallas_call | solution.py:234
  43.7 2.3 %shard_map.77 = (bf16[1024,1024]{1,0:T(8,128)(2,1)S(1)}, f32[1024,1024]{1,0:T(8,128)S(1)}, f32[1,1024]{1,0:T(1,128)S(1)}) custom-call(bf16[144,1024]{1,0:T(8,128)(2,1)S(1)} %constant_dynamic-update-slice_fusion.refs_0_, bf16[144,1024]{1,0:T(8,128)(2,1)S(1)} %collective-permute-done.1.refs_1_, bf16[144,1024]{1,0:T(8,128)(2,1)S(1)} %collective-permute-done.2.refs_2_, ...), custom_call_target="tpu_custom_call" | custom-call | flops 2147483648 | bytes 10719232 | tf_op jit(solution)/shard_map/pallas_call | solution.py:234
  46.1 5.3 %shard_map.78 = (bf16[144,1024]{1,0:T(8,128)(2,1)S(1)}, bf16[1024,1024]{1,0:T(8,128)(2,1)S(1)}, bf16[1024,1024]{1,0:T(8,128)(2,1)S(1)}, f32[1,1024]{1,0:T(1,128)...) custom-call(bf16[144,512]{1,0:T(8,128)(2,1)S(1)} %collective-permute, ...), custom_call_target="tpu_custom_call" | custom-call | flops 2415919104 | bytes 14540808 | tf_op jit(solution)/shard_map/pallas_call | solution.py:234
  52.7 2.0 %collective-permute-start.18 = (bf16[144,512]{1,0:T(8,128)(2,1)S(1)}, bf16[144,512]{1,0:T(8,128)(2,1)S(1)}, u32[]{:S(2)}, u32[]{:S(2)}) collective-permute-start(bf16[144,512]{1,0:T(8,128)(2,1)S(1)} %get-tuple-element.52), channel_id=1, source_target_pairs={{0,14},{1,15},{2,0},{3,1},{4,2},{5,3},{6,4},{7,5},{8,6},{9,7},{10,... | collective-permute-start | bytes 442376 | tf_op jit(solution)/shard_map/ppermute | solution.py:37
  54.8 2.4 %shard_map.79 = (f32[144,1024]{1,0:T(8,128)S(1)}, f32[144,1024]{1,0:T(8,128)S(1)}, f32[144,1024]{1,0:T(8,128)S(1)}, f32[144,1024]{1,0:T(8,128)S(1)}, f32[144,102...) custom-call(bf16[1024,1024]{1,0:T(8,128)(2,1)S(1)} %get-tuple-element.36.xa, ...), custom_call_target="tpu_custom_call" | custom-call | flops 2113929216 | bytes 10690560 | tf_op jit(solution)/shard_map/pallas_call | solution.py:234
  57.9 3.4 %collective-permute-start.25 = (bf16[144,1024]{1,0:T(8,128)(2,1)S(1)}, bf16[144,1024]{1,0:T(8,128)(2,1)S(1)}, u32[]{:S(2)}, u32[]{:S(2)}) collective-permute-start(bf16[144,1024]{1,0:T(8,128)(2,1)S(1)} %add_convert_fusion.7._down), channel_id=1, source_target_pairs={{0,14},{1,15},{2,0},{3,1},{4,2},{5,3},{6,4},{7,5},{8,6},{9,7},{10,... | collective-permute-start | bytes 884744 | tf_op jit(solution)/shard_map/ppermute | solution.py:37
  61.7 3.6 %shard_map.80 = (f32[144,1024]{1,0:T(8,128)S(1)}, f32[144,1024]{1,0:T(8,128)S(1)}, f32[144,1024]{1,0:T(8,128)S(1)}, f32[144,1024]{1,0:T(8,128)S(1)}, bf16[144,10...) custom-call(bf16[1024,1024]{1,0:T(8,128)(2,1)S(1)} %get-tuple-elemen, ...), custom_call_target="tpu_custom_call" | custom-call | flops 2415919104 | bytes 10993664 | tf_op jit(solution)/shard_map/pallas_call | solution.py:234
  66.1 3.0 %collective-permute-done.19 = f32[1,1024]{1,0:T(1,128)S(1)} collective-permute-done((f32[1,1024]{1,0:T(1,128)S(1)}, f32[1,1024]{1,0:T(1,128)S(1)}, u32[]{:S(2)}, u32[]{:S(2)}) %collective-permute-start.19) | collective-permute-done | bytes 4128 | tf_op jit(solution)/shard_map/ppermute | solution.py:57
  69.1 3.1 %collective-permute-start.20 = (f32[1,1024]{1,0:T(1,128)S(1)}, f32[1,1024]{1,0:T(1,128)S(1)}, u32[]{:S(2)}, u32[]{:S(2)}) collective-permute-start(f32[1,1024]{1,0:T(1,128)S(1)} %add.75), channel_id=1, source_target_pairs={{0,4},{1,5},{2,6},{3,7},{4,0},{5,1},{6,2},{7,3},{8,12},{9,13},{10,... | collective-permute-start | bytes 12296 | tf_op jit(solution)/shard_map/ppermute | solution.py:57
  74.5 3.9 %collective-permute-start.21 = (f32[1,1024]{1,0:T(1,128)S(1)}, f32[1,1024]{1,0:T(1,128)S(1)}, u32[]{:S(2)}, u32[]{:S(2)}) collective-permute-start(f32[1,1024]{1,0:T(1,128)S(1)} %add.76), channel_id=1, source_target_pairs={{0,8},{1,9},{2,10},{3,11},{4,12},{5,13},{6,14},{7,15},{8,0},{9,1},... | collective-permute-start | bytes 12296 | tf_op jit(solution)/shard_map/ppermute | solution.py:57
  78.5 3.3 %collective-permute-start.26 = (bf16[144,1024]{1,0:T(8,128)(2,1)S(1)}, bf16[144,1024]{1,0:T(8,128)(2,1)S(1)}, u32[]{:S(2)}, u32[]{:S(2)}) collective-permute-start(bf16[144,1024]{1,0:T(8,128)(2,1)S(1)} %add_convert_fusion.4), channel_id=1, source_target_pairs={{0,14},{1,15},{2,0},{3,1},{4,2},{5,3},{6,4},{7,5},{8,6},{9,7},{10,... | collective-permute-start | bytes 884744 | tf_op jit(solution)/shard_map/ppermute | solution.py:37
  82.1 5.9 %collective-permute-done.26 = bf16[144,1024]{1,0:T(8,128)(2,1)S(1)} collective-permute-done((bf16[144,1024]{1,0:T(8,128)(2,1)S(1)}, bf16[144,1024]{1,0:T(8,128)(2,1)S(1)}, u32[]{:S(2)}, u32[]{:S(2)}) %collective-permute-start.26) | collective-permute-done | bytes 294944 | tf_op jit(solution)/shard_map/ppermute | solution.py:37
  89.6 1.9 %collective-permute-done.23 = bf16[144,1024]{1,0:T(8,128)(2,1)S(1)} collective-permute-done((bf16[144,1024]{1,0:T(8,128)(2,1)S(1)}, bf16[144,1024]{1,0:T(8,128)(2,1)S(1)}, u32[]{:S(2)}, u32[]{:S(2)}) %collective-permute-start.23) | collective-permute-done | bytes 294944 | tf_op jit(solution)/shard_map/ppermute | solution.py:37
  92.3 1.7 %collective-permute-start.27 = (bf16[144,1024]{1,0:T(8,128)(2,1)S(1)}, bf16[144,1024]{1,0:T(8,128)(2,1)S(1)}, u32[]{:S(2)}, u32[]{:S(2)}) collective-permute-start(bf16[144,1024]{1,0:T(8,128)(2,1)S(1)} %add_convert_fusion.3), channel_id=1, source_target_pairs={{0,14},{1,15},{2,0},{3,1},{4,2},{5,3},{6,4},{7,5},{8,6},{9,7},{10,... | collective-permute-start | bytes 884744 | tf_op jit(solution)/shard_map/ppermute | solution.py:37
  94.0 1.7 %collective-permute-done.32 = bf16[144,1024]{1,0:T(8,128)(2,1)S(1)} collective-permute-done((bf16[144,1024]{1,0:T(8,128)(2,1)S(1)}, bf16[144,1024]{1,0:T(8,128)(2,1)S(1)}, u32[]{:S(2)}, u32[]{:S(2)}) %collective-permute-start.32) | collective-permute-done | bytes 294944 | tf_op jit(solution)/shard_map/ppermute | solution.py:41
  95.9 1.6 %collective-permute-start.33 = (bf16[144,1024]{1,0:T(8,128)(2,1)S(1)}, bf16[144,1024]{1,0:T(8,128)(2,1)S(1)}, u32[]{:S(2)}, u32[]{:S(2)}) collective-permute-start(bf16[144,1024]{1,0:T(8,128)(2,1)S(1)} %add_convert_fusion.1), channel_id=1, source_target_pairs={{0,32},{16,48},{32,64},{48,80},{64,96},{80,112},{96,0},{112,16},{1... | collective-permute-start | bytes 884744 | tf_op jit(solution)/shard_map/ppermute | solution.py:41
  97.5 2.0 %collective-permute-done.27 = bf16[144,1024]{1,0:T(8,128)(2,1)S(1)} collective-permute-done((bf16[144,1024]{1,0:T(8,128)(2,1)S(1)}, bf16[144,1024]{1,0:T(8,128)(2,1)S(1)}, u32[]{:S(2)}, u32[]{:S(2)}) %collective-permute-start.27) | collective-permute-done | bytes 294944 | tf_op jit(solution)/shard_map/ppermute | solution.py:37
  99.6 4.9 %collective-permute-done.24 = bf16[144,1024]{1,0:T(8,128)(2,1)S(1)} collective-permute-done((bf16[144,1024]{1,0:T(8,128)(2,1)S(1)}, bf16[144,1024]{1,0:T(8,128)(2,1)S(1)}, u32[]{:S(2)}, u32[]{:S(2)}) %collective-permute-start.24) | collective-permute-done | bytes 294944 | tf_op jit(solution)/shard_map/ppermute | solution.py:37
  106.5 2.8 %collective-permute-start.28 = (bf16[80,1024]{1,0:T(8,128)(2,1)S(1)}, bf16[80,1024]{1,0:T(8,128)(2,1)S(1)}, u32[]{:S(2)}, u32[]{:S(2)}) collective-permute-start(bf16[80,1024]{1,0:T(8,128)(2,1)S(1)} %maximum_maximum_fusion), channel_id=1, source_target_pairs={{0,1},{1,0},{2,3},{3,2},{4,5},{5,4},{6,7},{7,6},{8,9},{9,8},{10,11... | collective-permute-start | bytes 491528 | tf_op jit(solution)/shard_map/ppermute | solution.py:45
  111.2 2.8 %collective-permute-done.28 = bf16[80,1024]{1,0:T(8,128)(2,1)S(1)} collective-permute-done((bf16[80,1024]{1,0:T(8,128)(2,1)S(1)}, bf16[80,1024]{1,0:T(8,128)(2,1)S(1)}, u32[]{:S(2)}, u32[]{:S(2)}) %collective-permute-start.28) | collective-permute-done | bytes 163872 | tf_op jit(solution)/shard_map/ppermute | solution.py:45
  (78 shorter events, 20.2 us)
Async XLA Ops:
  0.6 7.4 %collective-permute-start = (bf16[72,1024]{1,0:T(8,128)(2,1)}, bf16[72,1024]{1,0:T(8,128)(2,1)S(1)}, u32[]{:S(2)}, u32[]{:S(2)}) collective-permute-start(bf16[72,1024]{1,0:T(8,128)(2,1)} %param.5), channel_id=1, source_target_pairs={{0,1},{1,0},{2,3},{3,2},{4,5},{5,4},{6,7},{7,6},{8,9},{9,8},{10,11... | collective-permute-start | bytes 442376 | tf_op jit(solution)/shard_map/ppermute | solution.py:45
  8.0 12.1 %collective-permute-start.4 = (bf16[144,1024]{1,0:T(8,128)(2,1)S(1)}, bf16[144,1024]{1,0:T(8,128)(2,1)S(1)}, u32[]{:S(2)}, u32[]{:S(2)}) collective-permute-start(bf16[144,1024]{1,0:T(8,128)(2,1)S(1)} %constant_dynamic-update-slice_fusion.refs_0_), channel_id=1, source_target_pairs={{0,2},{1,3},{2,4},{3,5},{4,6},{5,7},{6,8},{7,9},{8,10},{9,11},{10,... | collective-permute-start | bytes 884744 | tf_op jit(solution)/shard_map/ppermute | solution.py:37
  10.0 6.6 %collective-permute-start.7 = (bf16[72,1024]{1,0:T(8,128)(2,1)}, bf16[72,1024]{1,0:T(8,128)(2,1)S(1)}, u32[]{:S(2)}, u32[]{:S(2)}) collective-permute-start(bf16[72,1024]{1,0:T(8,128)(2,1)} %param.6), channel_id=1, source_target_pairs={{0,128},{16,144},{32,160},{48,176},{64,192},{80,208},{96,224},{112... | collective-permute-start | bytes 442376 | tf_op jit(solution)/shard_map/ppermute | solution.py:49
  12.5 9.2 %collective-permute-start.1 = (bf16[144,1024]{1,0:T(8,128)(2,1)S(1)}, bf16[144,1024]{1,0:T(8,128)(2,1)S(1)}, u32[]{:S(2)}, u32[]{:S(2)}) collective-permute-start(bf16[144,1024]{1,0:T(8,128)(2,1)S(1)} %constant_dynamic-update-slice_fusion.refs_0_), channel_id=1, source_target_pairs={{0,14},{1,15},{2,0},{3,1},{4,2},{5,3},{6,4},{7,5},{8,6},{9,7},{10,... | collective-permute-start | bytes 884744 | tf_op jit(solution)/shard_map/ppermute | solution.py:37
  16.6 9.2 %collective-permute-start.9 = (bf16[144,1024]{1,0:T(8,128)(2,1)S(1)}, bf16[144,1024]{1,0:T(8,128)(2,1)S(1)}, u32[]{:S(2)}, u32[]{:S(2)}) collective-permute-start(bf16[144,1024]{1,0:T(8,128)(2,1)S(1)} %constant_dynamic-update-slice_fusion.2.refs_0_), channel_id=1, source_target_pairs={{0,32},{16,48},{32,64},{48,80},{64,96},{80,112},{96,0},{112,16},{1... | collective-permute-start | bytes 884744 | tf_op jit(solution)/shard_map/ppermute | solution.py:41
  20.1 8.4 %collective-permute-start.5 = (bf16[144,1024]{1,0:T(8,128)(2,1)S(1)}, bf16[144,1024]{1,0:T(8,128)(2,1)S(1)}, u32[]{:S(2)}, u32[]{:S(2)}) collective-permute-start(bf16[144,1024]{1,0:T(8,128)(2,1)S(1)} %collective-permute-done.4.refs_6_), channel_id=1, source_target_pairs={{0,2},{1,3},{2,4},{3,5},{4,6},{5,7},{6,8},{7,9},{8,10},{9,11},{10,... | collective-permute-start | bytes 884744 | tf_op jit(solution)/shard_map/ppermute | solution.py:37
  21.7 7.9 %collective-permute-start.2 = (bf16[144,1024]{1,0:T(8,128)(2,1)S(1)}, bf16[144,1024]{1,0:T(8,128)(2,1)S(1)}, u32[]{:S(2)}, u32[]{:S(2)}) collective-permute-start(bf16[144,1024]{1,0:T(8,128)(2,1)S(1)} %collective-permute-done.1.refs_1_), channel_id=1, source_target_pairs={{0,14},{1,15},{2,0},{3,1},{4,2},{5,3},{6,4},{7,5},{8,6},{9,7},{10,... | collective-permute-start | bytes 884744 | tf_op jit(solution)/shard_map/ppermute | solution.py:37
  25.4 7.9 %collective-permute-start.8 = (bf16[144,1024]{1,0:T(8,128)(2,1)S(1)}, bf16[144,1024]{1,0:T(8,128)(2,1)S(1)}, u32[]{:S(2)}, u32[]{:S(2)}) collective-permute-start(bf16[144,1024]{1,0:T(8,128)(2,1)S(1)} %constant_dynamic-update-slice_fusion.2.refs_0_), channel_id=1, source_target_pairs={{0,96},{16,112},{32,0},{48,16},{64,32},{80,48},{96,64},{112,80},{1... | collective-permute-start | bytes 884744 | tf_op jit(solution)/shard_map/ppermute | solution.py:41
  25.9 8.0 %collective-permute-start.10 = (bf16[144,1024]{1,0:T(8,128)(2,1)S(1)}, bf16[144,1024]{1,0:T(8,128)(2,1)S(1)}, u32[]{:S(2)}, u32[]{:S(2)}) collective-permute-start(bf16[144,1024]{1,0:T(8,128)(2,1)S(1)} %collective-permute-done.9.refs_3_), channel_id=1, source_target_pairs={{0,32},{16,48},{32,64},{48,80},{64,96},{80,112},{96,0},{112,16},{1... | collective-permute-start | bytes 884744 | tf_op jit(solution)/shard_map/ppermute | solution.py:41
  28.5 7.9 %collective-permute-start.6 = (bf16[144,1024]{1,0:T(8,128)(2,1)S(1)}, bf16[144,1024]{1,0:T(8,128)(2,1)S(1)}, u32[]{:S(2)}, u32[]{:S(2)}) collective-permute-start(bf16[144,1024]{1,0:T(8,128)(2,1)S(1)} %collective-permute-done.5.refs_5_), channel_id=1, source_target_pairs={{0,2},{1,3},{2,4},{3,5},{4,6},{5,7},{6,8},{7,9},{8,10},{9,11},{10,... | collective-permute-start | bytes 884744 | tf_op jit(solution)/shard_map/ppermute | solution.py:37
  29.6 8.2 %collective-permute-start.3 = (bf16[144,1024]{1,0:T(8,128)(2,1)S(1)}, bf16[144,1024]{1,0:T(8,128)(2,1)S(1)}, u32[]{:S(2)}, u32[]{:S(2)}) collective-permute-start(bf16[144,1024]{1,0:T(8,128)(2,1)S(1)} %collective-permute-done.2.refs_2_), channel_id=1, source_target_pairs={{0,14},{1,15},{2,0},{3,1},{4,2},{5,3},{6,4},{7,5},{8,6},{9,7},{10,... | collective-permute-start | bytes 884744 | tf_op jit(solution)/shard_map/ppermute | solution.py:37
  33.3 8.2 %collective-permute-start.14 = (bf16[144,1024]{1,0:T(8,128)(2,1)S(1)}, bf16[144,1024]{1,0:T(8,128)(2,1)S(1)}, u32[]{:S(2)}, u32[]{:S(2)}) collective-permute-start(bf16[144,1024]{1,0:T(8,128)(2,1)S(1)} %collective-permute-done.9.refs_3_), channel_id=1, source_target_pairs={{0,16},{16,0},{32,48},{48,32},{64,80},{80,64},{96,112},{112,96},{1... | collective-permute-start | bytes 884744 | tf_op jit(solution)/shard_map/ppermute | solution.py:53
  33.8 7.7 %collective-permute-start.12 = (bf16[144,1024]{1,0:T(8,128)(2,1)S(1)}, bf16[144,1024]{1,0:T(8,128)(2,1)S(1)}, u32[]{:S(2)}, u32[]{:S(2)}) collective-permute-start(bf16[144,1024]{1,0:T(8,128)(2,1)S(1)} %collective-permute-done.8.refs_1_), channel_id=1, source_target_pairs={{0,16},{16,0},{32,48},{48,32},{64,80},{80,64},{96,112},{112,96},{1... | collective-permute-start | bytes 884744 | tf_op jit(solution)/shard_map/ppermute | solution.py:53
  37.8 8.3 %collective-permute-start.15 = (bf16[144,512]{1,0:T(8,128)(2,1)S(1)}, bf16[144,512]{1,0:T(8,128)(2,1)S(1)}, u32[]{:S(2)}, u32[]{:S(2)}) collective-permute-start(bf16[144,512]{1,0:T(8,128)(2,1)S(1)} %slice.38), channel_id=1, source_target_pairs={{0,2},{1,3},{2,4},{3,5},{4,6},{5,7},{6,8},{7,9},{8,10},{9,11},{10,... | collective-permute-start | bytes 442376 | tf_op jit(solution)/shard_map/ppermute | solution.py:37
  37.9 8.1 %collective-permute-start.16 = (bf16[144,512]{1,0:T(8,128)(2,1)S(1)}, bf16[144,512]{1,0:T(8,128)(2,1)S(1)}, u32[]{:S(2)}, u32[]{:S(2)}) collective-permute-start(bf16[144,512]{1,0:T(8,128)(2,1)S(1)} %slice.39), channel_id=1, source_target_pairs={{0,14},{1,15},{2,0},{3,1},{4,2},{5,3},{6,4},{7,5},{8,6},{9,7},{10,... | collective-permute-start | bytes 442376 | tf_op jit(solution)/shard_map/ppermute | solution.py:37
  51.4 9.9 %collective-permute-start.17 = (bf16[144,512]{1,0:T(8,128)(2,1)S(1)}, bf16[144,512]{1,0:T(8,128)(2,1)S(1)}, u32[]{:S(2)}, u32[]{:S(2)}) collective-permute-start(bf16[144,512]{1,0:T(8,128)(2,1)S(1)} %get-tuple-element.50), channel_id=1, source_target_pairs={{0,2},{1,3},{2,4},{3,5},{4,6},{5,7},{6,8},{7,9},{8,10},{9,11},{10,... | collective-permute-start | bytes 442376 | tf_op jit(solution)/shard_map/ppermute | solution.py:37
  57.9 15.9 %collective-permute-start.25 = (bf16[144,1024]{1,0:T(8,128)(2,1)S(1)}, bf16[144,1024]{1,0:T(8,128)(2,1)S(1)}, u32[]{:S(2)}, u32[]{:S(2)}) collective-permute-start(bf16[144,1024]{1,0:T(8,128)(2,1)S(1)} %add_convert_fusion.7._down), channel_id=1, source_target_pairs={{0,14},{1,15},{2,0},{3,1},{4,2},{5,3},{6,4},{7,5},{8,6},{9,7},{10,... | collective-permute-start | bytes 884744 | tf_op jit(solution)/shard_map/ppermute | solution.py:37
  61.4 13.1 %collective-permute-start.22 = (bf16[144,1024]{1,0:T(8,128)(2,1)S(1)}, bf16[144,1024]{1,0:T(8,128)(2,1)S(1)}, u32[]{:S(2)}, u32[]{:S(2)}) collective-permute-start(bf16[144,1024]{1,0:T(8,128)(2,1)S(1)} %add_convert_fusion.8._up), channel_id=1, source_target_pairs={{0,2},{1,3},{2,4},{3,5},{4,6},{5,7},{6,8},{7,9},{8,10},{9,11},{10,... | collective-permute-start | bytes 884744 | tf_op jit(solution)/shard_map/ppermute | solution.py:37
  72.3 6.2 %collective-permute-start.34 = (bf16[144,1024]{1,0:T(8,128)(2,1)S(1)}, bf16[144,1024]{1,0:T(8,128)(2,1)S(1)}, u32[]{:S(2)}, u32[]{:S(2)}) collective-permute-start(bf16[144,1024]{1,0:T(8,128)(2,1)S(1)} %get-tuple-element.66), channel_id=1, source_target_pairs={{0,16},{16,0},{32,48},{48,32},{64,80},{80,64},{96,112},{112,96},{1... | collective-permute-start | bytes 884744 | tf_op jit(solution)/shard_map/ppermute | solution.py:53
  72.3 9.6 %collective-permute-start.31 = (bf16[144,1024]{1,0:T(8,128)(2,1)S(1)}, bf16[144,1024]{1,0:T(8,128)(2,1)S(1)}, u32[]{:S(2)}, u32[]{:S(2)}) collective-permute-start(bf16[144,1024]{1,0:T(8,128)(2,1)S(1)} %get-tuple-element.64), channel_id=1, source_target_pairs={{0,16},{16,0},{32,48},{48,32},{64,80},{80,64},{96,112},{112,96},{1... | collective-permute-start | bytes 884744 | tf_op jit(solution)/shard_map/ppermute | solution.py:53
  73.8 18.5 %collective-permute-start.30 = (bf16[144,1024]{1,0:T(8,128)(2,1)S(1)}, bf16[144,1024]{1,0:T(8,128)(2,1)S(1)}, u32[]{:S(2)}, u32[]{:S(2)}) collective-permute-start(bf16[144,1024]{1,0:T(8,128)(2,1)S(1)} %get-tuple-element.62), channel_id=1, source_target_pairs={{0,16},{16,0},{32,48},{48,32},{64,80},{80,64},{96,112},{112,96},{1... | collective-permute-start | bytes 884744 | tf_op jit(solution)/shard_map/ppermute | solution.py:53
  73.8 30.8 %collective-permute-start.29 = (bf16[144,1024]{1,0:T(8,128)(2,1)S(1)}, bf16[144,1024]{1,0:T(8,128)(2,1)S(1)}, u32[]{:S(2)}, u32[]{:S(2)}) collective-permute-start(bf16[144,1024]{1,0:T(8,128)(2,1)S(1)} %get-tuple-element.60), channel_id=1, source_target_pairs={{0,16},{16,0},{32,48},{48,32},{64,80},{80,64},{96,112},{112,96},{1... | collective-permute-start | bytes 884744 | tf_op jit(solution)/shard_map/ppermute | solution.py:53
  74.5 21.4 %collective-permute-start.21 = (f32[1,1024]{1,0:T(1,128)S(1)}, f32[1,1024]{1,0:T(1,128)S(1)}, u32[]{:S(2)}, u32[]{:S(2)}) collective-permute-start(f32[1,1024]{1,0:T(1,128)S(1)} %add.76), channel_id=1, source_target_pairs={{0,8},{1,9},{2,10},{3,11},{4,12},{5,13},{6,14},{7,15},{8,0},{9,1},... | collective-permute-start | bytes 12296 | tf_op jit(solution)/shard_map/ppermute | solution.py:57
  78.5 9.5 %collective-permute-start.26 = (bf16[144,1024]{1,0:T(8,128)(2,1)S(1)}, bf16[144,1024]{1,0:T(8,128)(2,1)S(1)}, u32[]{:S(2)}, u32[]{:S(2)}) collective-permute-start(bf16[144,1024]{1,0:T(8,128)(2,1)S(1)} %add_convert_fusion.4), channel_id=1, source_target_pairs={{0,14},{1,15},{2,0},{3,1},{4,2},{5,3},{6,4},{7,5},{8,6},{9,7},{10,... | collective-permute-start | bytes 884744 | tf_op jit(solution)/shard_map/ppermute | solution.py:37
  81.9 9.7 %collective-permute-start.23 = (bf16[144,1024]{1,0:T(8,128)(2,1)S(1)}, bf16[144,1024]{1,0:T(8,128)(2,1)S(1)}, u32[]{:S(2)}, u32[]{:S(2)}) collective-permute-start(bf16[144,1024]{1,0:T(8,128)(2,1)S(1)} %add_convert_fusion.6), channel_id=1, source_target_pairs={{0,2},{1,3},{2,4},{3,5},{4,6},{5,7},{6,8},{7,9},{8,10},{9,11},{10,... | collective-permute-start | bytes 884744 | tf_op jit(solution)/shard_map/ppermute | solution.py:37
  88.0 7.8 %collective-permute-start.32 = (bf16[144,1024]{1,0:T(8,128)(2,1)S(1)}, bf16[144,1024]{1,0:T(8,128)(2,1)S(1)}, u32[]{:S(2)}, u32[]{:S(2)}) collective-permute-start(bf16[144,1024]{1,0:T(8,128)(2,1)S(1)} %add_convert_fusion.2), channel_id=1, source_target_pairs={{0,32},{16,48},{32,64},{48,80},{64,96},{80,112},{96,0},{112,16},{1... | collective-permute-start | bytes 884744 | tf_op jit(solution)/shard_map/ppermute | solution.py:41
  91.5 13.1 %collective-permute-start.35 = (bf16[144,1024]{1,0:T(8,128)(2,1)S(1)}, bf16[144,1024]{1,0:T(8,128)(2,1)S(1)}, u32[]{:S(2)}, u32[]{:S(2)}) collective-permute-start(bf16[144,1024]{1,0:T(8,128)(2,1)S(1)} %add_convert_fusion), channel_id=1, source_target_pairs={{0,96},{16,112},{32,0},{48,16},{64,32},{80,48},{96,64},{112,80},{1... | collective-permute-start | bytes 884744 | tf_op jit(solution)/shard_map/ppermute | solution.py:41
  92.3 7.2 %collective-permute-start.27 = (bf16[144,1024]{1,0:T(8,128)(2,1)S(1)}, bf16[144,1024]{1,0:T(8,128)(2,1)S(1)}, u32[]{:S(2)}, u32[]{:S(2)}) collective-permute-start(bf16[144,1024]{1,0:T(8,128)(2,1)S(1)} %add_convert_fusion.3), channel_id=1, source_target_pairs={{0,14},{1,15},{2,0},{3,1},{4,2},{5,3},{6,4},{7,5},{8,6},{9,7},{10,... | collective-permute-start | bytes 884744 | tf_op jit(solution)/shard_map/ppermute | solution.py:37
  95.7 8.8 %collective-permute-start.24 = (bf16[144,1024]{1,0:T(8,128)(2,1)S(1)}, bf16[144,1024]{1,0:T(8,128)(2,1)S(1)}, u32[]{:S(2)}, u32[]{:S(2)}) collective-permute-start(bf16[144,1024]{1,0:T(8,128)(2,1)S(1)} %add_convert_fusion.5), channel_id=1, source_target_pairs={{0,2},{1,3},{2,4},{3,5},{4,6},{5,7},{6,8},{7,9},{8,10},{9,11},{10,... | collective-permute-start | bytes 884744 | tf_op jit(solution)/shard_map/ppermute | solution.py:37
  95.9 8.8 %collective-permute-start.33 = (bf16[144,1024]{1,0:T(8,128)(2,1)S(1)}, bf16[144,1024]{1,0:T(8,128)(2,1)S(1)}, u32[]{:S(2)}, u32[]{:S(2)}) collective-permute-start(bf16[144,1024]{1,0:T(8,128)(2,1)S(1)} %add_convert_fusion.1), channel_id=1, source_target_pairs={{0,32},{16,48},{32,64},{48,80},{64,96},{80,112},{96,0},{112,16},{1... | collective-permute-start | bytes 884744 | tf_op jit(solution)/shard_map/ppermute | solution.py:41
  104.9 5.6 %collective-permute-start.36 = (bf16[72,1024]{1,0:T(8,128)(2,1)S(1)}, bf16[72,1024]{1,0:T(8,128)(2,1)S(1)}, u32[]{:S(2)}, u32[]{:S(2)}) collective-permute-start(bf16[72,1024]{1,0:T(8,128)(2,1)S(1)} %slice.56), channel_id=1, source_target_pairs={{0,128},{16,144},{32,160},{48,176},{64,192},{80,208},{96,224},{112... | collective-permute-start | bytes 442376 | tf_op jit(solution)/shard_map/ppermute | solution.py:49
  106.5 7.5 %collective-permute-start.28 = (bf16[80,1024]{1,0:T(8,128)(2,1)S(1)}, bf16[80,1024]{1,0:T(8,128)(2,1)S(1)}, u32[]{:S(2)}, u32[]{:S(2)}) collective-permute-start(bf16[80,1024]{1,0:T(8,128)(2,1)S(1)} %maximum_maximum_fusion), channel_id=1, source_target_pairs={{0,1},{1,0},{2,3},{3,2},{4,5},{5,4},{6,7},{7,6},{8,9},{9,8},{10,11... | collective-permute-start | bytes 491528 | tf_op jit(solution)/shard_map/ppermute | solution.py:45
  (6 other events, 25.6 us)

commit v5 on v4

--- a/solution.py
+++ b/solution.py
@@ -196,10 +196,9 @@
             outs[i][:, cols] = a * (pull[rows] - (xa[rows, cols].astype(F32) * a) * s)
 
 
-def caption_kernel(xa, x4, cx, yp, brow, sj, loss, _up, _down, *refs):
+def caption_kernel(xa, x4, cx, yp, brow, sj, _up, _down, *refs):
     own, away = refs[:4], refs[4:8]
-    t_ref = refs[9]
-    refs[8][...] = loss[...]
+    t_ref = refs[8]
     xlo, y, core, z, xhi = coords()
     same = core == xhi
     dims = (((1,), (1,)), ((), ()))
@@ -291,15 +290,42 @@
     )
 
 
-def run_captions(xa, x4, cx, yp, brow, sj, loss, up, down):
+def run_captions(xa, x4, cx, yp, brow, sj, up, down):
     return call(
         caption_kernel,
-        [sds((BL, N), F32)] * NY + [sds((BL, N), BF16)] * NY + [sds((1, N), F32)],
+        [sds((BL, N), F32)] * NY + [sds((BL, N), BF16)] * NY,
         2 * N * N * ROWS,
-        [xa, x4, cx, yp, brow, sj, loss, up, down],
+        [xa, x4, cx, yp, brow, sj, up, down],
         [pltpu.VMEM((ROWS, N), F32)],
-        unread=(7, 8),
-    )
+        unread=(6, 7),
+    )
+
+
+def add_after(groups, earlier, dtype=F32):
+    args = [v for group in groups for v in group]
+
+    def kernel(*refs):
+        outs = refs[len(args) + len(earlier) :]
+        at = 0
+        for out, group in zip(outs, groups):
+            total = refs[at][...].astype(F32)
+            for ref in refs[at + 1 : at + len(group)]:
+                total = total + ref[...].astype(F32)
+            out[...] = total.astype(dtype)
+            at += len(group)
+
+    return call(
+        kernel,
+        [sds(group[0].shape, dtype) for group in groups],
+        1,
+        args + list(earlier),
+        unread=range(len(args), len(args) + len(earlier)),
+        limit=16 * MIB,
+    )
+
+
+def together(*values):
+    return lax.optimization_barrier(values)
 
 
 def split(v):
@@ -308,26 +334,26 @@
 
 
 def shards(images, texts, pairs, log_scale, bias):
-    other_img, other_txt = swap_xhi(images), swap_xlo(texts)
+    other_img, other_txt = together(swap_xhi(images), swap_xlo(texts))
     up = down = jnp.concatenate([images, other_img], axis=0)
     block = jnp.concatenate([texts, other_txt], axis=0)
     ring = [[] for _ in range(NZ)]
     ring[0] = [up]
+    up, down = shift_z(up, 1), shift_z(down, -1)
     behind, ahead = shift_y(block, 1), shift_y(block, -1)
-    others = [swap_core(block)]
-    up, down = shift_z(up, 1), shift_z(down, -1)
+    up, down, block2 = together(up, down, swap_core(block))
     ring[NZ - 1], ring[1] = [up], [down]
+    up, down = shift_z(up, 1), shift_z(down, -1)
     across = shift_y(behind, 1)
-    others += [swap_core(ahead)]
-    last = swap_core(behind)
-    up, down = shift_z(up, 1), shift_z(down, -1)
+    up, down, ahead2, behind2 = together(up, down, swap_core(ahead), swap_core(behind))
     ring[NZ - 2], ring[2] = [up], [down]
-    others += [swap_core(across), last]
-    mine = [block, ahead, across, behind]
-    up, down = shift_z(up, 1), shift_z(down, -1)
+    up, down = shift_z(up, 1), shift_z(down, -1)
+    up, down, across2 = together(up, down, swap_core(across))
     ring[NZ - 3], ring[3] = [up], [down]
     left, right = shift_z(up[:, :HALF], 1), shift_z(down[:, HALF:], -1)
-    yp, ypt, brow, bcol = run_text(mine, others)
+    yp, ypt, brow, bcol = run_text(
+        [block, ahead, across, behind], [block2, ahead2, across2, behind2]
+    )
     xa, products, square = run_early([ring[k][0] for k in ORDER[:7]], ypt)
 
     x4, cy, cx, sj, si, arow, loss, up, down = run_middle(
@@ -338,27 +364,36 @@
     terms = {k: found[i] for i, k in enumerate(ORDER[:7])}
     up = (terms[3] + jnp.pad(wide(up), ((0, 0), (0, HALF)))).astype(BF16)
     down = (terms[5] + jnp.pad(wide(down), ((0, 0), (HALF, 0)))).astype(BF16)
-    cap = run_captions(xa, x4, cx, yp, brow, sj, loss, up, down)
-    up, down = shift_z(up, 1), shift_z(down, -1)
-    part = [cap[k] + wide(swap_core(cap[NY + k])) for k in range(NY)]
-    tup = shift_y(part[2].astype(BF16), 1)
-    tdown = shift_y(part[3].astype(BF16), -1)
-    up = shift_z((terms[2] + wide(up)).astype(BF16), 1)
-    down = shift_z((terms[6] + wide(down)).astype(BF16), -1)
-    tup = shift_y((part[1] + wide(tup)).astype(BF16), 1)
-    up = shift_z((terms[1] + wide(up)).astype(BF16), 1)
-    down = shift_z((terms[7] + wide(down)).astype(BF16), -1)
+    (loss,) = add_after([[loss]], (up, down))
+    lost = xor_z(loss, 1)
+    cap = run_captions(xa, x4, cx, yp, brow, sj, up, down)
+    up, down = shift_z(up, 1), shift_z(down, -1)
+    got = [swap_core(cap[NY + k]) for k in range(NY)]
+    up, down, lost = together(up, down, lost)
+    up = (terms[2] + wide(up)).astype(BF16)
+    down = (terms[6] + wide(down)).astype(BF16)
+    (loss,) = add_after([[loss, lost]], (up, down))
+    lost = xor_z(loss, 2)
+    tup, tdown = add_after([[cap[2], got[2]], [cap[3], got[3]]], (up, down), BF16)
+    tup, tdown = shift_y(tup, 1), shift_y(tdown, -1)
+    up, down = shift_z(up, 1), shift_z(down, -1)
+    up, down, lost = together(up, down, lost)
+    up = (terms[1] + wide(up)).astype(BF16)
+    down = (terms[7] + wide(down)).astype(BF16)
+    (loss,) = add_after([[loss, lost]], (up, down))
+    lost = xor_z(loss, 4)
+    (tup,) = add_after([[cap[1], got[1], tup]], (up, down), BF16)
+    tup = shift_y(tup, 1)
+    up, down = shift_z(up, 1), shift_z(down, -1)
     total = terms[0] + wide(up) + wide(down)
-
-    loss = cap[2 * NY]
-    for b in (1, 2, 4):
-        loss = loss + xor_z(loss, b)
+    loss = loss + lost
+
     high, low = split(loss)
     rows = jnp.concatenate([high, low, jnp.zeros((6, N), F32)], axis=0)
-    got = wide(swap_xhi(jnp.concatenate([total[SH:], rows], axis=0).astype(BF16)))
-    image_grad = total[:SH] + got[:SH]
-    loss = (high + low) + (got[SH : SH + 1] + got[SH + 1 : SH + 2])
-    total = part[0] + wide(tup) + wide(tdown)
+    away = wide(swap_xhi(jnp.concatenate([total[SH:], rows], axis=0).astype(BF16)))
+    image_grad = total[:SH] + away[:SH]
+    loss = (high + low) + (away[SH : SH + 1] + away[SH + 1 : SH + 2])
+    total = cap[0] + wide(got[0]) + wide(tup) + wide(tdown)
     text_grad = total[:SH] + wide(swap_xlo(total[SH:].astype(BF16)))
     return (loss.reshape(N), image_grad, text_grad)
 

time: 116 us -> 118 us (1.017)
  waiting for transfers between devices: 36.7 us -> 46.3 us
  starting transfers between devices: 55.3 us -> 48.1 us
    ppermute x6, waiting for transfers between devices: 1.74 us -> 6.3 us  [shift_y(): lax.ppermute(v, 'row', row_pairs(lambda x, y, c: (x, (y + d) % NY, c)))]
    ppermute x3, starting transfers between devices: 7.81 us -> 4.47 us  [xor_z(): return lax.ppermute(v, 'col', col_pairs(lambda z, h: (z ^ b, h)))]
    ppermute x3, waiting for transfers between devices: 3.93 us -> 6.83 us  [xor_z(): return lax.ppermute(v, 'col', col_pairs(lambda z, h: (z ^ b, h)))]
    ppermute x16, starting transfers between devices: 29.3 us -> 27.3 us  [shift_z(): return lax.ppermute(v, 'col', col_pairs(lambda z, h: ((z + d) % NZ, h)))]
    pallas_call x5 -> x10, Pallas kernels: 15.8 us -> 16 us  [call(): pl.pallas_call(kernel, out_shape=out_shape, in_specs=specs, out_specs=[vm...]
  transfers between devices with their start and end apart: 37 -> 37, of which waited for: 16 -> 12; matrix products, arithmetic and copies ran while one was open for 3% -> 3% of each run, Pallas kernels for 9% -> 9%
where the time goes in v5:
time: 118 us
  starting transfers between devices  48.1 us (41%)
  waiting for transfers between devices  46.3 us (39%)
  Pallas kernels  16 us (14%)
  other arithmetic  2.92 us (2%)
  between operations  2.23 us (2%)
  local copies, waits for them, and re-layouts  2.04 us (2%)
    ppermute x16, starting transfers between devices, shift_z(): return lax.ppermute(v, 'col', col_pairs(lambda z, h: ((z + d) % NZ, h)))  27.3 us
    ppermute x16, waiting for transfers between devices, shift_z(): return lax.ppermute(v, 'col', col_pairs(lambda z, h: ((z + d) % NZ, h)))  24.1 us
    pallas_call x10, Pallas kernels, call(): pl.pallas_call(kernel, out_shape=out_shape, in_specs=specs, out_specs=[vm...  16 us
    ppermute x6, starting transfers between devices, shift_y(): lax.ppermute(v, 'row', row_pairs(lambda x, y, c: (x, (y + d) % NY, c)))  7.26 us
    ppermute x2, waiting for transfers between devices, swap_xhi(): return lax.ppermute(v, 'col', col_pairs(lambda z, h: (z, 1 - h)))  6.99 us
    ppermute x3, waiting for transfers between devices, xor_z(): return lax.ppermute(v, 'col', col_pairs(lambda z, h: (z ^ b, h)))  6.83 us
    ppermute x6, waiting for transfers between devices, shift_y(): lax.ppermute(v, 'row', row_pairs(lambda x, y, c: (x, (y + d) % NY, c)))  6.3 us
    ppermute x2, starting transfers between devices, swap_xhi(): return lax.ppermute(v, 'col', col_pairs(lambda z, h: (z, 1 - h)))  5.23 us
  transfers between devices with their start and end apart: 37, of which 12 were waited for; matrix products, arithmetic and copies ran while one was open for 3% of the time, Pallas kernels for 9%

profile of v5, /device:TPU:8, one launch (start us, length us, event | category | flops | bytes accessed | tf_op | source)
XLA Modules:
  0.0 117.6 jit_solution(888909898461298413)
XLA Ops:
  0.6 3.1 %collective-permute-start = (bf16[72,1024]{1,0:T(8,128)(2,1)}, bf16[72,1024]{1,0:T(8,128)(2,1)S(1)}, u32[]{:S(2)}, u32[]{:S(2)}) collective-permute-start(bf16[72,1024]{1,0:T(8,128)(2,1)} %param.5), channel_id=1, source_target_pairs={{0,1},{1,0},{2,3},{3,2},{4,5},{5,4},{6,7},{7,6},{8,9},{9,8},{10,11... | collective-permute-start | bytes 442376 | tf_op jit(solution)/shard_map/ppermute | solution.py:45
  6.2 3.0 %collective-permute-done = bf16[72,1024]{1,0:T(8,128)(2,1)S(1)} collective-permute-done((bf16[72,1024]{1,0:T(8,128)(2,1)}, bf16[72,1024]{1,0:T(8,128)(2,1)S(1)}, u32[]{:S(2)}, u32[]{:S(2)}) %collective-permute-start) | collective-permute-done | bytes 147488 | tf_op jit(solution)/shard_map/ppermute | solution.py:45
  9.2 2.1 %collective-permute-done.1 = bf16[72,1024]{1,0:T(8,128)(2,1)S(1)} collective-permute-done((bf16[72,1024]{1,0:T(8,128)(2,1)}, bf16[72,1024]{1,0:T(8,128)(2,1)S(1)}, u32[]{:S(2)}, u32[]{:S(2)}) %collective-permute-start.1) | collective-permute-done | bytes 147488 | tf_op jit(solution)/shard_map/ppermute | solution.py:49
  11.4 2.0 %collective-permute-start.2 = (bf16[144,1024]{1,0:T(8,128)(2,1)S(1)}, bf16[144,1024]{1,0:T(8,128)(2,1)S(1)}, u32[]{:S(2)}, u32[]{:S(2)}) collective-permute-start(bf16[144,1024]{1,0:T(8,128)(2,1)S(1)} %constant_dynamic-update-slice_fusion.refs_0_), channel_id=1, source_target_pairs={{0,2},{1,3},{2,4},{3,5},{4,6},{5,7},{6,8},{7,9},{8,10},{9,11},{10,... | collective-permute-start | bytes 884744 | tf_op jit(solution)/shard_map/ppermute | solution.py:37
  13.4 4.0 %collective-permute-start.3 = (bf16[144,1024]{1,0:T(8,128)(2,1)S(1)}, bf16[144,1024]{1,0:T(8,128)(2,1)S(1)}, u32[]{:S(2)}, u32[]{:S(2)}) collective-permute-start(bf16[144,1024]{1,0:T(8,128)(2,1)S(1)} %constant_dynamic-update-slice_fusion.refs_0_), channel_id=1, source_target_pairs={{0,14},{1,15},{2,0},{3,1},{4,2},{5,3},{6,4},{7,5},{8,6},{9,7},{10,... | collective-permute-start | bytes 884744 | tf_op jit(solution)/shard_map/ppermute | solution.py:37
  17.4 1.6 %collective-permute-start.9 = (bf16[144,1024]{1,0:T(8,128)(2,1)S(1)}, bf16[144,1024]{1,0:T(8,128)(2,1)S(1)}, u32[]{:S(2)}, u32[]{:S(2)}) collective-permute-start(bf16[144,1024]{1,0:T(8,128)(2,1)S(1)} %constant_dynamic-update-slice_fusion.2.refs_0_), channel_id=1, source_target_pairs={{0,32},{16,48},{32,64},{48,80},{64,96},{80,112},{96,0},{112,16},{1... | collective-permute-start | bytes 884744 | tf_op jit(solution)/shard_map/ppermute | solution.py:41
  19.5 5.5 %collective-permute-done.2.refs_6_ = bf16[144,1024]{1,0:T(8,128)(2,1)S(1)} collective-permute-done((bf16[144,1024]{1,0:T(8,128)(2,1)S(1)}, bf16[144,1024]{1,0:T(8,128)(2,1)S(1)}, u32[]{:S(2)}, u32[]{:S(2)}) %collective-permute-start.2) | collective-permute-done | bytes 294944 | tf_op jit(solution)/shard_map/ppermute | solution.py:37
  25.0 3.2 %collective-permute-start.6 = (bf16[144,1024]{1,0:T(8,128)(2,1)S(1)}, bf16[144,1024]{1,0:T(8,128)(2,1)S(1)}, u32[]{:S(2)}, u32[]{:S(2)}) collective-permute-start(bf16[144,1024]{1,0:T(8,128)(2,1)S(1)} %collective-permute-done.3.refs_1_), channel_id=1, source_target_pairs={{0,14},{1,15},{2,0},{3,1},{4,2},{5,3},{6,4},{7,5},{8,6},{9,7},{10,... | collective-permute-start | bytes 884744 | tf_op jit(solution)/shard_map/ppermute | solution.py:37
  28.8 1.6 %collective-permute-start.13 = (bf16[144,1024]{1,0:T(8,128)(2,1)S(1)}, bf16[144,1024]{1,0:T(8,128)(2,1)S(1)}, u32[]{:S(2)}, u32[]{:S(2)}) collective-permute-start(bf16[144,1024]{1,0:T(8,128)(2,1)S(1)} %collective-permute-done.9.refs_3_), channel_id=1, source_target_pairs={{0,32},{16,48},{32,64},{48,80},{64,96},{80,112},{96,0},{112,16},{1... | collective-permute-start | bytes 884744 | tf_op jit(solution)/shard_map/ppermute | solution.py:41
  30.3 4.7 %collective-permute-done.5.refs_5_ = bf16[144,1024]{1,0:T(8,128)(2,1)S(1)} collective-permute-done((bf16[144,1024]{1,0:T(8,128)(2,1)S(1)}, bf16[144,1024]{1,0:T(8,128)(2,1)S(1)}, u32[]{:S(2)}, u32[]{:S(2)}) %collective-permute-start.5) | collective-permute-done | bytes 294944 | tf_op jit(solution)/shard_map/ppermute | solution.py:37
  35.0 1.9 %collective-permute-start.11 = (bf16[144,1024]{1,0:T(8,128)(2,1)S(1)}, bf16[144,1024]{1,0:T(8,128)(2,1)S(1)}, u32[]{:S(2)}, u32[]{:S(2)}) collective-permute-start(bf16[144,1024]{1,0:T(8,128)(2,1)S(1)} %collective-permute-done.5.refs_5_), channel_id=1, source_target_pairs={{0,2},{1,3},{2,4},{3,5},{4,6},{5,7},{6,8},{7,9},{8,10},{9,11},{10,... | collective-permute-start | bytes 884744 | tf_op jit(solution)/shard_map/ppermute | solution.py:37
  39.7 4.6 %collective-permute-done.11.refs_4_ = bf16[144,1024]{1,0:T(8,128)(2,1)S(1)} collective-permute-done((bf16[144,1024]{1,0:T(8,128)(2,1)S(1)}, bf16[144,1024]{1,0:T(8,128)(2,1)S(1)}, u32[]{:S(2)}, u32[]{:S(2)}) %collective-permute-start.11) | collective-permute-done | bytes 294944 | tf_op jit(solution)/shard_map/ppermute | solution.py:37
  44.3 1.7 %collective-permute-start.15 = (bf16[144,512]{1,0:T(8,128)(2,1)S(1)}, bf16[144,512]{1,0:T(8,128)(2,1)S(1)}, u32[]{:S(2)}, u32[]{:S(2)}) collective-permute-start(bf16[144,512]{1,0:T(8,128)(2,1)S(1)} %slice.29), channel_id=1, source_target_pairs={{0,2},{1,3},{2,4},{3,5},{4,6},{5,7},{6,8},{7,9},{8,10},{9,11},{10,... | collective-permute-start | bytes 442376 | tf_op jit(solution)/shard_map/ppermute | solution.py:37
  46.0 1.9 %collective-permute-start.16 = (bf16[144,512]{1,0:T(8,128)(2,1)S(1)}, bf16[144,512]{1,0:T(8,128)(2,1)S(1)}, u32[]{:S(2)}, u32[]{:S(2)}) collective-permute-start(bf16[144,512]{1,0:T(8,128)(2,1)S(1)} %slice.30), channel_id=1, source_target_pairs={{0,14},{1,15},{2,0},{3,1},{4,2},{5,3},{6,4},{7,5},{8,6},{9,7},{10,... | collective-permute-start | bytes 442376 | tf_op jit(solution)/shard_map/ppermute | solution.py:37
  47.9 2.1 %shard_map.76 = (bf16[1152,1024]{1,0:T(8,128)(2,1)S(1)}, bf16[1024,1152]{1,0:T(8,128)(2,1)S(1)}, f32[1,1024]{1,0:T(1,128)S(1)}, f32[1024,128]{1,0:T(8,128)S(1)}) custom-call(bf16[144,1024]{1,0:T(8,128)(2,1)S(1)} %constant_dynamic-update-slice_fusion.2.refs_0_, bf16[144,1024]{1,0:T(8,128)(2,1)S(1)} %collective-permute-done.7.refs_1_, ...), custom_call_target="tpu_custom_call" | custom-call | flops 67108864 | bytes 7606272 | tf_op jit(solution)/shard_map/pallas_call | solution.py:233
  50.1 2.3 %shard_map.77 = (bf16[1024,1024]{1,0:T(8,128)(2,1)S(1)}, f32[1024,1024]{1,0:T(8,128)S(1)}, f32[1,1024]{1,0:T(1,128)S(1)}) custom-call(bf16[144,1024]{1,0:T(8,128)(2,1)S(1)} %constant_dynamic-update-slice_fusion.refs_0_, bf16[144,1024]{1,0:T(8,128)(2,1)S(1)} %collective-permute-done.3.refs_1_, bf16[144,1024]{1,0:T(8,128)(2,1)S(1)} %collective-permute-done.6.refs_2_, ...), custom_call_target="tpu_custom_call" | custom-call | flops 2147483648 | bytes 10719232 | tf_op jit(solution)/shard_map/pallas_call | solution.py:233
  52.4 5.3 %shard_map.78 = (bf16[144,1024]{1,0:T(8,128)(2,1)S(1)}, bf16[1024,1024]{1,0:T(8,128)(2,1)S(1)}, bf16[1024,1024]{1,0:T(8,128)(2,1)S(1)}, f32[1,1024]{1,0:T(1,128)...) custom-call(bf16[144,512]{1,0:T(8,128)(2,1)S(1)} %collective-permute, ...), custom_call_target="tpu_custom_call" | custom-call | flops 2415919104 | bytes 14540808 | tf_op jit(solution)/shard_map/pallas_call | solution.py:233
  57.8 1.9 %collective-permute-start.18 = (bf16[144,512]{1,0:T(8,128)(2,1)S(1)}, bf16[144,512]{1,0:T(8,128)(2,1)S(1)}, u32[]{:S(2)}, u32[]{:S(2)}) collective-permute-start(bf16[144,512]{1,0:T(8,128)(2,1)S(1)} %get-tuple-element.79), channel_id=1, source_target_pairs={{0,14},{1,15},{2,0},{3,1},{4,2},{5,3},{6,4},{7,5},{8,6},{9,7},{10,... | collective-permute-start | bytes 442376 | tf_op jit(solution)/shard_map/ppermute | solution.py:37
  59.9 2.4 %shard_map.79 = (f32[144,1024]{1,0:T(8,128)S(1)}, f32[144,1024]{1,0:T(8,128)S(1)}, f32[144,1024]{1,0:T(8,128)S(1)}, f32[144,1024]{1,0:T(8,128)S(1)}, f32[144,102...) custom-call(bf16[1024,1024]{1,0:T(8,128)(2,1)S(1)} %get-tuple-element.72.xa, ...), custom_call_target="tpu_custom_call" | custom-call | flops 2113929216 | bytes 10690560 | tf_op jit(solution)/shard_map/pallas_call | solution.py:233
  63.9 2.2 %collective-permute-start.20 = (bf16[144,1024]{1,0:T(8,128)(2,1)S(1)}, bf16[144,1024]{1,0:T(8,128)(2,1)S(1)}, u32[]{:S(2)}, u32[]{:S(2)}) collective-permute-start(bf16[144,1024]{1,0:T(8,128)(2,1)S(1)} %add_convert_fusion.4.refs_2_._down), channel_id=1, source_target_pairs={{0,14},{1,15},{2,0},{3,1},{4,2},{5,3},{6,4},{7,5},{8,6},{9,7},{10,... | collective-permute-start | bytes 884744 | tf_op jit(solution)/shard_map/ppermute | solution.py:37
  67.4 3.6 %shard_map.83 = (f32[144,1024]{1,0:T(8,128)S(1)}, f32[144,1024]{1,0:T(8,128)S(1)}, f32[144,1024]{1,0:T(8,128)S(1)}, f32[144,1024]{1,0:T(8,128)S(1)}, bf16[144,10...) custom-call(bf16[1024,1024]{1,0:T(8,128)(2,1)S(1)} %get-tuple-elemen, ...), custom_call_target="tpu_custom_call" | custom-call | flops 2415919104 | bytes 10985472 | tf_op jit(solution)/shard_map/pallas_call | solution.py:233
  71.6 2.6 %collective-permute-done.19 = bf16[144,1024]{1,0:T(8,128)(2,1)S(1)} collective-permute-done((bf16[144,1024]{1,0:T(8,128)(2,1)S(1)}, bf16[144,1024]{1,0:T(8,128)(2,1)S(1)}, u32[]{:S(2)}, u32[]{:S(2)}) %collective-permute-start.19) | collective-permute-done | bytes 294944 | tf_op jit(solution)/shard_map/ppermute | solution.py:37
  74.5 2.1 %collective-permute-start.22 = (bf16[144,1024]{1,0:T(8,128)(2,1)S(1)}, bf16[144,1024]{1,0:T(8,128)(2,1)S(1)}, u32[]{:S(2)}, u32[]{:S(2)}) collective-permute-start(bf16[144,1024]{1,0:T(8,128)(2,1)S(1)} %add_convert_fusion.3.refs_2_.refs_4_), channel_id=1, source_target_pairs={{0,2},{1,3},{2,4},{3,5},{4,6},{5,7},{6,8},{7,9},{8,10},{9,11},{10,... | collective-permute-start | bytes 884744 | tf_op jit(solution)/shard_map/ppermute | solution.py:37
  78.7 4.6 %collective-permute-done.24.refs_1_ = f32[1,1024]{1,0:T(1,128)S(1)} collective-permute-done((f32[1,1024]{1,0:T(1,128)S(1)}, f32[1,1024]{1,0:T(1,128)S(1)}, u32[]{:S(2)}, u32[]{:S(2)}) %collective-permute-start.24) | collective-permute-done | bytes 4128 | tf_op jit(solution)/shard_map/ppermute | solution.py:57
  85.5 6.3 %collective-permute-done.33.refs_2_ = bf16[144,1024]{1,0:T(8,128)(2,1)S(1)} collective-permute-done((bf16[144,1024]{1,0:T(8,128)(2,1)S(1)}, bf16[144,1024]{1,0:T(8,128)(2,1)S(1)}, u32[]{:S(2)}, u32[]{:S(2)}) %collective-permute-start.33) | collective-permute-done | bytes 294944 | tf_op jit(solution)/shard_map/ppermute | solution.py:41
  91.9 1.6 %collective-permute-start.34 = (bf16[144,1024]{1,0:T(8,128)(2,1)S(1)}, bf16[144,1024]{1,0:T(8,128)(2,1)S(1)}, u32[]{:S(2)}, u32[]{:S(2)}) collective-permute-start(bf16[144,1024]{1,0:T(8,128)(2,1)S(1)} %shard_map.85), channel_id=1, source_target_pairs={{0,32},{16,48},{32,64},{48,80},{64,96},{80,112},{96,0},{112,16},{1... | collective-permute-start | bytes 884744 | tf_op jit(solution)/shard_map/ppermute | solution.py:41
  93.5 1.8 %collective-permute-start.25 = (f32[1,1024]{1,0:T(1,128)S(1)}, f32[1,1024]{1,0:T(1,128)S(1)}, u32[]{:S(2)}, u32[]{:S(2)}) collective-permute-start(f32[1,1024]{1,0:T(1,128)S(1)} %shard_map.82), channel_id=1, source_target_pairs={{0,8},{1,9},{2,10},{3,11},{4,12},{5,13},{6,14},{7,15},{8,0},{9,1},... | collective-permute-start | bytes 12296 | tf_op jit(solution)/shard_map/ppermute | solution.py:57
  95.4 3.4 %collective-permute-start.27 = (bf16[144,1024]{1,0:T(8,128)(2,1)S(1)}, bf16[144,1024]{1,0:T(8,128)(2,1)S(1)}, u32[]{:S(2)}, u32[]{:S(2)}) collective-permute-start(bf16[144,1024]{1,0:T(8,128)(2,1)S(1)} %add_convert_fusion.refs_3_.refs_4_), channel_id=1, source_target_pairs={{0,14},{1,15},{2,0},{3,1},{4,2},{5,3},{6,4},{7,5},{8,6},{9,7},{10,... | collective-permute-start | bytes 884744 | tf_op jit(solution)/shard_map/ppermute | solution.py:37
  98.8 2.3 %collective-permute-done.25 = f32[1,1024]{1,0:T(1,128)S(1)} collective-permute-done((f32[1,1024]{1,0:T(1,128)S(1)}, f32[1,1024]{1,0:T(1,128)S(1)}, u32[]{:S(2)}, u32[]{:S(2)}) %collective-permute-start.25) | collective-permute-done | bytes 4128 | tf_op jit(solution)/shard_map/ppermute | solution.py:57
  104.0 5.0 %collective-permute-done.26 = bf16[144,1024]{1,0:T(8,128)(2,1)S(1)} collective-permute-done((bf16[144,1024]{1,0:T(8,128)(2,1)S(1)}, bf16[144,1024]{1,0:T(8,128)(2,1)S(1)}, u32[]{:S(2)}, u32[]{:S(2)}) %collective-permute-start.26) | collective-permute-done | bytes 294944 | tf_op jit(solution)/shard_map/ppermute | solution.py:37
  109.3 2.1 %collective-permute-start.28 = (bf16[80,1024]{1,0:T(8,128)(2,1)S(1)}, bf16[80,1024]{1,0:T(8,128)(2,1)S(1)}, u32[]{:S(2)}, u32[]{:S(2)}) collective-permute-start(bf16[80,1024]{1,0:T(8,128)(2,1)S(1)} %maximum_maximum_fusion), channel_id=1, source_target_pairs={{0,1},{1,0},{2,3},{3,2},{4,5},{5,4},{6,7},{7,6},{8,9},{9,8},{10,11... | collective-permute-start | bytes 491528 | tf_op jit(solution)/shard_map/ppermute | solution.py:45
  112.2 4.0 %collective-permute-done.28 = bf16[80,1024]{1,0:T(8,128)(2,1)S(1)} collective-permute-done((bf16[80,1024]{1,0:T(8,128)(2,1)S(1)}, bf16[80,1024]{1,0:T(8,128)(2,1)S(1)}, u32[]{:S(2)}, u32[]{:S(2)}) %collective-permute-start.28) | collective-permute-done | bytes 163872 | tf_op jit(solution)/shard_map/ppermute | solution.py:45
  (78 shorter events, 18.6 us)
Async XLA Ops:
  0.6 8.5 %collective-permute-start = (bf16[72,1024]{1,0:T(8,128)(2,1)}, bf16[72,1024]{1,0:T(8,128)(2,1)S(1)}, u32[]{:S(2)}, u32[]{:S(2)}) collective-permute-start(bf16[72,1024]{1,0:T(8,128)(2,1)} %param.5), channel_id=1, source_target_pairs={{0,1},{1,0},{2,3},{3,2},{4,5},{5,4},{6,7},{7,6},{8,9},{9,8},{10,11... | collective-permute-start | bytes 442376 | tf_op jit(solution)/shard_map/ppermute | solution.py:45
  3.7 7.5 %collective-permute-start.1 = (bf16[72,1024]{1,0:T(8,128)(2,1)}, bf16[72,1024]{1,0:T(8,128)(2,1)S(1)}, u32[]{:S(2)}, u32[]{:S(2)}) collective-permute-start(bf16[72,1024]{1,0:T(8,128)(2,1)} %param.6), channel_id=1, source_target_pairs={{0,128},{16,144},{32,160},{48,176},{64,192},{80,208},{96,224},{112... | collective-permute-start | bytes 442376 | tf_op jit(solution)/shard_map/ppermute | solution.py:49
  11.3 8.2 %collective-permute-start.4 = (bf16[144,1024]{1,0:T(8,128)(2,1)S(1)}, bf16[144,1024]{1,0:T(8,128)(2,1)S(1)}, u32[]{:S(2)}, u32[]{:S(2)}) collective-permute-start(bf16[144,1024]{1,0:T(8,128)(2,1)S(1)} %constant_dynamic-update-slice_fusion.2.refs_0_), channel_id=1, source_target_pairs={{0,16},{16,0},{32,48},{48,32},{64,80},{80,64},{96,112},{112,96},{1... | collective-permute-start | bytes 884744 | tf_op jit(solution)/shard_map/ppermute | solution.py:53
  11.4 13.6 %collective-permute-start.2 = (bf16[144,1024]{1,0:T(8,128)(2,1)S(1)}, bf16[144,1024]{1,0:T(8,128)(2,1)S(1)}, u32[]{:S(2)}, u32[]{:S(2)}) collective-permute-start(bf16[144,1024]{1,0:T(8,128)(2,1)S(1)} %constant_dynamic-update-slice_fusion.refs_0_), channel_id=1, source_target_pairs={{0,2},{1,3},{2,4},{3,5},{4,6},{5,7},{6,8},{7,9},{8,10},{9,11},{10,... | collective-permute-start | bytes 884744 | tf_op jit(solution)/shard_map/ppermute | solution.py:37
  13.4 11.6 %collective-permute-start.3 = (bf16[144,1024]{1,0:T(8,128)(2,1)S(1)}, bf16[144,1024]{1,0:T(8,128)(2,1)S(1)}, u32[]{:S(2)}, u32[]{:S(2)}) collective-permute-start(bf16[144,1024]{1,0:T(8,128)(2,1)S(1)} %constant_dynamic-update-slice_fusion.refs_0_), channel_id=1, source_target_pairs={{0,14},{1,15},{2,0},{3,1},{4,2},{5,3},{6,4},{7,5},{8,6},{9,7},{10,... | collective-permute-start | bytes 884744 | tf_op jit(solution)/shard_map/ppermute | solution.py:37
  17.4 10.8 %collective-permute-start.9 = (bf16[144,1024]{1,0:T(8,128)(2,1)S(1)}, bf16[144,1024]{1,0:T(8,128)(2,1)S(1)}, u32[]{:S(2)}, u32[]{:S(2)}) collective-permute-start(bf16[144,1024]{1,0:T(8,128)(2,1)S(1)} %constant_dynamic-update-slice_fusion.2.refs_0_), channel_id=1, source_target_pairs={{0,32},{16,48},{32,64},{48,80},{64,96},{80,112},{96,0},{112,16},{1... | collective-permute-start | bytes 884744 | tf_op jit(solution)/shard_map/ppermute | solution.py:41
  19.0 9.2 %collective-permute-start.7 = (bf16[144,1024]{1,0:T(8,128)(2,1)S(1)}, bf16[144,1024]{1,0:T(8,128)(2,1)S(1)}, u32[]{:S(2)}, u32[]{:S(2)}) collective-permute-start(bf16[144,1024]{1,0:T(8,128)(2,1)S(1)} %constant_dynamic-update-slice_fusion.2.refs_0_), channel_id=1, source_target_pairs={{0,96},{16,112},{32,0},{48,16},{64,32},{80,48},{96,64},{112,80},{1... | collective-permute-start | bytes 884744 | tf_op jit(solution)/shard_map/ppermute | solution.py:41
  25.0 10.0 %collective-permute-start.5 = (bf16[144,1024]{1,0:T(8,128)(2,1)S(1)}, bf16[144,1024]{1,0:T(8,128)(2,1)S(1)}, u32[]{:S(2)}, u32[]{:S(2)}) collective-permute-start(bf16[144,1024]{1,0:T(8,128)(2,1)S(1)} %collective-permute-done.2.refs_6_), channel_id=1, source_target_pairs={{0,2},{1,3},{2,4},{3,5},{4,6},{5,7},{6,8},{7,9},{8,10},{9,11},{10,... | collective-permute-start | bytes 884744 | tf_op jit(solution)/shard_map/ppermute | solution.py:37
  25.0 10.0 %collective-permute-start.6 = (bf16[144,1024]{1,0:T(8,128)(2,1)S(1)}, bf16[144,1024]{1,0:T(8,128)(2,1)S(1)}, u32[]{:S(2)}, u32[]{:S(2)}) collective-permute-start(bf16[144,1024]{1,0:T(8,128)(2,1)S(1)} %collective-permute-done.3.refs_1_), channel_id=1, source_target_pairs={{0,14},{1,15},{2,0},{3,1},{4,2},{5,3},{6,4},{7,5},{8,6},{9,7},{10,... | collective-permute-start | bytes 884744 | tf_op jit(solution)/shard_map/ppermute | solution.py:37
  28.2 6.8 %collective-permute-start.10 = (bf16[144,1024]{1,0:T(8,128)(2,1)S(1)}, bf16[144,1024]{1,0:T(8,128)(2,1)S(1)}, u32[]{:S(2)}, u32[]{:S(2)}) collective-permute-start(bf16[144,1024]{1,0:T(8,128)(2,1)S(1)} %collective-permute-done.9.refs_3_), channel_id=1, source_target_pairs={{0,16},{16,0},{32,48},{48,32},{64,80},{80,64},{96,112},{112,96},{1... | collective-permute-start | bytes 884744 | tf_op jit(solution)/shard_map/ppermute | solution.py:53
  28.2 6.8 %collective-permute-start.8 = (bf16[144,1024]{1,0:T(8,128)(2,1)S(1)}, bf16[144,1024]{1,0:T(8,128)(2,1)S(1)}, u32[]{:S(2)}, u32[]{:S(2)}) collective-permute-start(bf16[144,1024]{1,0:T(8,128)(2,1)S(1)} %collective-permute-done.7.refs_1_), channel_id=1, source_target_pairs={{0,16},{16,0},{32,48},{48,32},{64,80},{80,64},{96,112},{112,96},{1... | collective-permute-start | bytes 884744 | tf_op jit(solution)/shard_map/ppermute | solution.py:53
  28.8 9.6 %collective-permute-start.13 = (bf16[144,1024]{1,0:T(8,128)(2,1)S(1)}, bf16[144,1024]{1,0:T(8,128)(2,1)S(1)}, u32[]{:S(2)}, u32[]{:S(2)}) collective-permute-start(bf16[144,1024]{1,0:T(8,128)(2,1)S(1)} %collective-permute-done.9.refs_3_), channel_id=1, source_target_pairs={{0,32},{16,48},{32,64},{48,80},{64,96},{80,112},{96,0},{112,16},{1... | collective-permute-start | bytes 884744 | tf_op jit(solution)/shard_map/ppermute | solution.py:41
  35.0 9.3 %collective-permute-start.11 = (bf16[144,1024]{1,0:T(8,128)(2,1)S(1)}, bf16[144,1024]{1,0:T(8,128)(2,1)S(1)}, u32[]{:S(2)}, u32[]{:S(2)}) collective-permute-start(bf16[144,1024]{1,0:T(8,128)(2,1)S(1)} %collective-permute-done.5.refs_5_), channel_id=1, source_target_pairs={{0,2},{1,3},{2,4},{3,5},{4,6},{5,7},{6,8},{7,9},{8,10},{9,11},{10,... | collective-permute-start | bytes 884744 | tf_op jit(solution)/shard_map/ppermute | solution.py:37
  37.0 7.3 %collective-permute-start.12 = (bf16[144,1024]{1,0:T(8,128)(2,1)S(1)}, bf16[144,1024]{1,0:T(8,128)(2,1)S(1)}, u32[]{:S(2)}, u32[]{:S(2)}) collective-permute-start(bf16[144,1024]{1,0:T(8,128)(2,1)S(1)} %collective-permute-done.6.refs_2_), channel_id=1, source_target_pairs={{0,14},{1,15},{2,0},{3,1},{4,2},{5,3},{6,4},{7,5},{8,6},{9,7},{10,... | collective-permute-start | bytes 884744 | tf_op jit(solution)/shard_map/ppermute | solution.py:37
  44.3 8.1 %collective-permute-start.15 = (bf16[144,512]{1,0:T(8,128)(2,1)S(1)}, bf16[144,512]{1,0:T(8,128)(2,1)S(1)}, u32[]{:S(2)}, u32[]{:S(2)}) collective-permute-start(bf16[144,512]{1,0:T(8,128)(2,1)S(1)} %slice.29), channel_id=1, source_target_pairs={{0,2},{1,3},{2,4},{3,5},{4,6},{5,7},{6,8},{7,9},{8,10},{9,11},{10,... | collective-permute-start | bytes 442376 | tf_op jit(solution)/shard_map/ppermute | solution.py:37
  63.9 7.7 %collective-permute-start.20 = (bf16[144,1024]{1,0:T(8,128)(2,1)S(1)}, bf16[144,1024]{1,0:T(8,128)(2,1)S(1)}, u32[]{:S(2)}, u32[]{:S(2)}) collective-permute-start(bf16[144,1024]{1,0:T(8,128)(2,1)S(1)} %add_convert_fusion.4.refs_2_._down), channel_id=1, source_target_pairs={{0,14},{1,15},{2,0},{3,1},{4,2},{5,3},{6,4},{7,5},{8,6},{9,7},{10,... | collective-permute-start | bytes 884744 | tf_op jit(solution)/shard_map/ppermute | solution.py:37
  66.2 8.0 %collective-permute-start.19 = (bf16[144,1024]{1,0:T(8,128)(2,1)S(1)}, bf16[144,1024]{1,0:T(8,128)(2,1)S(1)}, u32[]{:S(2)}, u32[]{:S(2)}) collective-permute-start(bf16[144,1024]{1,0:T(8,128)(2,1)S(1)} %add_convert_fusion.5.refs_1_._up), channel_id=1, source_target_pairs={{0,2},{1,3},{2,4},{3,5},{4,6},{5,7},{6,8},{7,9},{8,10},{9,11},{10,... | collective-permute-start | bytes 884744 | tf_op jit(solution)/shard_map/ppermute | solution.py:37
  71.0 7.0 %collective-permute-start.31 = (bf16[144,1024]{1,0:T(8,128)(2,1)S(1)}, bf16[144,1024]{1,0:T(8,128)(2,1)S(1)}, u32[]{:S(2)}, u32[]{:S(2)}) collective-permute-start(bf16[144,1024]{1,0:T(8,128)(2,1)S(1)} %get-tuple-element.100), channel_id=1, source_target_pairs={{0,16},{16,0},{32,48},{48,32},{64,80},{80,64},{96,112},{112,96},{1... | collective-permute-start | bytes 884744 | tf_op jit(solution)/shard_map/ppermute | solution.py:53
  71.1 6.9 %collective-permute-start.32 = (bf16[144,1024]{1,0:T(8,128)(2,1)S(1)}, bf16[144,1024]{1,0:T(8,128)(2,1)S(1)}, u32[]{:S(2)}, u32[]{:S(2)}) collective-permute-start(bf16[144,1024]{1,0:T(8,128)(2,1)S(1)} %get-tuple-element.102), channel_id=1, source_target_pairs={{0,16},{16,0},{32,48},{48,32},{64,80},{80,64},{96,112},{112,96},{1... | collective-permute-start | bytes 884744 | tf_op jit(solution)/shard_map/ppermute | solution.py:53
  74.3 10.5 %collective-permute-start.23 = (bf16[144,1024]{1,0:T(8,128)(2,1)S(1)}, bf16[144,1024]{1,0:T(8,128)(2,1)S(1)}, u32[]{:S(2)}, u32[]{:S(2)}) collective-permute-start(bf16[144,1024]{1,0:T(8,128)(2,1)S(1)} %add_convert_fusion.2.refs_3_.refs_5_), channel_id=1, source_target_pairs={{0,14},{1,15},{2,0},{3,1},{4,2},{5,3},{6,4},{7,5},{8,6},{9,7},{10,... | collective-permute-start | bytes 884744 | tf_op jit(solution)/shard_map/ppermute | solution.py:37
  74.5 10.8 %collective-permute-start.22 = (bf16[144,1024]{1,0:T(8,128)(2,1)S(1)}, bf16[144,1024]{1,0:T(8,128)(2,1)S(1)}, u32[]{:S(2)}, u32[]{:S(2)}) collective-permute-start(bf16[144,1024]{1,0:T(8,128)(2,1)S(1)} %add_convert_fusion.3.refs_2_.refs_4_), channel_id=1, source_target_pairs={{0,2},{1,3},{2,4},{3,5},{4,6},{5,7},{6,8},{7,9},{8,10},{9,11},{10,... | collective-permute-start | bytes 884744 | tf_op jit(solution)/shard_map/ppermute | solution.py:37
  76.6 6.7 %collective-permute-start.24 = (f32[1,1024]{1,0:T(1,128)S(1)}, f32[1,1024]{1,0:T(1,128)S(1)}, u32[]{:S(2)}, u32[]{:S(2)}) collective-permute-start(f32[1,1024]{1,0:T(1,128)S(1)} %shard_map.81.refs_0_), channel_id=1, source_target_pairs={{0,4},{1,5},{2,6},{3,7},{4,0},{5,1},{6,2},{7,3},{8,12},{9,13},{10,... | collective-permute-start | bytes 12296 | tf_op jit(solution)/shard_map/ppermute | solution.py:57
  78.1 7.4 %collective-permute-start.30 = (bf16[144,1024]{1,0:T(8,128)(2,1)S(1)}, bf16[144,1024]{1,0:T(8,128)(2,1)S(1)}, u32[]{:S(2)}, u32[]{:S(2)}) collective-permute-start(bf16[144,1024]{1,0:T(8,128)(2,1)S(1)} %get-tuple-element.98), channel_id=1, source_target_pairs={{0,16},{16,0},{32,48},{48,32},{64,80},{80,64},{96,112},{112,96},{1... | collective-permute-start | bytes 884744 | tf_op jit(solution)/shard_map/ppermute | solution.py:53
  78.1 24.2 %collective-permute-start.29 = (bf16[144,1024]{1,0:T(8,128)(2,1)S(1)}, bf16[144,1024]{1,0:T(8,128)(2,1)S(1)}, u32[]{:S(2)}, u32[]{:S(2)}) collective-permute-start(bf16[144,1024]{1,0:T(8,128)(2,1)S(1)} %get-tuple-element.96), channel_id=1, source_target_pairs={{0,16},{16,0},{32,48},{48,32},{64,80},{80,64},{96,112},{112,96},{1... | collective-permute-start | bytes 884744 | tf_op jit(solution)/shard_map/ppermute | solution.py:53
  83.3 8.5 %collective-permute-start.33 = (bf16[144,1024]{1,0:T(8,128)(2,1)S(1)}, bf16[144,1024]{1,0:T(8,128)(2,1)S(1)}, u32[]{:S(2)}, u32[]{:S(2)}) collective-permute-start(bf16[144,1024]{1,0:T(8,128)(2,1)S(1)} %get-tuple-element.103), channel_id=1, source_target_pairs={{0,32},{16,48},{32,64},{48,80},{64,96},{80,112},{96,0},{112,16},{1... | collective-permute-start | bytes 884744 | tf_op jit(solution)/shard_map/ppermute | solution.py:41
  84.8 17.5 %collective-permute-start.35 = (bf16[144,1024]{1,0:T(8,128)(2,1)S(1)}, bf16[144,1024]{1,0:T(8,128)(2,1)S(1)}, u32[]{:S(2)}, u32[]{:S(2)}) collective-permute-start(bf16[144,1024]{1,0:T(8,128)(2,1)S(1)} %get-tuple-element.104), channel_id=1, source_target_pairs={{0,96},{16,112},{32,0},{48,16},{64,32},{80,48},{96,64},{112,80},{1... | collective-permute-start | bytes 884744 | tf_op jit(solution)/shard_map/ppermute | solution.py:41
  91.9 10.4 %collective-permute-start.34 = (bf16[144,1024]{1,0:T(8,128)(2,1)S(1)}, bf16[144,1024]{1,0:T(8,128)(2,1)S(1)}, u32[]{:S(2)}, u32[]{:S(2)}) collective-permute-start(bf16[144,1024]{1,0:T(8,128)(2,1)S(1)} %shard_map.85), channel_id=1, source_target_pairs={{0,32},{16,48},{32,64},{48,80},{64,96},{80,112},{96,0},{112,16},{1... | collective-permute-start | bytes 884744 | tf_op jit(solution)/shard_map/ppermute | solution.py:41
  93.5 7.6 %collective-permute-start.25 = (f32[1,1024]{1,0:T(1,128)S(1)}, f32[1,1024]{1,0:T(1,128)S(1)}, u32[]{:S(2)}, u32[]{:S(2)}) collective-permute-start(f32[1,1024]{1,0:T(1,128)S(1)} %shard_map.82), channel_id=1, source_target_pairs={{0,8},{1,9},{2,10},{3,11},{4,12},{5,13},{6,14},{7,15},{8,0},{9,1},... | collective-permute-start | bytes 12296 | tf_op jit(solution)/shard_map/ppermute | solution.py:57
  95.4 8.6 %collective-permute-start.27 = (bf16[144,1024]{1,0:T(8,128)(2,1)S(1)}, bf16[144,1024]{1,0:T(8,128)(2,1)S(1)}, u32[]{:S(2)}, u32[]{:S(2)}) collective-permute-start(bf16[144,1024]{1,0:T(8,128)(2,1)S(1)} %add_convert_fusion.refs_3_.refs_4_), channel_id=1, source_target_pairs={{0,14},{1,15},{2,0},{3,1},{4,2},{5,3},{6,4},{7,5},{8,6},{9,7},{10,... | collective-permute-start | bytes 884744 | tf_op jit(solution)/shard_map/ppermute | solution.py:37
  101.1 7.9 %collective-permute-start.26 = (bf16[144,1024]{1,0:T(8,128)(2,1)S(1)}, bf16[144,1024]{1,0:T(8,128)(2,1)S(1)}, u32[]{:S(2)}, u32[]{:S(2)}) collective-permute-start(bf16[144,1024]{1,0:T(8,128)(2,1)S(1)} %add_convert_fusion.1.refs_2_.refs_3_), channel_id=1, source_target_pairs={{0,2},{1,3},{2,4},{3,5},{4,6},{5,7},{6,8},{7,9},{8,10},{9,11},{10,... | collective-permute-start | bytes 884744 | tf_op jit(solution)/shard_map/ppermute | solution.py:37
  102.5 8.9 %collective-permute-start.36 = (bf16[72,1024]{1,0:T(8,128)(2,1)S(1)}, bf16[72,1024]{1,0:T(8,128)(2,1)S(1)}, u32[]{:S(2)}, u32[]{:S(2)}) collective-permute-start(bf16[72,1024]{1,0:T(8,128)(2,1)S(1)} %slice.54), channel_id=1, source_target_pairs={{0,128},{16,144},{32,160},{48,176},{64,192},{80,208},{96,224},{112... | collective-permute-start | bytes 442376 | tf_op jit(solution)/shard_map/ppermute | solution.py:49
  109.3 6.9 %collective-permute-start.28 = (bf16[80,1024]{1,0:T(8,128)(2,1)S(1)}, bf16[80,1024]{1,0:T(8,128)(2,1)S(1)}, u32[]{:S(2)}, u32[]{:S(2)}) collective-permute-start(bf16[80,1024]{1,0:T(8,128)(2,1)S(1)} %maximum_maximum_fusion), channel_id=1, source_target_pairs={{0,1},{1,0},{2,3},{3,2},{4,5},{5,4},{6,7},{7,6},{8,9},{9,8},{10,11... | collective-permute-start | bytes 491528 | tf_op jit(solution)/shard_map/ppermute | solution.py:45
  (6 other events, 32.6 us)

commit v6 on v5

--- a/solution.py
+++ b/solution.py
@@ -1,3 +1,5 @@
+import functools
+
 import jax
 import jax.numpy as jnp
 from jax import lax
@@ -67,10 +69,13 @@
 
 
 def position(k):
-    return jnp.where(k < 4, k, jnp.where(k == 4, 7, k - 1))
-
-
-ORDER = (0, 1, 2, 3, 5, 6, 7, 4)
+    place = 0
+    for i, block in enumerate(ORDER):
+        place = jnp.where(k == block, i, place)
+    return place
+
+
+ORDER = (0, 1, 2, 6, 7, 3, 5, 4)
 EARLY = 7 * BL
 WIDE = 1024
 TAIL = 896
@@ -122,6 +127,53 @@
 
 LANES = 512
 TILE = 64
+MSG = BL + 16
+
+
+def encode(v):
+    high = v.astype(BF16).astype(F32)
+    low = v - high
+    row = lax.broadcasted_iota(jnp.int32, (16, HALF), 0)
+    out = jnp.zeros((16, HALF), F32)
+    for i, part in enumerate((high[:, :HALF], high[:, HALF:], low[:, :HALF], low[:, HALF:])):
+        out = jnp.where(row == i, part, out)
+    return out.astype(BF16)
+
+
+def decode(rows):
+    v = rows.astype(F32)
+    return jnp.concatenate([v[0:1] + v[2:3], v[1:2] + v[3:4]], axis=1)
+
+
+def from_side(up, down, parity):
+    z = lax.axis_index("col") // 2
+    return decode(jnp.where(z % 2 == parity, up[BL:, :HALF].astype(F32), down[BL:, :HALF].astype(F32)))
+
+
+def first_step_kernel(t_up, t_down, r_up, r_down, loss, m_up, m_down, pair):
+    m_up[:BL, :HALF] = (t_up[:, :HALF] + r_up[:BL, :].astype(F32)).astype(BF16)
+    m_up[:BL, HALF:] = t_up[:, HALF:].astype(BF16)
+    m_down[:BL, :HALF] = t_down[:, :HALF].astype(BF16)
+    m_down[:BL, HALF:] = (t_down[:, HALF:] + r_down[:BL, :].astype(F32)).astype(BF16)
+    ride = encode(decode(encode(loss[...])) + from_side(r_up, r_down, 1))
+    pair[...] = decode(ride)
+    for m in (m_up, m_down):
+        m[BL:, :HALF] = ride
+        m[BL:, HALF:] = jnp.zeros((MSG - BL, HALF), BF16)
+
+
+def step_kernel(parity, t_up, t_down, r_up, r_down, m_up, m_down, side):
+    for t, r, m in ((t_up, r_up, m_up), (t_down, r_down, m_down)):
+        m[:BL, :] = (t[...] + r[:BL, :].astype(F32)).astype(BF16)
+        m[BL:, :] = r[BL:, :]
+    side[...] = from_side(r_up, r_down, parity)
+
+
+def last_step_kernel(term, r_up, r_down, pair, side1, side2, own, far, loss):
+    total = term[...] + r_up[:BL, :].astype(F32) + r_down[:BL, :].astype(F32)
+    own[...] = total[:SH]
+    far[...] = total[SH:].astype(BF16)
+    loss[...] = (pair[...] + from_side(r_up, r_down, 0)) + (side1[...] + side2[...])
 
 
 def middle_kernel(
@@ -182,18 +234,23 @@
         term = ai * (pull - (x4[:, cols].astype(F32) * ai) * inner)
         out = out_left if n * LANES < HALF else out_right
         at = n * LANES % HALF
-        out[:, at : at + LANES] = term.astype(BF16)
+        out[:BL, at : at + LANES] = term.astype(BF16)
+    ride = encode(loss[...])
+    out_left[BL:, :] = ride
+    out_right[BL:, :] = ride
     sj[...] = jnp.sum(acc_sj[...].T, axis=0, keepdims=True) * scale
 
 
-def image_kernel(xa, yp, cy, arow, si, *outs):
+def image_kernel(places, xa, yp, cy, arow, si, *refs):
+    outs = refs[-len(places) :]
+    low, high = places[0] * BL, (places[-1] + 1) * BL
     for n in range(N // W):
         cols = slice(n * W, (n + 1) * W)
-        pull = jnp.dot(yp[:EARLY, :], cy[:, cols], preferred_element_type=F32)
+        pull = jnp.dot(yp[low:high, :], cy[:, cols], preferred_element_type=F32)
         a, s = arow[:, cols], si[:, cols]
-        for i in range(7):
-            rows = slice(i * BL, (i + 1) * BL)
-            outs[i][:, cols] = a * (pull[rows] - (xa[rows, cols].astype(F32) * a) * s)
+        for i, out in zip(places, outs):
+            u = xa[i * BL : (i + 1) * BL, cols].astype(F32) * a
+            out[:, cols] = a * (pull[i * BL - low : (i + 1) * BL - low] - u * s)
 
 
 def caption_kernel(xa, x4, cx, yp, brow, sj, _up, _down, *refs):
@@ -222,14 +279,15 @@
         away[k][...] = jnp.concatenate(there, axis=0).astype(BF16)
 
 
-def call(kernel, out_shape, flops, args, scratch=(), smem=(), unread=(), limit=32 * MIB):
+def call(kernel, out_shape, flops, args, scratch=(), smem=(), unread=(), limit=32 * MIB, moved=None):
     vm = pl.BlockSpec(memory_space=pltpu.VMEM)
     specs = [vm] * len(args)
     for i in smem:
         specs[i] = pl.BlockSpec(memory_space=pltpu.SMEM)
     for i in unread:
         specs[i] = pl.BlockSpec(memory_space=pl.ANY)
-    moved = sum(x.size * x.dtype.itemsize for x in list(args) + list(out_shape))
+    if moved is None:
+        moved = sum(x.size * x.dtype.itemsize for x in list(args) + list(out_shape))
     return pl.pallas_call(
         kernel,
         out_shape=out_shape,
@@ -272,7 +330,7 @@
     return call(
         middle_kernel,
         [sds((BL, N), BF16), sds((N, N), BF16), sds((N, N), BF16), row, row, row, row]
-        + [sds((BL, HALF), BF16)] * 2,
+        + [sds((MSG, HALF), BF16)] * 2,
         2 * N * N * ROWS,
         [left, right, part, square, pairs.reshape(1, N), log_scale, bias, yp, ypt, bcol],
         [
@@ -284,10 +342,15 @@
     )
 
 
-def run_images(xa, yp, cy, arow, si):
-    return call(
-        image_kernel, [sds((BL, N), F32)] * 7, 2 * N * N * EARLY, [xa, yp, cy, arow, si]
-    )
+def run_images(places, xa, yp, cy, arow, si, earlier=()):
+    found = call(
+        functools.partial(image_kernel, places),
+        [sds((BL, N), F32)] * len(places),
+        2 * N * N * BL * len(places),
+        [xa, yp, cy, arow, si, *earlier],
+        unread=range(5, 5 + len(earlier)),
+    )
+    return {ORDER[i]: v for i, v in zip(places, found)}
 
 
 def run_captions(xa, x4, cx, yp, brow, sj, up, down):
@@ -301,7 +364,7 @@
     )
 
 
-def add_after(groups, earlier, dtype=F32):
+def add_after(groups, earlier, dtype=F32, weight=1):
     args = [v for group in groups for v in group]
 
     def kernel(*refs):
@@ -321,6 +384,7 @@
         args + list(earlier),
         unread=range(len(args), len(args) + len(earlier)),
         limit=16 * MIB,
+        moved=weight,
     )
 
 
@@ -328,31 +392,25 @@
     return lax.optimization_barrier(values)
 
 
-def split(v):
-    high = lax.reduce_precision(v, 8, 7)
-    return high, lax.reduce_precision(v - high, 8, 7)
-
-
 def shards(images, texts, pairs, log_scale, bias):
-    other_img, other_txt = together(swap_xhi(images), swap_xlo(texts))
+    other_img, other_txt = swap_xhi(images), swap_xlo(texts)
     up = down = jnp.concatenate([images, other_img], axis=0)
     block = jnp.concatenate([texts, other_txt], axis=0)
     ring = [[] for _ in range(NZ)]
     ring[0] = [up]
-    up, down = shift_z(up, 1), shift_z(down, -1)
     behind, ahead = shift_y(block, 1), shift_y(block, -1)
+    across = shift_y(behind, 1)
+    up, down = shift_z(up, 1), shift_z(down, -1)
+    ring[NZ - 1], ring[1] = [up], [down]
+    up, down = shift_z(up, 1), shift_z(down, -1)
     up, down, block2 = together(up, down, swap_core(block))
-    ring[NZ - 1], ring[1] = [up], [down]
-    up, down = shift_z(up, 1), shift_z(down, -1)
-    across = shift_y(behind, 1)
-    up, down, ahead2, behind2 = together(up, down, swap_core(ahead), swap_core(behind))
     ring[NZ - 2], ring[2] = [up], [down]
     up, down = shift_z(up, 1), shift_z(down, -1)
-    up, down, across2 = together(up, down, swap_core(across))
     ring[NZ - 3], ring[3] = [up], [down]
     left, right = shift_z(up[:, :HALF], 1), shift_z(down[:, HALF:], -1)
     yp, ypt, brow, bcol = run_text(
-        [block, ahead, across, behind], [block2, ahead2, across2, behind2]
+        [block, ahead, across, behind],
+        [block2, swap_core(ahead), swap_core(across), swap_core(behind)],
     )
     xa, products, square = run_early([ring[k][0] for k in ORDER[:7]], ypt)
 
@@ -360,41 +418,35 @@
         left, right, products, square, pairs, log_scale, bias, yp, ypt, bcol
     )
     up, down = shift_z(up, 1), shift_z(down, -1)
-    found = run_images(xa, yp, cy, arow, si)
-    terms = {k: found[i] for i, k in enumerate(ORDER[:7])}
-    up = (terms[3] + jnp.pad(wide(up), ((0, 0), (0, HALF)))).astype(BF16)
-    down = (terms[5] + jnp.pad(wide(down), ((0, 0), (HALF, 0)))).astype(BF16)
-    (loss,) = add_after([[loss]], (up, down))
-    lost = xor_z(loss, 1)
+    terms = run_images((5, 6), xa, yp, cy, arow, si)
+    message, row, half = sds((MSG, N), BF16), sds((1, N), F32), sds((SH, N), F32)
+    up, down, pair = call(
+        first_step_kernel, [message, message, row], 1, [terms[3], terms[5], up, down, loss]
+    )
     cap = run_captions(xa, x4, cx, yp, brow, sj, up, down)
+    terms |= run_images((0, 1, 2, 3, 4), xa, yp, cy, arow, si, (up, down))
     up, down = shift_z(up, 1), shift_z(down, -1)
     got = [swap_core(cap[NY + k]) for k in range(NY)]
-    up, down, lost = together(up, down, lost)
-    up = (terms[2] + wide(up)).astype(BF16)
-    down = (terms[6] + wide(down)).astype(BF16)
-    (loss,) = add_after([[loss, lost]], (up, down))
-    lost = xor_z(loss, 2)
-    tup, tdown = add_after([[cap[2], got[2]], [cap[3], got[3]]], (up, down), BF16)
-    tup, tdown = shift_y(tup, 1), shift_y(tdown, -1)
-    up, down = shift_z(up, 1), shift_z(down, -1)
-    up, down, lost = together(up, down, lost)
-    up = (terms[1] + wide(up)).astype(BF16)
-    down = (terms[7] + wide(down)).astype(BF16)
-    (loss,) = add_after([[loss, lost]], (up, down))
-    lost = xor_z(loss, 4)
-    (tup,) = add_after([[cap[1], got[1], tup]], (up, down), BF16)
-    tup = shift_y(tup, 1)
-    up, down = shift_z(up, 1), shift_z(down, -1)
-    total = terms[0] + wide(up) + wide(down)
-    loss = loss + lost
-
-    high, low = split(loss)
-    rows = jnp.concatenate([high, low, jnp.zeros((6, N), F32)], axis=0)
-    away = wide(swap_xhi(jnp.concatenate([total[SH:], rows], axis=0).astype(BF16)))
-    image_grad = total[:SH] + away[:SH]
-    loss = (high + low) + (away[SH : SH + 1] + away[SH + 1 : SH + 2])
-    total = cap[0] + wide(got[0]) + wide(tup) + wide(tdown)
+    up, down, side1 = call(
+        functools.partial(step_kernel, 0), [message, message, row], 1, [terms[2], terms[6], up, down]
+    )
+    sends = add_after([[cap[k], got[k]] for k in (1, 2, 3)], (up, down), BF16)
+    up, down = shift_z(up, 1), shift_z(down, -1)
+    found = [shift_y(v, k) for k, v in zip((1, 2, -1), sends)]
+    up, down, side2 = call(
+        functools.partial(step_kernel, 1), [message, message, row], 1, [terms[1], terms[7], up, down]
+    )
+    up, down = shift_z(up, 1), shift_z(down, -1)
+    own, far, loss = call(
+        last_step_kernel,
+        [half, sds((SH, N), BF16), row],
+        1,
+        [terms[0], up, down, pair, side1, side2],
+    )
+    image_grad = own + wide(swap_xhi(far))
+    (total,) = add_after([[cap[0], got[0], *found]], ())
     text_grad = total[:SH] + wide(swap_xlo(total[SH:].astype(BF16)))
+    loss = loss + swap_xhi(loss)
     return (loss.reshape(N), image_grad, text_grad)
 
 

time: 118 us -> 105 us (0.89)
  waiting for transfers between devices: 46.3 us -> 33.1 us
    ppermute x3 -> x0, waiting for transfers between devices: 6.83 us -> none  [xor_z(): return lax.ppermute(v, 'col', col_pairs(lambda z, h: (z ^ b, h)))]
    ppermute x16, waiting for transfers between devices: 24.1 us -> 18.3 us  [shift_z(): return lax.ppermute(v, 'col', col_pairs(lambda z, h: ((z + d) % NZ, h)))]
    ppermute x3 -> x0, starting transfers between devices: 4.47 us -> none  [xor_z(): return lax.ppermute(v, 'col', col_pairs(lambda z, h: (z ^ b, h)))]
    ppermute x16, starting transfers between devices: 27.3 us -> 30.3 us  [shift_z(): return lax.ppermute(v, 'col', col_pairs(lambda z, h: ((z + d) % NZ, h)))]
    ppermute x2, waiting for transfers between devices: 2.1 us -> 0.6 us  [swap_xlo(): return lax.ppermute(v, 'row', row_pairs(lambda x, y, c: (1 - x, y, c)))]
    ppermute x2 -> x3, starting transfers between devices: 5.23 us -> 6.73 us  [swap_xhi(): return lax.ppermute(v, 'col', col_pairs(lambda z, h: (z, 1 - h)))]
    pallas_call x10 -> x12, Pallas kernels: 16 us -> 16.3 us  [call(): pl.pallas_call(kernel, out_shape=out_shape, in_specs=specs, out_specs=[vm...]
    ppermute x2 -> x3, waiting for transfers between devices: 6.99 us -> 6.99 us  [swap_xhi(): return lax.ppermute(v, 'col', col_pairs(lambda z, h: (z, 1 - h)))]
  transfers between devices with their start and end apart: 37 -> 35, of which waited for: 12 -> 14; matrix products, arithmetic and copies ran while one was open for 3% -> 3% of each run, Pallas kernels for 9% -> 11%
where the time goes in v6:
time: 105 us; the launch traced here: 104 us
  starting transfers between devices  48 us (46%)
  waiting for transfers between devices  33.1 us (32%)
  Pallas kernels  16.3 us (16%)
  between operations  2.14 us (2%)
  other arithmetic  2.1 us (2%)
  local copies, waits for them, and re-layouts  1.91 us (2%)
    ppermute x16, starting transfers between devices, shift_z(): return lax.ppermute(v, 'col', col_pairs(lambda z, h: ((z + d) % NZ, h)))  30.3 us
    ppermute x16, waiting for transfers between devices, shift_z(): return lax.ppermute(v, 'col', col_pairs(lambda z, h: ((z + d) % NZ, h)))  18.3 us
    pallas_call x12, Pallas kernels, call(): pl.pallas_call(kernel, out_shape=out_shape, in_specs=specs, out_specs=[vm...  16.3 us
    ppermute x6, starting transfers between devices, shift_y(): lax.ppermute(v, 'row', row_pairs(lambda x, y, c: (x, (y + d) % NY, c)))  7.3 us
    ppermute x3, waiting for transfers between devices, swap_xhi(): return lax.ppermute(v, 'col', col_pairs(lambda z, h: (z, 1 - h)))  6.99 us
    ppermute x6, waiting for transfers between devices, shift_y(): lax.ppermute(v, 'row', row_pairs(lambda x, y, c: (x, (y + d) % NY, c)))  6.93 us
    ppermute x3, starting transfers between devices, swap_xhi(): return lax.ppermute(v, 'col', col_pairs(lambda z, h: (z, 1 - h)))  6.73 us
    ppermute x2, starting transfers between devices, swap_xlo(): return lax.ppermute(v, 'row', row_pairs(lambda x, y, c: (1 - x, y, c)))  2.16 us
  transfers between devices with their start and end apart: 35, of which 14 were waited for; matrix products, arithmetic and copies ran while one was open for 3% of the time, Pallas kernels for 11%

profile of v6, /device:TPU:8, one launch (start us, length us, event | category | flops | bytes accessed | tf_op | source)
XLA Modules:
  0.0 103.5 jit_solution(6055763454471163739)
XLA Ops:
  0.6 3.1 %collective-permute-start = (bf16[72,1024]{1,0:T(8,128)(2,1)}, bf16[72,1024]{1,0:T(8,128)(2,1)S(1)}, u32[]{:S(2)}, u32[]{:S(2)}) collective-permute-start(bf16[72,1024]{1,0:T(8,128)(2,1)} %param.5), channel_id=1, source_target_pairs={{0,1},{1,0},{2,3},{3,2},{4,5},{5,4},{6,7},{7,6},{8,9},{9,8},{10,11... | collective-permute-start | bytes 442376 | tf_op jit(solution)/shard_map/ppermute | solution.py:47
  6.2 3.0 %collective-permute-done = bf16[72,1024]{1,0:T(8,128)(2,1)S(1)} collective-permute-done((bf16[72,1024]{1,0:T(8,128)(2,1)}, bf16[72,1024]{1,0:T(8,128)(2,1)S(1)}, u32[]{:S(2)}, u32[]{:S(2)}) %collective-permute-start) | collective-permute-done | bytes 147488 | tf_op jit(solution)/shard_map/ppermute | solution.py:47
  9.2 2.0 %collective-permute-start.2 = (bf16[144,1024]{1,0:T(8,128)(2,1)S(1)}, bf16[144,1024]{1,0:T(8,128)(2,1)S(1)}, u32[]{:S(2)}, u32[]{:S(2)}) collective-permute-start(bf16[144,1024]{1,0:T(8,128)(2,1)S(1)} %constant_dynamic-update-slice_fusion.refs_0_), channel_id=1, source_target_pairs={{0,2},{1,3},{2,4},{3,5},{4,6},{5,7},{6,8},{7,9},{8,10},{9,11},{10,... | collective-permute-start | bytes 884744 | tf_op jit(solution)/shard_map/ppermute | solution.py:39
  11.2 4.0 %collective-permute-start.1 = (bf16[144,1024]{1,0:T(8,128)(2,1)S(1)}, bf16[144,1024]{1,0:T(8,128)(2,1)S(1)}, u32[]{:S(2)}, u32[]{:S(2)}) collective-permute-start(bf16[144,1024]{1,0:T(8,128)(2,1)S(1)} %constant_dynamic-update-slice_fusion.refs_0_), channel_id=1, source_target_pairs={{0,14},{1,15},{2,0},{3,1},{4,2},{5,3},{6,4},{7,5},{8,6},{9,7},{10,... | collective-permute-start | bytes 884744 | tf_op jit(solution)/shard_map/ppermute | solution.py:39
  15.2 1.7 %collective-permute-start.10 = (bf16[144,1024]{1,0:T(8,128)(2,1)S(1)}, bf16[144,1024]{1,0:T(8,128)(2,1)S(1)}, u32[]{:S(2)}, u32[]{:S(2)}) collective-permute-start(bf16[144,1024]{1,0:T(8,128)(2,1)S(1)} %constant_dynamic-update-slice_fusion.2.refs_0_), channel_id=1, source_target_pairs={{0,32},{16,48},{32,64},{48,80},{64,96},{80,112},{96,0},{112,16},{1... | collective-permute-start | bytes 884744 | tf_op jit(solution)/shard_map/ppermute | solution.py:43
  16.9 3.2 %collective-permute-done.2.refs_4_ = bf16[144,1024]{1,0:T(8,128)(2,1)S(1)} collective-permute-done((bf16[144,1024]{1,0:T(8,128)(2,1)S(1)}, bf16[144,1024]{1,0:T(8,128)(2,1)S(1)}, u32[]{:S(2)}, u32[]{:S(2)}) %collective-permute-start.2) | collective-permute-done | bytes 294944 | tf_op jit(solution)/shard_map/ppermute | solution.py:39
  20.1 3.2 %collective-permute-start.4 = (bf16[144,1024]{1,0:T(8,128)(2,1)S(1)}, bf16[144,1024]{1,0:T(8,128)(2,1)S(1)}, u32[]{:S(2)}, u32[]{:S(2)}) collective-permute-start(bf16[144,1024]{1,0:T(8,128)(2,1)S(1)} %collective-permute-done.1.refs_1_), channel_id=1, source_target_pairs={{0,14},{1,15},{2,0},{3,1},{4,2},{5,3},{6,4},{7,5},{8,6},{9,7},{10,... | collective-permute-start | bytes 884744 | tf_op jit(solution)/shard_map/ppermute | solution.py:39
  23.8 1.6 %collective-permute-start.11 = (bf16[144,1024]{1,0:T(8,128)(2,1)S(1)}, bf16[144,1024]{1,0:T(8,128)(2,1)S(1)}, u32[]{:S(2)}, u32[]{:S(2)}) collective-permute-start(bf16[144,1024]{1,0:T(8,128)(2,1)S(1)} %collective-permute-done.10.refs_3_), channel_id=1, source_target_pairs={{0,32},{16,48},{32,64},{48,80},{64,96},{80,112},{96,0},{112,16},{1... | collective-permute-start | bytes 884744 | tf_op jit(solution)/shard_map/ppermute | solution.py:43
  25.4 2.7 %collective-permute-done.3.refs_3_ = bf16[144,1024]{1,0:T(8,128)(2,1)S(1)} collective-permute-done((bf16[144,1024]{1,0:T(8,128)(2,1)S(1)}, bf16[144,1024]{1,0:T(8,128)(2,1)S(1)}, u32[]{:S(2)}, u32[]{:S(2)}) %collective-permute-start.3) | collective-permute-done | bytes 294944 | tf_op jit(solution)/shard_map/ppermute | solution.py:39
  28.0 3.5 %collective-permute-start.7 = (bf16[144,1024]{1,0:T(8,128)(2,1)S(1)}, bf16[144,1024]{1,0:T(8,128)(2,1)S(1)}, u32[]{:S(2)}, u32[]{:S(2)}) collective-permute-start(bf16[144,1024]{1,0:T(8,128)(2,1)S(1)} %collective-permute-done.4.refs_2_), channel_id=1, source_target_pairs={{0,14},{1,15},{2,0},{3,1},{4,2},{5,3},{6,4},{7,5},{8,6},{9,7},{10,... | collective-permute-start | bytes 884744 | tf_op jit(solution)/shard_map/ppermute | solution.py:39
  33.5 2.3 %collective-permute-done.7.refs_5_ = bf16[144,1024]{1,0:T(8,128)(2,1)S(1)} collective-permute-done((bf16[144,1024]{1,0:T(8,128)(2,1)S(1)}, bf16[144,1024]{1,0:T(8,128)(2,1)S(1)}, u32[]{:S(2)}, u32[]{:S(2)}) %collective-permute-start.7) | collective-permute-done | bytes 294944 | tf_op jit(solution)/shard_map/ppermute | solution.py:39
  35.8 3.8 %collective-permute-start.16 = (bf16[144,512]{1,0:T(8,128)(2,1)S(1)}, bf16[144,512]{1,0:T(8,128)(2,1)S(1)}, u32[]{:S(2)}, u32[]{:S(2)}) collective-permute-start(bf16[144,512]{1,0:T(8,128)(2,1)S(1)} %slice.18), channel_id=1, source_target_pairs={{0,14},{1,15},{2,0},{3,1},{4,2},{5,3},{6,4},{7,5},{8,6},{9,7},{10,... | collective-permute-start | bytes 442376 | tf_op jit(solution)/shard_map/ppermute | solution.py:39
  39.9 1.8 %shard_map.76 = (bf16[1152,1024]{1,0:T(8,128)(2,1)S(1)}, bf16[1024,1152]{1,0:T(8,128)(2,1)S(1)}, f32[1,1024]{1,0:T(1,128)S(1)}, f32[1024,128]{1,0:T(8,128)S(1)}) custom-call(bf16[144,1024]{1,0:T(8,128)(2,1)S(1)} %constant_dynamic-update-slice_fusion.2.refs_0_, bf16[144,1024]{1,0:T(8,128)(2,1)S(1)} %collective-permute-done.9.refs_1_, ...), custom_call_target="tpu_custom_call" | custom-call | flops 67108864 | bytes 7606272 | tf_op jit(solution)/shard_map/pallas_call | solution.py:291
  41.7 2.3 %shard_map.77 = (bf16[1024,1024]{1,0:T(8,128)(2,1)S(1)}, f32[1024,1024]{1,0:T(8,128)S(1)}, f32[1,1024]{1,0:T(1,128)S(1)}) custom-call(bf16[144,1024]{1,0:T(8,128)(2,1)S(1)} %constant_dynamic-update-slice_fusion.refs_0_, bf16[144,1024]{1,0:T(8,128)(2,1)S(1)} %collective-permute-done.1.refs_1_, bf16[144,1024]{1,0:T(8,128)(2,1)S(1)} %collective-permute-done.4.refs_2_, ...), custom_call_target="tpu_custom_call" | custom-call | flops 2147483648 | bytes 10719232 | tf_op jit(solution)/shard_map/pallas_call | solution.py:291
  44.1 2.1 %collective-permute-done.15.left = bf16[144,512]{1,0:T(8,128)(2,1)S(1)} collective-permute-done((bf16[144,512]{1,0:T(8,128)(2,1)S(1)}, bf16[144,512]{1,0:T(8,128)(2,1)S(1)}, u32[]{:S(2)}, u32[]{:S(2)}) %collective-permute-start.15) | collective-permute-done | bytes 147488 | tf_op jit(solution)/shard_map/ppermute | solution.py:39
  46.2 5.3 %shard_map.78 = (bf16[144,1024]{1,0:T(8,128)(2,1)S(1)}, bf16[1024,1024]{1,0:T(8,128)(2,1)S(1)}, bf16[1024,1024]{1,0:T(8,128)(2,1)S(1)}, f32[1,1024]{1,0:T(1,128)...) custom-call(bf16[144,512]{1,0:T(8,128)(2,1)S(1)} %collective-permute, ...), custom_call_target="tpu_custom_call" | custom-call | flops 2415919104 | bytes 14573576 | tf_op jit(solution)/shard_map/pallas_call | solution.py:291
  51.6 3.2 %collective-permute-start.18 = (bf16[160,512]{1,0:T(8,128)(2,1)S(1)}, bf16[160,512]{1,0:T(8,128)(2,1)S(1)}, u32[]{:S(2)}, u32[]{:S(2)}) collective-permute-start(bf16[160,512]{1,0:T(8,128)(2,1)S(1)} %get-tuple-element.67), channel_id=1, source_target_pairs={{0,14},{1,15},{2,0},{3,1},{4,2},{5,3},{6,4},{7,5},{8,6},{9,7},{10,... | collective-permute-start | bytes 491528 | tf_op jit(solution)/shard_map/ppermute | solution.py:39
  55.6 3.4 %collective-permute-done.17.r_up = bf16[160,512]{1,0:T(8,128)(2,1)S(1)} collective-permute-done((bf16[160,512]{1,0:T(8,128)(2,1)S(1)}, bf16[160,512]{1,0:T(8,128)(2,1)S(1)}, u32[]{:S(2)}, u32[]{:S(2)}) %collective-permute-start.17) | collective-permute-done | bytes 163872 | tf_op jit(solution)/shard_map/ppermute | solution.py:39
  59.3 3.5 %collective-permute-start.20 = (bf16[160,1024]{1,0:T(8,128)(2,1)S(1)}, bf16[160,1024]{1,0:T(8,128)(2,1)S(1)}, u32[]{:S(2)}, u32[]{:S(2)}) collective-permute-start(bf16[160,1024]{1,0:T(8,128)(2,1)S(1)} %get-tuple-element.70.refs_1_._down), channel_id=1, source_target_pairs={{0,14},{1,15},{2,0},{3,1},{4,2},{5,3},{6,4},{7,5},{8,6},{9,7},{10,... | collective-permute-start | bytes 983048 | tf_op jit(solution)/shard_map/ppermute | solution.py:39
  62.8 3.4 %shard_map.85 = (f32[144,1024]{1,0:T(8,128)S(1)}, f32[144,1024]{1,0:T(8,128)S(1)}, f32[144,1024]{1,0:T(8,128)S(1)}, f32[144,1024]{1,0:T(8,128)S(1)}, bf16[144,10...) custom-call(bf16[1024,1024]{1,0:T(8,128)(2,1)S(1)} %get-tuple-elemen, ...), custom_call_target="tpu_custom_call" | custom-call | flops 2415919104 | bytes 11051008 | tf_op jit(solution)/shard_map/pallas_call | solution.py:291
  66.5 1.7 %shard_map.81 = (f32[144,1024]{1,0:T(8,128)S(1)}, f32[144,1024]{1,0:T(8,128)S(1)}, f32[144,1024]{1,0:T(8,128)S(1)}, f32[144,1024]{1,0:T(8,128)S(1)}, f32[144,1024]{1,0:T(8,128)S(1)}) custom-call(bf16[1024,1024]{1,0:T(8,128)(2,1)S(1)} %get-tuple-element.56.xa, bf16[1152,1024]{1,0:T(8,128)(2,1)S(1)} %get-tuple-element.57.yp, ...), custom_call_target="tpu_custom_call" | custom-call | flops 1509949440 | bytes 10166272 | tf_op jit(solution)/shard_map/pallas_call | solution.py:291
  68.4 2.1 %collective-permute-start.21 = (bf16[160,1024]{1,0:T(8,128)(2,1)S(1)}, bf16[160,1024]{1,0:T(8,128)(2,1)S(1)}, u32[]{:S(2)}, u32[]{:S(2)}) collective-permute-start(bf16[160,1024]{1,0:T(8,128)(2,1)S(1)} %get-tuple-element.76.refs_6_), channel_id=1, source_target_pairs={{0,2},{1,3},{2,4},{3,5},{4,6},{5,7},{6,8},{7,9},{8,10},{9,11},{10,... | collective-permute-start | bytes 983048 | tf_op jit(solution)/shard_map/ppermute | solution.py:39
  72.8 2.0 %collective-permute-start.31 = (bf16[144,1024]{1,0:T(8,128)(2,1)S(1)}, bf16[144,1024]{1,0:T(8,128)(2,1)S(1)}, u32[]{:S(2)}, u32[]{:S(2)}) collective-permute-start(bf16[144,1024]{1,0:T(8,128)(2,1)S(1)} %get-tuple-element.98), channel_id=1, source_target_pairs={{0,32},{16,48},{32,64},{48,80},{64,96},{80,112},{96,0},{112,16},{1... | collective-permute-start | bytes 884744 | tf_op jit(solution)/shard_map/ppermute | solution.py:43
  76.1 3.7 %collective-permute-done.21.r_up = bf16[160,1024]{1,0:T(8,128)(2,1)S(1)} collective-permute-done((bf16[160,1024]{1,0:T(8,128)(2,1)S(1)}, bf16[160,1024]{1,0:T(8,128)(2,1)S(1)}, u32[]{:S(2)}, u32[]{:S(2)}) %collective-permute-start.21) | collective-permute-done | bytes 327712 | tf_op jit(solution)/shard_map/ppermute | solution.py:39
  81.1 1.8 %collective-permute-start.23 = (bf16[160,1024]{1,0:T(8,128)(2,1)S(1)}, bf16[160,1024]{1,0:T(8,128)(2,1)S(1)}, u32[]{:S(2)}, u32[]{:S(2)}) collective-permute-start(bf16[160,1024]{1,0:T(8,128)(2,1)S(1)} %get-tuple-element.78), channel_id=1, source_target_pairs={{0,2},{1,3},{2,4},{3,5},{4,6},{5,7},{6,8},{7,9},{8,10},{9,11},{10,... | collective-permute-start | bytes 983048 | tf_op jit(solution)/shard_map/ppermute | solution.py:39
  82.9 1.5 %collective-permute-start.24 = (bf16[160,1024]{1,0:T(8,128)(2,1)S(1)}, bf16[160,1024]{1,0:T(8,128)(2,1)S(1)}, u32[]{:S(2)}, u32[]{:S(2)}) collective-permute-start(bf16[160,1024]{1,0:T(8,128)(2,1)S(1)} %get-tuple-element.79), channel_id=1, source_target_pairs={{0,14},{1,15},{2,0},{3,1},{4,2},{5,3},{6,4},{7,5},{8,6},{9,7},{10,... | collective-permute-start | bytes 983048 | tf_op jit(solution)/shard_map/ppermute | solution.py:39
  84.4 3.3 %collective-permute-done.31.refs_2_ = bf16[144,1024]{1,0:T(8,128)(2,1)S(1)} collective-permute-done((bf16[144,1024]{1,0:T(8,128)(2,1)S(1)}, bf16[144,1024]{1,0:T(8,128)(2,1)S(1)}, u32[]{:S(2)}, u32[]{:S(2)}) %collective-permute-start.31) | collective-permute-done | bytes 294944 | tf_op jit(solution)/shard_map/ppermute | solution.py:43
  87.7 3.7 %collective-permute-done.33.refs_4_ = bf16[144,1024]{1,0:T(8,128)(2,1)S(1)} collective-permute-done((bf16[144,1024]{1,0:T(8,128)(2,1)S(1)}, bf16[144,1024]{1,0:T(8,128)(2,1)S(1)}, u32[]{:S(2)}, u32[]{:S(2)}) %collective-permute-start.33) | collective-permute-done | bytes 294944 | tf_op jit(solution)/shard_map/ppermute | solution.py:43
  91.5 1.6 %collective-permute-start.34 = (bf16[72,1024]{1,0:T(8,128)(2,1)S(1)}, bf16[72,1024]{1,0:T(8,128)(2,1)S(1)}, u32[]{:S(2)}, u32[]{:S(2)}) collective-permute-start(bf16[72,1024]{1,0:T(8,128)(2,1)S(1)} %slice.23), channel_id=1, source_target_pairs={{0,128},{16,144},{32,160},{48,176},{64,192},{80,208},{96,224},{112... | collective-permute-start | bytes 442376 | tf_op jit(solution)/shard_map/ppermute | solution.py:51
  93.2 2.8 %collective-permute-start.25 = (f32[1,1024]{1,0:T(1,128)S(1)}, f32[1,1024]{1,0:T(1,128)S(1)}, u32[]{:S(2)}, u32[]{:S(2)}) collective-permute-start(f32[1,1024]{1,0:T(1,128)S(1)} %get-tuple-element.83), channel_id=1, source_target_pairs={{0,1},{1,0},{2,3},{3,2},{4,5},{5,4},{6,7},{7,6},{8,9},{9,8},{10,11... | collective-permute-start | bytes 12296 | tf_op jit(solution)/shard_map/ppermute | solution.py:47
  98.2 1.4 %collective-permute-done.25 = f32[1,1024]{1,0:T(1,128)S(1)} collective-permute-done((f32[1,1024]{1,0:T(1,128)S(1)}, f32[1,1024]{1,0:T(1,128)S(1)}, u32[]{:S(2)}, u32[]{:S(2)}) %collective-permute-start.25) | collective-permute-done | bytes 4128 | tf_op jit(solution)/shard_map/ppermute | solution.py:47
  100.2 2.6 %collective-permute-done.26 = bf16[72,1024]{1,0:T(8,128)(2,1)S(1)} collective-permute-done((bf16[72,1024]{1,0:T(8,128)(2,1)S(1)}, bf16[72,1024]{1,0:T(8,128)(2,1)S(1)}, u32[]{:S(2)}, u32[]{:S(2)}) %collective-permute-start.26) | collective-permute-done | bytes 147488 | tf_op jit(solution)/shard_map/ppermute | solution.py:47
  (62 shorter events, 14.1 us)
Async XLA Ops:
  0.6 8.5 %collective-permute-start = (bf16[72,1024]{1,0:T(8,128)(2,1)}, bf16[72,1024]{1,0:T(8,128)(2,1)S(1)}, u32[]{:S(2)}, u32[]{:S(2)}) collective-permute-start(bf16[72,1024]{1,0:T(8,128)(2,1)} %param.5), channel_id=1, source_target_pairs={{0,1},{1,0},{2,3},{3,2},{4,5},{5,4},{6,7},{7,6},{8,9},{9,8},{10,11... | collective-permute-start | bytes 442376 | tf_op jit(solution)/shard_map/ppermute | solution.py:47
  3.7 11.5 %collective-permute-start.5 = (bf16[72,1024]{1,0:T(8,128)(2,1)}, bf16[72,1024]{1,0:T(8,128)(2,1)S(1)}, u32[]{:S(2)}, u32[]{:S(2)}) collective-permute-start(bf16[72,1024]{1,0:T(8,128)(2,1)} %param.6), channel_id=1, source_target_pairs={{0,128},{16,144},{32,160},{48,176},{64,192},{80,208},{96,224},{112... | collective-permute-start | bytes 442376 | tf_op jit(solution)/shard_map/ppermute | solution.py:51
  9.2 10.9 %collective-permute-start.2 = (bf16[144,1024]{1,0:T(8,128)(2,1)S(1)}, bf16[144,1024]{1,0:T(8,128)(2,1)S(1)}, u32[]{:S(2)}, u32[]{:S(2)}) collective-permute-start(bf16[144,1024]{1,0:T(8,128)(2,1)S(1)} %constant_dynamic-update-slice_fusion.refs_0_), channel_id=1, source_target_pairs={{0,2},{1,3},{2,4},{3,5},{4,6},{5,7},{6,8},{7,9},{8,10},{9,11},{10,... | collective-permute-start | bytes 884744 | tf_op jit(solution)/shard_map/ppermute | solution.py:39
  11.2 8.9 %collective-permute-start.1 = (bf16[144,1024]{1,0:T(8,128)(2,1)S(1)}, bf16[144,1024]{1,0:T(8,128)(2,1)S(1)}, u32[]{:S(2)}, u32[]{:S(2)}) collective-permute-start(bf16[144,1024]{1,0:T(8,128)(2,1)S(1)} %constant_dynamic-update-slice_fusion.refs_0_), channel_id=1, source_target_pairs={{0,14},{1,15},{2,0},{3,1},{4,2},{5,3},{6,4},{7,5},{8,6},{9,7},{10,... | collective-permute-start | bytes 884744 | tf_op jit(solution)/shard_map/ppermute | solution.py:39
  15.2 8.6 %collective-permute-start.10 = (bf16[144,1024]{1,0:T(8,128)(2,1)S(1)}, bf16[144,1024]{1,0:T(8,128)(2,1)S(1)}, u32[]{:S(2)}, u32[]{:S(2)}) collective-permute-start(bf16[144,1024]{1,0:T(8,128)(2,1)S(1)} %constant_dynamic-update-slice_fusion.2.refs_0_), channel_id=1, source_target_pairs={{0,32},{16,48},{32,64},{48,80},{64,96},{80,112},{96,0},{112,16},{1... | collective-permute-start | bytes 884744 | tf_op jit(solution)/shard_map/ppermute | solution.py:43
  16.9 8.5 %collective-permute-start.6 = (bf16[144,1024]{1,0:T(8,128)(2,1)S(1)}, bf16[144,1024]{1,0:T(8,128)(2,1)S(1)}, u32[]{:S(2)}, u32[]{:S(2)}) collective-permute-start(bf16[144,1024]{1,0:T(8,128)(2,1)S(1)} %constant_dynamic-update-slice_fusion.2.refs_0_), channel_id=1, source_target_pairs={{0,16},{16,0},{32,48},{48,32},{64,80},{80,64},{96,112},{112,96},{1... | collective-permute-start | bytes 884744 | tf_op jit(solution)/shard_map/ppermute | solution.py:55
  20.1 7.9 %collective-permute-start.3 = (bf16[144,1024]{1,0:T(8,128)(2,1)S(1)}, bf16[144,1024]{1,0:T(8,128)(2,1)S(1)}, u32[]{:S(2)}, u32[]{:S(2)}) collective-permute-start(bf16[144,1024]{1,0:T(8,128)(2,1)S(1)} %collective-permute-done.2.refs_4_), channel_id=1, source_target_pairs={{0,2},{1,3},{2,4},{3,5},{4,6},{5,7},{6,8},{7,9},{8,10},{9,11},{10,... | collective-permute-start | bytes 884744 | tf_op jit(solution)/shard_map/ppermute | solution.py:39
  20.1 7.9 %collective-permute-start.4 = (bf16[144,1024]{1,0:T(8,128)(2,1)S(1)}, bf16[144,1024]{1,0:T(8,128)(2,1)S(1)}, u32[]{:S(2)}, u32[]{:S(2)}) collective-permute-start(bf16[144,1024]{1,0:T(8,128)(2,1)S(1)} %collective-permute-done.1.refs_1_), channel_id=1, source_target_pairs={{0,14},{1,15},{2,0},{3,1},{4,2},{5,3},{6,4},{7,5},{8,6},{9,7},{10,... | collective-permute-start | bytes 884744 | tf_op jit(solution)/shard_map/ppermute | solution.py:39
  23.3 8.2 %collective-permute-start.9 = (bf16[144,1024]{1,0:T(8,128)(2,1)S(1)}, bf16[144,1024]{1,0:T(8,128)(2,1)S(1)}, u32[]{:S(2)}, u32[]{:S(2)}) collective-permute-start(bf16[144,1024]{1,0:T(8,128)(2,1)S(1)} %constant_dynamic-update-slice_fusion.2.refs_0_), channel_id=1, source_target_pairs={{0,96},{16,112},{32,0},{48,16},{64,32},{80,48},{96,64},{112,80},{1... | collective-permute-start | bytes 884744 | tf_op jit(solution)/shard_map/ppermute | solution.py:43
  23.8 8.3 %collective-permute-start.11 = (bf16[144,1024]{1,0:T(8,128)(2,1)S(1)}, bf16[144,1024]{1,0:T(8,128)(2,1)S(1)}, u32[]{:S(2)}, u32[]{:S(2)}) collective-permute-start(bf16[144,1024]{1,0:T(8,128)(2,1)S(1)} %collective-permute-done.10.refs_3_), channel_id=1, source_target_pairs={{0,32},{16,48},{32,64},{48,80},{64,96},{80,112},{96,0},{112,16},{1... | collective-permute-start | bytes 884744 | tf_op jit(solution)/shard_map/ppermute | solution.py:43
  28.0 7.7 %collective-permute-start.7 = (bf16[144,1024]{1,0:T(8,128)(2,1)S(1)}, bf16[144,1024]{1,0:T(8,128)(2,1)S(1)}, u32[]{:S(2)}, u32[]{:S(2)}) collective-permute-start(bf16[144,1024]{1,0:T(8,128)(2,1)S(1)} %collective-permute-done.4.refs_2_), channel_id=1, source_target_pairs={{0,14},{1,15},{2,0},{3,1},{4,2},{5,3},{6,4},{7,5},{8,6},{9,7},{10,... | collective-permute-start | bytes 884744 | tf_op jit(solution)/shard_map/ppermute | solution.py:39
  31.5 8.0 %collective-permute-start.8 = (bf16[144,1024]{1,0:T(8,128)(2,1)S(1)}, bf16[144,1024]{1,0:T(8,128)(2,1)S(1)}, u32[]{:S(2)}, u32[]{:S(2)}) collective-permute-start(bf16[144,1024]{1,0:T(8,128)(2,1)S(1)} %collective-permute-done.3.refs_3_), channel_id=1, source_target_pairs={{0,2},{1,3},{2,4},{3,5},{4,6},{5,7},{6,8},{7,9},{8,10},{9,11},{10,... | collective-permute-start | bytes 884744 | tf_op jit(solution)/shard_map/ppermute | solution.py:39
  31.5 8.3 %collective-permute-start.14 = (bf16[144,1024]{1,0:T(8,128)(2,1)S(1)}, bf16[144,1024]{1,0:T(8,128)(2,1)S(1)}, u32[]{:S(2)}, u32[]{:S(2)}) collective-permute-start(bf16[144,1024]{1,0:T(8,128)(2,1)S(1)} %collective-permute-done.10.refs_3_), channel_id=1, source_target_pairs={{0,16},{16,0},{32,48},{48,32},{64,80},{80,64},{96,112},{112,96},{1... | collective-permute-start | bytes 884744 | tf_op jit(solution)/shard_map/ppermute | solution.py:55
  31.6 8.3 %collective-permute-start.12 = (bf16[144,1024]{1,0:T(8,128)(2,1)S(1)}, bf16[144,1024]{1,0:T(8,128)(2,1)S(1)}, u32[]{:S(2)}, u32[]{:S(2)}) collective-permute-start(bf16[144,1024]{1,0:T(8,128)(2,1)S(1)} %collective-permute-done.9.refs_1_), channel_id=1, source_target_pairs={{0,16},{16,0},{32,48},{48,32},{64,80},{80,64},{96,112},{112,96},{1... | collective-permute-start | bytes 884744 | tf_op jit(solution)/shard_map/ppermute | solution.py:55
  32.1 7.8 %collective-permute-start.13 = (bf16[144,1024]{1,0:T(8,128)(2,1)S(1)}, bf16[144,1024]{1,0:T(8,128)(2,1)S(1)}, u32[]{:S(2)}, u32[]{:S(2)}) collective-permute-start(bf16[144,1024]{1,0:T(8,128)(2,1)S(1)} %collective-permute-done.11.refs_2_), channel_id=1, source_target_pairs={{0,16},{16,0},{32,48},{48,32},{64,80},{80,64},{96,112},{112,96},{1... | collective-permute-start | bytes 884744 | tf_op jit(solution)/shard_map/ppermute | solution.py:55
  35.8 8.3 %collective-permute-start.16 = (bf16[144,512]{1,0:T(8,128)(2,1)S(1)}, bf16[144,512]{1,0:T(8,128)(2,1)S(1)}, u32[]{:S(2)}, u32[]{:S(2)}) collective-permute-start(bf16[144,512]{1,0:T(8,128)(2,1)S(1)} %slice.18), channel_id=1, source_target_pairs={{0,14},{1,15},{2,0},{3,1},{4,2},{5,3},{6,4},{7,5},{8,6},{9,7},{10,... | collective-permute-start | bytes 442376 | tf_op jit(solution)/shard_map/ppermute | solution.py:39
  39.6 6.6 %collective-permute-start.15 = (bf16[144,512]{1,0:T(8,128)(2,1)S(1)}, bf16[144,512]{1,0:T(8,128)(2,1)S(1)}, u32[]{:S(2)}, u32[]{:S(2)}) collective-permute-start(bf16[144,512]{1,0:T(8,128)(2,1)S(1)} %slice.17), channel_id=1, source_target_pairs={{0,2},{1,3},{2,4},{3,5},{4,6},{5,7},{6,8},{7,9},{8,10},{9,11},{10,... | collective-permute-start | bytes 442376 | tf_op jit(solution)/shard_map/ppermute | solution.py:39
  51.5 7.5 %collective-permute-start.17 = (bf16[160,512]{1,0:T(8,128)(2,1)S(1)}, bf16[160,512]{1,0:T(8,128)(2,1)S(1)}, u32[]{:S(2)}, u32[]{:S(2)}) collective-permute-start(bf16[160,512]{1,0:T(8,128)(2,1)S(1)} %get-tuple-element.66), channel_id=1, source_target_pairs={{0,2},{1,3},{2,4},{3,5},{4,6},{5,7},{6,8},{7,9},{8,10},{9,11},{10,... | collective-permute-start | bytes 491528 | tf_op jit(solution)/shard_map/ppermute | solution.py:39
  51.6 7.4 %collective-permute-start.18 = (bf16[160,512]{1,0:T(8,128)(2,1)S(1)}, bf16[160,512]{1,0:T(8,128)(2,1)S(1)}, u32[]{:S(2)}, u32[]{:S(2)}) collective-permute-start(bf16[160,512]{1,0:T(8,128)(2,1)S(1)} %get-tuple-element.67), channel_id=1, source_target_pairs={{0,14},{1,15},{2,0},{3,1},{4,2},{5,3},{6,4},{7,5},{8,6},{9,7},{10,... | collective-permute-start | bytes 491528 | tf_op jit(solution)/shard_map/ppermute | solution.py:39
  59.2 9.1 %collective-permute-start.19 = (bf16[160,1024]{1,0:T(8,128)(2,1)S(1)}, bf16[160,1024]{1,0:T(8,128)(2,1)S(1)}, u32[]{:S(2)}, u32[]{:S(2)}) collective-permute-start(bf16[160,1024]{1,0:T(8,128)(2,1)S(1)} %get-tuple-element.69.refs_0_._up), channel_id=1, source_target_pairs={{0,2},{1,3},{2,4},{3,5},{4,6},{5,7},{6,8},{7,9},{8,10},{9,11},{10,... | collective-permute-start | bytes 983048 | tf_op jit(solution)/shard_map/ppermute | solution.py:39
  59.3 9.0 %collective-permute-start.20 = (bf16[160,1024]{1,0:T(8,128)(2,1)S(1)}, bf16[160,1024]{1,0:T(8,128)(2,1)S(1)}, u32[]{:S(2)}, u32[]{:S(2)}) collective-permute-start(bf16[160,1024]{1,0:T(8,128)(2,1)S(1)} %get-tuple-element.70.refs_1_._down), channel_id=1, source_target_pairs={{0,14},{1,15},{2,0},{3,1},{4,2},{5,3},{6,4},{7,5},{8,6},{9,7},{10,... | collective-permute-start | bytes 983048 | tf_op jit(solution)/shard_map/ppermute | solution.py:39
  66.2 6.1 %collective-permute-start.28 = (bf16[144,1024]{1,0:T(8,128)(2,1)S(1)}, bf16[144,1024]{1,0:T(8,128)(2,1)S(1)}, u32[]{:S(2)}, u32[]{:S(2)}) collective-permute-start(bf16[144,1024]{1,0:T(8,128)(2,1)S(1)} %get-tuple-element.93), channel_id=1, source_target_pairs={{0,16},{16,0},{32,48},{48,32},{64,80},{80,64},{96,112},{112,96},{1... | collective-permute-start | bytes 884744 | tf_op jit(solution)/shard_map/ppermute | solution.py:55
  68.4 11.4 %collective-permute-start.21 = (bf16[160,1024]{1,0:T(8,128)(2,1)S(1)}, bf16[160,1024]{1,0:T(8,128)(2,1)S(1)}, u32[]{:S(2)}, u32[]{:S(2)}) collective-permute-start(bf16[160,1024]{1,0:T(8,128)(2,1)S(1)} %get-tuple-element.76.refs_6_), channel_id=1, source_target_pairs={{0,2},{1,3},{2,4},{3,5},{4,6},{5,7},{6,8},{7,9},{8,10},{9,11},{10,... | collective-permute-start | bytes 983048 | tf_op jit(solution)/shard_map/ppermute | solution.py:39
  71.1 9.9 %collective-permute-start.22 = (bf16[160,1024]{1,0:T(8,128)(2,1)S(1)}, bf16[160,1024]{1,0:T(8,128)(2,1)S(1)}, u32[]{:S(2)}, u32[]{:S(2)}) collective-permute-start(bf16[160,1024]{1,0:T(8,128)(2,1)S(1)} %get-tuple-element.77.refs_7_), channel_id=1, source_target_pairs={{0,14},{1,15},{2,0},{3,1},{4,2},{5,3},{6,4},{7,5},{8,6},{9,7},{10,... | collective-permute-start | bytes 983048 | tf_op jit(solution)/shard_map/ppermute | solution.py:39
  72.2 10.7 %collective-permute-start.27 = (bf16[144,1024]{1,0:T(8,128)(2,1)S(1)}, bf16[144,1024]{1,0:T(8,128)(2,1)S(1)}, u32[]{:S(2)}, u32[]{:S(2)}) collective-permute-start(bf16[144,1024]{1,0:T(8,128)(2,1)S(1)} %get-tuple-element.91), channel_id=1, source_target_pairs={{0,16},{16,0},{32,48},{48,32},{64,80},{80,64},{96,112},{112,96},{1... | collective-permute-start | bytes 884744 | tf_op jit(solution)/shard_map/ppermute | solution.py:55
  72.8 14.9 %collective-permute-start.31 = (bf16[144,1024]{1,0:T(8,128)(2,1)S(1)}, bf16[144,1024]{1,0:T(8,128)(2,1)S(1)}, u32[]{:S(2)}, u32[]{:S(2)}) collective-permute-start(bf16[144,1024]{1,0:T(8,128)(2,1)S(1)} %get-tuple-element.98), channel_id=1, source_target_pairs={{0,32},{16,48},{32,64},{48,80},{64,96},{80,112},{96,0},{112,16},{1... | collective-permute-start | bytes 884744 | tf_op jit(solution)/shard_map/ppermute | solution.py:43
  74.7 12.9 %collective-permute-start.32 = (bf16[144,1024]{1,0:T(8,128)(2,1)S(1)}, bf16[144,1024]{1,0:T(8,128)(2,1)S(1)}, u32[]{:S(2)}, u32[]{:S(2)}) collective-permute-start(bf16[144,1024]{1,0:T(8,128)(2,1)S(1)} %get-tuple-element.99), channel_id=1, source_target_pairs={{0,64},{16,80},{32,96},{48,112},{64,0},{80,16},{96,32},{112,48},{1... | collective-permute-start | bytes 884744 | tf_op jit(solution)/shard_map/ppermute | solution.py:43
  79.8 11.5 %collective-permute-start.33 = (bf16[144,1024]{1,0:T(8,128)(2,1)S(1)}, bf16[144,1024]{1,0:T(8,128)(2,1)S(1)}, u32[]{:S(2)}, u32[]{:S(2)}) collective-permute-start(bf16[144,1024]{1,0:T(8,128)(2,1)S(1)} %get-tuple-element.100), channel_id=1, source_target_pairs={{0,96},{16,112},{32,0},{48,16},{64,32},{80,48},{96,64},{112,80},{1... | collective-permute-start | bytes 884744 | tf_op jit(solution)/shard_map/ppermute | solution.py:43
  81.1 12.0 %collective-permute-start.23 = (bf16[160,1024]{1,0:T(8,128)(2,1)S(1)}, bf16[160,1024]{1,0:T(8,128)(2,1)S(1)}, u32[]{:S(2)}, u32[]{:S(2)}) collective-permute-start(bf16[160,1024]{1,0:T(8,128)(2,1)S(1)} %get-tuple-element.78), channel_id=1, source_target_pairs={{0,2},{1,3},{2,4},{3,5},{4,6},{5,7},{6,8},{7,9},{8,10},{9,11},{10,... | collective-permute-start | bytes 983048 | tf_op jit(solution)/shard_map/ppermute | solution.py:39
  82.9 10.2 %collective-permute-start.24 = (bf16[160,1024]{1,0:T(8,128)(2,1)S(1)}, bf16[160,1024]{1,0:T(8,128)(2,1)S(1)}, u32[]{:S(2)}, u32[]{:S(2)}) collective-permute-start(bf16[160,1024]{1,0:T(8,128)(2,1)S(1)} %get-tuple-element.79), channel_id=1, source_target_pairs={{0,14},{1,15},{2,0},{3,1},{4,2},{5,3},{6,4},{7,5},{8,6},{9,7},{10,... | collective-permute-start | bytes 983048 | tf_op jit(solution)/shard_map/ppermute | solution.py:39
  93.2 6.4 %collective-permute-start.25 = (f32[1,1024]{1,0:T(1,128)S(1)}, f32[1,1024]{1,0:T(1,128)S(1)}, u32[]{:S(2)}, u32[]{:S(2)}) collective-permute-start(f32[1,1024]{1,0:T(1,128)S(1)} %get-tuple-element.83), channel_id=1, source_target_pairs={{0,1},{1,0},{2,3},{3,2},{4,5},{5,4},{6,7},{7,6},{8,9},{9,8},{10,11... | collective-permute-start | bytes 12296 | tf_op jit(solution)/shard_map/ppermute | solution.py:47
  96.0 6.8 %collective-permute-start.26 = (bf16[72,1024]{1,0:T(8,128)(2,1)S(1)}, bf16[72,1024]{1,0:T(8,128)(2,1)S(1)}, u32[]{:S(2)}, u32[]{:S(2)}) collective-permute-start(bf16[72,1024]{1,0:T(8,128)(2,1)S(1)} %get-tuple-element.85), channel_id=1, source_target_pairs={{0,1},{1,0},{2,3},{3,2},{4,5},{5,4},{6,7},{7,6},{8,9},{9,8},{10,11... | collective-permute-start | bytes 442376 | tf_op jit(solution)/shard_map/ppermute | solution.py:47
  (4 other events, 14.1 us)

commit v7 on v6

--- a/solution.py
+++ b/solution.py
@@ -150,7 +150,7 @@
     return decode(jnp.where(z % 2 == parity, up[BL:, :HALF].astype(F32), down[BL:, :HALF].astype(F32)))
 
 
-def first_step_kernel(t_up, t_down, r_up, r_down, loss, m_up, m_down, pair):
+def first_step_kernel(t_up, t_down, r_up, r_down, loss, _cap, m_up, m_down, pair):
     m_up[:BL, :HALF] = (t_up[:, :HALF] + r_up[:BL, :].astype(F32)).astype(BF16)
     m_up[:BL, HALF:] = t_up[:, HALF:].astype(BF16)
     m_down[:BL, :HALF] = t_down[:, :HALF].astype(BF16)
@@ -253,7 +253,7 @@
             out[:, cols] = a * (pull[i * BL - low : (i + 1) * BL - low] - u * s)
 
 
-def caption_kernel(xa, x4, cx, yp, brow, sj, _up, _down, *refs):
+def caption_kernel(xa, x4, cx, yp, brow, sj, *refs):
     own, away = refs[:4], refs[4:8]
     t_ref = refs[8]
     xlo, y, core, z, xhi = coords()
@@ -353,14 +353,13 @@
     return {ORDER[i]: v for i, v in zip(places, found)}
 
 
-def run_captions(xa, x4, cx, yp, brow, sj, up, down):
+def run_captions(xa, x4, cx, yp, brow, sj):
     return call(
         caption_kernel,
         [sds((BL, N), F32)] * NY + [sds((BL, N), BF16)] * NY,
         2 * N * N * ROWS,
-        [xa, x4, cx, yp, brow, sj, up, down],
+        [xa, x4, cx, yp, brow, sj],
         [pltpu.VMEM((ROWS, N), F32)],
-        unread=(6, 7),
     )
 
 
@@ -419,11 +418,15 @@
     )
     up, down = shift_z(up, 1), shift_z(down, -1)
     terms = run_images((5, 6), xa, yp, cy, arow, si)
+    cap = run_captions(xa, x4, cx, yp, brow, sj)
     message, row, half = sds((MSG, N), BF16), sds((1, N), F32), sds((SH, N), F32)
     up, down, pair = call(
-        first_step_kernel, [message, message, row], 1, [terms[3], terms[5], up, down, loss]
-    )
-    cap = run_captions(xa, x4, cx, yp, brow, sj, up, down)
+        first_step_kernel,
+        [message, message, row],
+        1,
+        [terms[3], terms[5], up, down, loss, cap[NY]],
+        unread=(5,),
+    )
     terms |= run_images((0, 1, 2, 3, 4), xa, yp, cy, arow, si, (up, down))
     up, down = shift_z(up, 1), shift_z(down, -1)
     got = [swap_core(cap[NY + k]) for k in range(NY)]

time: 105 us -> 103 us (0.981)
  waiting for transfers between devices: 33.1 us -> 31.5 us
  transfers between devices with their start and end apart: 35 -> 35, of which waited for: 14 -> 12; matrix products, arithmetic and copies ran while one was open for 3% -> 3% of each run, Pallas kernels for 11% -> 11%
where the time goes in v7:
time: 103 us; the launch traced here: 102 us
  starting transfers between devices  48.1 us (47%)
  waiting for transfers between devices  31.5 us (31%)
  Pallas kernels  16.3 us (16%)
  between operations  2.15 us (2%)
  other arithmetic  2.1 us (2%)
  local copies, waits for them, and re-layouts  1.91 us (2%)
    ppermute x16, starting transfers between devices, shift_z(): return lax.ppermute(v, 'col', col_pairs(lambda z, h: ((z + d) % NZ, h)))  30.1 us
    ppermute x16, waiting for transfers between devices, shift_z(): return lax.ppermute(v, 'col', col_pairs(lambda z, h: ((z + d) % NZ, h)))  17.3 us
    pallas_call x12, Pallas kernels, call(): pl.pallas_call(kernel, out_shape=out_shape, in_specs=specs, out_specs=[vm...  16.3 us
    ppermute x6, starting transfers between devices, shift_y(): lax.ppermute(v, 'row', row_pairs(lambda x, y, c: (x, (y + d) % NY, c)))  7.99 us
    ppermute x3, waiting for transfers between devices, swap_xhi(): return lax.ppermute(v, 'col', col_pairs(lambda z, h: (z, 1 - h)))  7.48 us
    ppermute x3, starting transfers between devices, swap_xhi(): return lax.ppermute(v, 'col', col_pairs(lambda z, h: (z, 1 - h)))  6.73 us
    ppermute x6, waiting for transfers between devices, shift_y(): lax.ppermute(v, 'row', row_pairs(lambda x, y, c: (x, (y + d) % NY, c)))  6.69 us
    ppermute x2, starting transfers between devices, swap_xlo(): return lax.ppermute(v, 'row', row_pairs(lambda x, y, c: (1 - x, y, c)))  2.15 us
  transfers between devices with their start and end apart: 35, of which 12 were waited for; matrix products, arithmetic and copies ran while one was open for 3% of the time, Pallas kernels for 11%

profile of v7, /device:TPU:8, one launch (start us, length us, event | category | flops | bytes accessed | tf_op | source)
XLA Modules:
  0.0 102.0 jit_solution(16720373250325294714)
XLA Ops:
  0.6 3.1 %collective-permute-start = (bf16[72,1024]{1,0:T(8,128)(2,1)}, bf16[72,1024]{1,0:T(8,128)(2,1)S(1)}, u32[]{:S(2)}, u32[]{:S(2)}) collective-permute-start(bf16[72,1024]{1,0:T(8,128)(2,1)} %param.5), channel_id=1, source_target_pairs={{0,1},{1,0},{2,3},{3,2},{4,5},{5,4},{6,7},{7,6},{8,9},{9,8},{10,11... | collective-permute-start | bytes 442376 | tf_op jit(solution)/shard_map/ppermute | solution.py:47
  6.2 3.0 %collective-permute-done = bf16[72,1024]{1,0:T(8,128)(2,1)S(1)} collective-permute-done((bf16[72,1024]{1,0:T(8,128)(2,1)}, bf16[72,1024]{1,0:T(8,128)(2,1)S(1)}, u32[]{:S(2)}, u32[]{:S(2)}) %collective-permute-start) | collective-permute-done | bytes 147488 | tf_op jit(solution)/shard_map/ppermute | solution.py:47
  9.2 2.0 %collective-permute-start.2 = (bf16[144,1024]{1,0:T(8,128)(2,1)S(1)}, bf16[144,1024]{1,0:T(8,128)(2,1)S(1)}, u32[]{:S(2)}, u32[]{:S(2)}) collective-permute-start(bf16[144,1024]{1,0:T(8,128)(2,1)S(1)} %constant_dynamic-update-slice_fusion.refs_0_), channel_id=1, source_target_pairs={{0,2},{1,3},{2,4},{3,5},{4,6},{5,7},{6,8},{7,9},{8,10},{9,11},{10,... | collective-permute-start | bytes 884744 | tf_op jit(solution)/shard_map/ppermute | solution.py:39
  11.2 4.0 %collective-permute-start.1 = (bf16[144,1024]{1,0:T(8,128)(2,1)S(1)}, bf16[144,1024]{1,0:T(8,128)(2,1)S(1)}, u32[]{:S(2)}, u32[]{:S(2)}) collective-permute-start(bf16[144,1024]{1,0:T(8,128)(2,1)S(1)} %constant_dynamic-update-slice_fusion.refs_0_), channel_id=1, source_target_pairs={{0,14},{1,15},{2,0},{3,1},{4,2},{5,3},{6,4},{7,5},{8,6},{9,7},{10,... | collective-permute-start | bytes 884744 | tf_op jit(solution)/shard_map/ppermute | solution.py:39
  15.2 1.7 %collective-permute-start.10 = (bf16[144,1024]{1,0:T(8,128)(2,1)S(1)}, bf16[144,1024]{1,0:T(8,128)(2,1)S(1)}, u32[]{:S(2)}, u32[]{:S(2)}) collective-permute-start(bf16[144,1024]{1,0:T(8,128)(2,1)S(1)} %constant_dynamic-update-slice_fusion.2.refs_0_), channel_id=1, source_target_pairs={{0,32},{16,48},{32,64},{48,80},{64,96},{80,112},{96,0},{112,16},{1... | collective-permute-start | bytes 884744 | tf_op jit(solution)/shard_map/ppermute | solution.py:43
  16.9 3.2 %collective-permute-done.2.refs_4_ = bf16[144,1024]{1,0:T(8,128)(2,1)S(1)} collective-permute-done((bf16[144,1024]{1,0:T(8,128)(2,1)S(1)}, bf16[144,1024]{1,0:T(8,128)(2,1)S(1)}, u32[]{:S(2)}, u32[]{:S(2)}) %collective-permute-start.2) | collective-permute-done | bytes 294944 | tf_op jit(solution)/shard_map/ppermute | solution.py:39
  20.1 3.2 %collective-permute-start.4 = (bf16[144,1024]{1,0:T(8,128)(2,1)S(1)}, bf16[144,1024]{1,0:T(8,128)(2,1)S(1)}, u32[]{:S(2)}, u32[]{:S(2)}) collective-permute-start(bf16[144,1024]{1,0:T(8,128)(2,1)S(1)} %collective-permute-done.1.refs_1_), channel_id=1, source_target_pairs={{0,14},{1,15},{2,0},{3,1},{4,2},{5,3},{6,4},{7,5},{8,6},{9,7},{10,... | collective-permute-start | bytes 884744 | tf_op jit(solution)/shard_map/ppermute | solution.py:39
  23.8 1.6 %collective-permute-start.11 = (bf16[144,1024]{1,0:T(8,128)(2,1)S(1)}, bf16[144,1024]{1,0:T(8,128)(2,1)S(1)}, u32[]{:S(2)}, u32[]{:S(2)}) collective-permute-start(bf16[144,1024]{1,0:T(8,128)(2,1)S(1)} %collective-permute-done.10.refs_3_), channel_id=1, source_target_pairs={{0,32},{16,48},{32,64},{48,80},{64,96},{80,112},{96,0},{112,16},{1... | collective-permute-start | bytes 884744 | tf_op jit(solution)/shard_map/ppermute | solution.py:43
  25.4 2.7 %collective-permute-done.3.refs_3_ = bf16[144,1024]{1,0:T(8,128)(2,1)S(1)} collective-permute-done((bf16[144,1024]{1,0:T(8,128)(2,1)S(1)}, bf16[144,1024]{1,0:T(8,128)(2,1)S(1)}, u32[]{:S(2)}, u32[]{:S(2)}) %collective-permute-start.3) | collective-permute-done | bytes 294944 | tf_op jit(solution)/shard_map/ppermute | solution.py:39
  28.0 3.5 %collective-permute-start.7 = (bf16[144,1024]{1,0:T(8,128)(2,1)S(1)}, bf16[144,1024]{1,0:T(8,128)(2,1)S(1)}, u32[]{:S(2)}, u32[]{:S(2)}) collective-permute-start(bf16[144,1024]{1,0:T(8,128)(2,1)S(1)} %collective-permute-done.4.refs_2_), channel_id=1, source_target_pairs={{0,14},{1,15},{2,0},{3,1},{4,2},{5,3},{6,4},{7,5},{8,6},{9,7},{10,... | collective-permute-start | bytes 884744 | tf_op jit(solution)/shard_map/ppermute | solution.py:39
  33.5 2.3 %collective-permute-done.7.refs_5_ = bf16[144,1024]{1,0:T(8,128)(2,1)S(1)} collective-permute-done((bf16[144,1024]{1,0:T(8,128)(2,1)S(1)}, bf16[144,1024]{1,0:T(8,128)(2,1)S(1)}, u32[]{:S(2)}, u32[]{:S(2)}) %collective-permute-start.7) | collective-permute-done | bytes 294944 | tf_op jit(solution)/shard_map/ppermute | solution.py:39
  35.8 3.8 %collective-permute-start.16 = (bf16[144,512]{1,0:T(8,128)(2,1)S(1)}, bf16[144,512]{1,0:T(8,128)(2,1)S(1)}, u32[]{:S(2)}, u32[]{:S(2)}) collective-permute-start(bf16[144,512]{1,0:T(8,128)(2,1)S(1)} %slice.18), channel_id=1, source_target_pairs={{0,14},{1,15},{2,0},{3,1},{4,2},{5,3},{6,4},{7,5},{8,6},{9,7},{10,... | collective-permute-start | bytes 442376 | tf_op jit(solution)/shard_map/ppermute | solution.py:39
  39.9 1.8 %shard_map.76 = (bf16[1152,1024]{1,0:T(8,128)(2,1)S(1)}, bf16[1024,1152]{1,0:T(8,128)(2,1)S(1)}, f32[1,1024]{1,0:T(1,128)S(1)}, f32[1024,128]{1,0:T(8,128)S(1)}) custom-call(bf16[144,1024]{1,0:T(8,128)(2,1)S(1)} %constant_dynamic-update-slice_fusion.2.refs_0_, bf16[144,1024]{1,0:T(8,128)(2,1)S(1)} %collective-permute-done.9.refs_1_, ...), custom_call_target="tpu_custom_call" | custom-call | flops 67108864 | bytes 7606272 | tf_op jit(solution)/shard_map/pallas_call | solution.py:291
  41.7 2.3 %shard_map.77 = (bf16[1024,1024]{1,0:T(8,128)(2,1)S(1)}, f32[1024,1024]{1,0:T(8,128)S(1)}, f32[1,1024]{1,0:T(1,128)S(1)}) custom-call(bf16[144,1024]{1,0:T(8,128)(2,1)S(1)} %constant_dynamic-update-slice_fusion.refs_0_, bf16[144,1024]{1,0:T(8,128)(2,1)S(1)} %collective-permute-done.1.refs_1_, bf16[144,1024]{1,0:T(8,128)(2,1)S(1)} %collective-permute-done.4.refs_2_, ...), custom_call_target="tpu_custom_call" | custom-call | flops 2147483648 | bytes 10719232 | tf_op jit(solution)/shard_map/pallas_call | solution.py:291
  44.1 2.1 %collective-permute-done.15.left = bf16[144,512]{1,0:T(8,128)(2,1)S(1)} collective-permute-done((bf16[144,512]{1,0:T(8,128)(2,1)S(1)}, bf16[144,512]{1,0:T(8,128)(2,1)S(1)}, u32[]{:S(2)}, u32[]{:S(2)}) %collective-permute-start.15) | collective-permute-done | bytes 147488 | tf_op jit(solution)/shard_map/ppermute | solution.py:39
  46.2 5.3 %shard_map.78 = (bf16[144,1024]{1,0:T(8,128)(2,1)S(1)}, bf16[1024,1024]{1,0:T(8,128)(2,1)S(1)}, bf16[1024,1024]{1,0:T(8,128)(2,1)S(1)}, f32[1,1024]{1,0:T(1,128)...) custom-call(bf16[144,512]{1,0:T(8,128)(2,1)S(1)} %collective-permute, ...), custom_call_target="tpu_custom_call" | custom-call | flops 2415919104 | bytes 14573576 | tf_op jit(solution)/shard_map/pallas_call | solution.py:291
  51.6 3.2 %collective-permute-start.18 = (bf16[160,512]{1,0:T(8,128)(2,1)S(1)}, bf16[160,512]{1,0:T(8,128)(2,1)S(1)}, u32[]{:S(2)}, u32[]{:S(2)}) collective-permute-start(bf16[160,512]{1,0:T(8,128)(2,1)S(1)} %get-tuple-element.67), channel_id=1, source_target_pairs={{0,14},{1,15},{2,0},{3,1},{4,2},{5,3},{6,4},{7,5},{8,6},{9,7},{10,... | collective-permute-start | bytes 491528 | tf_op jit(solution)/shard_map/ppermute | solution.py:39
  55.6 3.4 %shard_map.80 = (f32[144,1024]{1,0:T(8,128)S(1)}, f32[144,1024]{1,0:T(8,128)S(1)}, f32[144,1024]{1,0:T(8,128)S(1)}, f32[144,1024]{1,0:T(8,128)S(1)}, bf16[144,10...) custom-call(bf16[1024,1024]{1,0:T(8,128)(2,1)S(1)} %get-tuple-elemen, ...), custom_call_target="tpu_custom_call" | custom-call | flops 2415919104 | bytes 10395648 | tf_op jit(solution)/shard_map/pallas_call | solution.py:291
  59.3 3.2 %collective-permute-start.20 = (bf16[160,1024]{1,0:T(8,128)(2,1)S(1)}, bf16[160,1024]{1,0:T(8,128)(2,1)S(1)}, u32[]{:S(2)}, u32[]{:S(2)}) collective-permute-start(bf16[160,1024]{1,0:T(8,128)(2,1)S(1)} %get-tuple-element.75.refs_1_), channel_id=1, source_target_pairs={{0,14},{1,15},{2,0},{3,1},{4,2},{5,3},{6,4},{7,5},{8,6},{9,7},{10,... | collective-permute-start | bytes 983048 | tf_op jit(solution)/shard_map/ppermute | solution.py:39
  62.5 1.7 %shard_map.82 = (f32[144,1024]{1,0:T(8,128)S(1)}, f32[144,1024]{1,0:T(8,128)S(1)}, f32[144,1024]{1,0:T(8,128)S(1)}, f32[144,1024]{1,0:T(8,128)S(1)}, f32[144,1024]{1,0:T(8,128)S(1)}) custom-call(bf16[1024,1024]{1,0:T(8,128)(2,1)S(1)} %get-tuple-element.56.xa, bf16[1152,1024]{1,0:T(8,128)(2,1)S(1)} %get-tuple-element.57.yp, ...), custom_call_target="tpu_custom_call" | custom-call | flops 1509949440 | bytes 10166272 | tf_op jit(solution)/shard_map/pallas_call | solution.py:291
  64.3 3.3 %collective-permute-done.19.r_up = bf16[160,1024]{1,0:T(8,128)(2,1)S(1)} collective-permute-done((bf16[160,1024]{1,0:T(8,128)(2,1)S(1)}, bf16[160,1024]{1,0:T(8,128)(2,1)S(1)}, u32[]{:S(2)}, u32[]{:S(2)}) %collective-permute-start.19) | collective-permute-done | bytes 327712 | tf_op jit(solution)/shard_map/ppermute | solution.py:39
  67.7 1.7 %collective-permute-start.21 = (bf16[160,1024]{1,0:T(8,128)(2,1)S(1)}, bf16[160,1024]{1,0:T(8,128)(2,1)S(1)}, u32[]{:S(2)}, u32[]{:S(2)}) collective-permute-start(bf16[160,1024]{1,0:T(8,128)(2,1)S(1)} %get-tuple-element.81.refs_6_), channel_id=1, source_target_pairs={{0,2},{1,3},{2,4},{3,5},{4,6},{5,7},{6,8},{7,9},{8,10},{9,11},{10,... | collective-permute-start | bytes 983048 | tf_op jit(solution)/shard_map/ppermute | solution.py:39
  69.9 1.8 %collective-permute-start.22 = (bf16[160,1024]{1,0:T(8,128)(2,1)S(1)}, bf16[160,1024]{1,0:T(8,128)(2,1)S(1)}, u32[]{:S(2)}, u32[]{:S(2)}) collective-permute-start(bf16[160,1024]{1,0:T(8,128)(2,1)S(1)} %get-tuple-element.82.refs_7_), channel_id=1, source_target_pairs={{0,14},{1,15},{2,0},{3,1},{4,2},{5,3},{6,4},{7,5},{8,6},{9,7},{10,... | collective-permute-start | bytes 983048 | tf_op jit(solution)/shard_map/ppermute | solution.py:39
  71.8 1.8 %collective-permute-start.31 = (bf16[144,1024]{1,0:T(8,128)(2,1)S(1)}, bf16[144,1024]{1,0:T(8,128)(2,1)S(1)}, u32[]{:S(2)}, u32[]{:S(2)}) collective-permute-start(bf16[144,1024]{1,0:T(8,128)(2,1)S(1)} %get-tuple-element.98), channel_id=1, source_target_pairs={{0,32},{16,48},{32,64},{48,80},{64,96},{80,112},{96,0},{112,16},{1... | collective-permute-start | bytes 884744 | tf_op jit(solution)/shard_map/ppermute | solution.py:43
  77.4 2.4 %collective-permute-done.22.r_down = bf16[160,1024]{1,0:T(8,128)(2,1)S(1)} collective-permute-done((bf16[160,1024]{1,0:T(8,128)(2,1)S(1)}, bf16[160,1024]{1,0:T(8,128)(2,1)S(1)}, u32[]{:S(2)}, u32[]{:S(2)}) %collective-permute-start.22) | collective-permute-done | bytes 327712 | tf_op jit(solution)/shard_map/ppermute | solution.py:39
  79.9 2.3 %collective-permute-start.23 = (bf16[160,1024]{1,0:T(8,128)(2,1)S(1)}, bf16[160,1024]{1,0:T(8,128)(2,1)S(1)}, u32[]{:S(2)}, u32[]{:S(2)}) collective-permute-start(bf16[160,1024]{1,0:T(8,128)(2,1)S(1)} %get-tuple-element.83), channel_id=1, source_target_pairs={{0,2},{1,3},{2,4},{3,5},{4,6},{5,7},{6,8},{7,9},{8,10},{9,11},{10,... | collective-permute-start | bytes 983048 | tf_op jit(solution)/shard_map/ppermute | solution.py:39
  83.2 1.8 %collective-permute-done.32.refs_3_ = bf16[144,1024]{1,0:T(8,128)(2,1)S(1)} collective-permute-done((bf16[144,1024]{1,0:T(8,128)(2,1)S(1)}, bf16[144,1024]{1,0:T(8,128)(2,1)S(1)}, u32[]{:S(2)}, u32[]{:S(2)}) %collective-permute-start.32) | collective-permute-done | bytes 294944 | tf_op jit(solution)/shard_map/ppermute | solution.py:43
  85.0 4.9 %collective-permute-done.33.refs_4_ = bf16[144,1024]{1,0:T(8,128)(2,1)S(1)} collective-permute-done((bf16[144,1024]{1,0:T(8,128)(2,1)S(1)}, bf16[144,1024]{1,0:T(8,128)(2,1)S(1)}, u32[]{:S(2)}, u32[]{:S(2)}) %collective-permute-start.33) | collective-permute-done | bytes 294944 | tf_op jit(solution)/shard_map/ppermute | solution.py:43
  90.1 1.6 %collective-permute-start.34 = (bf16[72,1024]{1,0:T(8,128)(2,1)S(1)}, bf16[72,1024]{1,0:T(8,128)(2,1)S(1)}, u32[]{:S(2)}, u32[]{:S(2)}) collective-permute-start(bf16[72,1024]{1,0:T(8,128)(2,1)S(1)} %slice.23), channel_id=1, source_target_pairs={{0,128},{16,144},{32,160},{48,176},{64,192},{80,208},{96,224},{112... | collective-permute-start | bytes 442376 | tf_op jit(solution)/shard_map/ppermute | solution.py:51
  91.8 2.8 %collective-permute-start.25 = (f32[1,1024]{1,0:T(1,128)S(1)}, f32[1,1024]{1,0:T(1,128)S(1)}, u32[]{:S(2)}, u32[]{:S(2)}) collective-permute-start(f32[1,1024]{1,0:T(1,128)S(1)} %get-tuple-element.88), channel_id=1, source_target_pairs={{0,1},{1,0},{2,3},{3,2},{4,5},{5,4},{6,7},{7,6},{8,9},{9,8},{10,11... | collective-permute-start | bytes 12296 | tf_op jit(solution)/shard_map/ppermute | solution.py:47
  96.2 1.4 %collective-permute-done.25 = f32[1,1024]{1,0:T(1,128)S(1)} collective-permute-done((f32[1,1024]{1,0:T(1,128)S(1)}, f32[1,1024]{1,0:T(1,128)S(1)}, u32[]{:S(2)}, u32[]{:S(2)}) %collective-permute-start.25) | collective-permute-done | bytes 4128 | tf_op jit(solution)/shard_map/ppermute | solution.py:47
  98.2 3.1 %collective-permute-done.26 = bf16[72,1024]{1,0:T(8,128)(2,1)S(1)} collective-permute-done((bf16[72,1024]{1,0:T(8,128)(2,1)S(1)}, bf16[72,1024]{1,0:T(8,128)(2,1)S(1)}, u32[]{:S(2)}, u32[]{:S(2)}) %collective-permute-start.26) | collective-permute-done | bytes 147488 | tf_op jit(solution)/shard_map/ppermute | solution.py:47
  (62 shorter events, 13.9 us)
Async XLA Ops:
  0.6 8.5 %collective-permute-start = (bf16[72,1024]{1,0:T(8,128)(2,1)}, bf16[72,1024]{1,0:T(8,128)(2,1)S(1)}, u32[]{:S(2)}, u32[]{:S(2)}) collective-permute-start(bf16[72,1024]{1,0:T(8,128)(2,1)} %param.5), channel_id=1, source_target_pairs={{0,1},{1,0},{2,3},{3,2},{4,5},{5,4},{6,7},{7,6},{8,9},{9,8},{10,11... | collective-permute-start | bytes 442376 | tf_op jit(solution)/shard_map/ppermute | solution.py:47
  3.7 11.5 %collective-permute-start.5 = (bf16[72,1024]{1,0:T(8,128)(2,1)}, bf16[72,1024]{1,0:T(8,128)(2,1)S(1)}, u32[]{:S(2)}, u32[]{:S(2)}) collective-permute-start(bf16[72,1024]{1,0:T(8,128)(2,1)} %param.6), channel_id=1, source_target_pairs={{0,128},{16,144},{32,160},{48,176},{64,192},{80,208},{96,224},{112... | collective-permute-start | bytes 442376 | tf_op jit(solution)/shard_map/ppermute | solution.py:51
  9.2 10.9 %collective-permute-start.2 = (bf16[144,1024]{1,0:T(8,128)(2,1)S(1)}, bf16[144,1024]{1,0:T(8,128)(2,1)S(1)}, u32[]{:S(2)}, u32[]{:S(2)}) collective-permute-start(bf16[144,1024]{1,0:T(8,128)(2,1)S(1)} %constant_dynamic-update-slice_fusion.refs_0_), channel_id=1, source_target_pairs={{0,2},{1,3},{2,4},{3,5},{4,6},{5,7},{6,8},{7,9},{8,10},{9,11},{10,... | collective-permute-start | bytes 884744 | tf_op jit(solution)/shard_map/ppermute | solution.py:39
  11.2 8.9 %collective-permute-start.1 = (bf16[144,1024]{1,0:T(8,128)(2,1)S(1)}, bf16[144,1024]{1,0:T(8,128)(2,1)S(1)}, u32[]{:S(2)}, u32[]{:S(2)}) collective-permute-start(bf16[144,1024]{1,0:T(8,128)(2,1)S(1)} %constant_dynamic-update-slice_fusion.refs_0_), channel_id=1, source_target_pairs={{0,14},{1,15},{2,0},{3,1},{4,2},{5,3},{6,4},{7,5},{8,6},{9,7},{10,... | collective-permute-start | bytes 884744 | tf_op jit(solution)/shard_map/ppermute | solution.py:39
  15.2 8.6 %collective-permute-start.10 = (bf16[144,1024]{1,0:T(8,128)(2,1)S(1)}, bf16[144,1024]{1,0:T(8,128)(2,1)S(1)}, u32[]{:S(2)}, u32[]{:S(2)}) collective-permute-start(bf16[144,1024]{1,0:T(8,128)(2,1)S(1)} %constant_dynamic-update-slice_fusion.2.refs_0_), channel_id=1, source_target_pairs={{0,32},{16,48},{32,64},{48,80},{64,96},{80,112},{96,0},{112,16},{1... | collective-permute-start | bytes 884744 | tf_op jit(solution)/shard_map/ppermute | solution.py:43
  16.9 8.5 %collective-permute-start.6 = (bf16[144,1024]{1,0:T(8,128)(2,1)S(1)}, bf16[144,1024]{1,0:T(8,128)(2,1)S(1)}, u32[]{:S(2)}, u32[]{:S(2)}) collective-permute-start(bf16[144,1024]{1,0:T(8,128)(2,1)S(1)} %constant_dynamic-update-slice_fusion.2.refs_0_), channel_id=1, source_target_pairs={{0,16},{16,0},{32,48},{48,32},{64,80},{80,64},{96,112},{112,96},{1... | collective-permute-start | bytes 884744 | tf_op jit(solution)/shard_map/ppermute | solution.py:55
  20.1 7.9 %collective-permute-start.3 = (bf16[144,1024]{1,0:T(8,128)(2,1)S(1)}, bf16[144,1024]{1,0:T(8,128)(2,1)S(1)}, u32[]{:S(2)}, u32[]{:S(2)}) collective-permute-start(bf16[144,1024]{1,0:T(8,128)(2,1)S(1)} %collective-permute-done.2.refs_4_), channel_id=1, source_target_pairs={{0,2},{1,3},{2,4},{3,5},{4,6},{5,7},{6,8},{7,9},{8,10},{9,11},{10,... | collective-permute-start | bytes 884744 | tf_op jit(solution)/shard_map/ppermute | solution.py:39
  20.1 7.9 %collective-permute-start.4 = (bf16[144,1024]{1,0:T(8,128)(2,1)S(1)}, bf16[144,1024]{1,0:T(8,128)(2,1)S(1)}, u32[]{:S(2)}, u32[]{:S(2)}) collective-permute-start(bf16[144,1024]{1,0:T(8,128)(2,1)S(1)} %collective-permute-done.1.refs_1_), channel_id=1, source_target_pairs={{0,14},{1,15},{2,0},{3,1},{4,2},{5,3},{6,4},{7,5},{8,6},{9,7},{10,... | collective-permute-start | bytes 884744 | tf_op jit(solution)/shard_map/ppermute | solution.py:39
  23.3 8.2 %collective-permute-start.9 = (bf16[144,1024]{1,0:T(8,128)(2,1)S(1)}, bf16[144,1024]{1,0:T(8,128)(2,1)S(1)}, u32[]{:S(2)}, u32[]{:S(2)}) collective-permute-start(bf16[144,1024]{1,0:T(8,128)(2,1)S(1)} %constant_dynamic-update-slice_fusion.2.refs_0_), channel_id=1, source_target_pairs={{0,96},{16,112},{32,0},{48,16},{64,32},{80,48},{96,64},{112,80},{1... | collective-permute-start | bytes 884744 | tf_op jit(solution)/shard_map/ppermute | solution.py:43
  23.8 8.3 %collective-permute-start.11 = (bf16[144,1024]{1,0:T(8,128)(2,1)S(1)}, bf16[144,1024]{1,0:T(8,128)(2,1)S(1)}, u32[]{:S(2)}, u32[]{:S(2)}) collective-permute-start(bf16[144,1024]{1,0:T(8,128)(2,1)S(1)} %collective-permute-done.10.refs_3_), channel_id=1, source_target_pairs={{0,32},{16,48},{32,64},{48,80},{64,96},{80,112},{96,0},{112,16},{1... | collective-permute-start | bytes 884744 | tf_op jit(solution)/shard_map/ppermute | solution.py:43
  28.0 7.7 %collective-permute-start.7 = (bf16[144,1024]{1,0:T(8,128)(2,1)S(1)}, bf16[144,1024]{1,0:T(8,128)(2,1)S(1)}, u32[]{:S(2)}, u32[]{:S(2)}) collective-permute-start(bf16[144,1024]{1,0:T(8,128)(2,1)S(1)} %collective-permute-done.4.refs_2_), channel_id=1, source_target_pairs={{0,14},{1,15},{2,0},{3,1},{4,2},{5,3},{6,4},{7,5},{8,6},{9,7},{10,... | collective-permute-start | bytes 884744 | tf_op jit(solution)/shard_map/ppermute | solution.py:39
  31.5 8.0 %collective-permute-start.8 = (bf16[144,1024]{1,0:T(8,128)(2,1)S(1)}, bf16[144,1024]{1,0:T(8,128)(2,1)S(1)}, u32[]{:S(2)}, u32[]{:S(2)}) collective-permute-start(bf16[144,1024]{1,0:T(8,128)(2,1)S(1)} %collective-permute-done.3.refs_3_), channel_id=1, source_target_pairs={{0,2},{1,3},{2,4},{3,5},{4,6},{5,7},{6,8},{7,9},{8,10},{9,11},{10,... | collective-permute-start | bytes 884744 | tf_op jit(solution)/shard_map/ppermute | solution.py:39
  31.5 8.3 %collective-permute-start.14 = (bf16[144,1024]{1,0:T(8,128)(2,1)S(1)}, bf16[144,1024]{1,0:T(8,128)(2,1)S(1)}, u32[]{:S(2)}, u32[]{:S(2)}) collective-permute-start(bf16[144,1024]{1,0:T(8,128)(2,1)S(1)} %collective-permute-done.10.refs_3_), channel_id=1, source_target_pairs={{0,16},{16,0},{32,48},{48,32},{64,80},{80,64},{96,112},{112,96},{1... | collective-permute-start | bytes 884744 | tf_op jit(solution)/shard_map/ppermute | solution.py:55
  31.6 8.3 %collective-permute-start.12 = (bf16[144,1024]{1,0:T(8,128)(2,1)S(1)}, bf16[144,1024]{1,0:T(8,128)(2,1)S(1)}, u32[]{:S(2)}, u32[]{:S(2)}) collective-permute-start(bf16[144,1024]{1,0:T(8,128)(2,1)S(1)} %collective-permute-done.9.refs_1_), channel_id=1, source_target_pairs={{0,16},{16,0},{32,48},{48,32},{64,80},{80,64},{96,112},{112,96},{1... | collective-permute-start | bytes 884744 | tf_op jit(solution)/shard_map/ppermute | solution.py:55
  32.1 7.8 %collective-permute-start.13 = (bf16[144,1024]{1,0:T(8,128)(2,1)S(1)}, bf16[144,1024]{1,0:T(8,128)(2,1)S(1)}, u32[]{:S(2)}, u32[]{:S(2)}) collective-permute-start(bf16[144,1024]{1,0:T(8,128)(2,1)S(1)} %collective-permute-done.11.refs_2_), channel_id=1, source_target_pairs={{0,16},{16,0},{32,48},{48,32},{64,80},{80,64},{96,112},{112,96},{1... | collective-permute-start | bytes 884744 | tf_op jit(solution)/shard_map/ppermute | solution.py:55
  35.8 8.3 %collective-permute-start.16 = (bf16[144,512]{1,0:T(8,128)(2,1)S(1)}, bf16[144,512]{1,0:T(8,128)(2,1)S(1)}, u32[]{:S(2)}, u32[]{:S(2)}) collective-permute-start(bf16[144,512]{1,0:T(8,128)(2,1)S(1)} %slice.18), channel_id=1, source_target_pairs={{0,14},{1,15},{2,0},{3,1},{4,2},{5,3},{6,4},{7,5},{8,6},{9,7},{10,... | collective-permute-start | bytes 442376 | tf_op jit(solution)/shard_map/ppermute | solution.py:39
  39.6 6.6 %collective-permute-start.15 = (bf16[144,512]{1,0:T(8,128)(2,1)S(1)}, bf16[144,512]{1,0:T(8,128)(2,1)S(1)}, u32[]{:S(2)}, u32[]{:S(2)}) collective-permute-start(bf16[144,512]{1,0:T(8,128)(2,1)S(1)} %slice.17), channel_id=1, source_target_pairs={{0,2},{1,3},{2,4},{3,5},{4,6},{5,7},{6,8},{7,9},{8,10},{9,11},{10,... | collective-permute-start | bytes 442376 | tf_op jit(solution)/shard_map/ppermute | solution.py:39
  51.5 7.6 %collective-permute-start.17 = (bf16[160,512]{1,0:T(8,128)(2,1)S(1)}, bf16[160,512]{1,0:T(8,128)(2,1)S(1)}, u32[]{:S(2)}, u32[]{:S(2)}) collective-permute-start(bf16[160,512]{1,0:T(8,128)(2,1)S(1)} %get-tuple-element.66), channel_id=1, source_target_pairs={{0,2},{1,3},{2,4},{3,5},{4,6},{5,7},{6,8},{7,9},{8,10},{9,11},{10,... | collective-permute-start | bytes 491528 | tf_op jit(solution)/shard_map/ppermute | solution.py:39
  51.6 7.5 %collective-permute-start.18 = (bf16[160,512]{1,0:T(8,128)(2,1)S(1)}, bf16[160,512]{1,0:T(8,128)(2,1)S(1)}, u32[]{:S(2)}, u32[]{:S(2)}) collective-permute-start(bf16[160,512]{1,0:T(8,128)(2,1)S(1)} %get-tuple-element.67), channel_id=1, source_target_pairs={{0,14},{1,15},{2,0},{3,1},{4,2},{5,3},{6,4},{7,5},{8,6},{9,7},{10,... | collective-permute-start | bytes 491528 | tf_op jit(solution)/shard_map/ppermute | solution.py:39
  59.2 8.4 %collective-permute-start.19 = (bf16[160,1024]{1,0:T(8,128)(2,1)S(1)}, bf16[160,1024]{1,0:T(8,128)(2,1)S(1)}, u32[]{:S(2)}, u32[]{:S(2)}) collective-permute-start(bf16[160,1024]{1,0:T(8,128)(2,1)S(1)} %get-tuple-element.74.refs_0_), channel_id=1, source_target_pairs={{0,2},{1,3},{2,4},{3,5},{4,6},{5,7},{6,8},{7,9},{8,10},{9,11},{10,... | collective-permute-start | bytes 983048 | tf_op jit(solution)/shard_map/ppermute | solution.py:39
  59.3 8.3 %collective-permute-start.20 = (bf16[160,1024]{1,0:T(8,128)(2,1)S(1)}, bf16[160,1024]{1,0:T(8,128)(2,1)S(1)}, u32[]{:S(2)}, u32[]{:S(2)}) collective-permute-start(bf16[160,1024]{1,0:T(8,128)(2,1)S(1)} %get-tuple-element.75.refs_1_), channel_id=1, source_target_pairs={{0,14},{1,15},{2,0},{3,1},{4,2},{5,3},{6,4},{7,5},{8,6},{9,7},{10,... | collective-permute-start | bytes 983048 | tf_op jit(solution)/shard_map/ppermute | solution.py:39
  62.5 9.1 %collective-permute-start.28 = (bf16[144,1024]{1,0:T(8,128)(2,1)S(1)}, bf16[144,1024]{1,0:T(8,128)(2,1)S(1)}, u32[]{:S(2)}, u32[]{:S(2)}) collective-permute-start(bf16[144,1024]{1,0:T(8,128)(2,1)S(1)} %get-tuple-element.93), channel_id=1, source_target_pairs={{0,16},{16,0},{32,48},{48,32},{64,80},{80,64},{96,112},{112,96},{1... | collective-permute-start | bytes 884744 | tf_op jit(solution)/shard_map/ppermute | solution.py:55
  67.7 8.4 %collective-permute-start.21 = (bf16[160,1024]{1,0:T(8,128)(2,1)S(1)}, bf16[160,1024]{1,0:T(8,128)(2,1)S(1)}, u32[]{:S(2)}, u32[]{:S(2)}) collective-permute-start(bf16[160,1024]{1,0:T(8,128)(2,1)S(1)} %get-tuple-element.81.refs_6_), channel_id=1, source_target_pairs={{0,2},{1,3},{2,4},{3,5},{4,6},{5,7},{6,8},{7,9},{8,10},{9,11},{10,... | collective-permute-start | bytes 983048 | tf_op jit(solution)/shard_map/ppermute | solution.py:39
  69.9 9.9 %collective-permute-start.22 = (bf16[160,1024]{1,0:T(8,128)(2,1)S(1)}, bf16[160,1024]{1,0:T(8,128)(2,1)S(1)}, u32[]{:S(2)}, u32[]{:S(2)}) collective-permute-start(bf16[160,1024]{1,0:T(8,128)(2,1)S(1)} %get-tuple-element.82.refs_7_), channel_id=1, source_target_pairs={{0,14},{1,15},{2,0},{3,1},{4,2},{5,3},{6,4},{7,5},{8,6},{9,7},{10,... | collective-permute-start | bytes 983048 | tf_op jit(solution)/shard_map/ppermute | solution.py:39
  71.6 10.6 %collective-permute-start.27 = (bf16[144,1024]{1,0:T(8,128)(2,1)S(1)}, bf16[144,1024]{1,0:T(8,128)(2,1)S(1)}, u32[]{:S(2)}, u32[]{:S(2)}) collective-permute-start(bf16[144,1024]{1,0:T(8,128)(2,1)S(1)} %get-tuple-element.73._cap), channel_id=1, source_target_pairs={{0,16},{16,0},{32,48},{48,32},{64,80},{80,64},{96,112},{112,96},{1... | collective-permute-start | bytes 884744 | tf_op jit(solution)/shard_map/ppermute | solution.py:55
  71.8 11.4 %collective-permute-start.31 = (bf16[144,1024]{1,0:T(8,128)(2,1)S(1)}, bf16[144,1024]{1,0:T(8,128)(2,1)S(1)}, u32[]{:S(2)}, u32[]{:S(2)}) collective-permute-start(bf16[144,1024]{1,0:T(8,128)(2,1)S(1)} %get-tuple-element.98), channel_id=1, source_target_pairs={{0,32},{16,48},{32,64},{48,80},{64,96},{80,112},{96,0},{112,16},{1... | collective-permute-start | bytes 884744 | tf_op jit(solution)/shard_map/ppermute | solution.py:43
  73.6 11.4 %collective-permute-start.32 = (bf16[144,1024]{1,0:T(8,128)(2,1)S(1)}, bf16[144,1024]{1,0:T(8,128)(2,1)S(1)}, u32[]{:S(2)}, u32[]{:S(2)}) collective-permute-start(bf16[144,1024]{1,0:T(8,128)(2,1)S(1)} %get-tuple-element.99), channel_id=1, source_target_pairs={{0,64},{16,80},{32,96},{48,112},{64,0},{80,16},{96,32},{112,48},{1... | collective-permute-start | bytes 884744 | tf_op jit(solution)/shard_map/ppermute | solution.py:43
  76.1 13.9 %collective-permute-start.33 = (bf16[144,1024]{1,0:T(8,128)(2,1)S(1)}, bf16[144,1024]{1,0:T(8,128)(2,1)S(1)}, u32[]{:S(2)}, u32[]{:S(2)}) collective-permute-start(bf16[144,1024]{1,0:T(8,128)(2,1)S(1)} %get-tuple-element.100), channel_id=1, source_target_pairs={{0,96},{16,112},{32,0},{48,16},{64,32},{80,48},{96,64},{112,80},{1... | collective-permute-start | bytes 884744 | tf_op jit(solution)/shard_map/ppermute | solution.py:43
  79.9 11.8 %collective-permute-start.23 = (bf16[160,1024]{1,0:T(8,128)(2,1)S(1)}, bf16[160,1024]{1,0:T(8,128)(2,1)S(1)}, u32[]{:S(2)}, u32[]{:S(2)}) collective-permute-start(bf16[160,1024]{1,0:T(8,128)(2,1)S(1)} %get-tuple-element.83), channel_id=1, source_target_pairs={{0,2},{1,3},{2,4},{3,5},{4,6},{5,7},{6,8},{7,9},{8,10},{9,11},{10,... | collective-permute-start | bytes 983048 | tf_op jit(solution)/shard_map/ppermute | solution.py:39
  82.2 9.5 %collective-permute-start.24 = (bf16[160,1024]{1,0:T(8,128)(2,1)S(1)}, bf16[160,1024]{1,0:T(8,128)(2,1)S(1)}, u32[]{:S(2)}, u32[]{:S(2)}) collective-permute-start(bf16[160,1024]{1,0:T(8,128)(2,1)S(1)} %get-tuple-element.84), channel_id=1, source_target_pairs={{0,14},{1,15},{2,0},{3,1},{4,2},{5,3},{6,4},{7,5},{8,6},{9,7},{10,... | collective-permute-start | bytes 983048 | tf_op jit(solution)/shard_map/ppermute | solution.py:39
  91.8 5.8 %collective-permute-start.25 = (f32[1,1024]{1,0:T(1,128)S(1)}, f32[1,1024]{1,0:T(1,128)S(1)}, u32[]{:S(2)}, u32[]{:S(2)}) collective-permute-start(f32[1,1024]{1,0:T(1,128)S(1)} %get-tuple-element.88), channel_id=1, source_target_pairs={{0,1},{1,0},{2,3},{3,2},{4,5},{5,4},{6,7},{7,6},{8,9},{9,8},{10,11... | collective-permute-start | bytes 12296 | tf_op jit(solution)/shard_map/ppermute | solution.py:47
  94.6 6.6 %collective-permute-start.26 = (bf16[72,1024]{1,0:T(8,128)(2,1)S(1)}, bf16[72,1024]{1,0:T(8,128)(2,1)S(1)}, u32[]{:S(2)}, u32[]{:S(2)}) collective-permute-start(bf16[72,1024]{1,0:T(8,128)(2,1)S(1)} %get-tuple-element.90), channel_id=1, source_target_pairs={{0,1},{1,0},{2,3},{3,2},{4,5},{5,4},{6,7},{7,6},{8,9},{9,8},{10,11... | collective-permute-start | bytes 442376 | tf_op jit(solution)/shard_map/ppermute | solution.py:47
  (4 other events, 14.3 us)

commit v8 on v7

--- a/solution.py
+++ b/solution.py
@@ -430,6 +430,7 @@
     terms |= run_images((0, 1, 2, 3, 4), xa, yp, cy, arow, si, (up, down))
     up, down = shift_z(up, 1), shift_z(down, -1)
     got = [swap_core(cap[NY + k]) for k in range(NY)]
+    up, down, *got[1:4] = together(up, down, *got[1:4])
     up, down, side1 = call(
         functools.partial(step_kernel, 0), [message, message, row], 1, [terms[2], terms[6], up, down]
     )

time: 103 us -> 102 us (level)
  starting transfers between devices: 48.1 us -> 46.9 us
    ppermute x6, waiting for transfers between devices: 6.69 us -> 9.02 us  [shift_y(): lax.ppermute(v, 'row', row_pairs(lambda x, y, c: (x, (y + d) % NY, c)))]
    ppermute x16, waiting for transfers between devices: 17.3 us -> 15.5 us  [shift_z(): return lax.ppermute(v, 'col', col_pairs(lambda z, h: ((z + d) % NZ, h)))]
    ppermute x6, starting transfers between devices: 7.99 us -> 6.77 us  [shift_y(): lax.ppermute(v, 'row', row_pairs(lambda x, y, c: (x, (y + d) % NY, c)))]
  transfers between devices with their start and end apart: 35 -> 35, of which waited for: 12 -> 13; matrix products, arithmetic and copies ran while one was open for 3% -> 3% of each run, Pallas kernels for 11% -> 11%
where the time goes in v8:
time: 102 us; the launch traced here: 101 us
  starting transfers between devices  46.9 us (46%)
  waiting for transfers between devices  32.1 us (31%)
  Pallas kernels  16.2 us (16%)
  between operations  2.15 us (2%)
  other arithmetic  2.1 us (2%)
  local copies, waits for them, and re-layouts  1.91 us (2%)
    ppermute x16, starting transfers between devices, shift_z(): return lax.ppermute(v, 'col', col_pairs(lambda z, h: ((z + d) % NZ, h)))  30.1 us
    pallas_call x12, Pallas kernels, call(): pl.pallas_call(kernel, out_shape=out_shape, in_specs=specs, out_specs=[vm...  16.2 us
    ppermute x16, waiting for transfers between devices, shift_z(): return lax.ppermute(v, 'col', col_pairs(lambda z, h: ((z + d) % NZ, h)))  15.5 us
    ppermute x6, waiting for transfers between devices, shift_y(): lax.ppermute(v, 'row', row_pairs(lambda x, y, c: (x, (y + d) % NY, c)))  9.02 us
    ppermute x3, waiting for transfers between devices, swap_xhi(): return lax.ppermute(v, 'col', col_pairs(lambda z, h: (z, 1 - h)))  7.43 us
    ppermute x6, starting transfers between devices, shift_y(): lax.ppermute(v, 'row', row_pairs(lambda x, y, c: (x, (y + d) % NY, c)))  6.77 us
    ppermute x3, starting transfers between devices, swap_xhi(): return lax.ppermute(v, 'col', col_pairs(lambda z, h: (z, 1 - h)))  6.73 us
    ppermute x2, starting transfers between devices, swap_xlo(): return lax.ppermute(v, 'row', row_pairs(lambda x, y, c: (1 - x, y, c)))  2.17 us
  transfers between devices with their start and end apart: 35, of which 13 were waited for; matrix products, arithmetic and copies ran while one was open for 3% of the time, Pallas kernels for 11%

profile of v8, /device:TPU:8, one launch (start us, length us, event | category | flops | bytes accessed | tf_op | source)
XLA Modules:
  0.0 101.5 jit_solution(12194321039387551051)
XLA Ops:
  0.6 3.1 %collective-permute-start = (bf16[72,1024]{1,0:T(8,128)(2,1)}, bf16[72,1024]{1,0:T(8,128)(2,1)S(1)}, u32[]{:S(2)}, u32[]{:S(2)}) collective-permute-start(bf16[72,1024]{1,0:T(8,128)(2,1)} %param.5), channel_id=1, source_target_pairs={{0,1},{1,0},{2,3},{3,2},{4,5},{5,4},{6,7},{7,6},{8,9},{9,8},{10,11... | collective-permute-start | bytes 442376 | tf_op jit(solution)/shard_map/ppermute | solution.py:47
  6.2 3.0 %collective-permute-done = bf16[72,1024]{1,0:T(8,128)(2,1)S(1)} collective-permute-done((bf16[72,1024]{1,0:T(8,128)(2,1)}, bf16[72,1024]{1,0:T(8,128)(2,1)S(1)}, u32[]{:S(2)}, u32[]{:S(2)}) %collective-permute-start) | collective-permute-done | bytes 147488 | tf_op jit(solution)/shard_map/ppermute | solution.py:47
  9.2 2.0 %collective-permute-start.2 = (bf16[144,1024]{1,0:T(8,128)(2,1)S(1)}, bf16[144,1024]{1,0:T(8,128)(2,1)S(1)}, u32[]{:S(2)}, u32[]{:S(2)}) collective-permute-start(bf16[144,1024]{1,0:T(8,128)(2,1)S(1)} %constant_dynamic-update-slice_fusion.refs_0_), channel_id=1, source_target_pairs={{0,2},{1,3},{2,4},{3,5},{4,6},{5,7},{6,8},{7,9},{8,10},{9,11},{10,... | collective-permute-start | bytes 884744 | tf_op jit(solution)/shard_map/ppermute | solution.py:39
  11.2 4.0 %collective-permute-start.1 = (bf16[144,1024]{1,0:T(8,128)(2,1)S(1)}, bf16[144,1024]{1,0:T(8,128)(2,1)S(1)}, u32[]{:S(2)}, u32[]{:S(2)}) collective-permute-start(bf16[144,1024]{1,0:T(8,128)(2,1)S(1)} %constant_dynamic-update-slice_fusion.refs_0_), channel_id=1, source_target_pairs={{0,14},{1,15},{2,0},{3,1},{4,2},{5,3},{6,4},{7,5},{8,6},{9,7},{10,... | collective-permute-start | bytes 884744 | tf_op jit(solution)/shard_map/ppermute | solution.py:39
  15.2 1.7 %collective-permute-start.10 = (bf16[144,1024]{1,0:T(8,128)(2,1)S(1)}, bf16[144,1024]{1,0:T(8,128)(2,1)S(1)}, u32[]{:S(2)}, u32[]{:S(2)}) collective-permute-start(bf16[144,1024]{1,0:T(8,128)(2,1)S(1)} %constant_dynamic-update-slice_fusion.2.refs_0_), channel_id=1, source_target_pairs={{0,32},{16,48},{32,64},{48,80},{64,96},{80,112},{96,0},{112,16},{1... | collective-permute-start | bytes 884744 | tf_op jit(solution)/shard_map/ppermute | solution.py:43
  16.9 3.2 %collective-permute-done.2.refs_4_ = bf16[144,1024]{1,0:T(8,128)(2,1)S(1)} collective-permute-done((bf16[144,1024]{1,0:T(8,128)(2,1)S(1)}, bf16[144,1024]{1,0:T(8,128)(2,1)S(1)}, u32[]{:S(2)}, u32[]{:S(2)}) %collective-permute-start.2) | collective-permute-done | bytes 294944 | tf_op jit(solution)/shard_map/ppermute | solution.py:39
  20.1 3.2 %collective-permute-start.4 = (bf16[144,1024]{1,0:T(8,128)(2,1)S(1)}, bf16[144,1024]{1,0:T(8,128)(2,1)S(1)}, u32[]{:S(2)}, u32[]{:S(2)}) collective-permute-start(bf16[144,1024]{1,0:T(8,128)(2,1)S(1)} %collective-permute-done.1.refs_1_), channel_id=1, source_target_pairs={{0,14},{1,15},{2,0},{3,1},{4,2},{5,3},{6,4},{7,5},{8,6},{9,7},{10,... | collective-permute-start | bytes 884744 | tf_op jit(solution)/shard_map/ppermute | solution.py:39
  23.8 1.6 %collective-permute-start.11 = (bf16[144,1024]{1,0:T(8,128)(2,1)S(1)}, bf16[144,1024]{1,0:T(8,128)(2,1)S(1)}, u32[]{:S(2)}, u32[]{:S(2)}) collective-permute-start(bf16[144,1024]{1,0:T(8,128)(2,1)S(1)} %collective-permute-done.10.refs_3_), channel_id=1, source_target_pairs={{0,32},{16,48},{32,64},{48,80},{64,96},{80,112},{96,0},{112,16},{1... | collective-permute-start | bytes 884744 | tf_op jit(solution)/shard_map/ppermute | solution.py:43
  25.4 2.7 %collective-permute-done.3.refs_3_ = bf16[144,1024]{1,0:T(8,128)(2,1)S(1)} collective-permute-done((bf16[144,1024]{1,0:T(8,128)(2,1)S(1)}, bf16[144,1024]{1,0:T(8,128)(2,1)S(1)}, u32[]{:S(2)}, u32[]{:S(2)}) %collective-permute-start.3) | collective-permute-done | bytes 294944 | tf_op jit(solution)/shard_map/ppermute | solution.py:39
  28.0 3.5 %collective-permute-start.7 = (bf16[144,1024]{1,0:T(8,128)(2,1)S(1)}, bf16[144,1024]{1,0:T(8,128)(2,1)S(1)}, u32[]{:S(2)}, u32[]{:S(2)}) collective-permute-start(bf16[144,1024]{1,0:T(8,128)(2,1)S(1)} %collective-permute-done.4.refs_2_), channel_id=1, source_target_pairs={{0,14},{1,15},{2,0},{3,1},{4,2},{5,3},{6,4},{7,5},{8,6},{9,7},{10,... | collective-permute-start | bytes 884744 | tf_op jit(solution)/shard_map/ppermute | solution.py:39
  33.5 2.3 %collective-permute-done.7.refs_5_ = bf16[144,1024]{1,0:T(8,128)(2,1)S(1)} collective-permute-done((bf16[144,1024]{1,0:T(8,128)(2,1)S(1)}, bf16[144,1024]{1,0:T(8,128)(2,1)S(1)}, u32[]{:S(2)}, u32[]{:S(2)}) %collective-permute-start.7) | collective-permute-done | bytes 294944 | tf_op jit(solution)/shard_map/ppermute | solution.py:39
  35.8 3.8 %collective-permute-start.16 = (bf16[144,512]{1,0:T(8,128)(2,1)S(1)}, bf16[144,512]{1,0:T(8,128)(2,1)S(1)}, u32[]{:S(2)}, u32[]{:S(2)}) collective-permute-start(bf16[144,512]{1,0:T(8,128)(2,1)S(1)} %slice.18), channel_id=1, source_target_pairs={{0,14},{1,15},{2,0},{3,1},{4,2},{5,3},{6,4},{7,5},{8,6},{9,7},{10,... | collective-permute-start | bytes 442376 | tf_op jit(solution)/shard_map/ppermute | solution.py:39
  39.9 1.8 %shard_map.76 = (bf16[1152,1024]{1,0:T(8,128)(2,1)S(1)}, bf16[1024,1152]{1,0:T(8,128)(2,1)S(1)}, f32[1,1024]{1,0:T(1,128)S(1)}, f32[1024,128]{1,0:T(8,128)S(1)}) custom-call(bf16[144,1024]{1,0:T(8,128)(2,1)S(1)} %constant_dynamic-update-slice_fusion.2.refs_0_, bf16[144,1024]{1,0:T(8,128)(2,1)S(1)} %collective-permute-done.9.refs_1_, ...), custom_call_target="tpu_custom_call" | custom-call | flops 67108864 | bytes 7606272 | tf_op jit(solution)/shard_map/pallas_call | solution.py:291
  41.7 2.3 %shard_map.77 = (bf16[1024,1024]{1,0:T(8,128)(2,1)S(1)}, f32[1024,1024]{1,0:T(8,128)S(1)}, f32[1,1024]{1,0:T(1,128)S(1)}) custom-call(bf16[144,1024]{1,0:T(8,128)(2,1)S(1)} %constant_dynamic-update-slice_fusion.refs_0_, bf16[144,1024]{1,0:T(8,128)(2,1)S(1)} %collective-permute-done.1.refs_1_, bf16[144,1024]{1,0:T(8,128)(2,1)S(1)} %collective-permute-done.4.refs_2_, ...), custom_call_target="tpu_custom_call" | custom-call | flops 2147483648 | bytes 10719232 | tf_op jit(solution)/shard_map/pallas_call | solution.py:291
  44.1 2.1 %collective-permute-done.15.left = bf16[144,512]{1,0:T(8,128)(2,1)S(1)} collective-permute-done((bf16[144,512]{1,0:T(8,128)(2,1)S(1)}, bf16[144,512]{1,0:T(8,128)(2,1)S(1)}, u32[]{:S(2)}, u32[]{:S(2)}) %collective-permute-start.15) | collective-permute-done | bytes 147488 | tf_op jit(solution)/shard_map/ppermute | solution.py:39
  46.2 5.3 %shard_map.78 = (bf16[144,1024]{1,0:T(8,128)(2,1)S(1)}, bf16[1024,1024]{1,0:T(8,128)(2,1)S(1)}, bf16[1024,1024]{1,0:T(8,128)(2,1)S(1)}, f32[1,1024]{1,0:T(1,128)...) custom-call(bf16[144,512]{1,0:T(8,128)(2,1)S(1)} %collective-permute, ...), custom_call_target="tpu_custom_call" | custom-call | flops 2415919104 | bytes 14573576 | tf_op jit(solution)/shard_map/pallas_call | solution.py:291
  51.6 3.2 %collective-permute-start.18 = (bf16[160,512]{1,0:T(8,128)(2,1)S(1)}, bf16[160,512]{1,0:T(8,128)(2,1)S(1)}, u32[]{:S(2)}, u32[]{:S(2)}) collective-permute-start(bf16[160,512]{1,0:T(8,128)(2,1)S(1)} %get-tuple-element.72), channel_id=1, source_target_pairs={{0,14},{1,15},{2,0},{3,1},{4,2},{5,3},{6,4},{7,5},{8,6},{9,7},{10,... | collective-permute-start | bytes 491528 | tf_op jit(solution)/shard_map/ppermute | solution.py:39
  55.6 3.4 %shard_map.80 = (f32[144,1024]{1,0:T(8,128)S(1)}, f32[144,1024]{1,0:T(8,128)S(1)}, f32[144,1024]{1,0:T(8,128)S(1)}, f32[144,1024]{1,0:T(8,128)S(1)}, bf16[144,10...) custom-call(bf16[1024,1024]{1,0:T(8,128)(2,1)S(1)} %get-tuple-elemen, ...), custom_call_target="tpu_custom_call" | custom-call | flops 2415919104 | bytes 10395648 | tf_op jit(solution)/shard_map/pallas_call | solution.py:291
  59.3 3.2 %collective-permute-start.20 = (bf16[160,1024]{1,0:T(8,128)(2,1)S(1)}, bf16[160,1024]{1,0:T(8,128)(2,1)S(1)}, u32[]{:S(2)}, u32[]{:S(2)}) collective-permute-start(bf16[160,1024]{1,0:T(8,128)(2,1)S(1)} %get-tuple-element.80.refs_1_), channel_id=1, source_target_pairs={{0,14},{1,15},{2,0},{3,1},{4,2},{5,3},{6,4},{7,5},{8,6},{9,7},{10,... | collective-permute-start | bytes 983048 | tf_op jit(solution)/shard_map/ppermute | solution.py:39
  63.0 1.7 %shard_map.82 = (f32[144,1024]{1,0:T(8,128)S(1)}, f32[144,1024]{1,0:T(8,128)S(1)}, f32[144,1024]{1,0:T(8,128)S(1)}, f32[144,1024]{1,0:T(8,128)S(1)}, f32[144,1024]{1,0:T(8,128)S(1)}) custom-call(bf16[1024,1024]{1,0:T(8,128)(2,1)S(1)} %get-tuple-element.61.xa, bf16[1152,1024]{1,0:T(8,128)(2,1)S(1)} %get-tuple-element.62.yp, ...), custom_call_target="tpu_custom_call" | custom-call | flops 1509949440 | bytes 10166272 | tf_op jit(solution)/shard_map/pallas_call | solution.py:291
  65.0 2.6 %collective-permute-done.19.r_up = bf16[160,1024]{1,0:T(8,128)(2,1)S(1)} collective-permute-done((bf16[160,1024]{1,0:T(8,128)(2,1)S(1)}, bf16[160,1024]{1,0:T(8,128)(2,1)S(1)}, u32[]{:S(2)}, u32[]{:S(2)}) %collective-permute-start.19) | collective-permute-done | bytes 327712 | tf_op jit(solution)/shard_map/ppermute | solution.py:39
  67.7 1.7 %collective-permute-start.24 = (bf16[160,1024]{1,0:T(8,128)(2,1)S(1)}, bf16[160,1024]{1,0:T(8,128)(2,1)S(1)}, u32[]{:S(2)}, u32[]{:S(2)}) collective-permute-start(bf16[160,1024]{1,0:T(8,128)(2,1)S(1)} %get-tuple-element.91.refs_6_), channel_id=1, source_target_pairs={{0,2},{1,3},{2,4},{3,5},{4,6},{5,7},{6,8},{7,9},{8,10},{9,11},{10,... | collective-permute-start | bytes 983048 | tf_op jit(solution)/shard_map/ppermute | solution.py:39
  69.4 1.7 %collective-permute-start.25 = (bf16[160,1024]{1,0:T(8,128)(2,1)S(1)}, bf16[160,1024]{1,0:T(8,128)(2,1)S(1)}, u32[]{:S(2)}, u32[]{:S(2)}) collective-permute-start(bf16[160,1024]{1,0:T(8,128)(2,1)S(1)} %get-tuple-element.92.refs_7_), channel_id=1, source_target_pairs={{0,14},{1,15},{2,0},{3,1},{4,2},{5,3},{6,4},{7,5},{8,6},{9,7},{10,... | collective-permute-start | bytes 983048 | tf_op jit(solution)/shard_map/ppermute | solution.py:39
  71.3 1.8 %collective-permute-start.31 = (bf16[144,1024]{1,0:T(8,128)(2,1)S(1)}, bf16[144,1024]{1,0:T(8,128)(2,1)S(1)}, u32[]{:S(2)}, u32[]{:S(2)}) collective-permute-start(bf16[144,1024]{1,0:T(8,128)(2,1)S(1)} %get-tuple-element.108), channel_id=1, source_target_pairs={{0,32},{16,48},{32,64},{48,80},{64,96},{80,112},{96,0},{112,16},{1... | collective-permute-start | bytes 884744 | tf_op jit(solution)/shard_map/ppermute | solution.py:43
  73.9 2.5 %collective-permute-done.24.r_up = bf16[160,1024]{1,0:T(8,128)(2,1)S(1)} collective-permute-done((bf16[160,1024]{1,0:T(8,128)(2,1)S(1)}, bf16[160,1024]{1,0:T(8,128)(2,1)S(1)}, u32[]{:S(2)}, u32[]{:S(2)}) %collective-permute-start.24) | collective-permute-done | bytes 327712 | tf_op jit(solution)/shard_map/ppermute | solution.py:39
  77.0 1.9 %collective-permute-start.26 = (bf16[160,1024]{1,0:T(8,128)(2,1)S(1)}, bf16[160,1024]{1,0:T(8,128)(2,1)S(1)}, u32[]{:S(2)}, u32[]{:S(2)}) collective-permute-start(bf16[160,1024]{1,0:T(8,128)(2,1)S(1)} %get-tuple-element.93), channel_id=1, source_target_pairs={{0,2},{1,3},{2,4},{3,5},{4,6},{5,7},{6,8},{7,9},{8,10},{9,11},{10,... | collective-permute-start | bytes 983048 | tf_op jit(solution)/shard_map/ppermute | solution.py:39
  78.9 1.5 %collective-permute-start.27 = (bf16[160,1024]{1,0:T(8,128)(2,1)S(1)}, bf16[160,1024]{1,0:T(8,128)(2,1)S(1)}, u32[]{:S(2)}, u32[]{:S(2)}) collective-permute-start(bf16[160,1024]{1,0:T(8,128)(2,1)S(1)} %get-tuple-element.94), channel_id=1, source_target_pairs={{0,14},{1,15},{2,0},{3,1},{4,2},{5,3},{6,4},{7,5},{8,6},{9,7},{10,... | collective-permute-start | bytes 983048 | tf_op jit(solution)/shard_map/ppermute | solution.py:39
  81.1 3.3 %collective-permute-done.32.refs_3_ = bf16[144,1024]{1,0:T(8,128)(2,1)S(1)} collective-permute-done((bf16[144,1024]{1,0:T(8,128)(2,1)S(1)}, bf16[144,1024]{1,0:T(8,128)(2,1)S(1)}, u32[]{:S(2)}, u32[]{:S(2)}) %collective-permute-start.32) | collective-permute-done | bytes 294944 | tf_op jit(solution)/shard_map/ppermute | solution.py:43
  84.5 4.9 %collective-permute-done.33.refs_4_ = bf16[144,1024]{1,0:T(8,128)(2,1)S(1)} collective-permute-done((bf16[144,1024]{1,0:T(8,128)(2,1)S(1)}, bf16[144,1024]{1,0:T(8,128)(2,1)S(1)}, u32[]{:S(2)}, u32[]{:S(2)}) %collective-permute-start.33) | collective-permute-done | bytes 294944 | tf_op jit(solution)/shard_map/ppermute | solution.py:43
  89.5 1.6 %collective-permute-start.34 = (bf16[72,1024]{1,0:T(8,128)(2,1)S(1)}, bf16[72,1024]{1,0:T(8,128)(2,1)S(1)}, u32[]{:S(2)}, u32[]{:S(2)}) collective-permute-start(bf16[72,1024]{1,0:T(8,128)(2,1)S(1)} %slice.23), channel_id=1, source_target_pairs={{0,128},{16,144},{32,160},{48,176},{64,192},{80,208},{96,224},{112... | collective-permute-start | bytes 442376 | tf_op jit(solution)/shard_map/ppermute | solution.py:51
  91.2 2.8 %collective-permute-start.28 = (f32[1,1024]{1,0:T(1,128)S(1)}, f32[1,1024]{1,0:T(1,128)S(1)}, u32[]{:S(2)}, u32[]{:S(2)}) collective-permute-start(f32[1,1024]{1,0:T(1,128)S(1)} %get-tuple-element.98), channel_id=1, source_target_pairs={{0,1},{1,0},{2,3},{3,2},{4,5},{5,4},{6,7},{7,6},{8,9},{9,8},{10,11... | collective-permute-start | bytes 12296 | tf_op jit(solution)/shard_map/ppermute | solution.py:47
  97.7 3.0 %collective-permute-done.29 = bf16[72,1024]{1,0:T(8,128)(2,1)S(1)} collective-permute-done((bf16[72,1024]{1,0:T(8,128)(2,1)S(1)}, bf16[72,1024]{1,0:T(8,128)(2,1)S(1)}, u32[]{:S(2)}, u32[]{:S(2)}) %collective-permute-start.29) | collective-permute-done | bytes 147488 | tf_op jit(solution)/shard_map/ppermute | solution.py:47
  (62 shorter events, 12.8 us)
Async XLA Ops:
  0.6 8.5 %collective-permute-start = (bf16[72,1024]{1,0:T(8,128)(2,1)}, bf16[72,1024]{1,0:T(8,128)(2,1)S(1)}, u32[]{:S(2)}, u32[]{:S(2)}) collective-permute-start(bf16[72,1024]{1,0:T(8,128)(2,1)} %param.5), channel_id=1, source_target_pairs={{0,1},{1,0},{2,3},{3,2},{4,5},{5,4},{6,7},{7,6},{8,9},{9,8},{10,11... | collective-permute-start | bytes 442376 | tf_op jit(solution)/shard_map/ppermute | solution.py:47
  3.7 11.5 %collective-permute-start.5 = (bf16[72,1024]{1,0:T(8,128)(2,1)}, bf16[72,1024]{1,0:T(8,128)(2,1)S(1)}, u32[]{:S(2)}, u32[]{:S(2)}) collective-permute-start(bf16[72,1024]{1,0:T(8,128)(2,1)} %param.6), channel_id=1, source_target_pairs={{0,128},{16,144},{32,160},{48,176},{64,192},{80,208},{96,224},{112... | collective-permute-start | bytes 442376 | tf_op jit(solution)/shard_map/ppermute | solution.py:51
  9.2 10.9 %collective-permute-start.2 = (bf16[144,1024]{1,0:T(8,128)(2,1)S(1)}, bf16[144,1024]{1,0:T(8,128)(2,1)S(1)}, u32[]{:S(2)}, u32[]{:S(2)}) collective-permute-start(bf16[144,1024]{1,0:T(8,128)(2,1)S(1)} %constant_dynamic-update-slice_fusion.refs_0_), channel_id=1, source_target_pairs={{0,2},{1,3},{2,4},{3,5},{4,6},{5,7},{6,8},{7,9},{8,10},{9,11},{10,... | collective-permute-start | bytes 884744 | tf_op jit(solution)/shard_map/ppermute | solution.py:39
  11.2 8.9 %collective-permute-start.1 = (bf16[144,1024]{1,0:T(8,128)(2,1)S(1)}, bf16[144,1024]{1,0:T(8,128)(2,1)S(1)}, u32[]{:S(2)}, u32[]{:S(2)}) collective-permute-start(bf16[144,1024]{1,0:T(8,128)(2,1)S(1)} %constant_dynamic-update-slice_fusion.refs_0_), channel_id=1, source_target_pairs={{0,14},{1,15},{2,0},{3,1},{4,2},{5,3},{6,4},{7,5},{8,6},{9,7},{10,... | collective-permute-start | bytes 884744 | tf_op jit(solution)/shard_map/ppermute | solution.py:39
  15.2 8.6 %collective-permute-start.10 = (bf16[144,1024]{1,0:T(8,128)(2,1)S(1)}, bf16[144,1024]{1,0:T(8,128)(2,1)S(1)}, u32[]{:S(2)}, u32[]{:S(2)}) collective-permute-start(bf16[144,1024]{1,0:T(8,128)(2,1)S(1)} %constant_dynamic-update-slice_fusion.2.refs_0_), channel_id=1, source_target_pairs={{0,32},{16,48},{32,64},{48,80},{64,96},{80,112},{96,0},{112,16},{1... | collective-permute-start | bytes 884744 | tf_op jit(solution)/shard_map/ppermute | solution.py:43
  16.9 8.5 %collective-permute-start.6 = (bf16[144,1024]{1,0:T(8,128)(2,1)S(1)}, bf16[144,1024]{1,0:T(8,128)(2,1)S(1)}, u32[]{:S(2)}, u32[]{:S(2)}) collective-permute-start(bf16[144,1024]{1,0:T(8,128)(2,1)S(1)} %constant_dynamic-update-slice_fusion.2.refs_0_), channel_id=1, source_target_pairs={{0,16},{16,0},{32,48},{48,32},{64,80},{80,64},{96,112},{112,96},{1... | collective-permute-start | bytes 884744 | tf_op jit(solution)/shard_map/ppermute | solution.py:55
  20.1 7.9 %collective-permute-start.3 = (bf16[144,1024]{1,0:T(8,128)(2,1)S(1)}, bf16[144,1024]{1,0:T(8,128)(2,1)S(1)}, u32[]{:S(2)}, u32[]{:S(2)}) collective-permute-start(bf16[144,1024]{1,0:T(8,128)(2,1)S(1)} %collective-permute-done.2.refs_4_), channel_id=1, source_target_pairs={{0,2},{1,3},{2,4},{3,5},{4,6},{5,7},{6,8},{7,9},{8,10},{9,11},{10,... | collective-permute-start | bytes 884744 | tf_op jit(solution)/shard_map/ppermute | solution.py:39
  20.1 7.9 %collective-permute-start.4 = (bf16[144,1024]{1,0:T(8,128)(2,1)S(1)}, bf16[144,1024]{1,0:T(8,128)(2,1)S(1)}, u32[]{:S(2)}, u32[]{:S(2)}) collective-permute-start(bf16[144,1024]{1,0:T(8,128)(2,1)S(1)} %collective-permute-done.1.refs_1_), channel_id=1, source_target_pairs={{0,14},{1,15},{2,0},{3,1},{4,2},{5,3},{6,4},{7,5},{8,6},{9,7},{10,... | collective-permute-start | bytes 884744 | tf_op jit(solution)/shard_map/ppermute | solution.py:39
  23.3 8.2 %collective-permute-start.9 = (bf16[144,1024]{1,0:T(8,128)(2,1)S(1)}, bf16[144,1024]{1,0:T(8,128)(2,1)S(1)}, u32[]{:S(2)}, u32[]{:S(2)}) collective-permute-start(bf16[144,1024]{1,0:T(8,128)(2,1)S(1)} %constant_dynamic-update-slice_fusion.2.refs_0_), channel_id=1, source_target_pairs={{0,96},{16,112},{32,0},{48,16},{64,32},{80,48},{96,64},{112,80},{1... | collective-permute-start | bytes 884744 | tf_op jit(solution)/shard_map/ppermute | solution.py:43
  23.8 8.3 %collective-permute-start.11 = (bf16[144,1024]{1,0:T(8,128)(2,1)S(1)}, bf16[144,1024]{1,0:T(8,128)(2,1)S(1)}, u32[]{:S(2)}, u32[]{:S(2)}) collective-permute-start(bf16[144,1024]{1,0:T(8,128)(2,1)S(1)} %collective-permute-done.10.refs_3_), channel_id=1, source_target_pairs={{0,32},{16,48},{32,64},{48,80},{64,96},{80,112},{96,0},{112,16},{1... | collective-permute-start | bytes 884744 | tf_op jit(solution)/shard_map/ppermute | solution.py:43
  28.0 7.7 %collective-permute-start.7 = (bf16[144,1024]{1,0:T(8,128)(2,1)S(1)}, bf16[144,1024]{1,0:T(8,128)(2,1)S(1)}, u32[]{:S(2)}, u32[]{:S(2)}) collective-permute-start(bf16[144,1024]{1,0:T(8,128)(2,1)S(1)} %collective-permute-done.4.refs_2_), channel_id=1, source_target_pairs={{0,14},{1,15},{2,0},{3,1},{4,2},{5,3},{6,4},{7,5},{8,6},{9,7},{10,... | collective-permute-start | bytes 884744 | tf_op jit(solution)/shard_map/ppermute | solution.py:39
  31.5 8.0 %collective-permute-start.8 = (bf16[144,1024]{1,0:T(8,128)(2,1)S(1)}, bf16[144,1024]{1,0:T(8,128)(2,1)S(1)}, u32[]{:S(2)}, u32[]{:S(2)}) collective-permute-start(bf16[144,1024]{1,0:T(8,128)(2,1)S(1)} %collective-permute-done.3.refs_3_), channel_id=1, source_target_pairs={{0,2},{1,3},{2,4},{3,5},{4,6},{5,7},{6,8},{7,9},{8,10},{9,11},{10,... | collective-permute-start | bytes 884744 | tf_op jit(solution)/shard_map/ppermute | solution.py:39
  31.5 8.3 %collective-permute-start.14 = (bf16[144,1024]{1,0:T(8,128)(2,1)S(1)}, bf16[144,1024]{1,0:T(8,128)(2,1)S(1)}, u32[]{:S(2)}, u32[]{:S(2)}) collective-permute-start(bf16[144,1024]{1,0:T(8,128)(2,1)S(1)} %collective-permute-done.10.refs_3_), channel_id=1, source_target_pairs={{0,16},{16,0},{32,48},{48,32},{64,80},{80,64},{96,112},{112,96},{1... | collective-permute-start | bytes 884744 | tf_op jit(solution)/shard_map/ppermute | solution.py:55
  31.6 8.3 %collective-permute-start.12 = (bf16[144,1024]{1,0:T(8,128)(2,1)S(1)}, bf16[144,1024]{1,0:T(8,128)(2,1)S(1)}, u32[]{:S(2)}, u32[]{:S(2)}) collective-permute-start(bf16[144,1024]{1,0:T(8,128)(2,1)S(1)} %collective-permute-done.9.refs_1_), channel_id=1, source_target_pairs={{0,16},{16,0},{32,48},{48,32},{64,80},{80,64},{96,112},{112,96},{1... | collective-permute-start | bytes 884744 | tf_op jit(solution)/shard_map/ppermute | solution.py:55
  32.1 7.8 %collective-permute-start.13 = (bf16[144,1024]{1,0:T(8,128)(2,1)S(1)}, bf16[144,1024]{1,0:T(8,128)(2,1)S(1)}, u32[]{:S(2)}, u32[]{:S(2)}) collective-permute-start(bf16[144,1024]{1,0:T(8,128)(2,1)S(1)} %collective-permute-done.11.refs_2_), channel_id=1, source_target_pairs={{0,16},{16,0},{32,48},{48,32},{64,80},{80,64},{96,112},{112,96},{1... | collective-permute-start | bytes 884744 | tf_op jit(solution)/shard_map/ppermute | solution.py:55
  35.8 8.3 %collective-permute-start.16 = (bf16[144,512]{1,0:T(8,128)(2,1)S(1)}, bf16[144,512]{1,0:T(8,128)(2,1)S(1)}, u32[]{:S(2)}, u32[]{:S(2)}) collective-permute-start(bf16[144,512]{1,0:T(8,128)(2,1)S(1)} %slice.18), channel_id=1, source_target_pairs={{0,14},{1,15},{2,0},{3,1},{4,2},{5,3},{6,4},{7,5},{8,6},{9,7},{10,... | collective-permute-start | bytes 442376 | tf_op jit(solution)/shard_map/ppermute | solution.py:39
  39.6 6.6 %collective-permute-start.15 = (bf16[144,512]{1,0:T(8,128)(2,1)S(1)}, bf16[144,512]{1,0:T(8,128)(2,1)S(1)}, u32[]{:S(2)}, u32[]{:S(2)}) collective-permute-start(bf16[144,512]{1,0:T(8,128)(2,1)S(1)} %slice.17), channel_id=1, source_target_pairs={{0,2},{1,3},{2,4},{3,5},{4,6},{5,7},{6,8},{7,9},{8,10},{9,11},{10,... | collective-permute-start | bytes 442376 | tf_op jit(solution)/shard_map/ppermute | solution.py:39
  51.5 7.6 %collective-permute-start.17 = (bf16[160,512]{1,0:T(8,128)(2,1)S(1)}, bf16[160,512]{1,0:T(8,128)(2,1)S(1)}, u32[]{:S(2)}, u32[]{:S(2)}) collective-permute-start(bf16[160,512]{1,0:T(8,128)(2,1)S(1)} %get-tuple-element.71), channel_id=1, source_target_pairs={{0,2},{1,3},{2,4},{3,5},{4,6},{5,7},{6,8},{7,9},{8,10},{9,11},{10,... | collective-permute-start | bytes 491528 | tf_op jit(solution)/shard_map/ppermute | solution.py:39
  51.6 7.5 %collective-permute-start.18 = (bf16[160,512]{1,0:T(8,128)(2,1)S(1)}, bf16[160,512]{1,0:T(8,128)(2,1)S(1)}, u32[]{:S(2)}, u32[]{:S(2)}) collective-permute-start(bf16[160,512]{1,0:T(8,128)(2,1)S(1)} %get-tuple-element.72), channel_id=1, source_target_pairs={{0,14},{1,15},{2,0},{3,1},{4,2},{5,3},{6,4},{7,5},{8,6},{9,7},{10,... | collective-permute-start | bytes 491528 | tf_op jit(solution)/shard_map/ppermute | solution.py:39
  59.2 8.4 %collective-permute-start.19 = (bf16[160,1024]{1,0:T(8,128)(2,1)S(1)}, bf16[160,1024]{1,0:T(8,128)(2,1)S(1)}, u32[]{:S(2)}, u32[]{:S(2)}) collective-permute-start(bf16[160,1024]{1,0:T(8,128)(2,1)S(1)} %get-tuple-element.79.refs_0_), channel_id=1, source_target_pairs={{0,2},{1,3},{2,4},{3,5},{4,6},{5,7},{6,8},{7,9},{8,10},{9,11},{10,... | collective-permute-start | bytes 983048 | tf_op jit(solution)/shard_map/ppermute | solution.py:39
  59.3 8.3 %collective-permute-start.20 = (bf16[160,1024]{1,0:T(8,128)(2,1)S(1)}, bf16[160,1024]{1,0:T(8,128)(2,1)S(1)}, u32[]{:S(2)}, u32[]{:S(2)}) collective-permute-start(bf16[160,1024]{1,0:T(8,128)(2,1)S(1)} %get-tuple-element.80.refs_1_), channel_id=1, source_target_pairs={{0,14},{1,15},{2,0},{3,1},{4,2},{5,3},{6,4},{7,5},{8,6},{9,7},{10,... | collective-permute-start | bytes 983048 | tf_op jit(solution)/shard_map/ppermute | solution.py:39
  67.7 8.7 %collective-permute-start.24 = (bf16[160,1024]{1,0:T(8,128)(2,1)S(1)}, bf16[160,1024]{1,0:T(8,128)(2,1)S(1)}, u32[]{:S(2)}, u32[]{:S(2)}) collective-permute-start(bf16[160,1024]{1,0:T(8,128)(2,1)S(1)} %get-tuple-element.91.refs_6_), channel_id=1, source_target_pairs={{0,2},{1,3},{2,4},{3,5},{4,6},{5,7},{6,8},{7,9},{8,10},{9,11},{10,... | collective-permute-start | bytes 983048 | tf_op jit(solution)/shard_map/ppermute | solution.py:39
  69.4 7.5 %collective-permute-start.25 = (bf16[160,1024]{1,0:T(8,128)(2,1)S(1)}, bf16[160,1024]{1,0:T(8,128)(2,1)S(1)}, u32[]{:S(2)}, u32[]{:S(2)}) collective-permute-start(bf16[160,1024]{1,0:T(8,128)(2,1)S(1)} %get-tuple-element.92.refs_7_), channel_id=1, source_target_pairs={{0,14},{1,15},{2,0},{3,1},{4,2},{5,3},{6,4},{7,5},{8,6},{9,7},{10,... | collective-permute-start | bytes 983048 | tf_op jit(solution)/shard_map/ppermute | solution.py:39
  71.1 7.8 %collective-permute-start.30 = (bf16[144,1024]{1,0:T(8,128)(2,1)S(1)}, bf16[144,1024]{1,0:T(8,128)(2,1)S(1)}, u32[]{:S(2)}, u32[]{:S(2)}) collective-permute-start(bf16[144,1024]{1,0:T(8,128)(2,1)S(1)} %get-tuple-element.78._cap), channel_id=1, source_target_pairs={{0,16},{16,0},{32,48},{48,32},{64,80},{80,64},{96,112},{112,96},{1... | collective-permute-start | bytes 884744 | tf_op jit(solution)/shard_map/ppermute | solution.py:55
  71.3 9.9 %collective-permute-start.31 = (bf16[144,1024]{1,0:T(8,128)(2,1)S(1)}, bf16[144,1024]{1,0:T(8,128)(2,1)S(1)}, u32[]{:S(2)}, u32[]{:S(2)}) collective-permute-start(bf16[144,1024]{1,0:T(8,128)(2,1)S(1)} %get-tuple-element.108), channel_id=1, source_target_pairs={{0,32},{16,48},{32,64},{48,80},{64,96},{80,112},{96,0},{112,16},{1... | collective-permute-start | bytes 884744 | tf_op jit(solution)/shard_map/ppermute | solution.py:43
  73.1 11.4 %collective-permute-start.32 = (bf16[144,1024]{1,0:T(8,128)(2,1)S(1)}, bf16[144,1024]{1,0:T(8,128)(2,1)S(1)}, u32[]{:S(2)}, u32[]{:S(2)}) collective-permute-start(bf16[144,1024]{1,0:T(8,128)(2,1)S(1)} %get-tuple-element.109), channel_id=1, source_target_pairs={{0,64},{16,80},{32,96},{48,112},{64,0},{80,16},{96,32},{112,48},{1... | collective-permute-start | bytes 884744 | tf_op jit(solution)/shard_map/ppermute | solution.py:43
  76.4 13.0 %collective-permute-start.33 = (bf16[144,1024]{1,0:T(8,128)(2,1)S(1)}, bf16[144,1024]{1,0:T(8,128)(2,1)S(1)}, u32[]{:S(2)}, u32[]{:S(2)}) collective-permute-start(bf16[144,1024]{1,0:T(8,128)(2,1)S(1)} %get-tuple-element.110), channel_id=1, source_target_pairs={{0,96},{16,112},{32,0},{48,16},{64,32},{80,48},{96,64},{112,80},{1... | collective-permute-start | bytes 884744 | tf_op jit(solution)/shard_map/ppermute | solution.py:43
  77.0 14.1 %collective-permute-start.26 = (bf16[160,1024]{1,0:T(8,128)(2,1)S(1)}, bf16[160,1024]{1,0:T(8,128)(2,1)S(1)}, u32[]{:S(2)}, u32[]{:S(2)}) collective-permute-start(bf16[160,1024]{1,0:T(8,128)(2,1)S(1)} %get-tuple-element.93), channel_id=1, source_target_pairs={{0,2},{1,3},{2,4},{3,5},{4,6},{5,7},{6,8},{7,9},{8,10},{9,11},{10,... | collective-permute-start | bytes 983048 | tf_op jit(solution)/shard_map/ppermute | solution.py:39
  78.9 12.3 %collective-permute-start.27 = (bf16[160,1024]{1,0:T(8,128)(2,1)S(1)}, bf16[160,1024]{1,0:T(8,128)(2,1)S(1)}, u32[]{:S(2)}, u32[]{:S(2)}) collective-permute-start(bf16[160,1024]{1,0:T(8,128)(2,1)S(1)} %get-tuple-element.94), channel_id=1, source_target_pairs={{0,14},{1,15},{2,0},{3,1},{4,2},{5,3},{6,4},{7,5},{8,6},{9,7},{10,... | collective-permute-start | bytes 983048 | tf_op jit(solution)/shard_map/ppermute | solution.py:39
  89.5 5.4 %collective-permute-start.34 = (bf16[72,1024]{1,0:T(8,128)(2,1)S(1)}, bf16[72,1024]{1,0:T(8,128)(2,1)S(1)}, u32[]{:S(2)}, u32[]{:S(2)}) collective-permute-start(bf16[72,1024]{1,0:T(8,128)(2,1)S(1)} %slice.23), channel_id=1, source_target_pairs={{0,128},{16,144},{32,160},{48,176},{64,192},{80,208},{96,224},{112... | collective-permute-start | bytes 442376 | tf_op jit(solution)/shard_map/ppermute | solution.py:51
  91.2 5.9 %collective-permute-start.28 = (f32[1,1024]{1,0:T(1,128)S(1)}, f32[1,1024]{1,0:T(1,128)S(1)}, u32[]{:S(2)}, u32[]{:S(2)}) collective-permute-start(f32[1,1024]{1,0:T(1,128)S(1)} %get-tuple-element.98), channel_id=1, source_target_pairs={{0,1},{1,0},{2,3},{3,2},{4,5},{5,4},{6,7},{7,6},{8,9},{9,8},{10,11... | collective-permute-start | bytes 12296 | tf_op jit(solution)/shard_map/ppermute | solution.py:47
  94.1 6.6 %collective-permute-start.29 = (bf16[72,1024]{1,0:T(8,128)(2,1)S(1)}, bf16[72,1024]{1,0:T(8,128)(2,1)S(1)}, u32[]{:S(2)}, u32[]{:S(2)}) collective-permute-start(bf16[72,1024]{1,0:T(8,128)(2,1)S(1)} %get-tuple-element.100), channel_id=1, source_target_pairs={{0,1},{1,0},{2,3},{3,2},{4,5},{5,4},{6,7},{7,6},{8,9},{9,8},{10,11... | collective-permute-start | bytes 442376 | tf_op jit(solution)/shard_map/ppermute | solution.py:47
  (4 other events, 10.9 us)
